TPU v7x, 512 devices: a whole 4x8x8 slice. The times are simulated.
512 devices in a mesh: dom: 32 (over z_lo, y, core), band: 16 (over z_hi, x).
Axes of the slice: x: 4, y: 8, z: 8 (z_hi: 4, z_lo: 2; z = z_hi * 2 + z_lo), core: 2. Of those that a mesh axis runs over, the one named last changes fastest.
Arguments:
- bands: bfloat16 [128, 192, 16, 128], P('band', 'dom'), may hold values from -6 to 6
- potential: float32 [192, 16, 128], P('dom'), may hold values from -3 to 1
- projectors: bfloat16 [192, 16, 32, 4, 128], P('dom'), may hold values from -0.14941406 to 0.14941406
- atom_ids: int32 [64, 32], P('dom'), may hold values from 0 to 1023, as said below
- strength: float32 [1024, 4], replicated, may hold values from 0.5 to 3
- rotation: bfloat16 [128, 128], replicated, may hold values from -0.5 to 0.5
Outputs:
- rotated: bfloat16 [128, 192, 16, 128], P('band', 'dom')
Inputs may be any that keep to these rules, and one draw needn't show every extreme that they name: `atom_ids`: block g lies in slab g // 2, and atom a is owned by slab a // 32. Each block names 32 distinct atoms, 16 owned by its own slab and the others owned by the slab just before or just after it in the periodic order; every atom is named by some block of its own slab.
All inputs are finite; a program needn't handle non-finite values.
Results may differ from a plain program's by a relative error of at most 0.005.
The roundings to bfloat16 on the way count: a program that leaves them out, or rounds other values in their place, can miss the bound.
Values may be sent and summed in bfloat16 or wider, within the bound.
No kernel may reach another device: no remote copies, remote signals or barrier semaphores. Data moves between devices by JAX's collectives and lax.ppermute only.
A program may use at most 64 MiB of HBM per device.

v0:
```python
import jax
import jax.numpy as jnp
from jax import lax
from jax.sharding import PartitionSpec as P

STENCIL = [
    -5369.0 / 1800.0,
    12.0 / 7.0,
    -15.0 / 56.0,
    10.0 / 189.0,
    -1.0 / 112.0,
    2.0 / 1925.0,
    -1.0 / 16632.0,
]
kinetic_scale = 0.5 / 0.49
centre = 12.0
half_width = 11.0


def passed_along(block, axis, distance):
    devices = range(lax.axis_size(axis))
    route = [((i - distance) % len(devices), i) for i in devices]
    return lax.ppermute(block, axis, route)


def padded_2(cells, sides, width):
    for axis, dim in sides:
        count = lax.axis_size(axis)
        head = lax.slice_in_dim(cells, 0, width, axis=dim)
        tail = lax.slice_in_dim(cells, cells.shape[dim] - width, cells.shape[dim], axis=dim)
        cells = jnp.concatenate(
            [
                lax.ppermute(tail, axis, [(i, (i + 1) % count) for i in range(count)]),
                cells,
                lax.ppermute(head, axis, [((i + 1) % count, i) for i in range(count)]),
            ],
            axis=dim,
        )
    return cells


def laplace_slab(padded, thickness):
    middle = padded[:, 6 : 6 + thickness]
    result = 3.0 * STENCIL[0] * middle
    for offset in range(1, 7):
        beside = (
            padded[:, 6 + offset : 6 + offset + thickness]
            + padded[:, 6 - offset : 6 - offset + thickness]
        )
        beside = beside + jnp.roll(middle, offset, 2) + jnp.roll(middle, -offset, 2)
        beside = beside + jnp.roll(middle, offset, 3) + jnp.roll(middle, -offset, 3)
        result = result + STENCIL[offset] * beside
    return result


def local(bands, potential, projectors, atom_ids, strength, rotation):
    local_bands, thickness, rows_total, depth = bands.shape
    blocks, slot_count = atom_ids.shape
    atom_count, proj_count = strength.shape
    block_rows = rows_total // blocks
    projector_view = projectors.reshape(
        thickness, blocks, block_rows, slot_count, proj_count, depth
    )
    slot_atoms = atom_ids.reshape(-1)
    slot_strength = strength[slot_atoms].reshape(blocks, slot_count, proj_count)
    dom_count = lax.axis_size("dom")
    per_owner = atom_count // dom_count
    dom_index = lax.axis_index("dom")
    owners = slot_atoms // per_owner
    relative = (owners - dom_index + 1 + dom_count) % dom_count
    local_rows = relative * per_owner + slot_atoms % per_owner

    def reduce_atoms(partial_value):
        atom_table = jax.ops.segment_sum(partial_value, local_rows, num_segments=3 * per_owner)
        below_part = atom_table[:per_owner]
        middle = atom_table[per_owner : 2 * per_owner]
        above_part = atom_table[2 * per_owner :]
        owned_sums = middle + passed_along(above_part, "dom", 1)
        owned_sums = owned_sums + passed_along(below_part, "dom", -1)
        neighbourhood = padded_2(owned_sums, (("dom", 0),), per_owner)
        return neighbourhood[local_rows]

    def apply_hamiltonian(vectors):
        padded = padded_2(vectors, (("dom", 1),), 6).astype(jnp.float32)
        values = padded[:, 6 : 6 + thickness]
        kinetic = -kinetic_scale * laplace_slab(padded, thickness)
        view = vectors.reshape(local_bands, thickness, blocks, block_rows, depth)
        partial_value = jnp.einsum(
            "xjwspz,bxjwz->jspb", projector_view, view, preferred_element_type=jnp.float32
        )
        partial_value = partial_value.reshape(blocks * slot_count, proj_count * local_bands)
        totals = reduce_atoms(partial_value).reshape(blocks, slot_count, proj_count, local_bands)
        weighted = (totals * slot_strength[..., None]).astype(jnp.bfloat16)
        nonlocal_term = jnp.einsum(
            "xjwspz,jspb->bxjwz", projector_view, weighted, preferred_element_type=jnp.float32
        )
        nonlocal_term = nonlocal_term.reshape(local_bands, thickness, rows_total, depth)
        return kinetic + potential[None] * values + nonlocal_term

    start_values = bands.astype(jnp.float32)
    first = ((apply_hamiltonian(bands) - centre * start_values) / half_width).astype(jnp.bfloat16)
    first_values = first.astype(jnp.float32)
    filtered = (
        2.0 * (apply_hamiltonian(first) - centre * first_values) / half_width - start_values
    ).astype(jnp.bfloat16)
    flat = filtered.reshape(local_bands, thickness * rows_total * depth)
    my_columns = lax.dynamic_slice_in_dim(
        rotation, lax.axis_index("band") * local_bands, local_bands, 1
    )
    summed = jnp.dot(
        my_columns.T,
        lax.all_gather(flat, "band", axis=0, tiled=True),
        preferred_element_type=jnp.float32,
    )
    rotated = summed.astype(jnp.bfloat16).reshape(bands.shape)
    return rotated


def solution(mesh):
    placed = (
        P("band", "dom", None, None),
        P("dom", None, None),
        P("dom", None, None, None, None),
        P("dom", None),
        P(),
        P(),
    )
    return jax.shard_map(
        local, mesh=mesh, in_specs=placed, out_specs=P("band", "dom", None, None), check_vma=False
    )
```

profile of v0, /device:TPU:1, one launch (start us, length us, event | category | flops | bytes accessed | tf_op | source)
XLA Modules:
  0.0 179.9 jit_solution(6429178628561802797)
XLA Ops:
  6.5 8.9 %collective-permute-start.1 = (bf16[8,6,16,128]{3,2,1,0:T(8,128)(2,1)}, bf16[8,6,16,128]{3,2,1,0:T(8,128)(2,1)}, u32[]{:S(2)}, u32[]{:S(2)}) collective-permute-start(bf16[8,6,16,128]{3,2,1,0:T(8,128)(2,1)} %param.6), channel_id=1, source_target_pairs={{16,0},{32,16},{48,32},{64,48},{80,64},{96,80},{112,96},{128,112},... | collective-permute-start | bytes 589832 | tf_op jit(solution)/shard_map/ppermute | solution.py:35
  15.5 1.9 %collective-permute-start = (bf16[8,6,16,128]{3,2,1,0:T(8,128)(2,1)}, bf16[8,6,16,128]{3,2,1,0:T(8,128)(2,1)}, u32[]{:S(2)}, u32[]{:S(2)}) collective-permute-start(bf16[8,6,16,128]{3,2,1,0:T(8,128)(2,1)} %param.6), channel_id=1, source_target_pairs={{0,16},{16,32},{32,48},{48,64},{64,80},{80,96},{96,112},{112,128},... | collective-permute-start | bytes 589832 | tf_op jit(solution)/shard_map/ppermute | solution.py:33
  18.2 4.1 %fusion.14 = f32[2,32,4,8]{1,3,2,0:T(8,128)S(1)} fusion(bf16[6,2,8,32,4,128]{5,4,3,2,1,0:T(4,128)(2,1)} %bitcast.56, bf16[8,6,2,8,128,1]{4,3,2,1,0,5:T(8,128)(2,1)} %bitcast.60), kind=kOutput, calls=%fused_computation.16 | convolution fusion | flops 25165824 | bytes 3350528 | tf_op jit(solution)/shard_map/xjwspz,bxjwz->jspb/dot_general | solution.py:88
  23.4 1.9 %collective-permute-start.2 = (f32[32,32]{1,0:T(8,128)S(1)}, f32[32,32]{1,0:T(8,128)S(1)}, u32[]{:S(2)}, u32[]{:S(2)}) collective-permute-start(f32[32,32]{1,0:T(8,128)S(1)} %get-tuple-element.105), channel_id=1, source_target_pairs={{496,0},{0,16},{16,32},{32,48},{48,64},{64,80},{80,96},{96,112},{1... | collective-permute-start | bytes 12296 | tf_op jit(solution)/shard_map/ppermute | solution.py:23
  25.3 2.4 %collective-permute-start.3 = (f32[32,32]{1,0:T(8,128)S(1)}, f32[32,32]{1,0:T(8,128)S(1)}, u32[]{:S(2)}, u32[]{:S(2)}) collective-permute-start(f32[32,32]{1,0:T(8,128)S(1)} %get-tuple-element.106), channel_id=1, source_target_pairs={{16,0},{32,16},{48,32},{64,48},{80,64},{96,80},{112,96},{128,112},... | collective-permute-start | bytes 12296 | tf_op jit(solution)/shard_map/ppermute | solution.py:23
  27.8 2.9 %collective-permute-done.3 = f32[32,32]{1,0:T(8,128)S(1)} collective-permute-done((f32[32,32]{1,0:T(8,128)S(1)}, f32[32,32]{1,0:T(8,128)S(1)}, u32[]{:S(2)}, u32[]{:S(2)}) %collective-permute-start.3) | collective-permute-done | bytes 4128 | tf_op jit(solution)/shard_map/ppermute | solution.py:23
  30.7 4.2 %collective-permute-start.5 = (f32[32,32]{1,0:T(8,128)S(1)}, f32[32,32]{1,0:T(8,128)S(1)}, u32[]{:S(2)}, u32[]{:S(2)}) collective-permute-start(f32[32,32]{1,0:T(8,128)S(1)} %fusion.114), channel_id=1, source_target_pairs={{16,0},{32,16},{48,32},{64,48},{80,64},{96,80},{112,96},{128,112},... | collective-permute-start | bytes 12296 | tf_op jit(solution)/shard_map/ppermute | solution.py:35
  34.9 1.9 %collective-permute-start.4 = (f32[32,32]{1,0:T(8,128)S(1)}, f32[32,32]{1,0:T(8,128)S(1)}, u32[]{:S(2)}, u32[]{:S(2)}) collective-permute-start(f32[32,32]{1,0:T(8,128)S(1)} %fusion.114), channel_id=1, source_target_pairs={{0,16},{16,32},{32,48},{48,64},{64,80},{80,96},{96,112},{112,128},... | collective-permute-start | bytes 12296 | tf_op jit(solution)/shard_map/ppermute | solution.py:33
  37.9 1.6 gather_fusion.1
  39.6 1.7 collective-permute-done.4
  43.1 1.1 maximum_convert_fusion
  47.6 3.1 %fusion.22 = bf16[8,6,16,128]{3,2,1,0:T(8,128)(2,1)S(1)} fusion(bf16[8,6,16,128]{3,2,1,0:T(8,128)(2,1)S(1)} %copy-done.2, f32[8,18,16,128]{3,2,1,0:T(8,128)S(1)} %maximum_convert_fusion, f32[8,6,15,128]{3,2,1,0:T(8,128)S(1)} %get-tuple-element.100, f32[8,6,1,128]{3,2,1,0:T(1,128)S(1)} %get-tuple-element.102, f32[8,6,1,128]{3,2,1,0:T(1,128)S(1)} %get-tuple-element.101, ...), kind=kLoop, calls=%fused_computation.24 | loop fusion | flops 7471104 | bytes 15384576 | tf_op jit(solution)/shard_map/convert_element_type | solution.py:101
  50.8 2.1 %fusion.17 = f32[2,32,4,8]{1,3,2,0:T(8,128)S(1)} fusion(bf16[6,2,8,32,4,128]{5,4,3,2,1,0:T(4,128)(2,1)S(1)} %bitcast.58, bf16[8,6,2,8,128,1]{4,3,2,1,0,5:T(8,128)(2,1)S(1)} %bitcast.61), kind=kOutput, calls=%fused_computation.17 | convolution fusion | flops 25165824 | bytes 3350528 | tf_op jit(solution)/shard_map/xjwspz,bxjwz->jspb/dot_general | solution.py:88
  54.0 1.9 %collective-permute-start.8 = (f32[32,32]{1,0:T(8,128)S(1)}, f32[32,32]{1,0:T(8,128)S(1)}, u32[]{:S(2)}, u32[]{:S(2)}) collective-permute-start(f32[32,32]{1,0:T(8,128)S(1)} %get-tuple-element.103), channel_id=1, source_target_pairs={{496,0},{0,16},{16,32},{32,48},{48,64},{64,80},{80,96},{96,112},{1... | collective-permute-start | bytes 12296 | tf_op jit(solution)/shard_map/ppermute | solution.py:23
  55.9 6.5 %collective-permute-start.9 = (f32[32,32]{1,0:T(8,128)S(1)}, f32[32,32]{1,0:T(8,128)S(1)}, u32[]{:S(2)}, u32[]{:S(2)}) collective-permute-start(f32[32,32]{1,0:T(8,128)S(1)} %get-tuple-element.104), channel_id=1, source_target_pairs={{16,0},{32,16},{48,32},{64,48},{80,64},{96,80},{112,96},{128,112},... | collective-permute-start | bytes 12296 | tf_op jit(solution)/shard_map/ppermute | solution.py:23
  63.2 6.3 %collective-permute-start.11 = (f32[32,32]{1,0:T(8,128)S(1)}, f32[32,32]{1,0:T(8,128)S(1)}, u32[]{:S(2)}, u32[]{:S(2)}) collective-permute-start(f32[32,32]{1,0:T(8,128)S(1)} %fusion.113), channel_id=1, source_target_pairs={{16,0},{32,16},{48,32},{64,48},{80,64},{96,80},{112,96},{128,112},... | collective-permute-start | bytes 12296 | tf_op jit(solution)/shard_map/ppermute | solution.py:35
  69.6 1.9 %collective-permute-start.10 = (f32[32,32]{1,0:T(8,128)S(1)}, f32[32,32]{1,0:T(8,128)S(1)}, u32[]{:S(2)}, u32[]{:S(2)}) collective-permute-start(f32[32,32]{1,0:T(8,128)S(1)} %fusion.113), channel_id=1, source_target_pairs={{0,16},{16,32},{32,48},{48,64},{64,80},{80,96},{96,112},{112,128},... | collective-permute-start | bytes 12296 | tf_op jit(solution)/shard_map/ppermute | solution.py:33
  71.5 5.7 %collective-permute-start.7 = (bf16[8,6,16,128]{3,2,1,0:T(8,128)(2,1)}, bf16[8,6,16,128]{3,2,1,0:T(8,128)(2,1)}, u32[]{:S(2)}, u32[]{:S(2)}) collective-permute-start(bf16[8,6,16,128]{3,2,1,0:T(8,128)(2,1)} %copy-done.3), channel_id=1, source_target_pairs={{16,0},{32,16},{48,32},{64,48},{80,64},{96,80},{112,96},{128,112},... | collective-permute-start | bytes 589832 | tf_op jit(solution)/shard_map/ppermute | solution.py:35
  77.2 2.1 %collective-permute-start.6 = (bf16[8,6,16,128]{3,2,1,0:T(8,128)(2,1)}, bf16[8,6,16,128]{3,2,1,0:T(8,128)(2,1)}, u32[]{:S(2)}, u32[]{:S(2)}) collective-permute-start(bf16[8,6,16,128]{3,2,1,0:T(8,128)(2,1)} %copy-done.3), channel_id=1, source_target_pairs={{0,16},{16,32},{32,48},{48,64},{64,80},{80,96},{96,112},{112,128},... | collective-permute-start | bytes 589832 | tf_op jit(solution)/shard_map/ppermute | solution.py:33
  80.9 3.4 %collective-permute-done.6 = bf16[8,6,16,128]{3,2,1,0:T(8,128)(2,1)} collective-permute-done((bf16[8,6,16,128]{3,2,1,0:T(8,128)(2,1)}, bf16[8,6,16,128]{3,2,1,0:T(8,128)(2,1)}, u32[]{:S(2)}, u32[]{:S(2)}) %collective-permute-start.6) | collective-permute-done | bytes 196640 | tf_op jit(solution)/shard_map/ppermute | solution.py:33
  84.3 1.1 maximum_convert_fusion.1
  88.2 3.4 %fusion.23 = bf16[8,6,16,128]{3,2,1,0:T(8,128)(2,1)S(1)} fusion(bf16[8,6,16,128]{3,2,1,0:T(8,128)(2,1)S(1)} %copy-done.2, f32[8,18,16,128]{3,2,1,0:T(8,128)S(1)} %maximum_convert_fusion.1, f32[8,6,15,128]{3,2,1,0:T(8,128)S(1)} %get-tuple-element.52, f32[8,6,1,128]{3,2,1,0:T(1,128)S(1)} %get-tuple-element.54, f32[8,6,1,128]{3,2,1,0:T(1,128)S(1)} %get-tuple-element.53, ...), kind=kLoop, calls=%fused_computation.25 | loop fusion | flops 7667712 | bytes 15581184 | tf_op jit(solution)/shard_map/convert_element_type | solution.py:105
  92.4 77.4 %all-gather.2.cloned.1.call-done = bf16[128,12288]{1,0:T(8,128)(2,1)} async-done(((bf16[8,12288]{1,0:T(8,128)(2,1)}), bf16[128,12288]{1,0:T(8,128)(2,1)}) %all-gather.2.cloned.1.call-update) | async-done | bytes 3145744 | tf_op jit(solution)/shard_map/all_gather | solution.py:112
  169.9 2.5 %convolution_convert_fusion = bf16[8,12288]{1,0:T(8,128)(2,1)S(1)} fusion(bf16[128,12288]{1,0:T(8,128)(2,1)} %all-gather.2.cloned.1.call-done, bf16[128,128]{1,0:T(8,128)(2,1)S(1)} %copy-done, s32[]{:T(128)S(6)} %select_n.73), kind=kOutput, calls=%fused_computation.5 | convolution fusion | flops 25264128 | bytes 3375108 | tf_op jit(solution)/shard_map/dot_general | solution.py:110
  (105 shorter events, 15.6 us)
Async XLA Ops:
  6.5 163.3 %copy-start = (bf16[128,128]{1,0:T(8,128)(2,1)S(1)}, bf16[128,128]{1,0:T(8,128)(2,1)}, u32[]{:S(2)}) copy-start(bf16[128,128]{1,0:T(8,128)(2,1)} %param.11) | copy-start | bytes 98308
  6.5 163.3 %all-gather.2.cloned.1.call-start = ((), (), s32[]{:S(2)}) async-start(), calls=%async_computation | async-start | bytes 3342336 | tf_op jit(solution)/shard_map/all_gather | solution.py:112
  6.5 36.3 %collective-permute-start.1 = (bf16[8,6,16,128]{3,2,1,0:T(8,128)(2,1)}, bf16[8,6,16,128]{3,2,1,0:T(8,128)(2,1)}, u32[]{:S(2)}, u32[]{:S(2)}) collective-permute-start(bf16[8,6,16,128]{3,2,1,0:T(8,128)(2,1)} %param.6), channel_id=1, source_target_pairs={{16,0},{32,16},{48,32},{64,48},{80,64},{96,80},{112,96},{128,112},... | collective-permute-start | bytes 589832 | tf_op jit(solution)/shard_map/ppermute | solution.py:35
  15.5 27.4 %collective-permute-start = (bf16[8,6,16,128]{3,2,1,0:T(8,128)(2,1)}, bf16[8,6,16,128]{3,2,1,0:T(8,128)(2,1)}, u32[]{:S(2)}, u32[]{:S(2)}) collective-permute-start(bf16[8,6,16,128]{3,2,1,0:T(8,128)(2,1)} %param.6), channel_id=1, source_target_pairs={{0,16},{16,32},{32,48},{48,64},{64,80},{80,96},{96,112},{112,128},... | collective-permute-start | bytes 589832 | tf_op jit(solution)/shard_map/ppermute | solution.py:33
  18.2 18.7 %copy-start.6 = (f32[1024,4]{0,1:T(4,128)S(1)}, f32[1024,4]{0,1:T(4,128)}, u32[]{:S(2)}) copy-start(f32[1024,4]{0,1:T(4,128)} %param.10) | copy-start | bytes 49156
  18.2 24.0 %copy-start.1 = (bf16[6,16,32,4,128]{4,3,2,1,0:T(4,128)(2,1)S(1)}, bf16[6,16,32,4,128]{4,3,2,1,0:T(4,128)(2,1)}, u32[]{:S(2)}) copy-start(bf16[6,16,32,4,128]{4,3,2,1,0:T(4,128)(2,1)} %param.8) | copy-start | bytes 9437188
  23.4 4.4 %collective-permute-start.2 = (f32[32,32]{1,0:T(8,128)S(1)}, f32[32,32]{1,0:T(8,128)S(1)}, u32[]{:S(2)}, u32[]{:S(2)}) collective-permute-start(f32[32,32]{1,0:T(8,128)S(1)} %get-tuple-element.105), channel_id=1, source_target_pairs={{496,0},{0,16},{16,32},{32,48},{48,64},{64,80},{80,96},{96,112},{1... | collective-permute-start | bytes 12296 | tf_op jit(solution)/shard_map/ppermute | solution.py:23
  25.3 5.3 %collective-permute-start.3 = (f32[32,32]{1,0:T(8,128)S(1)}, f32[32,32]{1,0:T(8,128)S(1)}, u32[]{:S(2)}, u32[]{:S(2)}) collective-permute-start(f32[32,32]{1,0:T(8,128)S(1)} %get-tuple-element.106), channel_id=1, source_target_pairs={{16,0},{32,16},{48,32},{64,48},{80,64},{96,80},{112,96},{128,112},... | collective-permute-start | bytes 12296 | tf_op jit(solution)/shard_map/ppermute | solution.py:23
  30.7 9.0 %collective-permute-start.5 = (f32[32,32]{1,0:T(8,128)S(1)}, f32[32,32]{1,0:T(8,128)S(1)}, u32[]{:S(2)}, u32[]{:S(2)}) collective-permute-start(f32[32,32]{1,0:T(8,128)S(1)} %fusion.114), channel_id=1, source_target_pairs={{16,0},{32,16},{48,32},{64,48},{80,64},{96,80},{112,96},{128,112},... | collective-permute-start | bytes 12296 | tf_op jit(solution)/shard_map/ppermute | solution.py:35
  34.9 6.4 %collective-permute-start.4 = (f32[32,32]{1,0:T(8,128)S(1)}, f32[32,32]{1,0:T(8,128)S(1)}, u32[]{:S(2)}, u32[]{:S(2)}) collective-permute-start(f32[32,32]{1,0:T(8,128)S(1)} %fusion.114), channel_id=1, source_target_pairs={{0,16},{16,32},{32,48},{48,64},{64,80},{80,96},{96,112},{112,128},... | collective-permute-start | bytes 12296 | tf_op jit(solution)/shard_map/ppermute | solution.py:33
  42.1 0.9 copy-start.2
  46.8 0.8 copy-start.5
  50.8 2.1 %copy-start.3 = (bf16[8,6,16,128]{3,2,1,0:T(8,128)(2,1)}, bf16[8,6,16,128]{3,2,1,0:T(8,128)(2,1)S(1)}, u32[]{:S(2)}) copy-start(bf16[8,6,16,128]{3,2,1,0:T(8,128)(2,1)S(1)} %fusion.22) | copy-start | bytes 589828
  54.0 8.4 %collective-permute-start.8 = (f32[32,32]{1,0:T(8,128)S(1)}, f32[32,32]{1,0:T(8,128)S(1)}, u32[]{:S(2)}, u32[]{:S(2)}) collective-permute-start(f32[32,32]{1,0:T(8,128)S(1)} %get-tuple-element.103), channel_id=1, source_target_pairs={{496,0},{0,16},{16,32},{32,48},{48,64},{64,80},{80,96},{96,112},{1... | collective-permute-start | bytes 12296 | tf_op jit(solution)/shard_map/ppermute | solution.py:23
  55.9 7.3 %collective-permute-start.9 = (f32[32,32]{1,0:T(8,128)S(1)}, f32[32,32]{1,0:T(8,128)S(1)}, u32[]{:S(2)}, u32[]{:S(2)}) collective-permute-start(f32[32,32]{1,0:T(8,128)S(1)} %get-tuple-element.104), channel_id=1, source_target_pairs={{16,0},{32,16},{48,32},{64,48},{80,64},{96,80},{112,96},{128,112},... | collective-permute-start | bytes 12296 | tf_op jit(solution)/shard_map/ppermute | solution.py:23
  63.2 16.1 %collective-permute-start.11 = (f32[32,32]{1,0:T(8,128)S(1)}, f32[32,32]{1,0:T(8,128)S(1)}, u32[]{:S(2)}, u32[]{:S(2)}) collective-permute-start(f32[32,32]{1,0:T(8,128)S(1)} %fusion.113), channel_id=1, source_target_pairs={{16,0},{32,16},{48,32},{64,48},{80,64},{96,80},{112,96},{128,112},... | collective-permute-start | bytes 12296 | tf_op jit(solution)/shard_map/ppermute | solution.py:35
  69.6 9.8 %collective-permute-start.10 = (f32[32,32]{1,0:T(8,128)S(1)}, f32[32,32]{1,0:T(8,128)S(1)}, u32[]{:S(2)}, u32[]{:S(2)}) collective-permute-start(f32[32,32]{1,0:T(8,128)S(1)} %fusion.113), channel_id=1, source_target_pairs={{0,16},{16,32},{32,48},{48,64},{64,80},{80,96},{96,112},{112,128},... | collective-permute-start | bytes 12296 | tf_op jit(solution)/shard_map/ppermute | solution.py:33
  71.5 9.4 %collective-permute-start.7 = (bf16[8,6,16,128]{3,2,1,0:T(8,128)(2,1)}, bf16[8,6,16,128]{3,2,1,0:T(8,128)(2,1)}, u32[]{:S(2)}, u32[]{:S(2)}) collective-permute-start(bf16[8,6,16,128]{3,2,1,0:T(8,128)(2,1)} %copy-done.3), channel_id=1, source_target_pairs={{16,0},{32,16},{48,32},{64,48},{80,64},{96,80},{112,96},{128,112},... | collective-permute-start | bytes 589832 | tf_op jit(solution)/shard_map/ppermute | solution.py:35
  77.2 7.0 %collective-permute-start.6 = (bf16[8,6,16,128]{3,2,1,0:T(8,128)(2,1)}, bf16[8,6,16,128]{3,2,1,0:T(8,128)(2,1)}, u32[]{:S(2)}, u32[]{:S(2)}) collective-permute-start(bf16[8,6,16,128]{3,2,1,0:T(8,128)(2,1)} %copy-done.3), channel_id=1, source_target_pairs={{0,16},{16,32},{32,48},{48,64},{64,80},{80,96},{96,112},{112,128},... | collective-permute-start | bytes 589832 | tf_op jit(solution)/shard_map/ppermute | solution.py:33
  80.2 4.1 %copy-start.4 = (bf16[8,6,16,128]{3,2,1,0:T(8,128)(2,1)S(1)}, bf16[8,6,16,128]{3,2,1,0:T(8,128)(2,1)}, u32[]{:S(2)}) copy-start(bf16[8,6,16,128]{3,2,1,0:T(8,128)(2,1)} %copy-done.3) | copy-start | bytes 589828
Sparse Core Ops, SparseCore 0:
  92.6 77.2 all-gather.1
where the time goes:
time: 181 us; the launch traced here: 180 us
  waiting for transfers between devices  86.2 us (48%)
  starting transfers between devices  45.8 us (25%)
  between operations  13.9 us (8%)
  local copies, waits for them, and re-layouts  13.4 us (7%)
  other arithmetic  10.5 us (6%)
  matrix products  10.1 us (6%)
    all_gather x1, waiting for transfers between devices, local(): lax.all_gather(flat, 'band', axis=0, tiled=True)  77.4 us
    ppermute x4, starting transfers between devices, padded_2(): lax.ppermute(head, axis, [((i + 1) % count, i) for i in range(count)])  25.2 us
    ppermute x4, starting transfers between devices, passed_along(): return lax.ppermute(block, axis, route)  12.7 us
    ppermute x4, starting transfers between devices, padded_2(): lax.ppermute(tail, axis, [(i, (i + 1) % count) for i in range(count)])  7.87 us
    dot_general x2, matrix products, apply_hamiltonian(): jnp.einsum('xjwspz,bxjwz->jspb', projector_view, view, preferred_element_...  6.26 us
    ppermute x4, waiting for transfers between devices, padded_2(): lax.ppermute(tail, axis, [(i, (i + 1) % count) for i in range(count)])  5.1 us
    slice x24, local copies, waits for them, and re-layouts, laplace_slab(): beside = beside + jnp.roll(middle, offset, 3) + jnp.roll(middle, -offset, 3)  4.4 us
    ppermute x4, waiting for transfers between devices, passed_along(): return lax.ppermute(block, axis, route)  3.72 us
  transfers between devices with their start and end apart: 13, of which 5 were waited for; matrix products, arithmetic and copies ran while one was open for 6% of the time, Pallas kernels for 0%

commit v1 on v0

v1 whole, which is shorter than its diff:
```python
import functools
import jax
import jax.numpy as jnp
import numpy as np
import ml_dtypes
from jax import lax
from jax.experimental import pallas as pl
from jax.experimental.pallas import tpu as pltpu
from jax.sharding import PartitionSpec as P

STENCIL = [
    -5369.0 / 1800.0,
    12.0 / 7.0,
    -15.0 / 56.0,
    10.0 / 189.0,
    -1.0 / 112.0,
    2.0 / 1925.0,
    -1.0 / 16632.0,
]
kinetic_scale = 0.5 / 0.49
centre = 12.0
half_width = 11.0
REACH = 6
F32, BF16 = jnp.float32, jnp.bfloat16
WEIGHTS = [-kinetic_scale * w for w in STENCIL]


def split3(x):
    hi = x.astype(BF16)
    rest = x - hi.astype(F32)
    mid = rest.astype(BF16)
    return hi, mid, (rest - mid.astype(F32)).astype(BF16)


def z_matrix(depth):
    full = np.zeros((depth, depth), np.float32)
    at = np.arange(depth)
    for offset in range(1, REACH + 1):
        full[at, (at + offset) % depth] += np.float32(WEIGHTS[offset])
        full[at, (at - offset) % depth] += np.float32(WEIGHTS[offset])
    hi = full.astype(ml_dtypes.bfloat16)
    rest = full - hi.astype(np.float32)
    mid = rest.astype(ml_dtypes.bfloat16)
    low = (rest - mid.astype(np.float32)).astype(ml_dtypes.bfloat16)
    return np.concatenate([hi, mid, low], 0)


def dot_t(a, b):
    return lax.dot_general(a, b, (((1,), (1,)), ((), ())), preferred_element_type=F32)


def one_hot(target, lanes):
    wide = jnp.broadcast_to(target, (target.shape[0], lanes))
    at = lax.broadcasted_iota(jnp.int32, wide.shape, 1)
    return jnp.where(wide == at, 1.0, 0.0).astype(BF16)


def scatter(partials, target_ref, tab_ref):
    slots = partials[0].shape[1]
    total = None
    for j, partial in enumerate(partials):
        hot = one_hot(target_ref[pl.ds(j * slots, slots), :], 3 * slots)
        for piece in split3(partial):
            part = jnp.dot(piece, hot, preferred_element_type=F32)
            total = part if total is None else total + part
    for tile in range(3):
        tab_ref[tile] = total[:, tile * slots : (tile + 1) * slots]


def gathered(tot_ref, strength_ref, target_ref, blocks):
    weighted = jnp.concatenate(
        [tot_ref[tile] * strength_ref[tile : tile + 1, :] for tile in range(3)], 1
    ).astype(BF16)
    slots = tot_ref.shape[2]
    out = []
    for j in range(blocks):
        hot = one_hot(target_ref[pl.ds(j * slots, slots), :], 3 * slots)
        out.append(dot_t(weighted, hot).astype(BF16))
    return out


def pair_rows(pair):
    return slice(16 * pair, 16 * pair + 16)


def project_pair(v, proj_ref, pair, even, odd):
    e = dot_t(v, proj_ref[2 * pair])
    o = dot_t(v, proj_ref[2 * pair + 1])
    return (e if even is None else even + e), (o if odd is None else odd + o)


def block_of(pair, rows_total, block_rows):
    return (2 * pair % rows_total) // block_rows


def project_kernel(dims, v_ref, proj_ref, target_ref, tab_ref):
    cells, rows_total, block_rows = dims
    blocks = rows_total // block_rows
    even, odd = [None] * blocks, [None] * blocks
    for pair in range(cells // 2):
        j = block_of(pair, rows_total, block_rows)
        even[j], odd[j] = project_pair(v_ref[pair_rows(pair), :], proj_ref, pair, even[j], odd[j])
    scatter([e[:8] + o[8:] for e, o in zip(even, odd)], target_ref, tab_ref)


def base_kernel(dims, side_ref, v_ref, on_ref, off_ref, pot_ref, zmat_ref, out_ref, wide_ref):
    cells, rows_total, _ = dims
    side = side_ref[0]
    on_at = pl.multiple_of(jnp.where(side == 0, 2 * cells, 0), cells)
    off_at = pl.multiple_of(jnp.where(side == 0, 0, 2 * cells), cells)
    step = 8
    for c in range(0, cells, step):
        rows = slice(8 * c, 8 * (c + step))
        shape = (step,) + wide_ref.shape[1:]
        wide_ref[pl.ds(on_at + c, step)] = on_ref[rows, :].astype(F32).reshape(shape)
        wide_ref[pl.ds(off_at + c, step)] = off_ref[rows, :].astype(F32).reshape(shape)
        wide_ref[cells + c : cells + c + step] = v_ref[rows, :].astype(F32).reshape(shape)
    depth = v_ref.shape[1]
    for c in range(0, cells, rows_total):
        rows = slice(8 * c, 8 * (c + rows_total))
        v = v_ref[rows, :]
        along_z = jnp.dot(jnp.concatenate([v, v, v], 1), zmat_ref[...], preferred_element_type=F32)
        for y in range(rows_total):
            at = cells + c + y
            mine = wide_ref[at]
            pot = pot_ref[c + y : c + y + 1, :] + (3.0 * WEIGHTS[0] - centre)
            total = pot * mine + along_z[8 * y : 8 * y + 8, :]
            for offset in range(1, REACH + 1):
                beside = wide_ref[at + offset * rows_total] + wide_ref[at - offset * rows_total]
                up = cells + c + (y + offset) % rows_total
                down = cells + c + (y - offset) % rows_total
                beside = beside + (wide_ref[up] + wide_ref[down])
                total = total + WEIGHTS[offset] * beside
            out_ref[8 * (c + y) : 8 * (c + y) + 8, :] = total


def nonlocal_pair(weighted, proj_ref, pair):
    both = jnp.concatenate([proj_ref[2 * pair], proj_ref[2 * pair + 1]], 1)
    value = jnp.dot(weighted, both, preferred_element_type=F32)
    half = value.shape[1] // 2
    return jnp.concatenate([value[:, :half], value[:, half:]], 0)


def first_kernel(dims, base_ref, tot_ref, strength_ref, target_ref, proj_ref, first_ref, tab_ref):
    cells, rows_total, block_rows = dims
    blocks = rows_total // block_rows
    weighted = gathered(tot_ref, strength_ref, target_ref, blocks)
    even, odd = [None] * blocks, [None] * blocks
    for pair in range(cells // 2):
        j = block_of(pair, rows_total, block_rows)
        rows = pair_rows(pair)
        value = (base_ref[rows, :] + nonlocal_pair(weighted[j], proj_ref, pair)) / half_width
        first = value.astype(BF16)
        first_ref[rows, :] = first
        even[j], odd[j] = project_pair(first, proj_ref, pair, even[j], odd[j])
    scatter([e[:8] + o[8:] for e, o in zip(even, odd)], target_ref, tab_ref)


def filtered_kernel(dims, base_ref, tot_ref, strength_ref, target_ref, proj_ref, start_ref, out_ref):
    cells, rows_total, block_rows = dims
    weighted = gathered(tot_ref, strength_ref, target_ref, rows_total // block_rows)
    for pair in range(cells // 2):
        j = block_of(pair, rows_total, block_rows)
        rows = pair_rows(pair)
        value = 2.0 * (base_ref[rows, :] + nonlocal_pair(weighted[j], proj_ref, pair)) / half_width
        out_ref[rows, :] = (value - start_ref[rows, :].astype(F32)).astype(BF16)


def call(kernel, name, outs, ins, flops, moved, scratch=(), smem=0):
    vmem = pl.BlockSpec(memory_space=pltpu.VMEM)
    scalar = pl.BlockSpec(memory_space=pltpu.SMEM)
    single = not isinstance(outs, (list, tuple))
    return pl.pallas_call(
        kernel,
        name=name,
        out_shape=outs,
        in_specs=[scalar] * smem + [vmem] * (len(ins) - smem),
        out_specs=vmem if single else [vmem] * len(outs),
        scratch_shapes=list(scratch),
        compiler_params=pltpu.CompilerParams(vmem_limit_bytes=32 * 1024 * 1024),
        cost_estimate=pl.CostEstimate(flops=flops, bytes_accessed=moved, transcendentals=0),
    )(*ins)


def swap_on_chip(x, axis):
    count = lax.axis_size(axis)
    return lax.ppermute(x, axis, [(i, i ^ 1) for i in range(count)])


def swap_across(x, axis):
    count = lax.axis_size(axis)
    return lax.ppermute(x, axis, [(i, (((i + 1) ^ 1) - 1) % count) for i in range(count)])


def local(bands, potential, projectors, atom_ids, strength, rotation):
    local_bands, thickness, rows_total, depth = bands.shape
    blocks, slot_count = atom_ids.shape
    atom_count, proj_count = strength.shape
    block_rows = rows_total // blocks
    cells = thickness * rows_total
    rows = cells * local_bands
    slots = slot_count * proj_count
    dims = (cells, rows_total, block_rows)
    dom_count = lax.axis_size("dom")
    band_count = lax.axis_size("band")
    per_owner = atom_count // dom_count
    dom = lax.axis_index("dom")
    side = dom % 2
    first_core = side == 0

    proj = projectors.reshape(cells, slots, depth)
    pot = potential.reshape(cells, depth)
    start = bands.reshape(local_bands, cells, depth).transpose(1, 0, 2).reshape(rows, depth)
    relative = (atom_ids // per_owner - dom + 1 + dom_count) % dom_count
    target = (relative * per_owner + atom_ids % per_owner) * proj_count
    target = target[..., None] + jnp.arange(proj_count, dtype=jnp.int32)
    target = target.reshape(blocks * slots, 1)
    by_owner = strength.reshape(dom_count, per_owner * proj_count)
    near = [
        lax.dynamic_slice_in_dim(by_owner, (dom + shift + dom_count) % dom_count, 1, 0)
        for shift in (-1, 0, 1)
    ]
    near_strength = jnp.concatenate(near, 0)
    zmat = jnp.asarray(z_matrix(depth))
    side_ref = side.astype(jnp.int32).reshape(1)

    tab_shape = jax.ShapeDtypeStruct((3, local_bands, slots), F32)
    slab_shape = jax.ShapeDtypeStruct((rows, depth), BF16)
    wide_shape = jax.ShapeDtypeStruct((rows, depth), F32)
    stream = 2 * rows * slots * depth
    proj_bytes = 2 * cells * slots * depth

    def summed(tab):
        below, middle, above = tab[0:1], tab[1:2], tab[2:3]
        near_tile = swap_on_chip(jnp.where(first_core, above, below), "dom")
        low = jnp.where(first_core, below, middle + near_tile)
        high = jnp.where(first_core, middle + near_tile, above)
        pair = jnp.concatenate([low, high], 0)
        pair = pair + swap_across(pair, "dom")
        low, high = pair[0:1], pair[1:2]
        other = swap_on_chip(jnp.where(first_core, high, low), "dom")
        return jnp.where(
            first_core,
            jnp.concatenate([low, high, other], 0),
            jnp.concatenate([other, low, high], 0),
        )

    def base(v, on_chip, across):
        return call(
            functools.partial(base_kernel, dims), "base", wide_shape,
            (side_ref, v, on_chip, across, pot, zmat), 6 * rows * depth * depth, 10 * rows * depth,
            scratch=[pltpu.VMEM((3 * cells, local_bands, depth), F32)], smem=1,
        )

    start_on, start_across = swap_on_chip(start, "dom"), swap_across(start, "dom")
    tab = call(
        functools.partial(project_kernel, dims), "project", tab_shape,
        (start, proj, target), stream, proj_bytes,
    )
    totals = summed(tab)
    first, tab = call(
        functools.partial(first_kernel, dims), "first", [slab_shape, tab_shape],
        (base(start, start_on, start_across), totals, near_strength, target, proj),
        2 * stream, proj_bytes,
    )
    first_on, first_across = swap_on_chip(first, "dom"), swap_across(first, "dom")
    totals = summed(tab)
    filtered = call(
        functools.partial(filtered_kernel, dims), "filtered", slab_shape,
        (base(first, first_on, first_across), totals, near_strength, target, proj, start),
        stream, proj_bytes,
    )
    share = cells // band_count
    pieces = filtered.reshape(band_count, share, local_bands, depth)
    pieces = lax.all_to_all(pieces, "band", 0, 0, tiled=True)
    turn = rotation.reshape(band_count, local_bands, band_count * local_bands)
    turned = jnp.einsum("gxbz,gbc->xcz", pieces, turn, preferred_element_type=F32).astype(BF16)
    turned = turned.reshape(share, band_count, local_bands, depth).transpose(1, 0, 2, 3)
    turned = lax.all_to_all(turned, "band", 0, 0, tiled=True)
    return turned.reshape(cells, local_bands, depth).transpose(1, 0, 2).reshape(bands.shape)


def solution(mesh):
    placed = (
        P("band", "dom", None, None),
        P("dom", None, None),
        P("dom", None, None, None, None),
        P("dom", None),
        P(),
        P(),
    )
    return jax.shard_map(
        local, mesh=mesh, in_specs=placed, out_specs=P("band", "dom", None, None), check_vma=False
    )
```

time: 181 us -> 98.8 us (0.55)
  waiting for transfers between devices: 86.2 us -> 3.24 us
  blocking collectives: 0 us -> 36.1 us
  between operations: 13.9 us -> 0.26 us
  Pallas kernels: 0 us -> 12 us
  starting transfers between devices: 45.8 us -> 34.9 us
  matrix products: 10.1 us -> 0.26 us
  other arithmetic: 10.5 us -> 2.19 us
  local copies, waits for them, and re-layouts: 13.4 us -> 9.1 us
    all_gather x1 -> x0, waiting for transfers between devices: 77.4 us -> none  [local(): lax.all_gather(flat, 'band', axis=0, tiled=True)]
    all_to_all x0 -> x2, blocking collectives: none -> 36.1 us  [the longest x1 21.2 us: local(): pieces = lax.all_to_all(pieces, 'band', 0, 0, tiled=True)]
    pallas_call x0 -> x5, Pallas kernels: none -> 12 us  [call(): pl.pallas_call(kernel, name=name, out_shape=outs, in_specs=[scalar] * sme...]
    ppermute x12 -> x10, starting transfers between devices: 45.8 us -> 34.9 us  [the longest x6 23.7 us: swap_on_chip(): return lax.ppermute(x, axis, [(i, i ^ 1) for i in range(count)])]
    dot_general x5 -> x1, matrix products: 10.1 us -> 0.26 us  [local(): jnp.einsum('gxbz,gbc->xcz', pieces, turn, preferred_element_type=F32)]
    convert_element_type x6 -> x0, other arithmetic: 8.8 us -> none  [the longest x1 3.43 us: local(): filtered = (2.0 * (apply_hamiltonian(first) - centre * first_values) / ha...]
    ppermute x12 -> x10, waiting for transfers between devices: 8.83 us -> 3.24 us  [the longest x6 2.73 us: swap_on_chip(): return lax.ppermute(x, axis, [(i, i ^ 1) for i in range(count)])]
    slice x50 -> x0, local copies, waits for them, and re-layouts: 5.5 us -> none  [the longest x24 4.4 us: laplace_slab(): beside = beside + jnp.roll(middle, offset, 3) + jnp.roll(middle, -offset, 3)]
  transfers between devices with their start and end apart: 13 -> 10, of which waited for: 5 -> 4; matrix products, arithmetic and copies ran while one was open for 6% -> 5% of each run, Pallas kernels for 0% -> 0%
where the time goes in v1:
time: 98.8 us; the launch traced here: 98 us
  blocking collectives  36.1 us (37%)
  starting transfers between devices  34.9 us (35%)
  Pallas kernels  12 us (12%)
  local copies, waits for them, and re-layouts  9.1 us (9%)
  waiting for transfers between devices  3.24 us (3%)
  other arithmetic  2.19 us (2%)
    ppermute x6, starting transfers between devices, swap_on_chip(): return lax.ppermute(x, axis, [(i, i ^ 1) for i in range(count)])  23.7 us
    all_to_all x1, blocking collectives, local(): pieces = lax.all_to_all(pieces, 'band', 0, 0, tiled=True)  21.2 us
    all_to_all x1, blocking collectives, local(): turned = lax.all_to_all(turned, 'band', 0, 0, tiled=True)  14.9 us
    pallas_call x5, Pallas kernels, call(): pl.pallas_call(kernel, name=name, out_shape=outs, in_specs=[scalar] * sme...  12 us
    ppermute x4, starting transfers between devices, swap_across(): lax.ppermute(x, axis, [(i, ((i + 1 ^ 1) - 1) % count) for i in range(coun...  11.1 us
    unnamed x15, local copies, waits for them, and re-layouts  4.53 us
    ppermute x6, waiting for transfers between devices, swap_on_chip(): return lax.ppermute(x, axis, [(i, i ^ 1) for i in range(count)])  2.73 us
  transfers between devices with their start and end apart: 10, of which 4 were waited for; matrix products, arithmetic and copies ran while one was open for 5% of the time, Pallas kernels for 0%

profile of v1, /device:TPU:1, one launch (start us, length us, event | category | flops | bytes accessed | tf_op | source)
XLA Modules:
  0.0 98.0 jit_solution(18035225320106670733)
XLA Ops:
  0.9 1.0 %copy.37 = bf16[8,96,128]{2,0,1:T(8,128)(2,1)S(1)} copy(bf16[8,96,128]{2,1,0:T(8,128)(2,1)} %bitcast.49) | data formatting | bytes 393216 | tf_op jit(solution)/shard_map/reshape | solution.py:213
  1.9 1.9 %copy-done.1 = bf16[6,16,32,4,128]{4,3,2,1,0:T(4,128)(2,1)S(1)} copy-done((bf16[6,16,32,4,128]{4,3,2,1,0:T(4,128)(2,1)S(1)}, bf16[6,16,32,4,128]{4,3,2,1,0:T(4,128)(2,1)}, u32[]{:S(2)}) %copy-start.1) | copy-done | bytes 3145752
  3.8 1.9 %project.1 = f32[3,8,128]{2,1,0:T(8,128)S(1)} custom-call(bf16[768,128]{1,0:T(8,128)(2,1)S(1)} %bitcast.39, bf16[96,128,128]{2,1,0:T(8,128)(2,1)S(1)} %bitcast.36, s32[256,1]{1,0:T(8,128)S(1)} %add.120.target_ref), custom_call_target="tpu_custom_call" | custom-call | flops 25165824 | bytes 3145728 | tf_op jit(solution)/shard_map/project/pallas_call | solution.py:173
  6.3 8.8 %collective-permute-start.2 = (f32[1,8,128]{2,1,0:T(8,128)}, f32[1,8,128]{2,1,0:T(8,128)}, u32[]{:S(2)}, u32[]{:S(2)}) collective-permute-start(f32[1,8,128]{2,1,0:T(8,128)} %slice_select_fusion.3), channel_id=1, source_target_pairs={{0,16},{16,0},{32,48},{48,32},{64,80},{80,64},{96,112},{112,96},{1... | collective-permute-start | bytes 12296 | tf_op jit(solution)/shard_map/ppermute | solution.py:187
  15.1 1.9 %collective-permute-start.1 = (bf16[768,128]{1,0:T(8,128)(2,1)S(1)}, bf16[768,128]{1,0:T(8,128)(2,1)}, u32[]{:S(2)}, u32[]{:S(2)}) collective-permute-start(bf16[768,128]{1,0:T(8,128)(2,1)S(1)} %bitcast.40), channel_id=1, source_target_pairs={{0,496},{16,32},{32,16},{48,64},{64,48},{80,96},{96,80},{112,128},... | collective-permute-start | bytes 589832 | tf_op jit(solution)/shard_map/ppermute | solution.py:192
  17.0 1.9 %collective-permute-start = (bf16[768,128]{1,0:T(8,128)(2,1)S(1)}, bf16[768,128]{1,0:T(8,128)(2,1)}, u32[]{:S(2)}, u32[]{:S(2)}) collective-permute-start(bf16[768,128]{1,0:T(8,128)(2,1)S(1)} %bitcast.41), channel_id=1, source_target_pairs={{0,16},{16,0},{32,48},{48,32},{64,80},{80,64},{96,112},{112,96},{1... | collective-permute-start | bytes 589832 | tf_op jit(solution)/shard_map/ppermute | solution.py:187
  19.0 1.7 %copy.23 = f32[1024,4]{1,0:T(8,128)} copy(f32[1024,4]{0,1:T(4,128)} %param.11) | data formatting | bytes 32768 | tf_op args[4]
  20.7 1.9 %reshape.62 = f32[32,128]{1,0:T(8,128)} reshape(f32[1024,4]{1,0:T(8,128)} %copy.23) | data formatting | bytes 32768 | tf_op jit(solution)/shard_map/reshape | solution.py:218
  23.4 3.6 %collective-permute-start.3 = (f32[2,8,128]{2,1,0:T(8,128)S(1)}, f32[2,8,128]{2,1,0:T(8,128)S(1)}, u32[]{:S(2)}, u32[]{:S(2)}) collective-permute-start(f32[2,8,128]{2,1,0:T(8,128)S(1)} %pad_maximum_fusion), channel_id=1, source_target_pairs={{0,496},{16,32},{32,16},{48,64},{64,48},{80,96},{96,80},{112,128},... | collective-permute-start | bytes 24584 | tf_op jit(solution)/shard_map/ppermute | solution.py:192
  27.0 0.8 constant_dynamic-slice_fusion.2
  28.3 4.5 %collective-permute-start.4 = (f32[1,8,128]{2,1,0:T(8,128)S(1)}, f32[1,8,128]{2,1,0:T(8,128)S(1)}, u32[]{:S(2)}, u32[]{:S(2)}) collective-permute-start(f32[1,8,128]{2,1,0:T(8,128)S(1)} %slice_select_fusion.1), channel_id=1, source_target_pairs={{0,16},{16,0},{32,48},{48,32},{64,80},{80,64},{96,112},{112,96},{1... | collective-permute-start | bytes 12296 | tf_op jit(solution)/shard_map/ppermute | solution.py:187
  33.7 0.9 copy-done.3
  34.6 1.8 %base.2.base_ref = f32[768,128]{1,0:T(8,128)S(1)} custom-call(s32[1]{0:T(128)} %bitcast.side_ref, bf16[768,128]{1,0:T(8,128)(2,1)S(1)} %bitcast.42, bf16[768,128]{1,0:T(8,128)(2,1)} %collective-permute-done.on_ref, bf16[768,128]{1,0:T(8,128)(2,1)} %collective-permute-done.1.off_ref, f32[96,128]{1,0:T(8,128)S(1)} %bitcast.45, bf16[384,128]{1,0:T(8,128)(2,1)S(1)} %copy-done.3), custom_call_target="tpu_custom_call" | custom-call | flops 75497472 | bytes 983040 | tf_op jit(solution)/shard_map/base/pallas_call | solution.py:173
  36.4 6.7 %first.1 = (bf16[768,128]{1,0:T(8,128)(2,1)S(1)}, f32[3,8,128]{2,1,0:T(8,128)S(1)}) custom-call(f32[768,128]{1,0:T(8,128)S(1)} %base.2.base_ref, f32[3,8,128]{2,1,0:T(8,128)S(1)} %maximum_select_fusion.tot_ref, f32[3,128]{1,0:T(4,128)S(1)} %pad_maximum_fusion.2.strength_ref, s32[256,1]{1,0:T(8,128)S(1)} %add.120.target_ref, bf16[96,128,128]{2,1,0:T(8,128)(2,1)S(1)} %bitcast.37), custom_call_target="tpu_custom_call" | custom-call | flops 50331648 | bytes 3145728 | tf_op jit(solution)/shard_map/first/pallas_call | solution.py:173
  43.1 2.3 %collective-permute-start.7 = (f32[1,8,128]{2,1,0:T(8,128)S(1)}, f32[1,8,128]{2,1,0:T(8,128)S(1)}, u32[]{:S(2)}, u32[]{:S(2)}) collective-permute-start(f32[1,8,128]{2,1,0:T(8,128)S(1)} %slice_select_fusion.6), channel_id=1, source_target_pairs={{0,16},{16,0},{32,48},{48,32},{64,80},{80,64},{96,112},{112,96},{1... | collective-permute-start | bytes 12296 | tf_op jit(solution)/shard_map/ppermute | solution.py:187
  45.4 0.8 collective-permute-done.7
  46.2 1.9 %collective-permute-start.8 = (f32[2,8,128]{2,1,0:T(8,128)S(1)}, f32[2,8,128]{2,1,0:T(8,128)S(1)}, u32[]{:S(2)}, u32[]{:S(2)}) collective-permute-start(f32[2,8,128]{2,1,0:T(8,128)S(1)} %pad_maximum_fusion.1), channel_id=1, source_target_pairs={{0,496},{16,32},{32,16},{48,64},{64,48},{80,96},{96,80},{112,128},... | collective-permute-start | bytes 24584 | tf_op jit(solution)/shard_map/ppermute | solution.py:192
  48.1 3.6 %collective-permute-start.6 = (bf16[768,128]{1,0:T(8,128)(2,1)S(1)}, bf16[768,128]{1,0:T(8,128)(2,1)S(1)}, u32[]{:S(2)}, u32[]{:S(2)}) collective-permute-start(bf16[768,128]{1,0:T(8,128)(2,1)S(1)} %get-tuple-element.7.v_ref), channel_id=1, source_target_pairs={{0,496},{16,32},{32,16},{48,64},{64,48},{80,96},{96,80},{112,128},... | collective-permute-start | bytes 589832 | tf_op jit(solution)/shard_map/ppermute | solution.py:192
  51.8 4.4 %collective-permute-start.5 = (bf16[768,128]{1,0:T(8,128)(2,1)S(1)}, bf16[768,128]{1,0:T(8,128)(2,1)S(1)}, u32[]{:S(2)}, u32[]{:S(2)}) collective-permute-start(bf16[768,128]{1,0:T(8,128)(2,1)S(1)} %get-tuple-element.7.v_ref), channel_id=1, source_target_pairs={{0,16},{16,0},{32,48},{48,32},{64,80},{80,64},{96,112},{112,96},{1... | collective-permute-start | bytes 589832 | tf_op jit(solution)/shard_map/ppermute | solution.py:187
  56.2 1.9 %collective-permute-start.9 = (f32[1,8,128]{2,1,0:T(8,128)S(1)}, f32[1,8,128]{2,1,0:T(8,128)S(1)}, u32[]{:S(2)}, u32[]{:S(2)}) collective-permute-start(f32[1,8,128]{2,1,0:T(8,128)S(1)} %slice_select_fusion), channel_id=1, source_target_pairs={{0,16},{16,0},{32,48},{48,32},{64,80},{80,64},{96,112},{112,96},{1... | collective-permute-start | bytes 12296 | tf_op jit(solution)/shard_map/ppermute | solution.py:187
  58.1 1.1 %collective-permute-done.9 = f32[1,8,128]{2,1,0:T(8,128)S(1)} collective-permute-done((f32[1,8,128]{2,1,0:T(8,128)S(1)}, f32[1,8,128]{2,1,0:T(8,128)S(1)}, u32[]{:S(2)}, u32[]{:S(2)}) %collective-permute-start.9) | collective-permute-done | bytes 4128 | tf_op jit(solution)/shard_map/ppermute | solution.py:187
  59.3 0.8 base.3.base_ref
  60.9 21.2 %all_to_all.10 = bf16[16,6,8,128]{3,2,1,0:T(8,128)(2,1)S(1)} all-to-all(bf16[16,6,8,128]{3,2,1,0:T(8,128)(2,1)S(1)} %bitcast.44), channel_id=1, replica_groups=mesh['dom'=32,'band'=16] {'band'}, dimensions={0} | all-to-all | bytes 393216 | tf_op jit(solution)/shard_map/all_to_all | solution.py:275
  82.4 14.9 %all_to_all.11 = bf16[16,6,8,128]{3,2,1,0:T(8,128)(2,1)S(1)} all-to-all(bf16[16,6,8,128]{3,2,1,0:T(8,128)(2,1)S(1)} %bitcast.47), channel_id=1, replica_groups=mesh['dom'=32,'band'=16] {'band'}, dimensions={0} | all-to-all | bytes 393216 | tf_op jit(solution)/shard_map/all_to_all | solution.py:279
  (40 shorter events, 5.4 us)
Async XLA Ops:
  0.0 82.1 %copy-start = (bf16[128,128]{1,0:T(8,128)(2,1)S(1)}, bf16[128,128]{1,0:T(8,128)(2,1)}, u32[]{:S(2)}) copy-start(bf16[128,128]{1,0:T(8,128)(2,1)} %param.12) | copy-start | bytes 98308
  0.0 33.7 %copy-start.5 = (f32[6,16,128]{2,1,0:T(8,128)S(1)}, f32[6,16,128]{2,1,0:T(8,128)}, u32[]{:S(2)}) copy-start(f32[6,16,128]{2,1,0:T(8,128)} %param.8) | copy-start | bytes 147460
  1.9 1.9 %copy-start.1 = (bf16[6,16,32,4,128]{4,3,2,1,0:T(4,128)(2,1)S(1)}, bf16[6,16,32,4,128]{4,3,2,1,0:T(4,128)(2,1)}, u32[]{:S(2)}) copy-start(bf16[6,16,32,4,128]{4,3,2,1,0:T(4,128)(2,1)} %param.9) | copy-start | bytes 9437188
  3.8 32.6 %copy-start.2 = (bf16[6,16,32,4,128]{4,3,2,1,0:T(4,128)(2,1)S(1)}, bf16[6,16,32,4,128]{4,3,2,1,0:T(4,128)(2,1)}, u32[]{:S(2)}) copy-start(bf16[6,16,32,4,128]{4,3,2,1,0:T(4,128)(2,1)} %param.9) | copy-start | bytes 9437188
  5.7 9.4 %copy-start.6 = (f32[3,8,128]{2,1,0:T(8,128)}, f32[3,8,128]{2,1,0:T(8,128)S(1)}, u32[]{:S(2)}) copy-start(f32[3,8,128]{2,1,0:T(8,128)S(1)} %project.1) | copy-start | bytes 36868
  6.3 16.4 %collective-permute-start.2 = (f32[1,8,128]{2,1,0:T(8,128)}, f32[1,8,128]{2,1,0:T(8,128)}, u32[]{:S(2)}, u32[]{:S(2)}) collective-permute-start(f32[1,8,128]{2,1,0:T(8,128)} %slice_select_fusion.3), channel_id=1, source_target_pairs={{0,16},{16,0},{32,48},{48,32},{64,80},{80,64},{96,112},{112,96},{1... | collective-permute-start | bytes 12296 | tf_op jit(solution)/shard_map/ppermute | solution.py:187
  15.1 18.6 %collective-permute-start.1 = (bf16[768,128]{1,0:T(8,128)(2,1)S(1)}, bf16[768,128]{1,0:T(8,128)(2,1)}, u32[]{:S(2)}, u32[]{:S(2)}) collective-permute-start(bf16[768,128]{1,0:T(8,128)(2,1)S(1)} %bitcast.40), channel_id=1, source_target_pairs={{0,496},{16,32},{32,16},{48,64},{64,48},{80,96},{96,80},{112,128},... | collective-permute-start | bytes 589832 | tf_op jit(solution)/shard_map/ppermute | solution.py:192
  17.0 16.7 %collective-permute-start = (bf16[768,128]{1,0:T(8,128)(2,1)S(1)}, bf16[768,128]{1,0:T(8,128)(2,1)}, u32[]{:S(2)}, u32[]{:S(2)}) collective-permute-start(bf16[768,128]{1,0:T(8,128)(2,1)S(1)} %bitcast.41), channel_id=1, source_target_pairs={{0,16},{16,0},{32,48},{48,32},{64,80},{80,64},{96,112},{112,96},{1... | collective-permute-start | bytes 589832 | tf_op jit(solution)/shard_map/ppermute | solution.py:187
  22.6 36.6 %copy-start.4 = (bf16[384,128]{1,0:T(8,128)(2,1)S(1)}, bf16[384,128]{1,0:T(8,128)(2,1)}, u32[]{:S(2)}) copy-start(bf16[384,128]{1,0:T(8,128)(2,1)} %constant.75.clone.zmat_ref) | copy-start | bytes 294916
  23.4 5.0 %collective-permute-start.3 = (f32[2,8,128]{2,1,0:T(8,128)S(1)}, f32[2,8,128]{2,1,0:T(8,128)S(1)}, u32[]{:S(2)}, u32[]{:S(2)}) collective-permute-start(f32[2,8,128]{2,1,0:T(8,128)S(1)} %pad_maximum_fusion), channel_id=1, source_target_pairs={{0,496},{16,32},{32,16},{48,64},{64,48},{80,96},{96,80},{112,128},... | collective-permute-start | bytes 24584 | tf_op jit(solution)/shard_map/ppermute | solution.py:192
  28.3 5.3 %collective-permute-start.4 = (f32[1,8,128]{2,1,0:T(8,128)S(1)}, f32[1,8,128]{2,1,0:T(8,128)S(1)}, u32[]{:S(2)}, u32[]{:S(2)}) collective-permute-start(f32[1,8,128]{2,1,0:T(8,128)S(1)} %slice_select_fusion.1), channel_id=1, source_target_pairs={{0,16},{16,0},{32,48},{48,32},{64,80},{80,64},{96,112},{112,96},{1... | collective-permute-start | bytes 12296 | tf_op jit(solution)/shard_map/ppermute | solution.py:187
  33.7 0.9 copy-start.3
  43.1 3.1 %collective-permute-start.7 = (f32[1,8,128]{2,1,0:T(8,128)S(1)}, f32[1,8,128]{2,1,0:T(8,128)S(1)}, u32[]{:S(2)}, u32[]{:S(2)}) collective-permute-start(f32[1,8,128]{2,1,0:T(8,128)S(1)} %slice_select_fusion.6), channel_id=1, source_target_pairs={{0,16},{16,0},{32,48},{48,32},{64,80},{80,64},{96,112},{112,96},{1... | collective-permute-start | bytes 12296 | tf_op jit(solution)/shard_map/ppermute | solution.py:187
  46.2 9.9 %collective-permute-start.8 = (f32[2,8,128]{2,1,0:T(8,128)S(1)}, f32[2,8,128]{2,1,0:T(8,128)S(1)}, u32[]{:S(2)}, u32[]{:S(2)}) collective-permute-start(f32[2,8,128]{2,1,0:T(8,128)S(1)} %pad_maximum_fusion.1), channel_id=1, source_target_pairs={{0,496},{16,32},{32,16},{48,64},{64,48},{80,96},{96,80},{112,128},... | collective-permute-start | bytes 24584 | tf_op jit(solution)/shard_map/ppermute | solution.py:192
  48.1 11.1 %collective-permute-start.6 = (bf16[768,128]{1,0:T(8,128)(2,1)S(1)}, bf16[768,128]{1,0:T(8,128)(2,1)S(1)}, u32[]{:S(2)}, u32[]{:S(2)}) collective-permute-start(bf16[768,128]{1,0:T(8,128)(2,1)S(1)} %get-tuple-element.7.v_ref), channel_id=1, source_target_pairs={{0,496},{16,32},{32,16},{48,64},{64,48},{80,96},{96,80},{112,128},... | collective-permute-start | bytes 589832 | tf_op jit(solution)/shard_map/ppermute | solution.py:192
  51.8 7.5 %collective-permute-start.5 = (bf16[768,128]{1,0:T(8,128)(2,1)S(1)}, bf16[768,128]{1,0:T(8,128)(2,1)S(1)}, u32[]{:S(2)}, u32[]{:S(2)}) collective-permute-start(bf16[768,128]{1,0:T(8,128)(2,1)S(1)} %get-tuple-element.7.v_ref), channel_id=1, source_target_pairs={{0,16},{16,0},{32,48},{48,32},{64,80},{80,64},{96,112},{112,96},{1... | collective-permute-start | bytes 589832 | tf_op jit(solution)/shard_map/ppermute | solution.py:187
  56.2 3.1 %collective-permute-start.9 = (f32[1,8,128]{2,1,0:T(8,128)S(1)}, f32[1,8,128]{2,1,0:T(8,128)S(1)}, u32[]{:S(2)}, u32[]{:S(2)}) collective-permute-start(f32[1,8,128]{2,1,0:T(8,128)S(1)} %slice_select_fusion), channel_id=1, source_target_pairs={{0,16},{16,0},{32,48},{48,32},{64,80},{80,64},{96,112},{112,96},{1... | collective-permute-start | bytes 12296 | tf_op jit(solution)/shard_map/ppermute | solution.py:187

commit v2 on v0

v2 whole, which is shorter than its diff:
```python
import functools
import jax
import jax.numpy as jnp
import numpy as np
from jax import lax
from jax.experimental import pallas as pl
from jax.experimental.pallas import tpu as pltpu
from jax.sharding import PartitionSpec as P

STENCIL = [
    -5369.0 / 1800.0,
    12.0 / 7.0,
    -15.0 / 56.0,
    10.0 / 189.0,
    -1.0 / 112.0,
    2.0 / 1925.0,
    -1.0 / 16632.0,
]
kinetic_scale = 0.5 / 0.49
centre = 12.0
half_width = 11.0
REACH = 6
F32, BF16 = jnp.float32, jnp.bfloat16
WEIGHTS = [-kinetic_scale * w for w in STENCIL]


def split3(x):
    hi = x.astype(BF16)
    rest = x - hi.astype(F32)
    mid = rest.astype(BF16)
    return hi, mid, (rest - mid.astype(F32)).astype(BF16)


def z_matrix(depth):
    row = lax.broadcasted_iota(jnp.int32, (depth, depth), 0)
    col = lax.broadcasted_iota(jnp.int32, (depth, depth), 1)
    apart = jnp.abs(row - col)
    apart = jnp.minimum(apart, depth - apart)
    full = jnp.zeros((depth, depth), F32)
    for offset in range(1, REACH + 1):
        full = jnp.where(apart == offset, np.float32(WEIGHTS[offset]), full)
    return jnp.concatenate(split3(full), 0)


def dot_t(a, b):
    return lax.dot_general(a, b, (((1,), (1,)), ((), ())), preferred_element_type=F32)


class Sizes:
    def __init__(self, bands, atom_ids, strength, dom_count):
        self.bands, self.thickness, self.rows, self.depth = bands
        self.blocks, self.slot_count = atom_ids
        self.atoms, self.projs = strength
        self.doms = dom_count
        self.owned = self.atoms // dom_count
        self.block_rows = self.rows // self.blocks
        self.cells = self.thickness * self.rows
        self.slots = self.slot_count * self.projs
        self.lanes = self.owned * self.projs
        self.tall = self.cells * self.bands
        assert self.owned & (self.owned - 1) == 0 and dom_count & (dom_count - 1) == 0


def one_hots(z, dom, ids_ref):
    ids = ids_ref[...]
    shift = z.owned.bit_length() - 1
    relative = ((ids >> shift) - dom + (1 + z.doms)) & (z.doms - 1)
    place = relative * z.owned + (ids & (z.owned - 1))
    slot = lax.broadcasted_iota(jnp.int32, (z.slot_count, z.slots), 0)
    lane = lax.broadcasted_iota(jnp.int32, (z.slot_count, z.slots), 1)
    inside = lane - slot * z.projs
    spread = jnp.where((inside >= 0) & (inside < z.projs), 1.0, 0.0).astype(BF16)
    wide = jnp.dot(place.astype(F32).astype(BF16), spread, preferred_element_type=F32)
    shape = (z.lanes, z.slots)
    row = lax.broadcasted_iota(jnp.int32, shape, 0)
    lane = lax.broadcasted_iota(jnp.int32, shape, 1)
    fits = (row >> shift) == lane % z.projs
    atom = (row & (z.owned - 1)).astype(F32)
    out = []
    for j in range(z.blocks):
        mine = jnp.broadcast_to(wide[j : j + 1, :], shape)
        tiles = [
            jnp.where(fits & (mine == atom + float(z.owned * tile)), 1.0, 0.0) for tile in range(3)
        ]
        out.append(jnp.concatenate(tiles, 0).astype(BF16))
    return out


def scatter(z, side, partials, hots_ref, send_ref, pair_ref):
    total = None
    for j, partial in enumerate(partials):
        hot = hots_ref[j]
        for piece in split3(partial):
            part = dot_t(piece, hot)
            total = part if total is None else total + part
    below, middle, above = (total[:, t * z.lanes : (t + 1) * z.lanes] for t in range(3))
    first_core = side == 0
    send_ref[...] = jnp.where(first_core, above, below)
    pair_ref[0] = jnp.where(first_core, below, middle)
    pair_ref[1] = jnp.where(first_core, middle, above)


def gathered(z, side, pair_ref, other_ref, strength_ref, hots_ref):
    first_core = side == 0
    low, high, other = pair_ref[0], pair_ref[1], other_ref[...]
    tiles = [
        jnp.where(first_core, low, other),
        jnp.where(first_core, high, low),
        jnp.where(first_core, other, high),
    ]
    weighted = [tile * strength_ref[t : t + 1, :] for t, tile in enumerate(tiles)]
    weighted = jnp.concatenate(weighted, 1).astype(BF16)
    return [
        jnp.dot(weighted, hots_ref[j], preferred_element_type=F32).astype(BF16)
        for j in range(z.blocks)
    ]


def pair_rows(pair):
    return slice(16 * pair, 16 * pair + 16)


def block_of(z, pair):
    return (2 * pair % z.rows) // z.block_rows


class Projector:
    def __init__(self, z, v_ref, proj_ref):
        self.z, self.v_ref, self.proj_ref = z, v_ref, proj_ref
        self.even, self.odd = [None] * z.blocks, [None] * z.blocks

    def add(self, pairs):
        for pair in pairs:
            j = block_of(self.z, pair)
            v = self.v_ref[pair_rows(pair), :]
            e, o = dot_t(v, self.proj_ref[2 * pair]), dot_t(v, self.proj_ref[2 * pair + 1])
            self.even[j] = e if self.even[j] is None else self.even[j] + e
            self.odd[j] = o if self.odd[j] is None else self.odd[j] + o

    def sums(self):
        b = self.z.bands
        return [e[:b] + o[b:] for e, o in zip(self.even, self.odd)]


CHUNKS = 6
PROJECT_LIMIT = 60000


def project_kernel(
    z, ids_hbm, bands_hbm, proj_hbm, v_ref, send_ref, pair_ref, hots_ref,
    proj_ref, ids_ref, bands_ref, ids_sem, bands_sem, proj_sems,
):
    dom = lax.axis_index("dom")
    step = z.cells // CHUNKS
    ids_copy = pltpu.make_async_copy(ids_hbm, ids_ref, ids_sem)
    ids_copy.start()
    bands_copy = pltpu.make_async_copy(bands_hbm, bands_ref, bands_sem)
    bands_copy.start()
    copies = []
    for c in range(CHUNKS):
        at = pl.ds(c * step, step)
        copies.append(pltpu.make_async_copy(proj_hbm.at[at], proj_ref.at[at], proj_sems.at[c]))
        copies[-1].start()
    ids_copy.wait()
    for j, hot in enumerate(one_hots(z, dom, ids_ref)):
        hots_ref[j] = hot
    bands_copy.wait()
    for x in range(z.thickness):
        slab = bands_ref[:, x * z.rows : (x + 1) * z.rows, :].astype(F32)
        turned = jnp.swapaxes(slab, 0, 1).reshape(z.rows * z.bands, z.depth)
        v_ref[x * z.rows * z.bands : (x + 1) * z.rows * z.bands, :] = turned.astype(BF16)
    projector = Projector(z, v_ref, proj_ref)
    for c in range(CHUNKS):
        copies[c].wait()
        projector.add(range(c * step // 2, (c + 1) * step // 2))
    scatter(z, dom & 1, projector.sums(), hots_ref, send_ref, pair_ref)


def near_strength(z, dom, strength_ref, out_ref):
    per_tile = 128 // z.owned
    row = lax.broadcasted_iota(jnp.int32, (z.projs, 128), 0)
    lane = lax.broadcasted_iota(jnp.int32, (z.projs, 128), 1)
    for t in range(3):
        owner = (dom + (t - 1) + z.doms) & (z.doms - 1)
        tile = strength_ref[:, pl.ds(pl.multiple_of(owner // per_tile * 128, 128), 128)]
        inside = owner % per_tile
        line = jnp.zeros((1, 128), F32)
        for p in range(z.projs):
            turned = pltpu.roll(tile, ((p + per_tile) - inside) % per_tile * z.owned, 1)
            keep = (row == p) & (lane >= p * z.owned) & (lane < (p + 1) * z.owned)
            line = line + jnp.sum(jnp.where(keep, turned, 0.0), axis=0, keepdims=True)
        out_ref[t : t + 1, :] = line


def base_body(z, dom, v_ref, on_ref, off_ref, pot_ref, out_ref, wide_ref):
    first_core = (dom & 1) == 0
    on_at = pl.multiple_of(jnp.where(first_core, 2 * z.cells, 0), z.cells)
    off_at = pl.multiple_of(jnp.where(first_core, 0, 2 * z.cells), z.cells)
    step, b = 8, z.bands
    for c in range(0, z.cells, step):
        rows = slice(b * c, b * (c + step))
        shape = (step, b, z.depth)
        wide_ref[pl.ds(on_at + c, step)] = on_ref[rows, :].astype(F32).reshape(shape)
        wide_ref[pl.ds(off_at + c, step)] = off_ref[rows, :].astype(F32).reshape(shape)
        wide_ref[z.cells + c : z.cells + c + step] = v_ref[rows, :].astype(F32).reshape(shape)
    zmat = z_matrix(z.depth)
    for c in range(0, z.cells, z.rows):
        v = v_ref[b * c : b * (c + z.rows), :]
        along_z = jnp.dot(jnp.concatenate([v, v, v], 1), zmat, preferred_element_type=F32)
        for y in range(z.rows):
            at = z.cells + c + y
            mine = wide_ref[at]
            pot = pot_ref[c + y : c + y + 1, :] + (3.0 * WEIGHTS[0] - centre)
            total = pot * mine + along_z[b * y : b * y + b, :]
            for offset in range(1, REACH + 1):
                beside = wide_ref[at + offset * z.rows] + wide_ref[at - offset * z.rows]
                up = z.cells + c + (y + offset) % z.rows
                down = z.cells + c + (y - offset) % z.rows
                beside = beside + (wide_ref[up] + wide_ref[down])
                total = total + WEIGHTS[offset] * beside
            out_ref[b * (c + y) : b * (c + y) + b, :] = total


def base_first_kernel(z, v_ref, on_ref, off_ref, pot_ref, strength_ref, out_ref, near_ref, wide_ref):
    dom = lax.axis_index("dom")
    near_strength(z, dom, strength_ref, near_ref)
    base_body(z, dom, v_ref, on_ref, off_ref, pot_ref, out_ref, wide_ref)


def base_kernel(z, v_ref, on_ref, off_ref, pot_ref, out_ref, wide_ref):
    base_body(z, lax.axis_index("dom"), v_ref, on_ref, off_ref, pot_ref, out_ref, wide_ref)


def nonlocal_pair(weighted, proj_ref, pair):
    both = jnp.concatenate([proj_ref[2 * pair], proj_ref[2 * pair + 1]], 1)
    value = jnp.dot(weighted, both, preferred_element_type=F32)
    half = value.shape[1] // 2
    return jnp.concatenate([value[:, :half], value[:, half:]], 0)


def first_kernel(z, base_ref, pair_in, other_ref, near_ref, hots_ref, proj_ref, first_ref, send_ref, pair_ref):
    side = lax.axis_index("dom") & 1
    weighted = gathered(z, side, pair_in, other_ref, near_ref, hots_ref)
    for pair in range(z.cells // 2):
        rows = pair_rows(pair)
        value = base_ref[rows, :] + nonlocal_pair(weighted[block_of(z, pair)], proj_ref, pair)
        first_ref[rows, :] = (value / half_width).astype(BF16)
    projector = Projector(z, first_ref, proj_ref)
    projector.add(range(z.cells // 2))
    scatter(z, side, projector.sums(), hots_ref, send_ref, pair_ref)


def filtered_kernel(z, base_ref, pair_in, other_ref, near_ref, hots_ref, proj_ref, start_ref, out_ref):
    side = lax.axis_index("dom") & 1
    weighted = gathered(z, side, pair_in, other_ref, near_ref, hots_ref)
    for pair in range(z.cells // 2):
        rows = pair_rows(pair)
        value = base_ref[rows, :] + nonlocal_pair(weighted[block_of(z, pair)], proj_ref, pair)
        out_ref[rows, :] = (2.0 * value / half_width - start_ref[rows, :].astype(F32)).astype(BF16)


VMEM = pl.BlockSpec(memory_space=pltpu.VMEM)
HBM = pl.BlockSpec(memory_space=pltpu.HBM)


def call(kernel, z, name, outs, ins, flops, moved, spaces, scratch=(), limit=12288):
    single = not isinstance(outs, (list, tuple))
    return pl.pallas_call(
        functools.partial(kernel, z),
        name=name,
        out_shape=outs,
        in_specs=spaces,
        out_specs=VMEM if single else [VMEM] * len(outs),
        scratch_shapes=list(scratch),
        compiler_params=pltpu.CompilerParams(vmem_limit_bytes=limit * 1024),
        cost_estimate=pl.CostEstimate(flops=flops, bytes_accessed=moved, transcendentals=0),
    )(*ins)


def shapes(z):
    tile = jax.ShapeDtypeStruct((z.bands, z.lanes), F32)
    pair = jax.ShapeDtypeStruct((2, z.bands, z.lanes), F32)
    slab = jax.ShapeDtypeStruct((z.tall, z.depth), BF16)
    wide = jax.ShapeDtypeStruct((z.tall, z.depth), F32)
    near = jax.ShapeDtypeStruct((8, z.lanes), F32)
    proj = jax.ShapeDtypeStruct((z.cells, z.slots, z.depth), BF16)
    hots = jax.ShapeDtypeStruct((z.blocks, 3 * z.lanes, z.slots), BF16)
    return tile, pair, slab, wide, near, proj, hots


def run_project(z, ids, bands, proj):
    tile, pair, slab, wide, near, projs, hots = shapes(z)
    stream = 2 * z.tall * z.slots * z.depth
    return call(
        project_kernel, z, "project", [slab, tile, pair, hots], (ids, bands, proj),
        stream, 2 * z.cells * z.slots * z.depth, [HBM] * 3,
        scratch=[
            pltpu.VMEM((z.cells, z.slots, z.depth), BF16),
            pltpu.VMEM((z.blocks, z.slot_count), jnp.int32),
            pltpu.VMEM((z.bands, z.cells, z.depth), BF16),
            pltpu.SemaphoreType.DMA,
            pltpu.SemaphoreType.DMA,
            pltpu.SemaphoreType.DMA((CHUNKS,)),
        ],
        limit=PROJECT_LIMIT,
    )


def wide_scratch(z):
    return [pltpu.VMEM((3 * z.cells, z.bands, z.depth), F32)]


def run_base_first(z, v, on_chip, across, pot, strength_t):
    tile, pair, slab, wide, near, projs, hots = shapes(z)
    return call(
        base_first_kernel, z, "base_first", [wide, near], (v, on_chip, across, pot, strength_t),
        6 * z.tall * z.depth * z.depth, 10 * z.tall * z.depth, [VMEM] * 5,
        scratch=wide_scratch(z),
    )


def run_base(z, v, on_chip, across, pot):
    tile, pair, slab, wide, near, projs, hots = shapes(z)
    return call(
        base_kernel, z, "base", wide, (v, on_chip, across, pot),
        6 * z.tall * z.depth * z.depth, 10 * z.tall * z.depth, [VMEM] * 4,
        scratch=wide_scratch(z),
    )


def run_first(z, base, pair_in, other, near_in, hots_in, proj):
    tile, pair, slab, wide, near, projs, hots = shapes(z)
    stream = 2 * z.tall * z.slots * z.depth
    return call(
        first_kernel, z, "first", [slab, tile, pair], (base, pair_in, other, near_in, hots_in, proj),
        2 * stream, 2 * z.cells * z.slots * z.depth, [VMEM] * 6,
    )


def run_filtered(z, base, pair_in, other, near_in, hots_in, proj, start):
    tile, pair, slab, wide, near, projs, hots = shapes(z)
    stream = 2 * z.tall * z.slots * z.depth
    return call(
        filtered_kernel, z, "filtered", slab, (base, pair_in, other, near_in, hots_in, proj, start),
        stream, 2 * z.cells * z.slots * z.depth, [VMEM] * 7,
    )


def swap_on_chip(x, axis):
    count = lax.axis_size(axis)
    return lax.ppermute(x, axis, [(i, i ^ 1) for i in range(count)])


def swap_across(x, axis):
    count = lax.axis_size(axis)
    return lax.ppermute(x, axis, [(i, (((i + 1) ^ 1) - 1) % count) for i in range(count)])


def local(bands, potential, projectors, atom_ids, strength, rotation):
    z = Sizes(bands.shape, atom_ids.shape, strength.shape, lax.axis_size("dom"))
    band_count = lax.axis_size("band")
    side = lax.axis_index("dom") % 2
    proj = projectors.reshape(z.cells, z.slots, z.depth)
    pot = potential.reshape(z.cells, z.depth)
    flat = bands.reshape(z.bands, z.cells, z.depth)
    mine = (lax.broadcasted_iota(jnp.int32, (2, 1, 1), 0) + side) == 1

    def pair_of_chips(send, pair):
        pair = pair + jnp.where(mine, swap_on_chip(send, "dom")[None], 0.0)
        return pair + swap_across(pair, "dom")

    def other_tile(pair):
        return swap_on_chip(jnp.where(side == 0, pair[1], pair[0]), "dom")

    start, send, pair, hots = run_project(z, atom_ids, flat, proj)
    start_across, start_on = swap_across(start, "dom"), swap_on_chip(start, "dom")
    pair = pair_of_chips(send, pair)
    base, near = run_base_first(z, start, start_on, start_across, pot, strength.T)
    other = other_tile(pair)
    first, send, pair = run_first(z, base, pair, other, near, hots, proj)

    first_across, first_on = swap_across(first, "dom"), swap_on_chip(first, "dom")
    pair = pair_of_chips(send, pair)
    base = run_base(z, first, first_on, first_across, pot)
    other = other_tile(pair)
    filtered = run_filtered(z, base, pair, other, near, hots, proj, start)

    share = z.cells // band_count
    pieces = filtered.reshape(band_count, share, z.bands, z.depth)
    pieces = lax.all_to_all(pieces, "band", 0, 0, tiled=True)
    turn = rotation.reshape(band_count, z.bands, band_count * z.bands)
    turned = jnp.einsum("gxbz,gbc->xcz", pieces, turn, preferred_element_type=F32).astype(BF16)
    turned = turned.reshape(share, band_count, z.bands, z.depth).transpose(1, 0, 2, 3)
    turned = lax.all_to_all(turned, "band", 0, 0, tiled=True)
    return turned.reshape(z.cells, z.bands, z.depth).transpose(1, 0, 2).reshape(bands.shape)


def solution(mesh):
    placed = (
        P("band", "dom", None, None),
        P("dom", None, None),
        P("dom", None, None, None, None),
        P("dom", None),
        P(),
        P(),
    )
    return jax.shard_map(
        local, mesh=mesh, in_specs=placed, out_specs=P("band", "dom", None, None), check_vma=False
    )
```

time: 181 us -> 87.1 us (0.48)
  waiting for transfers between devices: 86.2 us -> 2.05 us
  blocking collectives: 0 us -> 33.5 us
  between operations: 13.9 us -> 0.27 us
  starting transfers between devices: 45.8 us -> 35 us
  local copies, waits for them, and re-layouts: 13.4 us -> 2.61 us
  Pallas kernels: 0 us -> 10.5 us
  matrix products: 10.1 us -> 0.26 us
  other arithmetic: 10.5 us -> 1.71 us
    all_gather x1 -> x0, waiting for transfers between devices: 77.4 us -> none  [local(): lax.all_gather(flat, 'band', axis=0, tiled=True)]
    all_to_all x0 -> x2, blocking collectives: none -> 33.5 us  [the longest x1 19.3 us: local(): pieces = lax.all_to_all(pieces, 'band', 0, 0, tiled=True)]
    ppermute x12 -> x10, starting transfers between devices: 45.8 us -> 35 us  [the longest x6 23.9 us: swap_on_chip(): return lax.ppermute(x, axis, [(i, i ^ 1) for i in range(count)])]
    pallas_call x0 -> x5, Pallas kernels: none -> 10.5 us  [call(): pl.pallas_call(functools.partial(kernel, z), name=name, out_shape=outs, i...]
    dot_general x5 -> x1, matrix products: 10.1 us -> 0.26 us  [local(): jnp.einsum('gxbz,gbc->xcz', pieces, turn, preferred_element_type=F32)]
    convert_element_type x6 -> x0, other arithmetic: 8.8 us -> none  [the longest x1 3.43 us: local(): filtered = (2.0 * (apply_hamiltonian(first) - centre * first_values) / ha...]
    ppermute x12 -> x10, waiting for transfers between devices: 8.83 us -> 2.05 us  [the longest x6 2.04 us: swap_on_chip(): return lax.ppermute(x, axis, [(i, i ^ 1) for i in range(count)])]
    slice x50 -> x0, local copies, waits for them, and re-layouts: 5.5 us -> none  [the longest x24 4.4 us: laplace_slab(): beside = beside + jnp.roll(middle, offset, 3) + jnp.roll(middle, -offset, 3)]
  transfers between devices with their start and end apart: 13 -> 10, of which waited for: 5 -> 3; matrix products, arithmetic and copies ran while one was open for 6% -> 1% of each run, Pallas kernels for 0% -> 3%
where the time goes in v2:
time: 87.1 us; the launch traced here: 85.9 us
  starting transfers between devices  35 us (40%)
  blocking collectives  33.5 us (38%)
  Pallas kernels  10.5 us (12%)
  local copies, waits for them, and re-layouts  2.61 us (3%)
  waiting for transfers between devices  2.05 us (2%)
  other arithmetic  1.71 us (2%)
    ppermute x6, starting transfers between devices, swap_on_chip(): return lax.ppermute(x, axis, [(i, i ^ 1) for i in range(count)])  23.9 us
    all_to_all x1, blocking collectives, local(): pieces = lax.all_to_all(pieces, 'band', 0, 0, tiled=True)  19.3 us
    all_to_all x1, blocking collectives, local(): turned = lax.all_to_all(turned, 'band', 0, 0, tiled=True)  14.2 us
    ppermute x4, starting transfers between devices, swap_across(): lax.ppermute(x, axis, [(i, ((i + 1 ^ 1) - 1) % count) for i in range(coun...  11.1 us
    pallas_call x5, Pallas kernels, call(): pl.pallas_call(functools.partial(kernel, z), name=name, out_shape=outs, i...  10.5 us
    ppermute x6, waiting for transfers between devices, swap_on_chip(): return lax.ppermute(x, axis, [(i, i ^ 1) for i in range(count)])  2.04 us
    unnamed x16, local copies, waits for them, and re-layouts  1.87 us
  transfers between devices with their start and end apart: 10, of which 3 were waited for; matrix products, arithmetic and copies ran while one was open for 1% of the time, Pallas kernels for 3%

profile of v2, /device:TPU:1, one launch (start us, length us, event | category | flops | bytes accessed | tf_op | source)
XLA Modules:
  0.0 85.9 jit_solution(5333752375229378635)
XLA Ops:
  0.0 4.6 %project.1 = (bf16[768,128]{1,0:T(8,128)(2,1)}, f32[8,128]{1,0:T(8,128)}, f32[2,8,128]{2,1,0:T(8,128)}, bf16[2,384,128]{2,1,0:T(8,128)(2,1)}) custom-call(s32[2,32]{1,0:T(2,128)} %ids_hbm.1, bf16[8,96,128]{2,1,0:T(8,128)(2,1)} %bitcast.44, bf16[96,128,128]{2,1,0:T(8,128)(2,1)} %bitcast.35), custom_call_target="tpu_custom_call" | custom-call | flops 25165824 | bytes 3145728 | tf_op jit(solution)/shard_map/project/pallas_call | solution.py:268
  4.6 8.9 %collective-permute-start.2 = (f32[8,128]{1,0:T(8,128)}, f32[8,128]{1,0:T(8,128)S(1)}, u32[]{:S(2)}, u32[]{:S(2)}) collective-permute-start(f32[8,128]{1,0:T(8,128)} %get-tuple-element.17), channel_id=1, source_target_pairs={{0,16},{16,0},{32,48},{48,32},{64,80},{80,64},{96,112},{112,96},{1... | collective-permute-start | bytes 12296 | tf_op jit(solution)/shard_map/ppermute | solution.py:351
  13.6 1.0 %collective-permute-done.2 = f32[8,128]{1,0:T(8,128)S(1)} collective-permute-done((f32[8,128]{1,0:T(8,128)}, f32[8,128]{1,0:T(8,128)S(1)}, u32[]{:S(2)}, u32[]{:S(2)}) %collective-permute-start.2) | collective-permute-done | bytes 4128 | tf_op jit(solution)/shard_map/ppermute | solution.py:351
  14.5 0.8 select_add_fusion.1
  15.3 1.9 %collective-permute-start.3 = (f32[2,8,128]{2,1,0:T(8,128)S(1)}, f32[2,8,128]{2,1,0:T(8,128)S(1)}, u32[]{:S(2)}, u32[]{:S(2)}) collective-permute-start(f32[2,8,128]{2,1,0:T(8,128)S(1)} %select_add_fusion.1), channel_id=1, source_target_pairs={{0,496},{16,32},{32,16},{48,64},{64,48},{80,96},{96,80},{112,128},... | collective-permute-start | bytes 24584 | tf_op jit(solution)/shard_map/ppermute | solution.py:356
  17.2 3.6 %collective-permute-start.1 = (bf16[768,128]{1,0:T(8,128)(2,1)}, bf16[768,128]{1,0:T(8,128)(2,1)}, u32[]{:S(2)}, u32[]{:S(2)}) collective-permute-start(bf16[768,128]{1,0:T(8,128)(2,1)} %get-tuple-element.14.v_ref.start_ref), channel_id=1, source_target_pairs={{0,496},{16,32},{32,16},{48,64},{64,48},{80,96},{96,80},{112,128},... | collective-permute-start | bytes 589832 | tf_op jit(solution)/shard_map/ppermute | solution.py:356
  20.9 4.4 %collective-permute-start = (bf16[768,128]{1,0:T(8,128)(2,1)}, bf16[768,128]{1,0:T(8,128)(2,1)}, u32[]{:S(2)}, u32[]{:S(2)}) collective-permute-start(bf16[768,128]{1,0:T(8,128)(2,1)} %get-tuple-element.14.v_ref.start_ref), channel_id=1, source_target_pairs={{0,16},{16,0},{32,48},{48,32},{64,80},{80,64},{96,112},{112,96},{1... | collective-permute-start | bytes 589832 | tf_op jit(solution)/shard_map/ppermute | solution.py:351
  25.3 0.8 fusion.7.pair_in
  26.0 1.9 %collective-permute-start.4 = (f32[8,128]{1,0:T(8,128)S(1)}, f32[8,128]{1,0:T(8,128)S(1)}, u32[]{:S(2)}, u32[]{:S(2)}) collective-permute-start(f32[8,128]{1,0:T(8,128)S(1)} %fusion.4), channel_id=1, source_target_pairs={{0,16},{16,0},{32,48},{48,32},{64,80},{80,64},{96,112},{112,96},{1... | collective-permute-start | bytes 12296 | tf_op jit(solution)/shard_map/ppermute | solution.py:351
  28.0 0.9 %copy-done.4 = bf16[768,128]{1,0:T(8,128)(2,1)S(1)} copy-done((bf16[768,128]{1,0:T(8,128)(2,1)S(1)}, bf16[768,128]{1,0:T(8,128)(2,1)}, u32[]{:S(2)}) %copy-start.4) | copy-done | bytes 196632
  28.9 1.9 %base_first.1 = (f32[768,128]{1,0:T(8,128)S(1)}, f32[8,128]{1,0:T(8,128)S(1)}) custom-call(bf16[768,128]{1,0:T(8,128)(2,1)S(1)} %copy-done.4, bf16[768,128]{1,0:T(8,128)(2,1)} %collective-permute-done.on_ref, bf16[768,128]{1,0:T(8,128)(2,1)} %collective-permute-done.1.off_ref, f32[96,128]{1,0:T(8,128)S(1)} %bitcast.39, f32[4,1024]{1,0:T(4,128)S(1)} %bitcast.41), custom_call_target="tpu_custom_call" | custom-call | flops 75497472 | bytes 983040 | tf_op jit(solution)/shard_map/base_first/pallas_call | solution.py:268
  30.9 0.9 %copy-done.2 = bf16[2,384,128]{2,1,0:T(8,128)(2,1)S(1)} copy-done((bf16[2,384,128]{2,1,0:T(8,128)(2,1)S(1)}, bf16[2,384,128]{2,1,0:T(8,128)(2,1)}, u32[]{:S(2)}) %copy-start.2) | copy-done | bytes 196632
  31.8 2.4 %first.1 = (bf16[768,128]{1,0:T(8,128)(2,1)S(1)}, f32[8,128]{1,0:T(8,128)S(1)}, f32[2,8,128]{2,1,0:T(8,128)S(1)}) custom-call(f32[768,128]{1,0:T(8,128)S(1)} %get-tuple-element.15.base_ref, f32[2,8,128]{2,1,0:T(8,128)S(1)} %fusion.7.pair_in, f32[8,128]{1,0:T(8,128)S(1)} %collective-permute-done.4.other_ref, f32[8,128]{1,0:T(8,128)S(1)} %get-tuple-element.18.near_ref, ...), custom_call_target="tpu_custom_call" | custom-call | flops 50331648 | bytes 3145728 | tf_op jit(solution)/shard_map/first/pallas_call | solution.py:268
  34.3 2.4 %collective-permute-start.7 = (f32[8,128]{1,0:T(8,128)S(1)}, f32[8,128]{1,0:T(8,128)S(1)}, u32[]{:S(2)}, u32[]{:S(2)}) collective-permute-start(f32[8,128]{1,0:T(8,128)S(1)} %get-tuple-element.22), channel_id=1, source_target_pairs={{0,16},{16,0},{32,48},{48,32},{64,80},{80,64},{96,112},{112,96},{1... | collective-permute-start | bytes 12296 | tf_op jit(solution)/shard_map/ppermute | solution.py:351
  36.7 0.8 collective-permute-done.7
  37.6 1.9 %collective-permute-start.8 = (f32[2,8,128]{2,1,0:T(8,128)S(1)}, f32[2,8,128]{2,1,0:T(8,128)S(1)}, u32[]{:S(2)}, u32[]{:S(2)}) collective-permute-start(f32[2,8,128]{2,1,0:T(8,128)S(1)} %select_add_fusion), channel_id=1, source_target_pairs={{0,496},{16,32},{32,16},{48,64},{64,48},{80,96},{96,80},{112,128},... | collective-permute-start | bytes 24584 | tf_op jit(solution)/shard_map/ppermute | solution.py:356
  39.5 3.6 %collective-permute-start.6 = (bf16[768,128]{1,0:T(8,128)(2,1)S(1)}, bf16[768,128]{1,0:T(8,128)(2,1)S(1)}, u32[]{:S(2)}, u32[]{:S(2)}) collective-permute-start(bf16[768,128]{1,0:T(8,128)(2,1)S(1)} %get-tuple-element.20.v_ref), channel_id=1, source_target_pairs={{0,496},{16,32},{32,16},{48,64},{64,48},{80,96},{96,80},{112,128},... | collective-permute-start | bytes 589832 | tf_op jit(solution)/shard_map/ppermute | solution.py:356
  43.2 4.4 %collective-permute-start.5 = (bf16[768,128]{1,0:T(8,128)(2,1)S(1)}, bf16[768,128]{1,0:T(8,128)(2,1)S(1)}, u32[]{:S(2)}, u32[]{:S(2)}) collective-permute-start(bf16[768,128]{1,0:T(8,128)(2,1)S(1)} %get-tuple-element.20.v_ref), channel_id=1, source_target_pairs={{0,16},{16,0},{32,48},{48,32},{64,80},{80,64},{96,112},{112,96},{1... | collective-permute-start | bytes 589832 | tf_op jit(solution)/shard_map/ppermute | solution.py:351
  47.6 1.9 %collective-permute-start.9 = (f32[8,128]{1,0:T(8,128)S(1)}, f32[8,128]{1,0:T(8,128)S(1)}, u32[]{:S(2)}, u32[]{:S(2)}) collective-permute-start(f32[8,128]{1,0:T(8,128)S(1)} %fusion.3), channel_id=1, source_target_pairs={{0,16},{16,0},{32,48},{48,32},{64,80},{80,64},{96,112},{112,96},{1... | collective-permute-start | bytes 12296 | tf_op jit(solution)/shard_map/ppermute | solution.py:351
  49.6 0.9 %base.1.base_ref = f32[768,128]{1,0:T(8,128)S(1)} custom-call(bf16[768,128]{1,0:T(8,128)(2,1)S(1)} %get-tuple-element.20.v_ref, bf16[768,128]{1,0:T(8,128)(2,1)S(1)} %collective-permute-done.5.on_ref, bf16[768,128]{1,0:T(8,128)(2,1)S(1)} %collective-permute-done.6.off_ref, f32[96,128]{1,0:T(8,128)S(1)} %bitcast.40), custom_call_target="tpu_custom_call" | custom-call | flops 75497472 | bytes 983040 | tf_op jit(solution)/shard_map/base/pallas_call | solution.py:268
  50.7 0.6 filtered.1
  51.3 19.3 %all_to_all.10 = bf16[16,6,8,128]{3,2,1,0:T(8,128)(2,1)S(1)} all-to-all(bf16[16,6,8,128]{3,2,1,0:T(8,128)(2,1)S(1)} %bitcast.38), channel_id=1, replica_groups=mesh['dom'=32,'band'=16] {'band'}, dimensions={0} | all-to-all | bytes 393216 | tf_op jit(solution)/shard_map/all_to_all | solution.py:390
  70.9 14.2 %all_to_all.11 = bf16[16,6,8,128]{3,2,1,0:T(8,128)(2,1)S(1)} all-to-all(bf16[16,6,8,128]{3,2,1,0:T(8,128)(2,1)S(1)} %bitcast.42), channel_id=1, replica_groups=mesh['dom'=32,'band'=16] {'band'}, dimensions={0} | all-to-all | bytes 393216 | tf_op jit(solution)/shard_map/all_to_all | solution.py:394
  85.2 0.7 copy.16
  (29 shorter events, 0.8 us)
Async XLA Ops:
  0.0 70.6 %copy-start = (bf16[128,128]{1,0:T(8,128)(2,1)S(1)}, bf16[128,128]{1,0:T(8,128)(2,1)}, u32[]{:S(2)}) copy-start(bf16[128,128]{1,0:T(8,128)(2,1)} %param.11) | copy-start | bytes 98308
  0.0 30.9 %copy-start.1 = (bf16[6,16,32,4,128]{4,3,2,1,0:T(4,128)(2,1)S(1)}, bf16[6,16,32,4,128]{4,3,2,1,0:T(4,128)(2,1)}, u32[]{:S(2)}) copy-start(bf16[6,16,32,4,128]{4,3,2,1,0:T(4,128)(2,1)} %param.8) | copy-start | bytes 9437188
  0.0 28.0 %copy-start.7 = (f32[1024,4]{0,1:T(4,128)S(1)}, f32[1024,4]{0,1:T(4,128)}, u32[]{:S(2)}) copy-start(f32[1024,4]{0,1:T(4,128)} %param.10) | copy-start | bytes 49156
  0.0 28.0 %copy-start.6 = (f32[6,16,128]{2,1,0:T(8,128)S(1)}, f32[6,16,128]{2,1,0:T(8,128)}, u32[]{:S(2)}) copy-start(f32[6,16,128]{2,1,0:T(8,128)} %param.7) | copy-start | bytes 147460
  4.6 46.1 %copy-start.3 = (bf16[2,384,128]{2,1,0:T(8,128)(2,1)S(1)}, bf16[2,384,128]{2,1,0:T(8,128)(2,1)}, u32[]{:S(2)}) copy-start(bf16[2,384,128]{2,1,0:T(8,128)(2,1)} %get-tuple-element.19.hots_ref) | copy-start | bytes 589828
  4.6 9.9 %collective-permute-start.2 = (f32[8,128]{1,0:T(8,128)}, f32[8,128]{1,0:T(8,128)S(1)}, u32[]{:S(2)}, u32[]{:S(2)}) collective-permute-start(f32[8,128]{1,0:T(8,128)} %get-tuple-element.17), channel_id=1, source_target_pairs={{0,16},{16,0},{32,48},{48,32},{64,80},{80,64},{96,112},{112,96},{1... | collective-permute-start | bytes 12296 | tf_op jit(solution)/shard_map/ppermute | solution.py:351
  15.3 9.9 %collective-permute-start.3 = (f32[2,8,128]{2,1,0:T(8,128)S(1)}, f32[2,8,128]{2,1,0:T(8,128)S(1)}, u32[]{:S(2)}, u32[]{:S(2)}) collective-permute-start(f32[2,8,128]{2,1,0:T(8,128)S(1)} %select_add_fusion.1), channel_id=1, source_target_pairs={{0,496},{16,32},{32,16},{48,64},{64,48},{80,96},{96,80},{112,128},... | collective-permute-start | bytes 24584 | tf_op jit(solution)/shard_map/ppermute | solution.py:356
  17.2 10.7 %collective-permute-start.1 = (bf16[768,128]{1,0:T(8,128)(2,1)}, bf16[768,128]{1,0:T(8,128)(2,1)}, u32[]{:S(2)}, u32[]{:S(2)}) collective-permute-start(bf16[768,128]{1,0:T(8,128)(2,1)} %get-tuple-element.14.v_ref.start_ref), channel_id=1, source_target_pairs={{0,496},{16,32},{32,16},{48,64},{64,48},{80,96},{96,80},{112,128},... | collective-permute-start | bytes 589832 | tf_op jit(solution)/shard_map/ppermute | solution.py:356
  20.9 7.1 %collective-permute-start = (bf16[768,128]{1,0:T(8,128)(2,1)}, bf16[768,128]{1,0:T(8,128)(2,1)}, u32[]{:S(2)}, u32[]{:S(2)}) collective-permute-start(bf16[768,128]{1,0:T(8,128)(2,1)} %get-tuple-element.14.v_ref.start_ref), channel_id=1, source_target_pairs={{0,16},{16,0},{32,48},{48,32},{64,80},{80,64},{96,112},{112,96},{1... | collective-permute-start | bytes 589832 | tf_op jit(solution)/shard_map/ppermute | solution.py:351
  26.0 4.9 %collective-permute-start.4 = (f32[8,128]{1,0:T(8,128)S(1)}, f32[8,128]{1,0:T(8,128)S(1)}, u32[]{:S(2)}, u32[]{:S(2)}) collective-permute-start(f32[8,128]{1,0:T(8,128)S(1)} %fusion.4), channel_id=1, source_target_pairs={{0,16},{16,0},{32,48},{48,32},{64,80},{80,64},{96,112},{112,96},{1... | collective-permute-start | bytes 12296 | tf_op jit(solution)/shard_map/ppermute | solution.py:351
  28.0 0.9 %copy-start.4 = (bf16[768,128]{1,0:T(8,128)(2,1)S(1)}, bf16[768,128]{1,0:T(8,128)(2,1)}, u32[]{:S(2)}) copy-start(bf16[768,128]{1,0:T(8,128)(2,1)} %get-tuple-element.14.v_ref.start_ref) | copy-start | bytes 589828
  28.9 21.7 %copy-start.5 = (bf16[768,128]{1,0:T(8,128)(2,1)S(1)}, bf16[768,128]{1,0:T(8,128)(2,1)}, u32[]{:S(2)}) copy-start(bf16[768,128]{1,0:T(8,128)(2,1)} %get-tuple-element.14.v_ref.start_ref) | copy-start | bytes 589828
  30.9 0.9 %copy-start.2 = (bf16[2,384,128]{2,1,0:T(8,128)(2,1)S(1)}, bf16[2,384,128]{2,1,0:T(8,128)(2,1)}, u32[]{:S(2)}) copy-start(bf16[2,384,128]{2,1,0:T(8,128)(2,1)} %get-tuple-element.19.hots_ref) | copy-start | bytes 589828
  34.3 3.2 %collective-permute-start.7 = (f32[8,128]{1,0:T(8,128)S(1)}, f32[8,128]{1,0:T(8,128)S(1)}, u32[]{:S(2)}, u32[]{:S(2)}) collective-permute-start(f32[8,128]{1,0:T(8,128)S(1)} %get-tuple-element.22), channel_id=1, source_target_pairs={{0,16},{16,0},{32,48},{48,32},{64,80},{80,64},{96,112},{112,96},{1... | collective-permute-start | bytes 12296 | tf_op jit(solution)/shard_map/ppermute | solution.py:351
  37.6 9.9 %collective-permute-start.8 = (f32[2,8,128]{2,1,0:T(8,128)S(1)}, f32[2,8,128]{2,1,0:T(8,128)S(1)}, u32[]{:S(2)}, u32[]{:S(2)}) collective-permute-start(f32[2,8,128]{2,1,0:T(8,128)S(1)} %select_add_fusion), channel_id=1, source_target_pairs={{0,496},{16,32},{32,16},{48,64},{64,48},{80,96},{96,80},{112,128},... | collective-permute-start | bytes 24584 | tf_op jit(solution)/shard_map/ppermute | solution.py:356
  39.5 10.0 %collective-permute-start.6 = (bf16[768,128]{1,0:T(8,128)(2,1)S(1)}, bf16[768,128]{1,0:T(8,128)(2,1)S(1)}, u32[]{:S(2)}, u32[]{:S(2)}) collective-permute-start(bf16[768,128]{1,0:T(8,128)(2,1)S(1)} %get-tuple-element.20.v_ref), channel_id=1, source_target_pairs={{0,496},{16,32},{32,16},{48,64},{64,48},{80,96},{96,80},{112,128},... | collective-permute-start | bytes 589832 | tf_op jit(solution)/shard_map/ppermute | solution.py:356
  43.2 6.4 %collective-permute-start.5 = (bf16[768,128]{1,0:T(8,128)(2,1)S(1)}, bf16[768,128]{1,0:T(8,128)(2,1)S(1)}, u32[]{:S(2)}, u32[]{:S(2)}) collective-permute-start(bf16[768,128]{1,0:T(8,128)(2,1)S(1)} %get-tuple-element.20.v_ref), channel_id=1, source_target_pairs={{0,16},{16,0},{32,48},{48,32},{64,80},{80,64},{96,112},{112,96},{1... | collective-permute-start | bytes 589832 | tf_op jit(solution)/shard_map/ppermute | solution.py:351
  47.6 3.0 %collective-permute-start.9 = (f32[8,128]{1,0:T(8,128)S(1)}, f32[8,128]{1,0:T(8,128)S(1)}, u32[]{:S(2)}, u32[]{:S(2)}) collective-permute-start(f32[8,128]{1,0:T(8,128)S(1)} %fusion.3), channel_id=1, source_target_pairs={{0,16},{16,0},{32,48},{48,32},{64,80},{80,64},{96,112},{112,96},{1... | collective-permute-start | bytes 12296 | tf_op jit(solution)/shard_map/ppermute | solution.py:351

commit v3 on v2

--- a/solution.py
+++ b/solution.py
@@ -142,13 +142,25 @@
         return [e[:b] + o[b:] for e, o in zip(self.even, self.odd)]
 
 
+def turned(z, bands_ref, x):
+    plane = bands_ref[:, x * z.rows : (x + 1) * z.rows, :].astype(F32)
+    return jnp.swapaxes(plane, 0, 1)
+
+
+def turn_all(z, bands_ref, v_ref):
+    tall = z.rows * z.bands
+    for x in range(z.thickness):
+        plane = turned(z, bands_ref, x).reshape(tall, z.depth)
+        v_ref[x * tall : (x + 1) * tall, :] = plane.astype(BF16)
+
+
 CHUNKS = 6
-PROJECT_LIMIT = 60000
+PROJECT_LIMIT = 64900
 
 
 def project_kernel(
-    z, ids_hbm, bands_hbm, proj_hbm, v_ref, send_ref, pair_ref, hots_ref,
-    proj_ref, ids_ref, bands_ref, ids_sem, bands_sem, proj_sems,
+    z, ids_hbm, bands_hbm, proj_hbm, send_ref, kept_ref,
+    v_ref, hots_ref, proj_ref, ids_ref, bands_ref, ids_sem, bands_sem, proj_sems,
 ):
     dom = lax.axis_index("dom")
     step = z.cells // CHUNKS
@@ -165,15 +177,21 @@
     for j, hot in enumerate(one_hots(z, dom, ids_ref)):
         hots_ref[j] = hot
     bands_copy.wait()
-    for x in range(z.thickness):
-        slab = bands_ref[:, x * z.rows : (x + 1) * z.rows, :].astype(F32)
-        turned = jnp.swapaxes(slab, 0, 1).reshape(z.rows * z.bands, z.depth)
-        v_ref[x * z.rows * z.bands : (x + 1) * z.rows * z.bands, :] = turned.astype(BF16)
+    turn_all(z, bands_ref, v_ref)
     projector = Projector(z, v_ref, proj_ref)
     for c in range(CHUNKS):
         copies[c].wait()
         projector.add(range(c * step // 2, (c + 1) * step // 2))
-    scatter(z, dom & 1, projector.sums(), hots_ref, send_ref, pair_ref)
+    scatter(z, dom & 1, projector.sums(), hots_ref, send_ref, kept_ref)
+    ones = jnp.full(kept_ref.shape[1:], 1.0, F32)
+    kept_ref[2] = jnp.where((dom & 1) == 1, ones, 0.0)
+    kept_ref[3] = jnp.where((dom & 1) == 0, ones, 0.0)
+
+
+def stage_kernel(z, kept_ref, pair_ref, keep_ref):
+    for t in range(2):
+        pair_ref[t] = kept_ref[t]
+        keep_ref[t] = kept_ref[2 + t]
 
 
 def near_strength(z, dom, strength_ref, out_ref):
@@ -192,43 +210,87 @@
         out_ref[t : t + 1, :] = line
 
 
-def base_body(z, dom, v_ref, on_ref, off_ref, pot_ref, out_ref, wide_ref):
-    first_core = (dom & 1) == 0
-    on_at = pl.multiple_of(jnp.where(first_core, 2 * z.cells, 0), z.cells)
-    off_at = pl.multiple_of(jnp.where(first_core, 0, 2 * z.cells), z.cells)
-    step, b = 8, z.bands
-    for c in range(0, z.cells, step):
-        rows = slice(b * c, b * (c + step))
-        shape = (step, b, z.depth)
-        wide_ref[pl.ds(on_at + c, step)] = on_ref[rows, :].astype(F32).reshape(shape)
-        wide_ref[pl.ds(off_at + c, step)] = off_ref[rows, :].astype(F32).reshape(shape)
-        wide_ref[z.cells + c : z.cells + c + step] = v_ref[rows, :].astype(F32).reshape(shape)
+def base_body(z, dom, v_ref, wide_ref, write):
+    b = z.bands
     zmat = z_matrix(z.depth)
     for c in range(0, z.cells, z.rows):
         v = v_ref[b * c : b * (c + z.rows), :]
         along_z = jnp.dot(jnp.concatenate([v, v, v], 1), zmat, preferred_element_type=F32)
-        for y in range(z.rows):
-            at = z.cells + c + y
-            mine = wide_ref[at]
-            pot = pot_ref[c + y : c + y + 1, :] + (3.0 * WEIGHTS[0] - centre)
-            total = pot * mine + along_z[b * y : b * y + b, :]
-            for offset in range(1, REACH + 1):
-                beside = wide_ref[at + offset * z.rows] + wide_ref[at - offset * z.rows]
-                up = z.cells + c + (y + offset) % z.rows
-                down = z.cells + c + (y - offset) % z.rows
-                beside = beside + (wide_ref[up] + wide_ref[down])
-                total = total + WEIGHTS[offset] * beside
-            out_ref[b * (c + y) : b * (c + y) + b, :] = total
-
-
-def base_first_kernel(z, v_ref, on_ref, off_ref, pot_ref, strength_ref, out_ref, near_ref, wide_ref):
+        for y in range(0, z.rows, 2):
+            both = []
+            for at in (y, y + 1):
+                here = z.cells + c + at
+                total = wide_ref[here] * (write.pot(c + at) + (3.0 * WEIGHTS[0] - centre))
+                total = total + along_z[b * at : b * at + b, :]
+                for offset in range(1, REACH + 1):
+                    beside = wide_ref[here + offset * z.rows] + wide_ref[here - offset * z.rows]
+                    up = z.cells + c + (at + offset) % z.rows
+                    down = z.cells + c + (at - offset) % z.rows
+                    beside = beside + (wide_ref[up] + wide_ref[down])
+                    total = total + WEIGHTS[offset] * beside
+                both.append(total)
+            write((c + y) // 2, jnp.concatenate(both, 0))
+
+
+class Writer:
+    def __init__(self, pot_ref, put):
+        self.pot_ref, self.put = pot_ref, put
+
+    def pot(self, cell):
+        return self.pot_ref[cell : cell + 1, :]
+
+    def __call__(self, pair, value):
+        self.put(pair_rows(pair), value)
+
+
+def places(z, dom):
+    first_core = (dom & 1) == 0
+    on_at = pl.multiple_of(jnp.where(first_core, 2 * z.cells, 0), z.cells)
+    off_at = pl.multiple_of(jnp.where(first_core, 0, 2 * z.cells), z.cells)
+    return on_at, off_at
+
+
+def base_first_kernel(
+    z, bands_ref, on_ref, off_ref, pot_ref, strength_ref, ids_ref,
+    out_ref, near_ref, hots_ref, v_ref, wide_ref,
+):
     dom = lax.axis_index("dom")
+    on_at, off_at = places(z, dom)
+    for x in range(z.thickness):
+        at = x * z.rows
+        mine = turned(z, bands_ref, x)
+        wide_ref[z.cells + at : z.cells + at + z.rows] = mine
+        rows = slice(z.bands * at, z.bands * (at + z.rows))
+        v_ref[rows, :] = mine.reshape(z.rows * z.bands, z.depth).astype(BF16)
+        wide_ref[pl.ds(on_at + at, z.rows)] = turned(z, on_ref, x)
+        wide_ref[pl.ds(off_at + at, z.rows)] = turned(z, off_ref, x)
+
+    def put(rows, value):
+        out_ref[rows, :] = value
+
+    base_body(z, dom, v_ref, wide_ref, Writer(pot_ref, put))
     near_strength(z, dom, strength_ref, near_ref)
-    base_body(z, dom, v_ref, on_ref, off_ref, pot_ref, out_ref, wide_ref)
-
-
-def base_kernel(z, v_ref, on_ref, off_ref, pot_ref, out_ref, wide_ref):
-    base_body(z, lax.axis_index("dom"), v_ref, on_ref, off_ref, pot_ref, out_ref, wide_ref)
+    for j, hot in enumerate(one_hots(z, dom, ids_ref)):
+        hots_ref[j] = hot
+
+
+def smooth_kernel(z, v_ref, on_ref, off_ref, pot_ref, start_ref, out_ref, wide_ref):
+    dom = lax.axis_index("dom")
+    on_at, off_at = places(z, dom)
+    step, b = 8, z.bands
+
+    def tile(ref, c):
+        return ref[b * c : b * (c + step), :].astype(F32).reshape(step, b, z.depth)
+
+    for c in range(0, z.cells, step):
+        wide_ref[z.cells + c : z.cells + c + step] = tile(v_ref, c)
+        wide_ref[pl.ds(on_at + c, step)] = tile(on_ref, c)
+        wide_ref[pl.ds(off_at + c, step)] = tile(off_ref, c)
+
+    def put(rows, value):
+        out_ref[rows, :] = (2.0 * value / half_width - start_ref[rows, :].astype(F32)).astype(BF16)
+
+    base_body(z, dom, v_ref, wide_ref, Writer(pot_ref, put))
 
 
 def nonlocal_pair(weighted, proj_ref, pair):
@@ -250,27 +312,109 @@
     scatter(z, side, projector.sums(), hots_ref, send_ref, pair_ref)
 
 
-def filtered_kernel(z, base_ref, pair_in, other_ref, near_ref, hots_ref, proj_ref, start_ref, out_ref):
+def share_kernel(z, groups, pair_in, other_ref, near_ref, hots_ref, rotation_ref, out_ref, big_ref, tall_ref):
     side = lax.axis_index("dom") & 1
+    me = lax.axis_index("band")
+    b, all_bands = z.bands, groups * z.bands
     weighted = gathered(z, side, pair_in, other_ref, near_ref, hots_ref)
-    for pair in range(z.cells // 2):
-        rows = pair_rows(pair)
-        value = base_ref[rows, :] + nonlocal_pair(weighted[block_of(z, pair)], proj_ref, pair)
-        out_ref[rows, :] = (2.0 * value / half_width - start_ref[rows, :].astype(F32)).astype(BF16)
+    turn = rotation_ref[...].astype(F32).T.astype(BF16)
+    tall_ref[...] = jnp.zeros_like(tall_ref)
+    parts = []
+    for j in range(z.blocks):
+        tall_ref[pl.ds(pl.multiple_of(me * b, b), b), :] = weighted[j].astype(F32)
+        part = jnp.dot(turn, tall_ref[...].astype(BF16), preferred_element_type=F32)
+        parts.append((part * (2.0 / half_width)).reshape(groups, b, z.slots))
+    value = jnp.concatenate(parts, 1).reshape(groups * z.blocks * b, z.slots)
+    hi = value.astype(BF16)
+    low = (value - hi.astype(F32)).astype(BF16)
+    rows = z.blocks * b
+    for h in range(groups):
+        out_ref[h, :rows, :] = hi[h * rows : (h + 1) * rows, :]
+        out_ref[h, rows : 2 * rows, :] = low[h * rows : (h + 1) * rows, :]
+    wide = 2 * all_bands
+    row = lax.broadcasted_iota(jnp.int32, (wide, all_bands), 0)
+    col = lax.broadcasted_iota(jnp.int32, (wide, all_bands), 1)
+    spread = jnp.where((row // (2 * b)) * b + row % b == col, 1.0, 0.0).astype(BF16)
+    tall = jnp.dot(spread, turn, preferred_element_type=F32).astype(BF16)
+    big = dot_t(tall, spread)
+    row = lax.broadcasted_iota(jnp.int32, (wide, wide), 0)
+    col = lax.broadcasted_iota(jnp.int32, (wide, wide), 1)
+    same = (row // b) % 2 == (col // b) % 2
+    big_ref[...] = jnp.where(same, big, 0.0).astype(BF16)
+
+
+def turn_kernel(z, groups, piece_ref, share_ref, big_ref, out_ref):
+    rows = piece_ref.shape[1]
+    for pair in range(rows // 16):
+        at = slice(16 * pair, 16 * pair + 16)
+        stack = jnp.concatenate([piece_ref[g, at, :] for g in range(groups)], 0)
+        value = jnp.dot(big_ref[...], stack, preferred_element_type=F32).astype(BF16)
+        for h in range(groups):
+            out_ref[h, at, :] = value[16 * h : 16 * h + 16, :]
+    extra = share_ref.shape[1]
+    for h in range(groups):
+        out_ref[h, rows : rows + extra, :] = share_ref[h]
+
+
+def final_kernel(
+    z, groups, in_hbm, proj_hbm, out_hbm, in_ref, proj_ref, wide_ref, out_ref, in_sem, proj_sems, out_sems
+):
+    in_copy = pltpu.make_async_copy(in_hbm, in_ref, in_sem)
+    in_copy.start()
+    copies = []
+    for x in range(z.thickness):
+        at = pl.ds(x * z.rows, z.rows)
+        copies.append(pltpu.make_async_copy(proj_hbm.at[at], proj_ref.at[at], proj_sems.at[x]))
+        copies[-1].start()
+    in_copy.wait()
+    rows = z.tall // groups
+    part = z.blocks * z.bands
+    total = None
+    for g in range(groups):
+        one = in_ref[g, rows : rows + part, :].astype(F32)
+        one = one + in_ref[g, rows + part : rows + 2 * part, :].astype(F32)
+        total = one if total is None else total + one
+    b = z.bands
+    lefts = []
+    for j in range(z.blocks):
+        own = total[j * b : (j + 1) * b, :]
+        hi = own.astype(BF16)
+        low = (own - hi.astype(F32)).astype(BF16)
+        lefts.append(jnp.concatenate([hi, low], 0))
+    pairs = rows // 16
+    writes = []
+    for x in range(z.thickness):
+        copies[x].wait()
+        for pair in range(x * z.rows // 2, (x + 1) * z.rows // 2):
+            both = jnp.concatenate([proj_ref[2 * pair], proj_ref[2 * pair + 1]], 1)
+            value = jnp.dot(lefts[block_of(z, pair)], both, preferred_element_type=F32)
+            value = value[:b] + value[b:]
+            g, at = pair // pairs, 16 * (pair % pairs)
+            smooth = in_ref[g, at : at + 16, :].astype(F32)
+            wide_ref[2 * pair] = smooth[:b] + value[:, : z.depth]
+            wide_ref[2 * pair + 1] = smooth[b:] + value[:, z.depth :]
+        at = slice(x * z.rows, (x + 1) * z.rows)
+        out_ref[:, at, :] = jnp.swapaxes(wide_ref[at], 0, 1).astype(BF16)
+        at = pl.ds(x * z.rows, z.rows)
+        writes.append(pltpu.make_async_copy(out_ref.at[:, at, :], out_hbm.at[:, at, :], out_sems.at[x]))
+        writes[-1].start()
+    for write in writes:
+        write.wait()
 
 
 VMEM = pl.BlockSpec(memory_space=pltpu.VMEM)
 HBM = pl.BlockSpec(memory_space=pltpu.HBM)
 
 
-def call(kernel, z, name, outs, ins, flops, moved, spaces, scratch=(), limit=12288):
+def call(kernel, z, name, outs, ins, flops, moved, spaces, scratch=(), limit=12288, groups=None, out_space=None):
+    fixed = (z,) if groups is None else (z, groups)
     single = not isinstance(outs, (list, tuple))
     return pl.pallas_call(
-        functools.partial(kernel, z),
+        functools.partial(kernel, *fixed),
         name=name,
         out_shape=outs,
         in_specs=spaces,
-        out_specs=VMEM if single else [VMEM] * len(outs),
+        out_specs=(out_space or VMEM) if single else [VMEM] * len(outs),
         scratch_shapes=list(scratch),
         compiler_params=pltpu.CompilerParams(vmem_limit_bytes=limit * 1024),
         cost_estimate=pl.CostEstimate(flops=flops, bytes_accessed=moved, transcendentals=0),
@@ -288,14 +432,22 @@
     return tile, pair, slab, wide, near, proj, hots
 
 
+def run_stage(z, kept):
+    tile, pair, slab, wide, near, projs, hots = shapes(z)
+    return call(stage_kernel, z, "stage", [pair, pair], (kept,), 1000, 8 * pair.size, [VMEM])
+
+
 def run_project(z, ids, bands, proj):
     tile, pair, slab, wide, near, projs, hots = shapes(z)
+    kept = jax.ShapeDtypeStruct((4, z.bands, z.lanes), F32)
     stream = 2 * z.tall * z.slots * z.depth
     return call(
-        project_kernel, z, "project", [slab, tile, pair, hots], (ids, bands, proj),
-        stream, 2 * z.cells * z.slots * z.depth, [HBM] * 3,
+        project_kernel, z, "project", [tile, kept], (ids, bands, proj),
+        20 * stream, 2 * z.cells * z.slots * z.depth, [HBM] * 3,
         scratch=[
-            pltpu.VMEM((z.cells, z.slots, z.depth), BF16),
+            pltpu.VMEM(slab.shape, BF16),
+            pltpu.VMEM(hots.shape, BF16),
+            pltpu.VMEM(projs.shape, BF16),
             pltpu.VMEM((z.blocks, z.slot_count), jnp.int32),
             pltpu.VMEM((z.bands, z.cells, z.depth), BF16),
             pltpu.SemaphoreType.DMA,
@@ -310,20 +462,21 @@
     return [pltpu.VMEM((3 * z.cells, z.bands, z.depth), F32)]
 
 
-def run_base_first(z, v, on_chip, across, pot, strength_t):
+def run_base_first(z, bands, on_chip, across, pot, strength_t, ids):
     tile, pair, slab, wide, near, projs, hots = shapes(z)
     return call(
-        base_first_kernel, z, "base_first", [wide, near], (v, on_chip, across, pot, strength_t),
+        base_first_kernel, z, "base_first", [wide, near, hots, slab],
+        (bands, on_chip, across, pot, strength_t, ids),
+        300 * z.tall * z.depth * z.depth, 10 * z.tall * z.depth, [VMEM] * 6,
+        scratch=wide_scratch(z),
+    )
+
+
+def run_smooth(z, v, on_chip, across, pot, start):
+    tile, pair, slab, wide, near, projs, hots = shapes(z)
+    return call(
+        smooth_kernel, z, "smooth", slab, (v, on_chip, across, pot, start),
         6 * z.tall * z.depth * z.depth, 10 * z.tall * z.depth, [VMEM] * 5,
-        scratch=wide_scratch(z),
-    )
-
-
-def run_base(z, v, on_chip, across, pot):
-    tile, pair, slab, wide, near, projs, hots = shapes(z)
-    return call(
-        base_kernel, z, "base", wide, (v, on_chip, across, pot),
-        6 * z.tall * z.depth * z.depth, 10 * z.tall * z.depth, [VMEM] * 4,
         scratch=wide_scratch(z),
     )
 
@@ -337,12 +490,43 @@
     )
 
 
-def run_filtered(z, base, pair_in, other, near_in, hots_in, proj, start):
-    tile, pair, slab, wide, near, projs, hots = shapes(z)
-    stream = 2 * z.tall * z.slots * z.depth
-    return call(
-        filtered_kernel, z, "filtered", slab, (base, pair_in, other, near_in, hots_in, proj, start),
-        stream, 2 * z.cells * z.slots * z.depth, [VMEM] * 7,
+def run_share(z, groups, pair_in, other, near_in, hots_in, rotation):
+    all_bands = groups * z.bands
+    outs = [
+        jax.ShapeDtypeStruct((groups, 2 * z.blocks * z.bands, z.slots), BF16),
+        jax.ShapeDtypeStruct((2 * all_bands, 2 * all_bands), BF16),
+    ]
+    return call(
+        share_kernel, z, "share", outs, (pair_in, other, near_in, hots_in, rotation),
+        20 * all_bands * all_bands * z.slots, 6 * all_bands * all_bands, [VMEM] * 5,
+        scratch=[pltpu.VMEM((all_bands, z.slots), F32)], groups=groups,
+    )
+
+
+def run_turn(z, groups, piece, share, big):
+    rows, extra = piece.shape[1], share.shape[1]
+    out = jax.ShapeDtypeStruct((groups, rows + extra, z.depth), BF16)
+    return call(
+        turn_kernel, z, "turn", out, (piece, share, big),
+        4 * z.tall * groups * z.bands * z.depth, 4 * z.tall * z.depth, [VMEM] * 3, groups=groups,
+    )
+
+
+def run_final(z, groups, turned_pieces, proj):
+    out = jax.ShapeDtypeStruct((z.bands, z.cells, z.depth), BF16)
+    return call(
+        final_kernel, z, "final", out, (turned_pieces, proj),
+        2 * z.tall * z.slots * z.depth, 2 * z.cells * z.slots * z.depth, [HBM] * 2,
+        scratch=[
+            pltpu.VMEM(turned_pieces.shape, BF16),
+            pltpu.VMEM(proj.shape, BF16),
+            pltpu.VMEM((z.cells, z.bands, z.depth), F32),
+            pltpu.VMEM(out.shape, BF16),
+            pltpu.SemaphoreType.DMA,
+            pltpu.SemaphoreType.DMA((z.thickness,)),
+            pltpu.SemaphoreType.DMA((z.thickness,)),
+        ],
+        groups=groups, limit=PROJECT_LIMIT, out_space=HBM,
     )
 
 
@@ -358,41 +542,38 @@
 
 def local(bands, potential, projectors, atom_ids, strength, rotation):
     z = Sizes(bands.shape, atom_ids.shape, strength.shape, lax.axis_size("dom"))
-    band_count = lax.axis_size("band")
-    side = lax.axis_index("dom") % 2
+    groups = lax.axis_size("band")
     proj = projectors.reshape(z.cells, z.slots, z.depth)
     pot = potential.reshape(z.cells, z.depth)
     flat = bands.reshape(z.bands, z.cells, z.depth)
-    mine = (lax.broadcasted_iota(jnp.int32, (2, 1, 1), 0) + side) == 1
-
-    def pair_of_chips(send, pair):
-        pair = pair + jnp.where(mine, swap_on_chip(send, "dom")[None], 0.0)
+
+    def pair_of_chips(send, pair, keep):
+        pair = pair + keep * swap_on_chip(send, "dom")[None]
         return pair + swap_across(pair, "dom")
 
-    def other_tile(pair):
-        return swap_on_chip(jnp.where(side == 0, pair[1], pair[0]), "dom")
-
-    start, send, pair, hots = run_project(z, atom_ids, flat, proj)
-    start_across, start_on = swap_across(start, "dom"), swap_on_chip(start, "dom")
-    pair = pair_of_chips(send, pair)
-    base, near = run_base_first(z, start, start_on, start_across, pot, strength.T)
-    other = other_tile(pair)
+    def other_tile(pair, keep):
+        return swap_on_chip(jnp.sum(keep * pair, 0), "dom")
+
+    start_across, start_on = swap_across(flat, "dom"), swap_on_chip(flat, "dom")
+    send, kept = run_project(z, atom_ids, flat, proj)
+    pair, keep = run_stage(z, kept)
+    pair = pair_of_chips(send, pair, keep)
+    base, near, hots, start = run_base_first(
+        z, flat, start_on, start_across, pot, strength.T, atom_ids
+    )
+    other = other_tile(pair, keep)
     first, send, pair = run_first(z, base, pair, other, near, hots, proj)
 
     first_across, first_on = swap_across(first, "dom"), swap_on_chip(first, "dom")
-    pair = pair_of_chips(send, pair)
-    base = run_base(z, first, first_on, first_across, pot)
-    other = other_tile(pair)
-    filtered = run_filtered(z, base, pair, other, near, hots, proj, start)
-
-    share = z.cells // band_count
-    pieces = filtered.reshape(band_count, share, z.bands, z.depth)
+    smooth = run_smooth(z, first, first_on, first_across, pot, start)
+    pieces = smooth.reshape(groups, z.tall // groups, z.depth)
     pieces = lax.all_to_all(pieces, "band", 0, 0, tiled=True)
-    turn = rotation.reshape(band_count, z.bands, band_count * z.bands)
-    turned = jnp.einsum("gxbz,gbc->xcz", pieces, turn, preferred_element_type=F32).astype(BF16)
-    turned = turned.reshape(share, band_count, z.bands, z.depth).transpose(1, 0, 2, 3)
-    turned = lax.all_to_all(turned, "band", 0, 0, tiled=True)
-    return turned.reshape(z.cells, z.bands, z.depth).transpose(1, 0, 2).reshape(bands.shape)
+    pair = pair_of_chips(send, pair, keep)
+    other = other_tile(pair, keep)
+    share, big = run_share(z, groups, pair, other, near, hots, rotation)
+    turned_pieces = run_turn(z, groups, pieces, share, big)
+    turned_pieces = lax.all_to_all(turned_pieces, "band", 0, 0, tiled=True)
+    return run_final(z, groups, turned_pieces, proj).reshape(bands.shape)
 
 
 def solution(mesh):

time: 87.1 us -> 92.9 us (1.067)
  starting transfers between devices: 35 us -> 50.5 us
  blocking collectives: 33.5 us -> 21.7 us
  Pallas kernels: 10.5 us -> 14.2 us
  waiting for transfers between devices: 2.05 us -> 4.15 us
  other arithmetic: 1.71 us -> 0.02 us
  local copies, waits for them, and re-layouts: 2.61 us -> 1.41 us
    all_to_all x2 -> x1, blocking collectives: 33.5 us -> 21.7 us  [local(): turned_pieces = lax.all_to_all(turned_pieces, 'band', 0, 0, tiled=True)]
    all_to_all x0 -> x1, starting transfers between devices: none -> 10.9 us  [local(): pieces = lax.all_to_all(pieces, 'band', 0, 0, tiled=True)]
    ppermute x6, starting transfers between devices: 23.9 us -> 30.5 us  [swap_on_chip(): return lax.ppermute(x, axis, [(i, i ^ 1) for i in range(count)])]
    pallas_call x5 -> x8, Pallas kernels: 10.5 us -> 14.2 us  [call(): pl.pallas_call(functools.partial(kernel, *fixed), name=name, out_shape=ou...]
    ppermute x4, waiting for transfers between devices: 0.01 us -> 3.05 us  [swap_across(): lax.ppermute(x, axis, [(i, ((i + 1 ^ 1) - 1) % count) for i in range(coun...]
    ppermute x4, starting transfers between devices: 11.1 us -> 9.06 us  [swap_across(): lax.ppermute(x, axis, [(i, ((i + 1 ^ 1) - 1) % count) for i in range(coun...]
    add x4 -> x2, other arithmetic: 1.69 us -> 0.01 us  [pair_of_chips(): pair = pair + keep * swap_on_chip(send, 'dom')[None]]
    ppermute x6, waiting for transfers between devices: 2.04 us -> 1.1 us  [swap_on_chip(): return lax.ppermute(x, axis, [(i, i ^ 1) for i in range(count)])]
  transfers between devices with their start and end apart: 10 -> 11, of which waited for: 3 -> 3; matrix products, arithmetic and copies ran while one was open for 1% -> 0% of each run, Pallas kernels for 3% -> 4%
where the time goes in v3:
time: 92.9 us; the launch traced here: 92.3 us
  starting transfers between devices  50.5 us (54%)
  blocking collectives  21.7 us (23%)
  Pallas kernels  14.2 us (15%)
  waiting for transfers between devices  4.15 us (4%)
  local copies, waits for them, and re-layouts  1.41 us (2%)
    ppermute x6, starting transfers between devices, swap_on_chip(): return lax.ppermute(x, axis, [(i, i ^ 1) for i in range(count)])  30.5 us
    all_to_all x1, blocking collectives, local(): turned_pieces = lax.all_to_all(turned_pieces, 'band', 0, 0, tiled=True)  21.7 us
    pallas_call x8, Pallas kernels, call(): pl.pallas_call(functools.partial(kernel, *fixed), name=name, out_shape=ou...  14.2 us
    all_to_all x1, starting transfers between devices, local(): pieces = lax.all_to_all(pieces, 'band', 0, 0, tiled=True)  10.9 us
    ppermute x4, starting transfers between devices, swap_across(): lax.ppermute(x, axis, [(i, ((i + 1 ^ 1) - 1) % count) for i in range(coun...  9.06 us
    ppermute x4, waiting for transfers between devices, swap_across(): lax.ppermute(x, axis, [(i, ((i + 1 ^ 1) - 1) % count) for i in range(coun...  3.05 us
  transfers between devices with their start and end apart: 11, of which 3 were waited for; matrix products, arithmetic and copies ran while one was open for 0% of the time, Pallas kernels for 4%

profile of v3, /device:TPU:1, one launch (start us, length us, event | category | flops | bytes accessed | tf_op | source)
XLA Modules:
  0.0 92.3 jit_solution(6338920808446267149)
XLA Ops:
  0.0 4.5 %project.1 = (f32[8,128]{1,0:T(8,128)}, f32[4,8,128]{2,1,0:T(8,128)}) custom-call(s32[2,32]{1,0:T(2,128)} %ids_hbm.1, bf16[8,96,128]{2,1,0:T(8,128)(2,1)} %bitcast.9, bf16[96,128,128]{2,1,0:T(8,128)(2,1)} %bitcast.6), custom_call_target="tpu_custom_call" | custom-call | flops 503316480 | bytes 3145728 | tf_op jit(solution)/shard_map/project/pallas_call | solution.py:412
  4.5 8.8 %collective-permute-start.2 = (f32[8,128]{1,0:T(8,128)}, f32[8,128]{1,0:T(8,128)S(1)}, u32[]{:S(2)}, u32[]{:S(2)}) collective-permute-start(f32[8,128]{1,0:T(8,128)} %get-tuple-element.22), channel_id=1, source_target_pairs={{0,16},{16,0},{32,48},{48,32},{64,80},{80,64},{96,112},{112,96},{1... | collective-permute-start | bytes 12296 | tf_op jit(solution)/shard_map/ppermute | solution.py:535
  13.3 0.7 copy-done.4
  14.0 0.3 collective-permute-done.2
  14.3 1.9 %collective-permute-start.3 = (f32[2,8,128]{2,1,0:T(8,128)S(1)}, f32[2,8,128]{2,1,0:T(8,128)S(1)}, u32[]{:S(2)}, u32[]{:S(2)}) collective-permute-start(f32[2,8,128]{2,1,0:T(8,128)S(1)} %multiply_add_fusion.1), channel_id=1, source_target_pairs={{0,496},{16,32},{32,16},{48,64},{64,48},{80,96},{96,80},{112,128},... | collective-permute-start | bytes 24584 | tf_op jit(solution)/shard_map/ppermute | solution.py:540
  16.2 2.3 %collective-permute-start = (bf16[8,96,128]{2,1,0:T(8,128)(2,1)S(1)}, bf16[8,96,128]{2,1,0:T(8,128)(2,1)S(1)}, u32[]{:S(2)}, u32[]{:S(2)}) collective-permute-start(bf16[8,96,128]{2,1,0:T(8,128)(2,1)S(1)} %bitcast.10), channel_id=1, source_target_pairs={{0,16},{16,0},{32,48},{48,32},{64,80},{80,64},{96,112},{112,96},{1... | collective-permute-start | bytes 589832 | tf_op jit(solution)/shard_map/ppermute | solution.py:535
  18.5 3.3 %collective-permute-start.1 = (bf16[8,96,128]{2,1,0:T(8,128)(2,1)S(1)}, bf16[8,96,128]{2,1,0:T(8,128)(2,1)S(1)}, u32[]{:S(2)}, u32[]{:S(2)}) collective-permute-start(bf16[8,96,128]{2,1,0:T(8,128)(2,1)S(1)} %bitcast.11), channel_id=1, source_target_pairs={{0,496},{16,32},{32,16},{48,64},{64,48},{80,96},{96,80},{112,128},... | collective-permute-start | bytes 589832 | tf_op jit(solution)/shard_map/ppermute | solution.py:540
  21.8 4.4 %collective-permute-start.4 = (f32[8,128]{1,0:T(8,128)S(1)}, f32[8,128]{1,0:T(8,128)S(1)}, u32[]{:S(2)}, u32[]{:S(2)}) collective-permute-start(f32[8,128]{1,0:T(8,128)S(1)} %get-tuple-element.33), channel_id=1, source_target_pairs={{0,16},{16,0},{32,48},{48,32},{64,80},{80,64},{96,112},{112,96},{1... | collective-permute-start | bytes 12296 | tf_op jit(solution)/shard_map/ppermute | solution.py:535
  26.3 1.2 %base_first.1 = (f32[768,128]{1,0:T(8,128)S(1)}, f32[8,128]{1,0:T(8,128)S(1)}, bf16[2,384,128]{2,1,0:T(8,128)(2,1)S(1)}, bf16[768,128]{1,0:T(8,128)(2,1)S(1)}) custom-call(bf16[8,96,128]{2,1,0:T(8,128)(2,1)S(1)} %bitcast.12, bf16[8,96,128]{2,1,0:T(8,128)(2,1)S(1)} %collective-permute-done.on_ref, bf16[8,96,128]{2,1,0:T(8,128)(2,1)S(1)} %collective-permute-done.1.off_ref, ...), custom_call_target="tpu_custom_call" | custom-call | flops 3774873600 | bytes 983040 | tf_op jit(solution)/shard_map/base_first/pallas_call | solution.py:412
  27.5 0.7 copy-done
  28.1 2.5 %first.1 = (bf16[768,128]{1,0:T(8,128)(2,1)S(1)}, f32[8,128]{1,0:T(8,128)S(1)}, f32[2,8,128]{2,1,0:T(8,128)S(1)}) custom-call(f32[768,128]{1,0:T(8,128)S(1)} %get-tuple-element.18.base_ref, f32[2,8,128]{2,1,0:T(8,128)S(1)} %get-tuple-element.34.pair_in, f32[8,128]{1,0:T(8,128)S(1)} %collective-permute-done.4.other_ref, ...), custom_call_target="tpu_custom_call" | custom-call | flops 50331648 | bytes 3145728 | tf_op jit(solution)/shard_map/first/pallas_call | solution.py:412
  30.6 3.4 %collective-permute-start.5 = (bf16[768,128]{1,0:T(8,128)(2,1)S(1)}, bf16[768,128]{1,0:T(8,128)(2,1)S(1)}, u32[]{:S(2)}, u32[]{:S(2)}) collective-permute-start(bf16[768,128]{1,0:T(8,128)(2,1)S(1)} %get-tuple-element.25.v_ref), channel_id=1, source_target_pairs={{0,16},{16,0},{32,48},{48,32},{64,80},{80,64},{96,112},{112,96},{1... | collective-permute-start | bytes 589832 | tf_op jit(solution)/shard_map/ppermute | solution.py:535
  34.0 1.9 %collective-permute-start.6 = (bf16[768,128]{1,0:T(8,128)(2,1)S(1)}, bf16[768,128]{1,0:T(8,128)(2,1)S(1)}, u32[]{:S(2)}, u32[]{:S(2)}) collective-permute-start(bf16[768,128]{1,0:T(8,128)(2,1)S(1)} %get-tuple-element.25.v_ref), channel_id=1, source_target_pairs={{0,496},{16,32},{32,16},{48,64},{64,48},{80,96},{96,80},{112,128},... | collective-permute-start | bytes 589832 | tf_op jit(solution)/shard_map/ppermute | solution.py:540
  36.0 5.6 %collective-permute-start.7 = (f32[8,128]{1,0:T(8,128)S(1)}, f32[8,128]{1,0:T(8,128)S(1)}, u32[]{:S(2)}, u32[]{:S(2)}) collective-permute-start(f32[8,128]{1,0:T(8,128)S(1)} %get-tuple-element.28), channel_id=1, source_target_pairs={{0,16},{16,0},{32,48},{48,32},{64,80},{80,64},{96,112},{112,96},{1... | collective-permute-start | bytes 12296 | tf_op jit(solution)/shard_map/ppermute | solution.py:535
  41.6 1.7 %smooth.1 = bf16[768,128]{1,0:T(8,128)(2,1)} custom-call(bf16[768,128]{1,0:T(8,128)(2,1)S(1)} %get-tuple-element.25.v_ref, bf16[768,128]{1,0:T(8,128)(2,1)S(1)} %collective-permute-done.5.on_ref, bf16[768,128]{1,0:T(8,128)(2,1)S(1)} %collective-permute-done.6.off_ref, f32[96,128]{1,0:T(8,128)S(1)} %bitcast.14, bf16[768,128]{1,0:T(8,128)(2,1)S(1)} %get-tuple-element.26.start_ref), custom_call_target="tpu_custom_call" | custom-call | flops 75497472 | bytes 983040 | tf_op jit(solution)/shard_map/smooth/pallas_call | solution.py:412
  43.2 10.9 %all-to-all-start = ((bf16[16,48,128]{2,1,0:T(8,128)(2,1)}), bf16[16,48,128]{2,1,0:T(8,128)(2,1)S(1)}, u32[]{:S(2)}, u32[]{:S(2)}) async-start(bf16[16,48,128]{2,1,0:T(8,128)(2,1)} %bitcast.4), calls=%async_computation | async-start | bytes 393216 | tf_op jit(solution)/shard_map/all_to_all | solution.py:570
  54.2 1.9 %collective-permute-start.8 = (f32[2,8,128]{2,1,0:T(8,128)S(1)}, f32[2,8,128]{2,1,0:T(8,128)S(1)}, u32[]{:S(2)}, u32[]{:S(2)}) collective-permute-start(f32[2,8,128]{2,1,0:T(8,128)S(1)} %multiply_add_fusion), channel_id=1, source_target_pairs={{0,496},{16,32},{32,16},{48,64},{64,48},{80,96},{96,80},{112,128},... | collective-permute-start | bytes 24584 | tf_op jit(solution)/shard_map/ppermute | solution.py:540
  56.1 3.0 %collective-permute-done.8 = f32[2,8,128]{2,1,0:T(8,128)S(1)} collective-permute-done((f32[2,8,128]{2,1,0:T(8,128)S(1)}, f32[2,8,128]{2,1,0:T(8,128)S(1)}, u32[]{:S(2)}, u32[]{:S(2)}) %collective-permute-start.8) | collective-permute-done | bytes 8224 | tf_op jit(solution)/shard_map/ppermute | solution.py:540
  59.2 6.1 %collective-permute-start.9 = (f32[8,128]{1,0:T(8,128)S(1)}, f32[8,128]{1,0:T(8,128)S(1)}, u32[]{:S(2)}, u32[]{:S(2)}) collective-permute-start(f32[8,128]{1,0:T(8,128)S(1)} %get-tuple-element.31), channel_id=1, source_target_pairs={{0,16},{16,0},{32,48},{48,32},{64,80},{80,64},{96,112},{112,96},{1... | collective-permute-start | bytes 12296 | tf_op jit(solution)/shard_map/ppermute | solution.py:535
  65.3 0.8 collective-permute-done.9.other_ref
  66.1 0.5 share.1
  66.6 0.2 turn.1
  66.9 21.7 %all_to_all.10.in_hbm = bf16[16,80,128]{2,1,0:T(8,128)(2,1)} all-to-all(bf16[16,80,128]{2,1,0:T(8,128)(2,1)S(1)} %turn.1), channel_id=1, replica_groups=mesh['dom'=32,'band'=16] {'band'}, dimensions={0} | all-to-all | bytes 655360 | tf_op jit(solution)/shard_map/all_to_all | solution.py:575
  88.6 3.7 %final.1 = bf16[8,96,128]{2,1,0:T(8,128)(2,1)} custom-call(bf16[16,80,128]{2,1,0:T(8,128)(2,1)} %all_to_all.10.in_hbm, bf16[96,128,128]{2,1,0:T(8,128)(2,1)} %bitcast.7), custom_call_target="tpu_custom_call" | custom-call | flops 25165824 | bytes 3145728 | tf_op jit(solution)/shard_map/final/pallas_call | solution.py:412
  (25 shorter events, 0.1 us)
Async XLA Ops:
  0.0 16.2 %copy-start.1 = (bf16[8,6,16,128]{3,2,1,0:T(8,128)(2,1)S(1)}, bf16[8,6,16,128]{3,2,1,0:T(8,128)(2,1)}, u32[]{:S(2)}) copy-start(bf16[8,6,16,128]{3,2,1,0:T(8,128)(2,1)} %param.6) | copy-start | bytes 589828
  0.0 26.2 %copy-start.5 = (s32[2,32]{1,0:T(2,128)S(1)}, s32[2,32]{1,0:T(2,128)}, u32[]{:S(2)}) copy-start(s32[2,32]{1,0:T(2,128)} %ids_hbm.1) | copy-start | bytes 772
  0.0 26.2 %copy-start.2 = (f32[6,16,128]{2,1,0:T(8,128)S(1)}, f32[6,16,128]{2,1,0:T(8,128)}, u32[]{:S(2)}) copy-start(f32[6,16,128]{2,1,0:T(8,128)} %param.7) | copy-start | bytes 147460
  0.0 26.2 %copy-start.6 = (f32[1024,4]{0,1:T(4,128)S(1)}, f32[1024,4]{0,1:T(4,128)}, u32[]{:S(2)}) copy-start(f32[1024,4]{0,1:T(4,128)} %param.10) | copy-start | bytes 49156
  4.5 9.8 %collective-permute-start.2 = (f32[8,128]{1,0:T(8,128)}, f32[8,128]{1,0:T(8,128)S(1)}, u32[]{:S(2)}, u32[]{:S(2)}) collective-permute-start(f32[8,128]{1,0:T(8,128)} %get-tuple-element.22), channel_id=1, source_target_pairs={{0,16},{16,0},{32,48},{48,32},{64,80},{80,64},{96,112},{112,96},{1... | collective-permute-start | bytes 12296 | tf_op jit(solution)/shard_map/ppermute | solution.py:535
  13.3 0.7 copy-start.4
  14.3 7.5 %collective-permute-start.3 = (f32[2,8,128]{2,1,0:T(8,128)S(1)}, f32[2,8,128]{2,1,0:T(8,128)S(1)}, u32[]{:S(2)}, u32[]{:S(2)}) collective-permute-start(f32[2,8,128]{2,1,0:T(8,128)S(1)} %multiply_add_fusion.1), channel_id=1, source_target_pairs={{0,496},{16,32},{32,16},{48,64},{64,48},{80,96},{96,80},{112,128},... | collective-permute-start | bytes 24584 | tf_op jit(solution)/shard_map/ppermute | solution.py:540
  16.2 10.0 %collective-permute-start = (bf16[8,96,128]{2,1,0:T(8,128)(2,1)S(1)}, bf16[8,96,128]{2,1,0:T(8,128)(2,1)S(1)}, u32[]{:S(2)}, u32[]{:S(2)}) collective-permute-start(bf16[8,96,128]{2,1,0:T(8,128)(2,1)S(1)} %bitcast.10), channel_id=1, source_target_pairs={{0,16},{16,0},{32,48},{48,32},{64,80},{80,64},{96,112},{112,96},{1... | collective-permute-start | bytes 589832 | tf_op jit(solution)/shard_map/ppermute | solution.py:535
  18.5 7.7 %collective-permute-start.1 = (bf16[8,96,128]{2,1,0:T(8,128)(2,1)S(1)}, bf16[8,96,128]{2,1,0:T(8,128)(2,1)S(1)}, u32[]{:S(2)}, u32[]{:S(2)}) collective-permute-start(bf16[8,96,128]{2,1,0:T(8,128)(2,1)S(1)} %bitcast.11), channel_id=1, source_target_pairs={{0,496},{16,32},{32,16},{48,64},{64,48},{80,96},{96,80},{112,128},... | collective-permute-start | bytes 589832 | tf_op jit(solution)/shard_map/ppermute | solution.py:540
  21.8 5.6 %collective-permute-start.4 = (f32[8,128]{1,0:T(8,128)S(1)}, f32[8,128]{1,0:T(8,128)S(1)}, u32[]{:S(2)}, u32[]{:S(2)}) collective-permute-start(f32[8,128]{1,0:T(8,128)S(1)} %get-tuple-element.33), channel_id=1, source_target_pairs={{0,16},{16,0},{32,48},{48,32},{64,80},{80,64},{96,112},{112,96},{1... | collective-permute-start | bytes 12296 | tf_op jit(solution)/shard_map/ppermute | solution.py:535
  26.2 1.9 %copy-start = (bf16[6,16,32,4,128]{4,3,2,1,0:T(4,128)(2,1)S(1)}, bf16[6,16,32,4,128]{4,3,2,1,0:T(4,128)(2,1)}, u32[]{:S(2)}) copy-start(bf16[6,16,32,4,128]{4,3,2,1,0:T(4,128)(2,1)} %param.8) | copy-start | bytes 9437188
  27.4 38.7 %copy-start.3 = (bf16[128,128]{1,0:T(8,128)(2,1)S(1)}, bf16[128,128]{1,0:T(8,128)(2,1)}, u32[]{:S(2)}) copy-start(bf16[128,128]{1,0:T(8,128)(2,1)} %rotation_ref.1) | copy-start | bytes 98308
  30.6 11.0 %collective-permute-start.5 = (bf16[768,128]{1,0:T(8,128)(2,1)S(1)}, bf16[768,128]{1,0:T(8,128)(2,1)S(1)}, u32[]{:S(2)}, u32[]{:S(2)}) collective-permute-start(bf16[768,128]{1,0:T(8,128)(2,1)S(1)} %get-tuple-element.25.v_ref), channel_id=1, source_target_pairs={{0,16},{16,0},{32,48},{48,32},{64,80},{80,64},{96,112},{112,96},{1... | collective-permute-start | bytes 589832 | tf_op jit(solution)/shard_map/ppermute | solution.py:535
  34.0 7.5 %collective-permute-start.6 = (bf16[768,128]{1,0:T(8,128)(2,1)S(1)}, bf16[768,128]{1,0:T(8,128)(2,1)S(1)}, u32[]{:S(2)}, u32[]{:S(2)}) collective-permute-start(bf16[768,128]{1,0:T(8,128)(2,1)S(1)} %get-tuple-element.25.v_ref), channel_id=1, source_target_pairs={{0,496},{16,32},{32,16},{48,64},{64,48},{80,96},{96,80},{112,128},... | collective-permute-start | bytes 589832 | tf_op jit(solution)/shard_map/ppermute | solution.py:540
  36.0 18.2 %collective-permute-start.7 = (f32[8,128]{1,0:T(8,128)S(1)}, f32[8,128]{1,0:T(8,128)S(1)}, u32[]{:S(2)}, u32[]{:S(2)}) collective-permute-start(f32[8,128]{1,0:T(8,128)S(1)} %get-tuple-element.28), channel_id=1, source_target_pairs={{0,16},{16,0},{32,48},{48,32},{64,80},{80,64},{96,112},{112,96},{1... | collective-permute-start | bytes 12296 | tf_op jit(solution)/shard_map/ppermute | solution.py:535
  43.2 23.4 %all-to-all-start = ((bf16[16,48,128]{2,1,0:T(8,128)(2,1)}), bf16[16,48,128]{2,1,0:T(8,128)(2,1)S(1)}, u32[]{:S(2)}, u32[]{:S(2)}) async-start(bf16[16,48,128]{2,1,0:T(8,128)(2,1)} %bitcast.4), calls=%async_computation | async-start | bytes 393216 | tf_op jit(solution)/shard_map/all_to_all | solution.py:570
  54.2 5.0 %collective-permute-start.8 = (f32[2,8,128]{2,1,0:T(8,128)S(1)}, f32[2,8,128]{2,1,0:T(8,128)S(1)}, u32[]{:S(2)}, u32[]{:S(2)}) collective-permute-start(f32[2,8,128]{2,1,0:T(8,128)S(1)} %multiply_add_fusion), channel_id=1, source_target_pairs={{0,496},{16,32},{32,16},{48,64},{64,48},{80,96},{96,80},{112,128},... | collective-permute-start | bytes 24584 | tf_op jit(solution)/shard_map/ppermute | solution.py:540
  59.2 6.9 %collective-permute-start.9 = (f32[8,128]{1,0:T(8,128)S(1)}, f32[8,128]{1,0:T(8,128)S(1)}, u32[]{:S(2)}, u32[]{:S(2)}) collective-permute-start(f32[8,128]{1,0:T(8,128)S(1)} %get-tuple-element.31), channel_id=1, source_target_pairs={{0,16},{16,0},{32,48},{48,32},{64,80},{80,64},{96,112},{112,96},{1... | collective-permute-start | bytes 12296 | tf_op jit(solution)/shard_map/ppermute | solution.py:535

commit v4 on v2

--- a/solution.py
+++ b/solution.py
@@ -142,37 +142,32 @@
         return [e[:b] + o[b:] for e, o in zip(self.even, self.odd)]
 
 
-CHUNKS = 6
-PROJECT_LIMIT = 60000
-
-
-def project_kernel(
-    z, ids_hbm, bands_hbm, proj_hbm, v_ref, send_ref, pair_ref, hots_ref,
-    proj_ref, ids_ref, bands_ref, ids_sem, bands_sem, proj_sems,
-):
+def turned(z, bands_ref, x):
+    plane = bands_ref[:, x * z.rows : (x + 1) * z.rows, :].astype(F32)
+    return jnp.swapaxes(plane, 0, 1)
+
+
+def turn_all(z, bands_ref, v_ref):
+    tall = z.rows * z.bands
+    for x in range(z.thickness):
+        plane = turned(z, bands_ref, x).reshape(tall, z.depth)
+        v_ref[x * tall : (x + 1) * tall, :] = plane.astype(BF16)
+
+
+def keep_kernel(z, keep_ref):
+    side = lax.axis_index("dom") & 1
+    ones = jnp.full(keep_ref.shape[1:], 1.0, F32)
+    keep_ref[0] = jnp.where(side == 1, ones, 0.0)
+    keep_ref[1] = jnp.where(side == 0, ones, 0.0)
+
+
+def project_kernel(z, ids_ref, bands_ref, proj_ref, keep_ref, send_ref, pair_ref, v_ref, hots_ref):
     dom = lax.axis_index("dom")
-    step = z.cells // CHUNKS
-    ids_copy = pltpu.make_async_copy(ids_hbm, ids_ref, ids_sem)
-    ids_copy.start()
-    bands_copy = pltpu.make_async_copy(bands_hbm, bands_ref, bands_sem)
-    bands_copy.start()
-    copies = []
-    for c in range(CHUNKS):
-        at = pl.ds(c * step, step)
-        copies.append(pltpu.make_async_copy(proj_hbm.at[at], proj_ref.at[at], proj_sems.at[c]))
-        copies[-1].start()
-    ids_copy.wait()
+    turn_all(z, bands_ref, v_ref)
     for j, hot in enumerate(one_hots(z, dom, ids_ref)):
         hots_ref[j] = hot
-    bands_copy.wait()
-    for x in range(z.thickness):
-        slab = bands_ref[:, x * z.rows : (x + 1) * z.rows, :].astype(F32)
-        turned = jnp.swapaxes(slab, 0, 1).reshape(z.rows * z.bands, z.depth)
-        v_ref[x * z.rows * z.bands : (x + 1) * z.rows * z.bands, :] = turned.astype(BF16)
     projector = Projector(z, v_ref, proj_ref)
-    for c in range(CHUNKS):
-        copies[c].wait()
-        projector.add(range(c * step // 2, (c + 1) * step // 2))
+    projector.add(range(z.cells // 2))
     scatter(z, dom & 1, projector.sums(), hots_ref, send_ref, pair_ref)
 
 
@@ -192,43 +187,81 @@
         out_ref[t : t + 1, :] = line
 
 
-def base_body(z, dom, v_ref, on_ref, off_ref, pot_ref, out_ref, wide_ref):
-    first_core = (dom & 1) == 0
-    on_at = pl.multiple_of(jnp.where(first_core, 2 * z.cells, 0), z.cells)
-    off_at = pl.multiple_of(jnp.where(first_core, 0, 2 * z.cells), z.cells)
-    step, b = 8, z.bands
-    for c in range(0, z.cells, step):
-        rows = slice(b * c, b * (c + step))
-        shape = (step, b, z.depth)
-        wide_ref[pl.ds(on_at + c, step)] = on_ref[rows, :].astype(F32).reshape(shape)
-        wide_ref[pl.ds(off_at + c, step)] = off_ref[rows, :].astype(F32).reshape(shape)
-        wide_ref[z.cells + c : z.cells + c + step] = v_ref[rows, :].astype(F32).reshape(shape)
+def base_body(z, dom, v_ref, wide_ref, write):
+    b = z.bands
     zmat = z_matrix(z.depth)
     for c in range(0, z.cells, z.rows):
         v = v_ref[b * c : b * (c + z.rows), :]
         along_z = jnp.dot(jnp.concatenate([v, v, v], 1), zmat, preferred_element_type=F32)
-        for y in range(z.rows):
-            at = z.cells + c + y
-            mine = wide_ref[at]
-            pot = pot_ref[c + y : c + y + 1, :] + (3.0 * WEIGHTS[0] - centre)
-            total = pot * mine + along_z[b * y : b * y + b, :]
-            for offset in range(1, REACH + 1):
-                beside = wide_ref[at + offset * z.rows] + wide_ref[at - offset * z.rows]
-                up = z.cells + c + (y + offset) % z.rows
-                down = z.cells + c + (y - offset) % z.rows
-                beside = beside + (wide_ref[up] + wide_ref[down])
-                total = total + WEIGHTS[offset] * beside
-            out_ref[b * (c + y) : b * (c + y) + b, :] = total
+        for y in range(0, z.rows, 2):
+            both = []
+            for at in (y, y + 1):
+                here = z.cells + c + at
+                total = wide_ref[here] * (write.pot(c + at) + (3.0 * WEIGHTS[0] - centre))
+                total = total + along_z[b * at : b * at + b, :]
+                for offset in range(1, REACH + 1):
+                    beside = wide_ref[here + offset * z.rows] + wide_ref[here - offset * z.rows]
+                    up = z.cells + c + (at + offset) % z.rows
+                    down = z.cells + c + (at - offset) % z.rows
+                    beside = beside + (wide_ref[up] + wide_ref[down])
+                    total = total + WEIGHTS[offset] * beside
+                both.append(total)
+            write((c + y) // 2, jnp.concatenate(both, 0))
+
+
+class Writer:
+    def __init__(self, pot_ref, put):
+        self.pot_ref, self.put = pot_ref, put
+
+    def pot(self, cell):
+        return self.pot_ref[cell : cell + 1, :]
+
+    def __call__(self, pair, value):
+        self.put(pair_rows(pair), value)
+
+
+def places(z, dom):
+    first_core = (dom & 1) == 0
+    on_at = pl.multiple_of(jnp.where(first_core, 2 * z.cells, 0), z.cells)
+    off_at = pl.multiple_of(jnp.where(first_core, 0, 2 * z.cells), z.cells)
+    return on_at, off_at
 
 
 def base_first_kernel(z, v_ref, on_ref, off_ref, pot_ref, strength_ref, out_ref, near_ref, wide_ref):
     dom = lax.axis_index("dom")
+    on_at, off_at = places(z, dom)
+    for x in range(z.thickness):
+        at = x * z.rows
+        rows = slice(z.bands * at, z.bands * (at + z.rows))
+        mine = v_ref[rows, :].astype(F32).reshape(z.rows, z.bands, z.depth)
+        wide_ref[z.cells + at : z.cells + at + z.rows] = mine
+        wide_ref[pl.ds(on_at + at, z.rows)] = turned(z, on_ref, x)
+        wide_ref[pl.ds(off_at + at, z.rows)] = turned(z, off_ref, x)
+
+    def put(rows, value):
+        out_ref[rows, :] = value
+
+    base_body(z, dom, v_ref, wide_ref, Writer(pot_ref, put))
     near_strength(z, dom, strength_ref, near_ref)
-    base_body(z, dom, v_ref, on_ref, off_ref, pot_ref, out_ref, wide_ref)
 
 
 def base_kernel(z, v_ref, on_ref, off_ref, pot_ref, out_ref, wide_ref):
-    base_body(z, lax.axis_index("dom"), v_ref, on_ref, off_ref, pot_ref, out_ref, wide_ref)
+    dom = lax.axis_index("dom")
+    on_at, off_at = places(z, dom)
+    step, b = 8, z.bands
+
+    def tile(ref, c):
+        return ref[b * c : b * (c + step), :].astype(F32).reshape(step, b, z.depth)
+
+    for c in range(0, z.cells, step):
+        wide_ref[z.cells + c : z.cells + c + step] = tile(v_ref, c)
+        wide_ref[pl.ds(on_at + c, step)] = tile(on_ref, c)
+        wide_ref[pl.ds(off_at + c, step)] = tile(off_ref, c)
+
+    def put(rows, value):
+        out_ref[rows, :] = value
+
+    base_body(z, dom, v_ref, wide_ref, Writer(pot_ref, put))
 
 
 def nonlocal_pair(weighted, proj_ref, pair):
@@ -260,7 +293,6 @@
 
 
 VMEM = pl.BlockSpec(memory_space=pltpu.VMEM)
-HBM = pl.BlockSpec(memory_space=pltpu.HBM)
 
 
 def call(kernel, z, name, outs, ins, flops, moved, spaces, scratch=(), limit=12288):
@@ -288,21 +320,16 @@
     return tile, pair, slab, wide, near, proj, hots
 
 
-def run_project(z, ids, bands, proj):
-    tile, pair, slab, wide, near, projs, hots = shapes(z)
-    stream = 2 * z.tall * z.slots * z.depth
+def run_keep(z):
+    tile, pair, slab, wide, near, projs, hots = shapes(z)
+    return call(keep_kernel, z, "keep", pair, (), 4000 * z.tall * z.slots * z.depth, 40_000_000, [])
+
+
+def run_project(z, ids, bands, proj, keep):
+    tile, pair, slab, wide, near, projs, hots = shapes(z)
     return call(
-        project_kernel, z, "project", [slab, tile, pair, hots], (ids, bands, proj),
-        stream, 2 * z.cells * z.slots * z.depth, [HBM] * 3,
-        scratch=[
-            pltpu.VMEM((z.cells, z.slots, z.depth), BF16),
-            pltpu.VMEM((z.blocks, z.slot_count), jnp.int32),
-            pltpu.VMEM((z.bands, z.cells, z.depth), BF16),
-            pltpu.SemaphoreType.DMA,
-            pltpu.SemaphoreType.DMA,
-            pltpu.SemaphoreType.DMA((CHUNKS,)),
-        ],
-        limit=PROJECT_LIMIT,
+        project_kernel, z, "project", [tile, pair, slab, hots], (ids, bands, proj, keep),
+        2 * z.tall * z.slots * z.depth, 2 * z.cells * z.slots * z.depth, [VMEM] * 4,
     )
 
 
@@ -358,41 +385,42 @@
 
 def local(bands, potential, projectors, atom_ids, strength, rotation):
     z = Sizes(bands.shape, atom_ids.shape, strength.shape, lax.axis_size("dom"))
-    band_count = lax.axis_size("band")
-    side = lax.axis_index("dom") % 2
+    groups = lax.axis_size("band")
     proj = projectors.reshape(z.cells, z.slots, z.depth)
     pot = potential.reshape(z.cells, z.depth)
     flat = bands.reshape(z.bands, z.cells, z.depth)
-    mine = (lax.broadcasted_iota(jnp.int32, (2, 1, 1), 0) + side) == 1
-
-    def pair_of_chips(send, pair):
-        pair = pair + jnp.where(mine, swap_on_chip(send, "dom")[None], 0.0)
-        return pair + swap_across(pair, "dom")
-
-    def other_tile(pair):
-        return swap_on_chip(jnp.where(side == 0, pair[1], pair[0]), "dom")
-
-    start, send, pair, hots = run_project(z, atom_ids, flat, proj)
-    start_across, start_on = swap_across(start, "dom"), swap_on_chip(start, "dom")
-    pair = pair_of_chips(send, pair)
+
+    def exchange(send, pair, keep, slab):
+        across = swap_across(slab, "dom")
+        pair = pair + keep * swap_on_chip(send, "dom")[None]
+        pair, slab = lax.optimization_barrier((pair, slab))
+        pair = pair + swap_across(pair, "dom")
+        return pair, swap_on_chip(slab, "dom"), across
+
+    def other_tile(pair, keep):
+        return swap_on_chip(jnp.sum(keep * pair, 0), "dom")
+
+    keep = run_keep(z)
+    flat, keep = lax.optimization_barrier((flat, keep))
+    send, pair, start, hots = run_project(z, atom_ids, flat, proj, keep)
+    pair, start_on, start_across = exchange(send, pair, keep, flat)
     base, near = run_base_first(z, start, start_on, start_across, pot, strength.T)
-    other = other_tile(pair)
+    other = other_tile(pair, keep)
     first, send, pair = run_first(z, base, pair, other, near, hots, proj)
 
-    first_across, first_on = swap_across(first, "dom"), swap_on_chip(first, "dom")
-    pair = pair_of_chips(send, pair)
+    pair, first_on, first_across = exchange(send, pair, keep, first)
     base = run_base(z, first, first_on, first_across, pot)
-    other = other_tile(pair)
+    other = other_tile(pair, keep)
     filtered = run_filtered(z, base, pair, other, near, hots, proj, start)
 
-    share = z.cells // band_count
-    pieces = filtered.reshape(band_count, share, z.bands, z.depth)
+    share = z.cells // groups
+    pieces = filtered.reshape(groups, share, z.bands, z.depth)
     pieces = lax.all_to_all(pieces, "band", 0, 0, tiled=True)
-    turn = rotation.reshape(band_count, z.bands, band_count * z.bands)
-    turned = jnp.einsum("gxbz,gbc->xcz", pieces, turn, preferred_element_type=F32).astype(BF16)
-    turned = turned.reshape(share, band_count, z.bands, z.depth).transpose(1, 0, 2, 3)
-    turned = lax.all_to_all(turned, "band", 0, 0, tiled=True)
-    return turned.reshape(z.cells, z.bands, z.depth).transpose(1, 0, 2).reshape(bands.shape)
+    turn = rotation.reshape(groups, z.bands, groups * z.bands)
+    rotated = jnp.einsum("gxbz,gbc->xcz", pieces, turn, preferred_element_type=F32).astype(BF16)
+    rotated = rotated.reshape(share, groups, z.bands, z.depth).transpose(1, 0, 2, 3)
+    rotated = lax.all_to_all(rotated, "band", 0, 0, tiled=True)
+    return rotated.reshape(z.cells, z.bands, z.depth).transpose(1, 0, 2).reshape(bands.shape)
 
 
 def solution(mesh):

time: 87.1 us -> 82.8 us (0.951)
  Pallas kernels: 10.5 us -> 7.01 us
  blocking collectives: 33.5 us -> 35.4 us
  other arithmetic: 1.71 us -> 0.02 us
    pallas_call x5 -> x6, Pallas kernels: 10.5 us -> 7.01 us  [call(): pl.pallas_call(functools.partial(kernel, z), name=name, out_shape=outs, i...]
    add x4 -> x2, other arithmetic: 1.69 us -> 0.01 us  [exchange(): pair = pair + keep * swap_on_chip(send, 'dom')[None]]
    all_to_all x1, blocking collectives: 14.2 us -> 15.6 us  [local(): rotated = lax.all_to_all(rotated, 'band', 0, 0, tiled=True)]
    unnamed x16 -> x12, local copies, waits for them, and re-layouts: 1.87 us -> 1.99 us
  transfers between devices with their start and end apart: 10 -> 10, of which waited for: 3 -> 4; matrix products, arithmetic and copies ran while one was open for 1% -> 0% of each run, Pallas kernels for 3% -> 2%
where the time goes in v4:
time: 82.8 us; the launch traced here: 82.4 us
  blocking collectives  35.4 us (43%)
  starting transfers between devices  34.8 us (42%)
  Pallas kernels  7.01 us (8%)
  local copies, waits for them, and re-layouts  2.73 us (3%)
  waiting for transfers between devices  1.88 us (2%)
    ppermute x6, starting transfers between devices, swap_on_chip(): return lax.ppermute(x, axis, [(i, i ^ 1) for i in range(count)])  23.7 us
    all_to_all x1, blocking collectives, local(): pieces = lax.all_to_all(pieces, 'band', 0, 0, tiled=True)  19.9 us
    all_to_all x1, blocking collectives, local(): rotated = lax.all_to_all(rotated, 'band', 0, 0, tiled=True)  15.6 us
    ppermute x4, starting transfers between devices, swap_across(): lax.ppermute(x, axis, [(i, ((i + 1 ^ 1) - 1) % count) for i in range(coun...  11.1 us
    pallas_call x6, Pallas kernels, call(): pl.pallas_call(functools.partial(kernel, z), name=name, out_shape=outs, i...  7.01 us
    unnamed x12, local copies, waits for them, and re-layouts  1.99 us
    ppermute x6, waiting for transfers between devices, swap_on_chip(): return lax.ppermute(x, axis, [(i, i ^ 1) for i in range(count)])  1.87 us
  transfers between devices with their start and end apart: 10, of which 4 were waited for; matrix products, arithmetic and copies ran while one was open for 0% of the time, Pallas kernels for 2%

profile of v4, /device:TPU:1, one launch (start us, length us, event | category | flops | bytes accessed | tf_op | source)
XLA Modules:
  0.0 82.4 jit_solution(12880936994127175617)
XLA Ops:
  0.1 0.9 %copy-done.3 = bf16[8,6,16,128]{3,2,1,0:T(8,128)(2,1)S(1)} copy-done((bf16[8,6,16,128]{3,2,1,0:T(8,128)(2,1)S(1)}, bf16[8,6,16,128]{3,2,1,0:T(8,128)(2,1)}, u32[]{:S(2)}) %copy-start.3) | copy-done | bytes 196632
  0.9 1.1 %copy-done.1 = bf16[6,16,32,4,128]{4,3,2,1,0:T(4,128)(2,1)S(1)} copy-done((bf16[6,16,32,4,128]{4,3,2,1,0:T(4,128)(2,1)S(1)}, bf16[6,16,32,4,128]{4,3,2,1,0:T(4,128)(2,1)}, u32[]{:S(2)}) %copy-start.1) | copy-done | bytes 3145752
  2.0 2.0 %project.1 = (f32[8,128]{1,0:T(8,128)S(1)}, f32[2,8,128]{2,1,0:T(8,128)S(1)}, bf16[768,128]{1,0:T(8,128)(2,1)S(1)}, bf16[2,384,128]{2,1,0:T(8,128)(2,1)S(1)}) custom-call(s32[2,32]{1,0:T(2,128)S(1)} %copy-done.5, bf16[8,96,128]{2,1,0:T(8,128)(2,1)S(1)} %bitcast.37, bf16[96,128,128]{2,1,0:T(8,128)(2,1)S(1)} %bitcast.31, f32[2,8,128]{2,1,0:T(8,128)S(1)} %keep.1.keep_ref), custom_call_target="tpu_custom_call" | custom-call | flops 25165824 | bytes 3145728 | tf_op jit(solution)/shard_map/project/pallas_call | solution.py:300
  4.0 8.8 %collective-permute-start = (f32[8,128]{1,0:T(8,128)S(1)}, f32[8,128]{1,0:T(8,128)S(1)}, u32[]{:S(2)}, u32[]{:S(2)}) collective-permute-start(f32[8,128]{1,0:T(8,128)S(1)} %get-tuple-element.24), channel_id=1, source_target_pairs={{0,16},{16,0},{32,48},{48,32},{64,80},{80,64},{96,112},{112,96},{1... | collective-permute-start | bytes 12296 | tf_op jit(solution)/shard_map/ppermute | solution.py:378
  12.8 0.8 collective-permute-done
  13.6 1.9 %collective-permute-start.3 = (f32[2,8,128]{2,1,0:T(8,128)S(1)}, f32[2,8,128]{2,1,0:T(8,128)S(1)}, u32[]{:S(2)}, u32[]{:S(2)}) collective-permute-start(f32[2,8,128]{2,1,0:T(8,128)S(1)} %multiply_add_fusion.1), channel_id=1, source_target_pairs={{0,496},{16,32},{32,16},{48,64},{64,48},{80,96},{96,80},{112,128},... | collective-permute-start | bytes 24584 | tf_op jit(solution)/shard_map/ppermute | solution.py:383
  15.5 3.6 %collective-permute-start.2 = (bf16[8,96,128]{2,1,0:T(8,128)(2,1)S(1)}, bf16[8,96,128]{2,1,0:T(8,128)(2,1)S(1)}, u32[]{:S(2)}, u32[]{:S(2)}) collective-permute-start(bf16[8,96,128]{2,1,0:T(8,128)(2,1)S(1)} %bitcast.38), channel_id=1, source_target_pairs={{0,496},{16,32},{32,16},{48,64},{64,48},{80,96},{96,80},{112,128},... | collective-permute-start | bytes 589832 | tf_op jit(solution)/shard_map/ppermute | solution.py:383
  19.2 4.4 %collective-permute-start.1 = (bf16[8,96,128]{2,1,0:T(8,128)(2,1)S(1)}, bf16[8,96,128]{2,1,0:T(8,128)(2,1)S(1)}, u32[]{:S(2)}, u32[]{:S(2)}) collective-permute-start(bf16[8,96,128]{2,1,0:T(8,128)(2,1)S(1)} %bitcast.39), channel_id=1, source_target_pairs={{0,16},{16,0},{32,48},{48,32},{64,80},{80,64},{96,112},{112,96},{1... | collective-permute-start | bytes 589832 | tf_op jit(solution)/shard_map/ppermute | solution.py:378
  23.6 1.9 %collective-permute-start.4 = (f32[8,128]{1,0:T(8,128)S(1)}, f32[8,128]{1,0:T(8,128)S(1)}, u32[]{:S(2)}, u32[]{:S(2)}) collective-permute-start(f32[8,128]{1,0:T(8,128)S(1)} %get-tuple-element.37), channel_id=1, source_target_pairs={{0,16},{16,0},{32,48},{48,32},{64,80},{80,64},{96,112},{112,96},{1... | collective-permute-start | bytes 12296 | tf_op jit(solution)/shard_map/ppermute | solution.py:378
  25.5 1.0 %base_first.1 = (f32[768,128]{1,0:T(8,128)S(1)}, f32[8,128]{1,0:T(8,128)S(1)}) custom-call(bf16[768,128]{1,0:T(8,128)(2,1)S(1)} %get-tuple-element.22.v_ref.start_ref, bf16[8,96,128]{2,1,0:T(8,128)(2,1)S(1)} %collective-permute-done.1.on_ref, bf16[8,96,128]{2,1,0:T(8,128)(2,1)S(1)} %collective-permute-done.2.off_ref, f32[96,128]{1,0:T(8,128)S(1)} %bitcast.35, ...), custom_call_target="tpu_custom_call" | custom-call | flops 75497472 | bytes 983040 | tf_op jit(solution)/shard_map/base_first/pallas_call | solution.py:300
  26.6 2.5 %first.1 = (bf16[768,128]{1,0:T(8,128)(2,1)S(1)}, f32[8,128]{1,0:T(8,128)S(1)}, f32[2,8,128]{2,1,0:T(8,128)S(1)}) custom-call(f32[768,128]{1,0:T(8,128)S(1)} %get-tuple-element.26.base_ref, f32[2,8,128]{2,1,0:T(8,128)S(1)} %get-tuple-element.38.pair_in, f32[8,128]{1,0:T(8,128)S(1)} %collective-permute-done.4.other_ref, ...), custom_call_target="tpu_custom_call" | custom-call | flops 50331648 | bytes 3145728 | tf_op jit(solution)/shard_map/first/pallas_call | solution.py:300
  29.1 2.4 %collective-permute-start.5 = (f32[8,128]{1,0:T(8,128)S(1)}, f32[8,128]{1,0:T(8,128)S(1)}, u32[]{:S(2)}, u32[]{:S(2)}) collective-permute-start(f32[8,128]{1,0:T(8,128)S(1)} %get-tuple-element.32), channel_id=1, source_target_pairs={{0,16},{16,0},{32,48},{48,32},{64,80},{80,64},{96,112},{112,96},{1... | collective-permute-start | bytes 12296 | tf_op jit(solution)/shard_map/ppermute | solution.py:378
  31.5 0.8 collective-permute-done.5
  32.3 1.9 %collective-permute-start.8 = (f32[2,8,128]{2,1,0:T(8,128)S(1)}, f32[2,8,128]{2,1,0:T(8,128)S(1)}, u32[]{:S(2)}, u32[]{:S(2)}) collective-permute-start(f32[2,8,128]{2,1,0:T(8,128)S(1)} %multiply_add_fusion), channel_id=1, source_target_pairs={{0,496},{16,32},{32,16},{48,64},{64,48},{80,96},{96,80},{112,128},... | collective-permute-start | bytes 24584 | tf_op jit(solution)/shard_map/ppermute | solution.py:383
  34.2 3.6 %collective-permute-start.7 = (bf16[768,128]{1,0:T(8,128)(2,1)S(1)}, bf16[768,128]{1,0:T(8,128)(2,1)S(1)}, u32[]{:S(2)}, u32[]{:S(2)}) collective-permute-start(bf16[768,128]{1,0:T(8,128)(2,1)S(1)} %get-tuple-element.33.v_ref), channel_id=1, source_target_pairs={{0,496},{16,32},{32,16},{48,64},{64,48},{80,96},{96,80},{112,128},... | collective-permute-start | bytes 589832 | tf_op jit(solution)/shard_map/ppermute | solution.py:383
  37.8 4.4 %collective-permute-start.6 = (bf16[768,128]{1,0:T(8,128)(2,1)S(1)}, bf16[768,128]{1,0:T(8,128)(2,1)S(1)}, u32[]{:S(2)}, u32[]{:S(2)}) collective-permute-start(bf16[768,128]{1,0:T(8,128)(2,1)S(1)} %get-tuple-element.33.v_ref), channel_id=1, source_target_pairs={{0,16},{16,0},{32,48},{48,32},{64,80},{80,64},{96,112},{112,96},{1... | collective-permute-start | bytes 589832 | tf_op jit(solution)/shard_map/ppermute | solution.py:378
  42.2 1.9 %collective-permute-start.9 = (f32[8,128]{1,0:T(8,128)S(1)}, f32[8,128]{1,0:T(8,128)S(1)}, u32[]{:S(2)}, u32[]{:S(2)}) collective-permute-start(f32[8,128]{1,0:T(8,128)S(1)} %get-tuple-element.35), channel_id=1, source_target_pairs={{0,16},{16,0},{32,48},{48,32},{64,80},{80,64},{96,112},{112,96},{1... | collective-permute-start | bytes 12296 | tf_op jit(solution)/shard_map/ppermute | solution.py:378
  44.2 0.9 %base.1.base_ref = f32[768,128]{1,0:T(8,128)S(1)} custom-call(bf16[768,128]{1,0:T(8,128)(2,1)S(1)} %get-tuple-element.33.v_ref, bf16[768,128]{1,0:T(8,128)(2,1)S(1)} %collective-permute-done.6.on_ref, bf16[768,128]{1,0:T(8,128)(2,1)S(1)} %collective-permute-done.7.off_ref, f32[96,128]{1,0:T(8,128)S(1)} %bitcast.36), custom_call_target="tpu_custom_call" | custom-call | flops 75497472 | bytes 983040 | tf_op jit(solution)/shard_map/base/pallas_call | solution.py:300
  45.1 0.2 collective-permute-done.9.other_ref
  45.3 0.7 filtered.1
  45.9 19.9 %all_to_all.10 = bf16[16,6,8,128]{3,2,1,0:T(8,128)(2,1)S(1)} all-to-all(bf16[16,6,8,128]{3,2,1,0:T(8,128)(2,1)S(1)} %bitcast.34), channel_id=1, replica_groups=mesh['dom'=32,'band'=16] {'band'}, dimensions={0} | all-to-all | bytes 393216 | tf_op jit(solution)/shard_map/all_to_all | solution.py:418
  65.8 0.3 fusion.1
  66.1 15.6 %all_to_all.11 = bf16[16,6,8,128]{3,2,1,0:T(8,128)(2,1)S(1)} all-to-all(bf16[16,6,8,128]{3,2,1,0:T(8,128)(2,1)S(1)} %bitcast.41), channel_id=1, replica_groups=mesh['dom'=32,'band'=16] {'band'}, dimensions={0} | all-to-all | bytes 393216 | tf_op jit(solution)/shard_map/all_to_all | solution.py:422
  81.7 0.7 copy.16
  (23 shorter events, 0.2 us)
Async XLA Ops:
  0.0 65.8 %copy-start = (bf16[128,128]{1,0:T(8,128)(2,1)S(1)}, bf16[128,128]{1,0:T(8,128)(2,1)}, u32[]{:S(2)}) copy-start(bf16[128,128]{1,0:T(8,128)(2,1)} %param.11) | copy-start | bytes 98308
  0.0 0.9 %copy-start.3 = (bf16[8,6,16,128]{3,2,1,0:T(8,128)(2,1)S(1)}, bf16[8,6,16,128]{3,2,1,0:T(8,128)(2,1)}, u32[]{:S(2)}) copy-start(bf16[8,6,16,128]{3,2,1,0:T(8,128)(2,1)} %param.6) | copy-start | bytes 589828
  0.0 0.9 %copy-start.5 = (s32[2,32]{1,0:T(2,128)S(1)}, s32[2,32]{1,0:T(2,128)}, u32[]{:S(2)}) copy-start(s32[2,32]{1,0:T(2,128)} %ids_ref.1) | copy-start | bytes 772
  0.0 2.0 %copy-start.1 = (bf16[6,16,32,4,128]{4,3,2,1,0:T(4,128)(2,1)S(1)}, bf16[6,16,32,4,128]{4,3,2,1,0:T(4,128)(2,1)}, u32[]{:S(2)}) copy-start(bf16[6,16,32,4,128]{4,3,2,1,0:T(4,128)(2,1)} %param.8) | copy-start | bytes 9437188
  0.0 25.5 %copy-start.2 = (f32[6,16,128]{2,1,0:T(8,128)S(1)}, f32[6,16,128]{2,1,0:T(8,128)}, u32[]{:S(2)}) copy-start(f32[6,16,128]{2,1,0:T(8,128)} %param.7) | copy-start | bytes 147460
  0.1 25.5 %copy-start.4 = (f32[1024,4]{0,1:T(4,128)S(1)}, f32[1024,4]{0,1:T(4,128)}, u32[]{:S(2)}) copy-start(f32[1024,4]{0,1:T(4,128)} %param.10) | copy-start | bytes 49156
  4.0 9.6 %collective-permute-start = (f32[8,128]{1,0:T(8,128)S(1)}, f32[8,128]{1,0:T(8,128)S(1)}, u32[]{:S(2)}, u32[]{:S(2)}) collective-permute-start(f32[8,128]{1,0:T(8,128)S(1)} %get-tuple-element.24), channel_id=1, source_target_pairs={{0,16},{16,0},{32,48},{48,32},{64,80},{80,64},{96,112},{112,96},{1... | collective-permute-start | bytes 12296 | tf_op jit(solution)/shard_map/ppermute | solution.py:378
  13.6 9.9 %collective-permute-start.3 = (f32[2,8,128]{2,1,0:T(8,128)S(1)}, f32[2,8,128]{2,1,0:T(8,128)S(1)}, u32[]{:S(2)}, u32[]{:S(2)}) collective-permute-start(f32[2,8,128]{2,1,0:T(8,128)S(1)} %multiply_add_fusion.1), channel_id=1, source_target_pairs={{0,496},{16,32},{32,16},{48,64},{64,48},{80,96},{96,80},{112,128},... | collective-permute-start | bytes 24584 | tf_op jit(solution)/shard_map/ppermute | solution.py:383
  15.5 10.0 %collective-permute-start.2 = (bf16[8,96,128]{2,1,0:T(8,128)(2,1)S(1)}, bf16[8,96,128]{2,1,0:T(8,128)(2,1)S(1)}, u32[]{:S(2)}, u32[]{:S(2)}) collective-permute-start(bf16[8,96,128]{2,1,0:T(8,128)(2,1)S(1)} %bitcast.38), channel_id=1, source_target_pairs={{0,496},{16,32},{32,16},{48,64},{64,48},{80,96},{96,80},{112,128},... | collective-permute-start | bytes 589832 | tf_op jit(solution)/shard_map/ppermute | solution.py:383
  19.2 6.3 %collective-permute-start.1 = (bf16[8,96,128]{2,1,0:T(8,128)(2,1)S(1)}, bf16[8,96,128]{2,1,0:T(8,128)(2,1)S(1)}, u32[]{:S(2)}, u32[]{:S(2)}) collective-permute-start(bf16[8,96,128]{2,1,0:T(8,128)(2,1)S(1)} %bitcast.39), channel_id=1, source_target_pairs={{0,16},{16,0},{32,48},{48,32},{64,80},{80,64},{96,112},{112,96},{1... | collective-permute-start | bytes 589832 | tf_op jit(solution)/shard_map/ppermute | solution.py:378
  23.6 3.1 %collective-permute-start.4 = (f32[8,128]{1,0:T(8,128)S(1)}, f32[8,128]{1,0:T(8,128)S(1)}, u32[]{:S(2)}, u32[]{:S(2)}) collective-permute-start(f32[8,128]{1,0:T(8,128)S(1)} %get-tuple-element.37), channel_id=1, source_target_pairs={{0,16},{16,0},{32,48},{48,32},{64,80},{80,64},{96,112},{112,96},{1... | collective-permute-start | bytes 12296 | tf_op jit(solution)/shard_map/ppermute | solution.py:378
  29.1 3.2 %collective-permute-start.5 = (f32[8,128]{1,0:T(8,128)S(1)}, f32[8,128]{1,0:T(8,128)S(1)}, u32[]{:S(2)}, u32[]{:S(2)}) collective-permute-start(f32[8,128]{1,0:T(8,128)S(1)} %get-tuple-element.32), channel_id=1, source_target_pairs={{0,16},{16,0},{32,48},{48,32},{64,80},{80,64},{96,112},{112,96},{1... | collective-permute-start | bytes 12296 | tf_op jit(solution)/shard_map/ppermute | solution.py:378
  32.3 9.9 %collective-permute-start.8 = (f32[2,8,128]{2,1,0:T(8,128)S(1)}, f32[2,8,128]{2,1,0:T(8,128)S(1)}, u32[]{:S(2)}, u32[]{:S(2)}) collective-permute-start(f32[2,8,128]{2,1,0:T(8,128)S(1)} %multiply_add_fusion), channel_id=1, source_target_pairs={{0,496},{16,32},{32,16},{48,64},{64,48},{80,96},{96,80},{112,128},... | collective-permute-start | bytes 24584 | tf_op jit(solution)/shard_map/ppermute | solution.py:383
  34.2 10.0 %collective-permute-start.7 = (bf16[768,128]{1,0:T(8,128)(2,1)S(1)}, bf16[768,128]{1,0:T(8,128)(2,1)S(1)}, u32[]{:S(2)}, u32[]{:S(2)}) collective-permute-start(bf16[768,128]{1,0:T(8,128)(2,1)S(1)} %get-tuple-element.33.v_ref), channel_id=1, source_target_pairs={{0,496},{16,32},{32,16},{48,64},{64,48},{80,96},{96,80},{112,128},... | collective-permute-start | bytes 589832 | tf_op jit(solution)/shard_map/ppermute | solution.py:383
  37.8 6.3 %collective-permute-start.6 = (bf16[768,128]{1,0:T(8,128)(2,1)S(1)}, bf16[768,128]{1,0:T(8,128)(2,1)S(1)}, u32[]{:S(2)}, u32[]{:S(2)}) collective-permute-start(bf16[768,128]{1,0:T(8,128)(2,1)S(1)} %get-tuple-element.33.v_ref), channel_id=1, source_target_pairs={{0,16},{16,0},{32,48},{48,32},{64,80},{80,64},{96,112},{112,96},{1... | collective-permute-start | bytes 589832 | tf_op jit(solution)/shard_map/ppermute | solution.py:378
  42.2 3.1 %collective-permute-start.9 = (f32[8,128]{1,0:T(8,128)S(1)}, f32[8,128]{1,0:T(8,128)S(1)}, u32[]{:S(2)}, u32[]{:S(2)}) collective-permute-start(f32[8,128]{1,0:T(8,128)S(1)} %get-tuple-element.35), channel_id=1, source_target_pairs={{0,16},{16,0},{32,48},{48,32},{64,80},{80,64},{96,112},{112,96},{1... | collective-permute-start | bytes 12296 | tf_op jit(solution)/shard_map/ppermute | solution.py:378

commit v5 on v4

--- a/solution.py
+++ b/solution.py
@@ -86,27 +86,48 @@
     return out
 
 
-def scatter(z, side, partials, hots_ref, send_ref, pair_ref):
+def scatter(z, partials, hots_ref, tab_ref):
     total = None
     for j, partial in enumerate(partials):
         hot = hots_ref[j]
         for piece in split3(partial):
             part = dot_t(piece, hot)
             total = part if total is None else total + part
-    below, middle, above = (total[:, t * z.lanes : (t + 1) * z.lanes] for t in range(3))
+    for t in range(3):
+        tab_ref[t] = total[:, t * z.lanes : (t + 1) * z.lanes]
+
+
+def mate_tiles(side, tab_ref, mate_ref):
     first_core = side == 0
-    send_ref[...] = jnp.where(first_core, above, below)
-    pair_ref[0] = jnp.where(first_core, below, middle)
-    pair_ref[1] = jnp.where(first_core, middle, above)
-
-
-def gathered(z, side, pair_ref, other_ref, strength_ref, hots_ref):
-    first_core = side == 0
-    low, high, other = pair_ref[0], pair_ref[1], other_ref[...]
+    mate_ref[0] = jnp.where(first_core, tab_ref[1], tab_ref[0])
+    mate_ref[1] = jnp.where(first_core, tab_ref[2], tab_ref[1])
+
+
+def meet_kernel(z, tab_ref, mate_ref, got_ref, slab_in, slab_ref, chip_ref, far_ref):
+    first_core = (lax.axis_index("dom") & 1) == 0
+    low, high = mate_ref[0] + got_ref[0], mate_ref[1] + got_ref[1]
+    chip_ref[0], chip_ref[1] = low, high
+    below, above = tab_ref[0], tab_ref[2]
+    far_ref[...] = jnp.where(first_core, below, above)
+    pair = jnp.concatenate(
+        [jnp.where(first_core, below, high), jnp.where(first_core, low, above)], 0
+    )
+    for n, piece in enumerate(split3(pair)):
+        slab_ref[z.tall + n * 2 * z.bands : z.tall + (n + 1) * 2 * z.bands, :] = piece
+
+
+def gathered(z, tab_ref, chip_ref, across_ref, far_ref, strength_ref, hots_ref):
+    first_core = (lax.axis_index("dom") & 1) == 0
+    got = None
+    for n in range(3):
+        piece = across_ref[z.tall + n * 2 * z.bands : z.tall + (n + 1) * 2 * z.bands, :].astype(F32)
+        got = piece if got is None else got + piece
+    got = [got[: z.bands], got[z.bands :]]
+    low, high, far = chip_ref[0], chip_ref[1], far_ref[...]
     tiles = [
-        jnp.where(first_core, low, other),
-        jnp.where(first_core, high, low),
-        jnp.where(first_core, other, high),
+        jnp.where(first_core, tab_ref[0] + got[0], low + far),
+        jnp.where(first_core, low + got[1], high + got[0]),
+        jnp.where(first_core, high + far, tab_ref[2] + got[1]),
     ]
     weighted = [tile * strength_ref[t : t + 1, :] for t, tile in enumerate(tiles)]
     weighted = jnp.concatenate(weighted, 1).astype(BF16)
@@ -154,21 +175,19 @@
         v_ref[x * tall : (x + 1) * tall, :] = plane.astype(BF16)
 
 
-def keep_kernel(z, keep_ref):
-    side = lax.axis_index("dom") & 1
-    ones = jnp.full(keep_ref.shape[1:], 1.0, F32)
-    keep_ref[0] = jnp.where(side == 1, ones, 0.0)
-    keep_ref[1] = jnp.where(side == 0, ones, 0.0)
-
-
-def project_kernel(z, ids_ref, bands_ref, proj_ref, keep_ref, send_ref, pair_ref, v_ref, hots_ref):
+def pause_kernel(z, out_ref):
+    out_ref[...] = jnp.zeros_like(out_ref)
+
+
+def project_kernel(z, pause_ref, ids_ref, bands_ref, proj_ref, tab_ref, mate_ref, v_ref, hots_ref):
     dom = lax.axis_index("dom")
     turn_all(z, bands_ref, v_ref)
     for j, hot in enumerate(one_hots(z, dom, ids_ref)):
         hots_ref[j] = hot
     projector = Projector(z, v_ref, proj_ref)
     projector.add(range(z.cells // 2))
-    scatter(z, dom & 1, projector.sums(), hots_ref, send_ref, pair_ref)
+    scatter(z, projector.sums(), hots_ref, tab_ref)
+    mate_tiles(dom & 1, tab_ref, mate_ref)
 
 
 def near_strength(z, dom, strength_ref, out_ref):
@@ -227,25 +246,7 @@
     return on_at, off_at
 
 
-def base_first_kernel(z, v_ref, on_ref, off_ref, pot_ref, strength_ref, out_ref, near_ref, wide_ref):
-    dom = lax.axis_index("dom")
-    on_at, off_at = places(z, dom)
-    for x in range(z.thickness):
-        at = x * z.rows
-        rows = slice(z.bands * at, z.bands * (at + z.rows))
-        mine = v_ref[rows, :].astype(F32).reshape(z.rows, z.bands, z.depth)
-        wide_ref[z.cells + at : z.cells + at + z.rows] = mine
-        wide_ref[pl.ds(on_at + at, z.rows)] = turned(z, on_ref, x)
-        wide_ref[pl.ds(off_at + at, z.rows)] = turned(z, off_ref, x)
-
-    def put(rows, value):
-        out_ref[rows, :] = value
-
-    base_body(z, dom, v_ref, wide_ref, Writer(pot_ref, put))
-    near_strength(z, dom, strength_ref, near_ref)
-
-
-def base_kernel(z, v_ref, on_ref, off_ref, pot_ref, out_ref, wide_ref):
+def fill_and_base(z, v_ref, on_ref, off_ref, pot_ref, out_ref, wide_ref):
     dom = lax.axis_index("dom")
     on_at, off_at = places(z, dom)
     step, b = 8, z.bands
@@ -262,6 +263,15 @@
         out_ref[rows, :] = value
 
     base_body(z, dom, v_ref, wide_ref, Writer(pot_ref, put))
+
+
+def base_first_kernel(z, v_ref, on_ref, off_ref, pot_ref, strength_ref, out_ref, near_ref, wide_ref):
+    fill_and_base(z, v_ref, on_ref, off_ref, pot_ref, out_ref, wide_ref)
+    near_strength(z, lax.axis_index("dom"), strength_ref, near_ref)
+
+
+def base_kernel(z, v_ref, on_ref, off_ref, pot_ref, out_ref, wide_ref):
+    fill_and_base(z, v_ref, on_ref, off_ref, pot_ref, out_ref, wide_ref)
 
 
 def nonlocal_pair(weighted, proj_ref, pair):
@@ -271,21 +281,24 @@
     return jnp.concatenate([value[:, :half], value[:, half:]], 0)
 
 
-def first_kernel(z, base_ref, pair_in, other_ref, near_ref, hots_ref, proj_ref, first_ref, send_ref, pair_ref):
-    side = lax.axis_index("dom") & 1
-    weighted = gathered(z, side, pair_in, other_ref, near_ref, hots_ref)
+def first_kernel(
+    z, base_ref, tab_in, chip_ref, across_ref, far_ref, near_ref, hots_ref, proj_ref, first_ref, tab_ref, mate_ref
+):
+    weighted = gathered(z, tab_in, chip_ref, across_ref, far_ref, near_ref, hots_ref)
     for pair in range(z.cells // 2):
         rows = pair_rows(pair)
         value = base_ref[rows, :] + nonlocal_pair(weighted[block_of(z, pair)], proj_ref, pair)
         first_ref[rows, :] = (value / half_width).astype(BF16)
     projector = Projector(z, first_ref, proj_ref)
     projector.add(range(z.cells // 2))
-    scatter(z, side, projector.sums(), hots_ref, send_ref, pair_ref)
-
-
-def filtered_kernel(z, base_ref, pair_in, other_ref, near_ref, hots_ref, proj_ref, start_ref, out_ref):
-    side = lax.axis_index("dom") & 1
-    weighted = gathered(z, side, pair_in, other_ref, near_ref, hots_ref)
+    scatter(z, projector.sums(), hots_ref, tab_ref)
+    mate_tiles(lax.axis_index("dom") & 1, tab_ref, mate_ref)
+
+
+def filtered_kernel(
+    z, base_ref, tab_ref, chip_ref, across_ref, far_ref, near_ref, hots_ref, proj_ref, start_ref, out_ref
+):
+    weighted = gathered(z, tab_ref, chip_ref, across_ref, far_ref, near_ref, hots_ref)
     for pair in range(z.cells // 2):
         rows = pair_rows(pair)
         value = base_ref[rows, :] + nonlocal_pair(weighted[block_of(z, pair)], proj_ref, pair)
@@ -295,82 +308,36 @@
 VMEM = pl.BlockSpec(memory_space=pltpu.VMEM)
 
 
-def call(kernel, z, name, outs, ins, flops, moved, spaces, scratch=(), limit=12288):
+def call(kernel, z, name, outs, ins, flops, moved, scratch=(), aliases=None):
     single = not isinstance(outs, (list, tuple))
     return pl.pallas_call(
         functools.partial(kernel, z),
         name=name,
         out_shape=outs,
-        in_specs=spaces,
+        in_specs=[VMEM] * len(ins),
         out_specs=VMEM if single else [VMEM] * len(outs),
         scratch_shapes=list(scratch),
-        compiler_params=pltpu.CompilerParams(vmem_limit_bytes=limit * 1024),
+        input_output_aliases=aliases or {},
+        compiler_params=pltpu.CompilerParams(vmem_limit_bytes=12288 * 1024),
         cost_estimate=pl.CostEstimate(flops=flops, bytes_accessed=moved, transcendentals=0),
     )(*ins)
 
 
-def shapes(z):
-    tile = jax.ShapeDtypeStruct((z.bands, z.lanes), F32)
-    pair = jax.ShapeDtypeStruct((2, z.bands, z.lanes), F32)
-    slab = jax.ShapeDtypeStruct((z.tall, z.depth), BF16)
-    wide = jax.ShapeDtypeStruct((z.tall, z.depth), F32)
-    near = jax.ShapeDtypeStruct((8, z.lanes), F32)
-    proj = jax.ShapeDtypeStruct((z.cells, z.slots, z.depth), BF16)
-    hots = jax.ShapeDtypeStruct((z.blocks, 3 * z.lanes, z.slots), BF16)
-    return tile, pair, slab, wide, near, proj, hots
-
-
-def run_keep(z):
-    tile, pair, slab, wide, near, projs, hots = shapes(z)
-    return call(keep_kernel, z, "keep", pair, (), 4000 * z.tall * z.slots * z.depth, 40_000_000, [])
-
-
-def run_project(z, ids, bands, proj, keep):
-    tile, pair, slab, wide, near, projs, hots = shapes(z)
-    return call(
-        project_kernel, z, "project", [tile, pair, slab, hots], (ids, bands, proj, keep),
-        2 * z.tall * z.slots * z.depth, 2 * z.cells * z.slots * z.depth, [VMEM] * 4,
-    )
-
-
-def wide_scratch(z):
-    return [pltpu.VMEM((3 * z.cells, z.bands, z.depth), F32)]
-
-
-def run_base_first(z, v, on_chip, across, pot, strength_t):
-    tile, pair, slab, wide, near, projs, hots = shapes(z)
-    return call(
-        base_first_kernel, z, "base_first", [wide, near], (v, on_chip, across, pot, strength_t),
-        6 * z.tall * z.depth * z.depth, 10 * z.tall * z.depth, [VMEM] * 5,
-        scratch=wide_scratch(z),
-    )
-
-
-def run_base(z, v, on_chip, across, pot):
-    tile, pair, slab, wide, near, projs, hots = shapes(z)
-    return call(
-        base_kernel, z, "base", wide, (v, on_chip, across, pot),
-        6 * z.tall * z.depth * z.depth, 10 * z.tall * z.depth, [VMEM] * 4,
-        scratch=wide_scratch(z),
-    )
-
-
-def run_first(z, base, pair_in, other, near_in, hots_in, proj):
-    tile, pair, slab, wide, near, projs, hots = shapes(z)
-    stream = 2 * z.tall * z.slots * z.depth
-    return call(
-        first_kernel, z, "first", [slab, tile, pair], (base, pair_in, other, near_in, hots_in, proj),
-        2 * stream, 2 * z.cells * z.slots * z.depth, [VMEM] * 6,
-    )
-
-
-def run_filtered(z, base, pair_in, other, near_in, hots_in, proj, start):
-    tile, pair, slab, wide, near, projs, hots = shapes(z)
-    stream = 2 * z.tall * z.slots * z.depth
-    return call(
-        filtered_kernel, z, "filtered", slab, (base, pair_in, other, near_in, hots_in, proj, start),
-        stream, 2 * z.cells * z.slots * z.depth, [VMEM] * 7,
-    )
+class Shapes:
+    def __init__(self, z):
+        self.tile = jax.ShapeDtypeStruct((z.bands, z.lanes), F32)
+        self.pair = jax.ShapeDtypeStruct((2, z.bands, z.lanes), F32)
+        self.tab = jax.ShapeDtypeStruct((3, z.bands, z.lanes), F32)
+        self.slab = jax.ShapeDtypeStruct((z.tall, z.depth), BF16)
+        self.message = jax.ShapeDtypeStruct((z.tall + 6 * z.bands, z.depth), BF16)
+        self.base = jax.ShapeDtypeStruct((z.tall, z.depth), F32)
+        self.near = jax.ShapeDtypeStruct((8, z.lanes), F32)
+        self.hots = jax.ShapeDtypeStruct((z.blocks, 3 * z.lanes, z.slots), BF16)
+        self.wide = [pltpu.VMEM((3 * z.cells, z.bands, z.depth), F32)]
+        self.stream = 2 * z.tall * z.slots * z.depth
+        self.proj_bytes = 2 * z.cells * z.slots * z.depth
+        self.stencil = 6 * z.tall * z.depth * z.depth
+        self.slab_bytes = 10 * z.tall * z.depth
 
 
 def swap_on_chip(x, axis):
@@ -381,6 +348,11 @@
 def swap_across(x, axis):
     count = lax.axis_size(axis)
     return lax.ppermute(x, axis, [(i, (((i + 1) ^ 1) - 1) % count) for i in range(count)])
+
+
+def swap_far(x, axis):
+    count = lax.axis_size(axis)
+    return lax.ppermute(x, axis, [(i, (i + 2 * (i % 2) * 2 - 2) % count) for i in range(count)])
 
 
 def local(bands, potential, projectors, atom_ids, strength, rotation):
@@ -390,28 +362,41 @@
     pot = potential.reshape(z.cells, z.depth)
     flat = bands.reshape(z.bands, z.cells, z.depth)
 
-    def exchange(send, pair, keep, slab):
+    s = Shapes(z)
+
+    def exchange(tab, mate, slab):
+        got = swap_on_chip(mate, "dom")
+        slab, chip, far = call(
+            meet_kernel, z, "meet", [s.message, s.pair, s.tile], (tab, mate, got, slab),
+            1000, 1000, aliases={3: 0},
+        )
         across = swap_across(slab, "dom")
-        pair = pair + keep * swap_on_chip(send, "dom")[None]
-        pair, slab = lax.optimization_barrier((pair, slab))
-        pair = pair + swap_across(pair, "dom")
-        return pair, swap_on_chip(slab, "dom"), across
-
-    def other_tile(pair, keep):
-        return swap_on_chip(jnp.sum(keep * pair, 0), "dom")
-
-    keep = run_keep(z)
-    flat, keep = lax.optimization_barrier((flat, keep))
-    send, pair, start, hots = run_project(z, atom_ids, flat, proj, keep)
-    pair, start_on, start_across = exchange(send, pair, keep, flat)
-    base, near = run_base_first(z, start, start_on, start_across, pot, strength.T)
-    other = other_tile(pair, keep)
-    first, send, pair = run_first(z, base, pair, other, near, hots, proj)
-
-    pair, first_on, first_across = exchange(send, pair, keep, first)
-    base = run_base(z, first, first_on, first_across, pot)
-    other = other_tile(pair, keep)
-    filtered = run_filtered(z, base, pair, other, near, hots, proj, start)
+        far = swap_far(far, "dom")
+        return slab, swap_on_chip(slab, "dom"), across, (tab, chip, across, far)
+
+    pause = call(pause_kernel, z, "pause", s.tile, (), 4000 * s.stream, 40_000_000)
+    tab, mate, start, hots = call(
+        project_kernel, z, "project", [s.tab, s.pair, s.message, s.hots],
+        (pause, atom_ids, flat, proj), s.stream, s.proj_bytes,
+    )
+    start, on_chip, across, sums = exchange(tab, mate, start)
+    base, near = call(
+        base_first_kernel, z, "base_first", [s.base, s.near],
+        (start, on_chip, across, pot, strength.T), s.stencil, s.slab_bytes, scratch=s.wide,
+    )
+    first, tab, mate = call(
+        first_kernel, z, "first", [s.message, s.tab, s.pair],
+        (base,) + sums + (near, hots, proj), 2 * s.stream, s.proj_bytes,
+    )
+    first, on_chip, across, sums = exchange(tab, mate, first)
+    base = call(
+        base_kernel, z, "base", s.base, (first, on_chip, across, pot),
+        s.stencil, s.slab_bytes, scratch=s.wide,
+    )
+    filtered = call(
+        filtered_kernel, z, "filtered", s.slab, (base,) + sums + (near, hots, proj, start),
+        s.stream, s.proj_bytes,
+    )
 
     share = z.cells // groups
     pieces = filtered.reshape(groups, share, z.bands, z.depth)

time: 82.8 us -> 80.7 us (0.975)
  waiting for transfers between devices: 1.88 us -> 7.32 us
  starting transfers between devices: 34.8 us -> 29.5 us
  blocking collectives: 35.4 us -> 33.5 us
    ppermute x4 -> x2, starting transfers between devices: 11.1 us -> 3.84 us  [swap_across(): lax.ppermute(x, axis, [(i, ((i + 1 ^ 1) - 1) % count) for i in range(coun...]
    ppermute x0 -> x2, waiting for transfers between devices: none -> 5.7 us  [swap_far(): lax.ppermute(x, axis, [(i, (i + 2 * (i % 2) * 2 - 2) % count) for i in ra...]
    ppermute x0 -> x2, starting transfers between devices: none -> 5.33 us  [swap_far(): lax.ppermute(x, axis, [(i, (i + 2 * (i % 2) * 2 - 2) % count) for i in ra...]
    ppermute x6 -> x4, starting transfers between devices: 23.7 us -> 20.4 us  [swap_on_chip(): return lax.ppermute(x, axis, [(i, i ^ 1) for i in range(count)])]
    all_to_all x1, blocking collectives: 15.6 us -> 14.5 us  [local(): rotated = lax.all_to_all(rotated, 'band', 0, 0, tiled=True)]
    all_to_all x1, blocking collectives: 19.9 us -> 19 us  [local(): pieces = lax.all_to_all(pieces, 'band', 0, 0, tiled=True)]
    ppermute x6 -> x4, waiting for transfers between devices: 1.87 us -> 1.62 us  [swap_on_chip(): return lax.ppermute(x, axis, [(i, i ^ 1) for i in range(count)])]
    pallas_call x6 -> x8, Pallas kernels: 7.01 us -> 6.89 us  [call(): pl.pallas_call(functools.partial(kernel, z), name=name, out_shape=outs, i...]
  transfers between devices with their start and end apart: 10 -> 8, of which waited for: 4 -> 4; matrix products, arithmetic and copies ran while one was open for 0% -> 0% of each run, Pallas kernels for 2% -> 2%
where the time goes in v5:
time: 80.7 us; the launch traced here: 80.3 us
  blocking collectives  33.5 us (42%)
  starting transfers between devices  29.5 us (37%)
  waiting for transfers between devices  7.32 us (9%)
  Pallas kernels  6.89 us (9%)
  local copies, waits for them, and re-layouts  2.62 us (3%)
    ppermute x4, starting transfers between devices, swap_on_chip(): return lax.ppermute(x, axis, [(i, i ^ 1) for i in range(count)])  20.4 us
    all_to_all x1, blocking collectives, local(): pieces = lax.all_to_all(pieces, 'band', 0, 0, tiled=True)  19 us
    all_to_all x1, blocking collectives, local(): rotated = lax.all_to_all(rotated, 'band', 0, 0, tiled=True)  14.5 us
    pallas_call x8, Pallas kernels, call(): pl.pallas_call(functools.partial(kernel, z), name=name, out_shape=outs, i...  6.89 us
    ppermute x2, waiting for transfers between devices, swap_far(): lax.ppermute(x, axis, [(i, (i + 2 * (i % 2) * 2 - 2) % count) for i in ra...  5.7 us
    ppermute x2, starting transfers between devices, swap_far(): lax.ppermute(x, axis, [(i, (i + 2 * (i % 2) * 2 - 2) % count) for i in ra...  5.33 us
    ppermute x2, starting transfers between devices, swap_across(): lax.ppermute(x, axis, [(i, ((i + 1 ^ 1) - 1) % count) for i in range(coun...  3.84 us
    unnamed x12, local copies, waits for them, and re-layouts  1.88 us
  transfers between devices with their start and end apart: 8, of which 4 were waited for; matrix products, arithmetic and copies ran while one was open for 0% of the time, Pallas kernels for 2%

profile of v5, /device:TPU:1, one launch (start us, length us, event | category | flops | bytes accessed | tf_op | source)
XLA Modules:
  0.0 80.3 jit_solution(6459770207625162370)
XLA Ops:
  0.0 0.0 copy-start.3
  0.1 0.6 copy-done.5
  0.7 1.2 %copy-done.1 = bf16[6,16,32,4,128]{4,3,2,1,0:T(4,128)(2,1)S(1)} copy-done((bf16[6,16,32,4,128]{4,3,2,1,0:T(4,128)(2,1)S(1)}, bf16[6,16,32,4,128]{4,3,2,1,0:T(4,128)(2,1)}, u32[]{:S(2)}) %copy-start.1) | copy-done | bytes 3145752
  1.9 2.0 %project.1 = (f32[3,8,128]{2,1,0:T(8,128)S(1)}, f32[2,8,128]{2,1,0:T(8,128)S(1)}, bf16[816,128]{1,0:T(8,128)(2,1)S(1)}, bf16[2,384,128]{2,1,0:T(8,128)(2,1)S(1)}) custom-call(f32[8,128]{1,0:T(8,128)S(1)} %pause.1.pause_ref, s32[2,32]{1,0:T(2,128)S(1)} %copy-done.5, bf16[8,96,128]{2,1,0:T(8,128)(2,1)S(1)} %bitcast.35, bf16[96,128,128]{2,1,0:T(8,128)(2,1)S(1)} %bitcast.31), custom_call_target="tpu_custom_call" | custom-call | flops 25165824 | bytes 3145728 | tf_op jit(solution)/shard_map/project/pallas_call | solution.py:313
  3.9 8.8 %collective-permute-start = (f32[2,8,128]{2,1,0:T(8,128)S(1)}, f32[2,8,128]{2,1,0:T(8,128)S(1)}, u32[]{:S(2)}, u32[]{:S(2)}) collective-permute-start(f32[2,8,128]{2,1,0:T(8,128)S(1)} %get-tuple-element.21.mate_ref), channel_id=1, source_target_pairs={{0,16},{16,0},{32,48},{48,32},{64,80},{80,64},{96,112},{112,96},{1... | collective-permute-start | bytes 24584 | tf_op jit(solution)/shard_map/ppermute | solution.py:345
  12.7 0.8 %collective-permute-done.got_ref = f32[2,8,128]{2,1,0:T(8,128)S(1)} collective-permute-done((f32[2,8,128]{2,1,0:T(8,128)S(1)}, f32[2,8,128]{2,1,0:T(8,128)S(1)}, u32[]{:S(2)}, u32[]{:S(2)}) %collective-permute-start) | collective-permute-done | bytes 8224 | tf_op jit(solution)/shard_map/ppermute | solution.py:345
  13.5 1.9 %collective-permute-start.2 = (bf16[816,128]{1,0:T(8,128)(2,1)S(1)}, bf16[816,128]{1,0:T(8,128)(2,1)S(1)}, u32[]{:S(2)}, u32[]{:S(2)}) collective-permute-start(bf16[816,128]{1,0:T(8,128)(2,1)S(1)} %get-tuple-element.23.v_ref.start_ref), channel_id=1, source_target_pairs={{0,496},{16,32},{32,16},{48,64},{64,48},{80,96},{96,80},{112,128},... | collective-permute-start | bytes 626696 | tf_op jit(solution)/shard_map/ppermute | solution.py:350
  15.4 2.3 %collective-permute-start.1 = (bf16[816,128]{1,0:T(8,128)(2,1)S(1)}, bf16[816,128]{1,0:T(8,128)(2,1)S(1)}, u32[]{:S(2)}, u32[]{:S(2)}) collective-permute-start(bf16[816,128]{1,0:T(8,128)(2,1)S(1)} %get-tuple-element.23.v_ref.start_ref), channel_id=1, source_target_pairs={{0,16},{16,0},{32,48},{48,32},{64,80},{80,64},{96,112},{112,96},{1... | collective-permute-start | bytes 626696 | tf_op jit(solution)/shard_map/ppermute | solution.py:345
  17.7 3.4 %collective-permute-start.3 = (f32[8,128]{1,0:T(8,128)S(1)}, f32[8,128]{1,0:T(8,128)S(1)}, u32[]{:S(2)}, u32[]{:S(2)}) collective-permute-start(f32[8,128]{1,0:T(8,128)S(1)} %get-tuple-element.26), channel_id=1, source_target_pairs={{0,480},{16,48},{32,0},{48,80},{64,32},{80,112},{96,64},{112,144},... | collective-permute-start | bytes 12296 | tf_op jit(solution)/shard_map/ppermute | solution.py:355
  21.2 0.9 %base_first.1 = (f32[768,128]{1,0:T(8,128)S(1)}, f32[8,128]{1,0:T(8,128)S(1)}) custom-call(bf16[816,128]{1,0:T(8,128)(2,1)S(1)} %get-tuple-element.23.v_ref.start_ref, bf16[816,128]{1,0:T(8,128)(2,1)S(1)} %collective-permute-done.1.on_ref, bf16[816,128]{1,0:T(8,128)(2,1)S(1)} %collective-permute-done.2.off_ref.across_ref, f32[96,128]{1,0:T(8,128)S(1)} %bitcast.36, ...), custom_call_target="tpu_custom_call" | custom-call | flops 75497472 | bytes 983040 | tf_op jit(solution)/shard_map/base_first/pallas_call | solution.py:313
  22.1 2.1 %collective-permute-done.3.far_ref = f32[8,128]{1,0:T(8,128)S(1)} collective-permute-done((f32[8,128]{1,0:T(8,128)S(1)}, f32[8,128]{1,0:T(8,128)S(1)}, u32[]{:S(2)}, u32[]{:S(2)}) %collective-permute-start.3) | collective-permute-done | bytes 4128 | tf_op jit(solution)/shard_map/ppermute | solution.py:355
  24.2 2.5 %first.1 = (bf16[816,128]{1,0:T(8,128)(2,1)S(1)}, f32[3,8,128]{2,1,0:T(8,128)S(1)}, f32[2,8,128]{2,1,0:T(8,128)S(1)}) custom-call(f32[768,128]{1,0:T(8,128)S(1)} %get-tuple-element.24.base_ref, f32[3,8,128]{2,1,0:T(8,128)S(1)} %get-tuple-element.20.tab_ref.tab_in, f32[2,8,128]{2,1,0:T(8,128)S(1)} %get-tuple-element.25.chip_ref, ...), custom_call_target="tpu_custom_call" | custom-call | flops 50331648 | bytes 3145728 | tf_op jit(solution)/shard_map/first/pallas_call | solution.py:313
  26.6 2.9 %collective-permute-start.4 = (f32[2,8,128]{2,1,0:T(8,128)S(1)}, f32[2,8,128]{2,1,0:T(8,128)S(1)}, u32[]{:S(2)}, u32[]{:S(2)}) collective-permute-start(f32[2,8,128]{2,1,0:T(8,128)S(1)} %get-tuple-element.30.mate_ref), channel_id=1, source_target_pairs={{0,16},{16,0},{32,48},{48,32},{64,80},{80,64},{96,112},{112,96},{1... | collective-permute-start | bytes 24584 | tf_op jit(solution)/shard_map/ppermute | solution.py:345
  29.5 0.8 %collective-permute-done.4.got_ref = f32[2,8,128]{2,1,0:T(8,128)S(1)} collective-permute-done((f32[2,8,128]{2,1,0:T(8,128)S(1)}, f32[2,8,128]{2,1,0:T(8,128)S(1)}, u32[]{:S(2)}, u32[]{:S(2)}) %collective-permute-start.4) | collective-permute-done | bytes 8224 | tf_op jit(solution)/shard_map/ppermute | solution.py:345
  30.4 1.9 %collective-permute-start.6 = (bf16[816,128]{1,0:T(8,128)(2,1)S(1)}, bf16[816,128]{1,0:T(8,128)(2,1)S(1)}, u32[]{:S(2)}, u32[]{:S(2)}) collective-permute-start(bf16[816,128]{1,0:T(8,128)(2,1)S(1)} %get-tuple-element.32.v_ref), channel_id=1, source_target_pairs={{0,496},{16,32},{32,16},{48,64},{64,48},{80,96},{96,80},{112,128},... | collective-permute-start | bytes 626696 | tf_op jit(solution)/shard_map/ppermute | solution.py:350
  32.3 6.4 %collective-permute-start.5 = (bf16[816,128]{1,0:T(8,128)(2,1)S(1)}, bf16[816,128]{1,0:T(8,128)(2,1)S(1)}, u32[]{:S(2)}, u32[]{:S(2)}) collective-permute-start(bf16[816,128]{1,0:T(8,128)(2,1)S(1)} %get-tuple-element.32.v_ref), channel_id=1, source_target_pairs={{0,16},{16,0},{32,48},{48,32},{64,80},{80,64},{96,112},{112,96},{1... | collective-permute-start | bytes 626696 | tf_op jit(solution)/shard_map/ppermute | solution.py:345
  38.7 1.9 %collective-permute-start.7 = (f32[8,128]{1,0:T(8,128)S(1)}, f32[8,128]{1,0:T(8,128)S(1)}, u32[]{:S(2)}, u32[]{:S(2)}) collective-permute-start(f32[8,128]{1,0:T(8,128)S(1)} %get-tuple-element.34), channel_id=1, source_target_pairs={{0,480},{16,48},{32,0},{48,80},{64,32},{80,112},{96,64},{112,144},... | collective-permute-start | bytes 12296 | tf_op jit(solution)/shard_map/ppermute | solution.py:355
  40.6 0.9 %base.1.base_ref = f32[768,128]{1,0:T(8,128)S(1)} custom-call(bf16[816,128]{1,0:T(8,128)(2,1)S(1)} %get-tuple-element.32.v_ref, bf16[816,128]{1,0:T(8,128)(2,1)S(1)} %collective-permute-done.5.on_ref, bf16[816,128]{1,0:T(8,128)(2,1)S(1)} %collective-permute-done.6.off_ref.across_ref, f32[96,128]{1,0:T(8,128)S(1)} %bitcast.37), custom_call_target="tpu_custom_call" | custom-call | flops 75497472 | bytes 983040 | tf_op jit(solution)/shard_map/base/pallas_call | solution.py:313
  41.5 3.6 %collective-permute-done.7.far_ref = f32[8,128]{1,0:T(8,128)S(1)} collective-permute-done((f32[8,128]{1,0:T(8,128)S(1)}, f32[8,128]{1,0:T(8,128)S(1)}, u32[]{:S(2)}, u32[]{:S(2)}) %collective-permute-start.7) | collective-permute-done | bytes 4128 | tf_op jit(solution)/shard_map/ppermute | solution.py:355
  45.2 0.6 filtered.1
  45.8 19.0 %all_to_all.10 = bf16[16,6,8,128]{3,2,1,0:T(8,128)(2,1)S(1)} all-to-all(bf16[16,6,8,128]{3,2,1,0:T(8,128)(2,1)S(1)} %bitcast.34), channel_id=1, replica_groups=mesh['dom'=32,'band'=16] {'band'}, dimensions={0} | all-to-all | bytes 393216 | tf_op jit(solution)/shard_map/all_to_all | solution.py:403
  64.8 0.3 fusion.1
  65.1 14.5 %all_to_all.11 = bf16[16,6,8,128]{3,2,1,0:T(8,128)(2,1)S(1)} all-to-all(bf16[16,6,8,128]{3,2,1,0:T(8,128)(2,1)S(1)} %bitcast.39), channel_id=1, replica_groups=mesh['dom'=32,'band'=16] {'band'}, dimensions={0} | all-to-all | bytes 393216 | tf_op jit(solution)/shard_map/all_to_all | solution.py:407
  79.6 0.7 copy.18
  (17 shorter events, 0.1 us)
Async XLA Ops:
  0.0 64.8 %copy-start = (bf16[128,128]{1,0:T(8,128)(2,1)S(1)}, bf16[128,128]{1,0:T(8,128)(2,1)}, u32[]{:S(2)}) copy-start(bf16[128,128]{1,0:T(8,128)(2,1)} %param.11) | copy-start | bytes 98308
  0.0 0.7 copy-start.5
  0.0 1.9 %copy-start.1 = (bf16[6,16,32,4,128]{4,3,2,1,0:T(4,128)(2,1)S(1)}, bf16[6,16,32,4,128]{4,3,2,1,0:T(4,128)(2,1)}, u32[]{:S(2)}) copy-start(bf16[6,16,32,4,128]{4,3,2,1,0:T(4,128)(2,1)} %param.8) | copy-start | bytes 9437188
  0.0 1.9 %copy-start.2 = (bf16[8,6,16,128]{3,2,1,0:T(8,128)(2,1)S(1)}, bf16[8,6,16,128]{3,2,1,0:T(8,128)(2,1)}, u32[]{:S(2)}) copy-start(bf16[8,6,16,128]{3,2,1,0:T(8,128)(2,1)} %param.6) | copy-start | bytes 589828
  0.0 21.1 %copy-start.3 = (f32[6,16,128]{2,1,0:T(8,128)S(1)}, f32[6,16,128]{2,1,0:T(8,128)}, u32[]{:S(2)}) copy-start(f32[6,16,128]{2,1,0:T(8,128)} %param.7) | copy-start | bytes 147460
  0.0 21.1 %copy-start.4 = (f32[1024,4]{0,1:T(4,128)S(1)}, f32[1024,4]{0,1:T(4,128)}, u32[]{:S(2)}) copy-start(f32[1024,4]{0,1:T(4,128)} %param.10) | copy-start | bytes 49156
  3.9 9.6 %collective-permute-start = (f32[2,8,128]{2,1,0:T(8,128)S(1)}, f32[2,8,128]{2,1,0:T(8,128)S(1)}, u32[]{:S(2)}, u32[]{:S(2)}) collective-permute-start(f32[2,8,128]{2,1,0:T(8,128)S(1)} %get-tuple-element.21.mate_ref), channel_id=1, source_target_pairs={{0,16},{16,0},{32,48},{48,32},{64,80},{80,64},{96,112},{112,96},{1... | collective-permute-start | bytes 24584 | tf_op jit(solution)/shard_map/ppermute | solution.py:345
  13.5 7.6 %collective-permute-start.2 = (bf16[816,128]{1,0:T(8,128)(2,1)S(1)}, bf16[816,128]{1,0:T(8,128)(2,1)S(1)}, u32[]{:S(2)}, u32[]{:S(2)}) collective-permute-start(bf16[816,128]{1,0:T(8,128)(2,1)S(1)} %get-tuple-element.23.v_ref.start_ref), channel_id=1, source_target_pairs={{0,496},{16,32},{32,16},{48,64},{64,48},{80,96},{96,80},{112,128},... | collective-permute-start | bytes 626696 | tf_op jit(solution)/shard_map/ppermute | solution.py:350
  15.4 5.7 %collective-permute-start.1 = (bf16[816,128]{1,0:T(8,128)(2,1)S(1)}, bf16[816,128]{1,0:T(8,128)(2,1)S(1)}, u32[]{:S(2)}, u32[]{:S(2)}) collective-permute-start(bf16[816,128]{1,0:T(8,128)(2,1)S(1)} %get-tuple-element.23.v_ref.start_ref), channel_id=1, source_target_pairs={{0,16},{16,0},{32,48},{48,32},{64,80},{80,64},{96,112},{112,96},{1... | collective-permute-start | bytes 626696 | tf_op jit(solution)/shard_map/ppermute | solution.py:345
  17.7 6.5 %collective-permute-start.3 = (f32[8,128]{1,0:T(8,128)S(1)}, f32[8,128]{1,0:T(8,128)S(1)}, u32[]{:S(2)}, u32[]{:S(2)}) collective-permute-start(f32[8,128]{1,0:T(8,128)S(1)} %get-tuple-element.26), channel_id=1, source_target_pairs={{0,480},{16,48},{32,0},{48,80},{64,32},{80,112},{96,64},{112,144},... | collective-permute-start | bytes 12296 | tf_op jit(solution)/shard_map/ppermute | solution.py:355
  26.6 3.7 %collective-permute-start.4 = (f32[2,8,128]{2,1,0:T(8,128)S(1)}, f32[2,8,128]{2,1,0:T(8,128)S(1)}, u32[]{:S(2)}, u32[]{:S(2)}) collective-permute-start(f32[2,8,128]{2,1,0:T(8,128)S(1)} %get-tuple-element.30.mate_ref), channel_id=1, source_target_pairs={{0,16},{16,0},{32,48},{48,32},{64,80},{80,64},{96,112},{112,96},{1... | collective-permute-start | bytes 24584 | tf_op jit(solution)/shard_map/ppermute | solution.py:345
  30.4 10.3 %collective-permute-start.6 = (bf16[816,128]{1,0:T(8,128)(2,1)S(1)}, bf16[816,128]{1,0:T(8,128)(2,1)S(1)}, u32[]{:S(2)}, u32[]{:S(2)}) collective-permute-start(bf16[816,128]{1,0:T(8,128)(2,1)S(1)} %get-tuple-element.32.v_ref), channel_id=1, source_target_pairs={{0,496},{16,32},{32,16},{48,64},{64,48},{80,96},{96,80},{112,128},... | collective-permute-start | bytes 626696 | tf_op jit(solution)/shard_map/ppermute | solution.py:350
  32.3 8.3 %collective-permute-start.5 = (bf16[816,128]{1,0:T(8,128)(2,1)S(1)}, bf16[816,128]{1,0:T(8,128)(2,1)S(1)}, u32[]{:S(2)}, u32[]{:S(2)}) collective-permute-start(bf16[816,128]{1,0:T(8,128)(2,1)S(1)} %get-tuple-element.32.v_ref), channel_id=1, source_target_pairs={{0,16},{16,0},{32,48},{48,32},{64,80},{80,64},{96,112},{112,96},{1... | collective-permute-start | bytes 626696 | tf_op jit(solution)/shard_map/ppermute | solution.py:345
  38.7 6.5 %collective-permute-start.7 = (f32[8,128]{1,0:T(8,128)S(1)}, f32[8,128]{1,0:T(8,128)S(1)}, u32[]{:S(2)}, u32[]{:S(2)}) collective-permute-start(f32[8,128]{1,0:T(8,128)S(1)} %get-tuple-element.34), channel_id=1, source_target_pairs={{0,480},{16,48},{32,0},{48,80},{64,32},{80,112},{96,64},{112,144},... | collective-permute-start | bytes 12296 | tf_op jit(solution)/shard_map/ppermute | solution.py:355

commit v6 on v5

--- a/solution.py
+++ b/solution.py
@@ -97,32 +97,42 @@
         tab_ref[t] = total[:, t * z.lanes : (t + 1) * z.lanes]
 
 
-def mate_tiles(side, tab_ref, mate_ref):
+def mate_tiles(side, tab_ref):
     first_core = side == 0
-    mate_ref[0] = jnp.where(first_core, tab_ref[1], tab_ref[0])
-    mate_ref[1] = jnp.where(first_core, tab_ref[2], tab_ref[1])
-
-
-def meet_kernel(z, tab_ref, mate_ref, got_ref, slab_in, slab_ref, chip_ref, far_ref):
-    first_core = (lax.axis_index("dom") & 1) == 0
-    low, high = mate_ref[0] + got_ref[0], mate_ref[1] + got_ref[1]
+    return [
+        jnp.where(first_core, tab_ref[1], tab_ref[0]),
+        jnp.where(first_core, tab_ref[2], tab_ref[1]),
+    ]
+
+
+def put_tiles(z, tiles, slab_ref):
+    for n, piece in enumerate(split3(jnp.concatenate(tiles, 0))):
+        slab_ref[z.tall + n * 2 * z.bands : z.tall + (n + 1) * 2 * z.bands, :] = piece
+
+
+def get_tiles(z, slab_ref):
+    total = None
+    for n in range(3):
+        piece = slab_ref[z.tall + n * 2 * z.bands : z.tall + (n + 1) * 2 * z.bands, :].astype(F32)
+        total = piece if total is None else total + piece
+    return [total[: z.bands], total[z.bands :]]
+
+
+def meet_kernel(z, tab_ref, got_ref, slab_in, slab_ref, chip_ref, far_ref):
+    side = lax.axis_index("dom") & 1
+    first_core = side == 0
+    mate, got = mate_tiles(side, tab_ref), get_tiles(z, got_ref)
+    low, high = mate[0] + got[0], mate[1] + got[1]
     chip_ref[0], chip_ref[1] = low, high
     below, above = tab_ref[0], tab_ref[2]
     far_ref[...] = jnp.where(first_core, below, above)
-    pair = jnp.concatenate(
-        [jnp.where(first_core, below, high), jnp.where(first_core, low, above)], 0
-    )
-    for n, piece in enumerate(split3(pair)):
-        slab_ref[z.tall + n * 2 * z.bands : z.tall + (n + 1) * 2 * z.bands, :] = piece
+    pair = [jnp.where(first_core, below, high), jnp.where(first_core, low, above)]
+    put_tiles(z, pair, slab_ref)
 
 
 def gathered(z, tab_ref, chip_ref, across_ref, far_ref, strength_ref, hots_ref):
     first_core = (lax.axis_index("dom") & 1) == 0
-    got = None
-    for n in range(3):
-        piece = across_ref[z.tall + n * 2 * z.bands : z.tall + (n + 1) * 2 * z.bands, :].astype(F32)
-        got = piece if got is None else got + piece
-    got = [got[: z.bands], got[z.bands :]]
+    got = get_tiles(z, across_ref)
     low, high, far = chip_ref[0], chip_ref[1], far_ref[...]
     tiles = [
         jnp.where(first_core, tab_ref[0] + got[0], low + far),
@@ -148,19 +158,20 @@
 class Projector:
     def __init__(self, z, v_ref, proj_ref):
         self.z, self.v_ref, self.proj_ref = z, v_ref, proj_ref
-        self.even, self.odd = [None] * z.blocks, [None] * z.blocks
+        self.total = [None] * z.blocks
 
     def add(self, pairs):
+        b = self.z.bands
         for pair in pairs:
             j = block_of(self.z, pair)
-            v = self.v_ref[pair_rows(pair), :]
-            e, o = dot_t(v, self.proj_ref[2 * pair]), dot_t(v, self.proj_ref[2 * pair + 1])
-            self.even[j] = e if self.even[j] is None else self.even[j] + e
-            self.odd[j] = o if self.odd[j] is None else self.odd[j] + o
+            v = self.v_ref[pair_rows(pair), :].astype(F32)
+            v = jnp.concatenate([v[:b], v[b:]], 1).astype(BF16)
+            both = jnp.concatenate([self.proj_ref[2 * pair], self.proj_ref[2 * pair + 1]], 1)
+            part = dot_t(v, both)
+            self.total[j] = part if self.total[j] is None else self.total[j] + part
 
     def sums(self):
-        b = self.z.bands
-        return [e[:b] + o[b:] for e, o in zip(self.even, self.odd)]
+        return self.total
 
 
 def turned(z, bands_ref, x):
@@ -179,7 +190,7 @@
     out_ref[...] = jnp.zeros_like(out_ref)
 
 
-def project_kernel(z, pause_ref, ids_ref, bands_ref, proj_ref, tab_ref, mate_ref, v_ref, hots_ref):
+def project_kernel(z, pause_ref, ids_ref, bands_ref, proj_ref, tab_ref, v_ref, hots_ref):
     dom = lax.axis_index("dom")
     turn_all(z, bands_ref, v_ref)
     for j, hot in enumerate(one_hots(z, dom, ids_ref)):
@@ -187,7 +198,7 @@
     projector = Projector(z, v_ref, proj_ref)
     projector.add(range(z.cells // 2))
     scatter(z, projector.sums(), hots_ref, tab_ref)
-    mate_tiles(dom & 1, tab_ref, mate_ref)
+    put_tiles(z, mate_tiles(dom & 1, tab_ref), v_ref)
 
 
 def near_strength(z, dom, strength_ref, out_ref):
@@ -239,16 +250,11 @@
         self.put(pair_rows(pair), value)
 
 
-def places(z, dom):
+def fill_and_base(z, v_ref, on_ref, pot_ref, out_ref, wide_ref):
+    dom = lax.axis_index("dom")
     first_core = (dom & 1) == 0
     on_at = pl.multiple_of(jnp.where(first_core, 2 * z.cells, 0), z.cells)
     off_at = pl.multiple_of(jnp.where(first_core, 0, 2 * z.cells), z.cells)
-    return on_at, off_at
-
-
-def fill_and_base(z, v_ref, on_ref, off_ref, pot_ref, out_ref, wide_ref):
-    dom = lax.axis_index("dom")
-    on_at, off_at = places(z, dom)
     step, b = 8, z.bands
 
     def tile(ref, c):
@@ -257,7 +263,7 @@
     for c in range(0, z.cells, step):
         wide_ref[z.cells + c : z.cells + c + step] = tile(v_ref, c)
         wide_ref[pl.ds(on_at + c, step)] = tile(on_ref, c)
-        wide_ref[pl.ds(off_at + c, step)] = tile(off_ref, c)
+        wide_ref[pl.ds(off_at + c, step)] = jnp.zeros((step, b, z.depth), F32)
 
     def put(rows, value):
         out_ref[rows, :] = value
@@ -265,13 +271,33 @@
     base_body(z, dom, v_ref, wide_ref, Writer(pot_ref, put))
 
 
-def base_first_kernel(z, v_ref, on_ref, off_ref, pot_ref, strength_ref, out_ref, near_ref, wide_ref):
-    fill_and_base(z, v_ref, on_ref, off_ref, pot_ref, out_ref, wide_ref)
+def add_across(z, base_ref, across_ref, acc_ref):
+    side = lax.axis_index("dom") & 1
+    tall = z.rows * z.bands
+    last = z.thickness - 1
+
+    def at(plane, c):
+        there = jnp.where(side == 0, plane, last - plane)
+        return pl.ds(pl.multiple_of(there * tall + c, 32), 32)
+
+    for c in range(0, tall, 32):
+        planes = [across_ref[at(q, c), :].astype(F32) for q in range(z.thickness)]
+        for x in range(z.thickness):
+            total = base_ref[at(x, c), :]
+            for q in range(x, z.thickness):
+                offset = x - q + z.thickness
+                if offset <= REACH:
+                    total = total + WEIGHTS[offset] * planes[q]
+            acc_ref[at(x, c), :] = total
+
+
+def base_first_kernel(z, v_ref, on_ref, pot_ref, strength_ref, out_ref, near_ref, wide_ref):
+    fill_and_base(z, v_ref, on_ref, pot_ref, out_ref, wide_ref)
     near_strength(z, lax.axis_index("dom"), strength_ref, near_ref)
 
 
-def base_kernel(z, v_ref, on_ref, off_ref, pot_ref, out_ref, wide_ref):
-    fill_and_base(z, v_ref, on_ref, off_ref, pot_ref, out_ref, wide_ref)
+def base_kernel(z, v_ref, on_ref, pot_ref, out_ref, wide_ref):
+    fill_and_base(z, v_ref, on_ref, pot_ref, out_ref, wide_ref)
 
 
 def nonlocal_pair(weighted, proj_ref, pair):
@@ -282,26 +308,28 @@
 
 
 def first_kernel(
-    z, base_ref, tab_in, chip_ref, across_ref, far_ref, near_ref, hots_ref, proj_ref, first_ref, tab_ref, mate_ref
+    z, base_ref, tab_in, chip_ref, across_ref, far_ref, near_ref, hots_ref, proj_ref, first_ref, tab_ref, acc_ref
 ):
+    add_across(z, base_ref, across_ref, acc_ref)
     weighted = gathered(z, tab_in, chip_ref, across_ref, far_ref, near_ref, hots_ref)
     for pair in range(z.cells // 2):
         rows = pair_rows(pair)
-        value = base_ref[rows, :] + nonlocal_pair(weighted[block_of(z, pair)], proj_ref, pair)
+        value = acc_ref[rows, :] + nonlocal_pair(weighted[block_of(z, pair)], proj_ref, pair)
         first_ref[rows, :] = (value / half_width).astype(BF16)
     projector = Projector(z, first_ref, proj_ref)
     projector.add(range(z.cells // 2))
     scatter(z, projector.sums(), hots_ref, tab_ref)
-    mate_tiles(lax.axis_index("dom") & 1, tab_ref, mate_ref)
+    put_tiles(z, mate_tiles(lax.axis_index("dom") & 1, tab_ref), first_ref)
 
 
 def filtered_kernel(
-    z, base_ref, tab_ref, chip_ref, across_ref, far_ref, near_ref, hots_ref, proj_ref, start_ref, out_ref
+    z, base_ref, tab_ref, chip_ref, across_ref, far_ref, near_ref, hots_ref, proj_ref, start_ref, out_ref, acc_ref
 ):
+    add_across(z, base_ref, across_ref, acc_ref)
     weighted = gathered(z, tab_ref, chip_ref, across_ref, far_ref, near_ref, hots_ref)
     for pair in range(z.cells // 2):
         rows = pair_rows(pair)
-        value = base_ref[rows, :] + nonlocal_pair(weighted[block_of(z, pair)], proj_ref, pair)
+        value = acc_ref[rows, :] + nonlocal_pair(weighted[block_of(z, pair)], proj_ref, pair)
         out_ref[rows, :] = (2.0 * value / half_width - start_ref[rows, :].astype(F32)).astype(BF16)
 
 
@@ -334,6 +362,7 @@
         self.near = jax.ShapeDtypeStruct((8, z.lanes), F32)
         self.hots = jax.ShapeDtypeStruct((z.blocks, 3 * z.lanes, z.slots), BF16)
         self.wide = [pltpu.VMEM((3 * z.cells, z.bands, z.depth), F32)]
+        self.acc = [pltpu.VMEM((z.tall, z.depth), F32)]
         self.stream = 2 * z.tall * z.slots * z.depth
         self.proj_bytes = 2 * z.cells * z.slots * z.depth
         self.stencil = 6 * z.tall * z.depth * z.depth
@@ -364,38 +393,37 @@
 
     s = Shapes(z)
 
-    def exchange(tab, mate, slab):
-        got = swap_on_chip(mate, "dom")
+    def exchange(tab, slab):
+        on_chip = swap_on_chip(slab, "dom")
         slab, chip, far = call(
-            meet_kernel, z, "meet", [s.message, s.pair, s.tile], (tab, mate, got, slab),
-            1000, 1000, aliases={3: 0},
+            meet_kernel, z, "meet", [s.message, s.pair, s.tile], (tab, on_chip, slab),
+            1000, 1000, aliases={2: 0},
         )
         across = swap_across(slab, "dom")
         far = swap_far(far, "dom")
-        return slab, swap_on_chip(slab, "dom"), across, (tab, chip, across, far)
+        return slab, on_chip, (tab, chip, across, far)
 
     pause = call(pause_kernel, z, "pause", s.tile, (), 4000 * s.stream, 40_000_000)
-    tab, mate, start, hots = call(
-        project_kernel, z, "project", [s.tab, s.pair, s.message, s.hots],
+    tab, start, hots = call(
+        project_kernel, z, "project", [s.tab, s.message, s.hots],
         (pause, atom_ids, flat, proj), s.stream, s.proj_bytes,
     )
-    start, on_chip, across, sums = exchange(tab, mate, start)
+    start, on_chip, sums = exchange(tab, start)
     base, near = call(
         base_first_kernel, z, "base_first", [s.base, s.near],
-        (start, on_chip, across, pot, strength.T), s.stencil, s.slab_bytes, scratch=s.wide,
-    )
-    first, tab, mate = call(
-        first_kernel, z, "first", [s.message, s.tab, s.pair],
-        (base,) + sums + (near, hots, proj), 2 * s.stream, s.proj_bytes,
-    )
-    first, on_chip, across, sums = exchange(tab, mate, first)
+        (start, on_chip, pot, strength.T), s.stencil, s.slab_bytes, scratch=s.wide,
+    )
+    first, tab = call(
+        first_kernel, z, "first", [s.message, s.tab],
+        (base,) + sums + (near, hots, proj), 2 * s.stream, s.proj_bytes, scratch=s.acc,
+    )
+    first, on_chip, sums = exchange(tab, first)
     base = call(
-        base_kernel, z, "base", s.base, (first, on_chip, across, pot),
-        s.stencil, s.slab_bytes, scratch=s.wide,
+        base_kernel, z, "base", s.base, (first, on_chip, pot), s.stencil, s.slab_bytes, scratch=s.wide,
     )
     filtered = call(
         filtered_kernel, z, "filtered", s.slab, (base,) + sums + (near, hots, proj, start),
-        s.stream, s.proj_bytes,
+        s.stream, s.proj_bytes, scratch=s.acc,
     )
 
     share = z.cells // groups

time: 80.7 us -> 72.7 us (0.901)
  the two profiles are of different devices: /device:TPU:1 before, /device:TPU:56 now
where the time goes in v6:
time: 72.7 us; the launch traced here: 72.4 us
  blocking collectives  38.8 us (53%)
  starting transfers between devices  14.3 us (20%)
  waiting for transfers between devices  10.9 us (15%)
  Pallas kernels  5.39 us (7%)
  local copies, waits for them, and re-layouts  2.62 us (4%)
    all_to_all x1, blocking collectives, local(): pieces = lax.all_to_all(pieces, 'band', 0, 0, tiled=True)  24.6 us
    all_to_all x1, blocking collectives, local(): rotated = lax.all_to_all(rotated, 'band', 0, 0, tiled=True)  14.3 us
    ppermute x2, waiting for transfers between devices, swap_far(): lax.ppermute(x, axis, [(i, (i + 2 * (i % 2) * 2 - 2) % count) for i in ra...  8.06 us
    ppermute x2, starting transfers between devices, swap_far(): lax.ppermute(x, axis, [(i, (i + 2 * (i % 2) * 2 - 2) % count) for i in ra...  5.48 us
    pallas_call x8, Pallas kernels, call(): pl.pallas_call(functools.partial(kernel, z), name=name, out_shape=outs, i...  5.39 us
    ppermute x2, starting transfers between devices, swap_across(): lax.ppermute(x, axis, [(i, ((i + 1 ^ 1) - 1) % count) for i in range(coun...  4.92 us
    ppermute x2, starting transfers between devices, swap_on_chip(): return lax.ppermute(x, axis, [(i, i ^ 1) for i in range(count)])  3.86 us
    ppermute x2, waiting for transfers between devices, swap_on_chip(): return lax.ppermute(x, axis, [(i, i ^ 1) for i in range(count)])  2.85 us
  transfers between devices with their start and end apart: 6, of which 4 were waited for; matrix products, arithmetic and copies ran while one was open for 0% of the time, Pallas kernels for 2%

profile of v6, /device:TPU:56, one launch (start us, length us, event | category | flops | bytes accessed | tf_op | source)
XLA Modules:
  0.0 72.4 jit_solution(2481151251062732586)
XLA Ops:
  0.0 0.0 copy-start.3
  0.0 0.0 copy-start.4
  0.1 0.6 copy-done.5
  0.7 1.2 %copy-done.1 = bf16[6,16,32,4,128]{4,3,2,1,0:T(4,128)(2,1)S(1)} copy-done((bf16[6,16,32,4,128]{4,3,2,1,0:T(4,128)(2,1)S(1)}, bf16[6,16,32,4,128]{4,3,2,1,0:T(4,128)(2,1)}, u32[]{:S(2)}) %copy-start.1) | copy-done | bytes 3145752
  1.9 1.2 %project.1 = (f32[3,8,128]{2,1,0:T(8,128)S(1)}, bf16[816,128]{1,0:T(8,128)(2,1)S(1)}, bf16[2,384,128]{2,1,0:T(8,128)(2,1)S(1)}) custom-call(f32[8,128]{1,0:T(8,128)S(1)} %pause.1.pause_ref, s32[2,32]{1,0:T(2,128)S(1)} %copy-done.5, bf16[8,96,128]{2,1,0:T(8,128)(2,1)S(1)} %bitcast.35, bf16[96,128,128]{2,1,0:T(8,128)(2,1)S(1)} %bitcast.31), custom_call_target="tpu_custom_call" | custom-call | flops 25165824 | bytes 3145728 | tf_op jit(solution)/shard_map/project/pallas_call | solution.py:341
  3.1 1.9 %collective-permute-start = (bf16[816,128]{1,0:T(8,128)(2,1)S(1)}, bf16[816,128]{1,0:T(8,128)(2,1)S(1)}, u32[]{:S(2)}, u32[]{:S(2)}) collective-permute-start(bf16[816,128]{1,0:T(8,128)(2,1)S(1)} %get-tuple-element.19.slab_in), channel_id=1, source_target_pairs={{0,16},{16,0},{32,48},{48,32},{64,80},{80,64},{96,112},{112,96},{1... | collective-permute-start | bytes 626696 | tf_op jit(solution)/shard_map/ppermute | solution.py:374
  5.1 1.4 %collective-permute-done.got_ref.on_ref = bf16[816,128]{1,0:T(8,128)(2,1)S(1)} collective-permute-done((bf16[816,128]{1,0:T(8,128)(2,1)S(1)}, bf16[816,128]{1,0:T(8,128)(2,1)S(1)}, u32[]{:S(2)}, u32[]{:S(2)}) %collective-permute-start) | collective-permute-done | bytes 208928 | tf_op jit(solution)/shard_map/ppermute | solution.py:374
  6.5 3.0 %collective-permute-start.1 = (bf16[816,128]{1,0:T(8,128)(2,1)S(1)}, bf16[816,128]{1,0:T(8,128)(2,1)S(1)}, u32[]{:S(2)}, u32[]{:S(2)}) collective-permute-start(bf16[816,128]{1,0:T(8,128)(2,1)S(1)} %get-tuple-element.20.v_ref.start_ref), channel_id=1, source_target_pairs={{0,496},{16,32},{32,16},{48,64},{64,48},{80,96},{96,80},{112,128},... | collective-permute-start | bytes 626696 | tf_op jit(solution)/shard_map/ppermute | solution.py:379
  9.5 3.3 %collective-permute-start.2 = (f32[8,128]{1,0:T(8,128)S(1)}, f32[8,128]{1,0:T(8,128)S(1)}, u32[]{:S(2)}, u32[]{:S(2)}) collective-permute-start(f32[8,128]{1,0:T(8,128)S(1)} %get-tuple-element.23), channel_id=1, source_target_pairs={{0,480},{16,48},{32,0},{48,80},{64,32},{80,112},{96,64},{112,144},... | collective-permute-start | bytes 12296 | tf_op jit(solution)/shard_map/ppermute | solution.py:384
  12.8 0.9 %base_first.1 = (f32[768,128]{1,0:T(8,128)S(1)}, f32[8,128]{1,0:T(8,128)S(1)}) custom-call(bf16[816,128]{1,0:T(8,128)(2,1)S(1)} %get-tuple-element.20.v_ref.start_ref, bf16[816,128]{1,0:T(8,128)(2,1)S(1)} %collective-permute-done.got_ref.on_ref, f32[96,128]{1,0:T(8,128)S(1)} %bitcast.36, f32[4,1024]{1,0:T(4,128)S(1)} %bitcast.38), custom_call_target="tpu_custom_call" | custom-call | flops 75497472 | bytes 983040 | tf_op jit(solution)/shard_map/base_first/pallas_call | solution.py:341
  13.7 3.5 %collective-permute-done.2.far_ref = f32[8,128]{1,0:T(8,128)S(1)} collective-permute-done((f32[8,128]{1,0:T(8,128)S(1)}, f32[8,128]{1,0:T(8,128)S(1)}, u32[]{:S(2)}, u32[]{:S(2)}) %collective-permute-start.2) | collective-permute-done | bytes 4128 | tf_op jit(solution)/shard_map/ppermute | solution.py:384
  17.1 1.8 %first.1 = (bf16[816,128]{1,0:T(8,128)(2,1)S(1)}, f32[3,8,128]{2,1,0:T(8,128)S(1)}) custom-call(f32[768,128]{1,0:T(8,128)S(1)} %get-tuple-element.21.base_ref, f32[3,8,128]{2,1,0:T(8,128)S(1)} %get-tuple-element.18.tab_ref.tab_in, f32[2,8,128]{2,1,0:T(8,128)S(1)} %get-tuple-element.22.chip_ref, bf16[816,128]{1,0:T(8,128)(2,1)S(1)} %collective-permute-done.1.across_ref, ...), custom_call_target="tpu_custom_call" | custom-call | flops 50331648 | bytes 3145728 | tf_op jit(solution)/shard_map/first/pallas_call | solution.py:341
  18.9 1.9 %collective-permute-start.3 = (bf16[816,128]{1,0:T(8,128)(2,1)S(1)}, bf16[816,128]{1,0:T(8,128)(2,1)S(1)}, u32[]{:S(2)}, u32[]{:S(2)}) collective-permute-start(bf16[816,128]{1,0:T(8,128)(2,1)S(1)} %get-tuple-element.27.slab_in), channel_id=1, source_target_pairs={{0,16},{16,0},{32,48},{48,32},{64,80},{80,64},{96,112},{112,96},{1... | collective-permute-start | bytes 626696 | tf_op jit(solution)/shard_map/ppermute | solution.py:374
  20.8 1.4 %collective-permute-done.3.got_ref.on_ref = bf16[816,128]{1,0:T(8,128)(2,1)S(1)} collective-permute-done((bf16[816,128]{1,0:T(8,128)(2,1)S(1)}, bf16[816,128]{1,0:T(8,128)(2,1)S(1)}, u32[]{:S(2)}, u32[]{:S(2)}) %collective-permute-start.3) | collective-permute-done | bytes 208928 | tf_op jit(solution)/shard_map/ppermute | solution.py:374
  22.3 1.9 %collective-permute-start.4 = (bf16[816,128]{1,0:T(8,128)(2,1)S(1)}, bf16[816,128]{1,0:T(8,128)(2,1)S(1)}, u32[]{:S(2)}, u32[]{:S(2)}) collective-permute-start(bf16[816,128]{1,0:T(8,128)(2,1)S(1)} %get-tuple-element.28.v_ref), channel_id=1, source_target_pairs={{0,496},{16,32},{32,16},{48,64},{64,48},{80,96},{96,80},{112,128},... | collective-permute-start | bytes 626696 | tf_op jit(solution)/shard_map/ppermute | solution.py:379
  24.2 2.2 %collective-permute-start.5 = (f32[8,128]{1,0:T(8,128)S(1)}, f32[8,128]{1,0:T(8,128)S(1)}, u32[]{:S(2)}, u32[]{:S(2)}) collective-permute-start(f32[8,128]{1,0:T(8,128)S(1)} %get-tuple-element.30), channel_id=1, source_target_pairs={{0,480},{16,48},{32,0},{48,80},{64,32},{80,112},{96,64},{112,144},... | collective-permute-start | bytes 12296 | tf_op jit(solution)/shard_map/ppermute | solution.py:384
  26.4 0.8 %base.1.base_ref = f32[768,128]{1,0:T(8,128)S(1)} custom-call(bf16[816,128]{1,0:T(8,128)(2,1)S(1)} %get-tuple-element.28.v_ref, bf16[816,128]{1,0:T(8,128)(2,1)S(1)} %collective-permute-done.3.got_ref.on_ref, f32[96,128]{1,0:T(8,128)S(1)} %bitcast.37), custom_call_target="tpu_custom_call" | custom-call | flops 75497472 | bytes 983040 | tf_op jit(solution)/shard_map/base/pallas_call | solution.py:341
  27.3 4.6 %collective-permute-done.5.far_ref = f32[8,128]{1,0:T(8,128)S(1)} collective-permute-done((f32[8,128]{1,0:T(8,128)S(1)}, f32[8,128]{1,0:T(8,128)S(1)}, u32[]{:S(2)}, u32[]{:S(2)}) %collective-permute-start.5) | collective-permute-done | bytes 4128 | tf_op jit(solution)/shard_map/ppermute | solution.py:384
  31.9 0.0 collective-permute-done.4.across_ref
  31.9 0.7 filtered.1
  32.6 24.6 %all_to_all.10 = bf16[16,6,8,128]{3,2,1,0:T(8,128)(2,1)S(1)} all-to-all(bf16[16,6,8,128]{3,2,1,0:T(8,128)(2,1)S(1)} %bitcast.34), channel_id=1, replica_groups=mesh['dom'=32,'band'=16] {'band'}, dimensions={0} | all-to-all | bytes 393216 | tf_op jit(solution)/shard_map/all_to_all | solution.py:431
  57.1 0.3 fusion.1
  57.4 14.3 %all_to_all.11 = bf16[16,6,8,128]{3,2,1,0:T(8,128)(2,1)S(1)} all-to-all(bf16[16,6,8,128]{3,2,1,0:T(8,128)(2,1)S(1)} %bitcast.39), channel_id=1, replica_groups=mesh['dom'=32,'band'=16] {'band'}, dimensions={0} | all-to-all | bytes 393216 | tf_op jit(solution)/shard_map/all_to_all | solution.py:435
  71.7 0.7 copy.18
  (13 shorter events, 0.1 us)
Async XLA Ops:
  0.0 57.1 %copy-start = (bf16[128,128]{1,0:T(8,128)(2,1)S(1)}, bf16[128,128]{1,0:T(8,128)(2,1)}, u32[]{:S(2)}) copy-start(bf16[128,128]{1,0:T(8,128)(2,1)} %param.11) | copy-start | bytes 98308
  0.0 0.7 copy-start.5
  0.0 1.9 %copy-start.1 = (bf16[6,16,32,4,128]{4,3,2,1,0:T(4,128)(2,1)S(1)}, bf16[6,16,32,4,128]{4,3,2,1,0:T(4,128)(2,1)}, u32[]{:S(2)}) copy-start(bf16[6,16,32,4,128]{4,3,2,1,0:T(4,128)(2,1)} %param.8) | copy-start | bytes 9437188
  0.0 1.9 %copy-start.2 = (bf16[8,6,16,128]{3,2,1,0:T(8,128)(2,1)S(1)}, bf16[8,6,16,128]{3,2,1,0:T(8,128)(2,1)}, u32[]{:S(2)}) copy-start(bf16[8,6,16,128]{3,2,1,0:T(8,128)(2,1)} %param.6) | copy-start | bytes 589828
  0.0 12.8 %copy-start.3 = (f32[6,16,128]{2,1,0:T(8,128)S(1)}, f32[6,16,128]{2,1,0:T(8,128)}, u32[]{:S(2)}) copy-start(f32[6,16,128]{2,1,0:T(8,128)} %param.7) | copy-start | bytes 147460
  0.0 12.8 %copy-start.4 = (f32[1024,4]{0,1:T(4,128)S(1)}, f32[1024,4]{0,1:T(4,128)}, u32[]{:S(2)}) copy-start(f32[1024,4]{0,1:T(4,128)} %param.10) | copy-start | bytes 49156
  3.1 3.4 %collective-permute-start = (bf16[816,128]{1,0:T(8,128)(2,1)S(1)}, bf16[816,128]{1,0:T(8,128)(2,1)S(1)}, u32[]{:S(2)}, u32[]{:S(2)}) collective-permute-start(bf16[816,128]{1,0:T(8,128)(2,1)S(1)} %get-tuple-element.19.slab_in), channel_id=1, source_target_pairs={{0,16},{16,0},{32,48},{48,32},{64,80},{80,64},{96,112},{112,96},{1... | collective-permute-start | bytes 626696 | tf_op jit(solution)/shard_map/ppermute | solution.py:374
  6.5 10.6 %collective-permute-start.1 = (bf16[816,128]{1,0:T(8,128)(2,1)S(1)}, bf16[816,128]{1,0:T(8,128)(2,1)S(1)}, u32[]{:S(2)}, u32[]{:S(2)}) collective-permute-start(bf16[816,128]{1,0:T(8,128)(2,1)S(1)} %get-tuple-element.20.v_ref.start_ref), channel_id=1, source_target_pairs={{0,496},{16,32},{32,16},{48,64},{64,48},{80,96},{96,80},{112,128},... | collective-permute-start | bytes 626696 | tf_op jit(solution)/shard_map/ppermute | solution.py:379
  9.5 7.6 %collective-permute-start.2 = (f32[8,128]{1,0:T(8,128)S(1)}, f32[8,128]{1,0:T(8,128)S(1)}, u32[]{:S(2)}, u32[]{:S(2)}) collective-permute-start(f32[8,128]{1,0:T(8,128)S(1)} %get-tuple-element.23), channel_id=1, source_target_pairs={{0,480},{16,48},{32,0},{48,80},{64,32},{80,112},{96,64},{112,144},... | collective-permute-start | bytes 12296 | tf_op jit(solution)/shard_map/ppermute | solution.py:384
  18.9 3.4 %collective-permute-start.3 = (bf16[816,128]{1,0:T(8,128)(2,1)S(1)}, bf16[816,128]{1,0:T(8,128)(2,1)S(1)}, u32[]{:S(2)}, u32[]{:S(2)}) collective-permute-start(bf16[816,128]{1,0:T(8,128)(2,1)S(1)} %get-tuple-element.27.slab_in), channel_id=1, source_target_pairs={{0,16},{16,0},{32,48},{48,32},{64,80},{80,64},{96,112},{112,96},{1... | collective-permute-start | bytes 626696 | tf_op jit(solution)/shard_map/ppermute | solution.py:374
  22.3 9.6 %collective-permute-start.4 = (bf16[816,128]{1,0:T(8,128)(2,1)S(1)}, bf16[816,128]{1,0:T(8,128)(2,1)S(1)}, u32[]{:S(2)}, u32[]{:S(2)}) collective-permute-start(bf16[816,128]{1,0:T(8,128)(2,1)S(1)} %get-tuple-element.28.v_ref), channel_id=1, source_target_pairs={{0,496},{16,32},{32,16},{48,64},{64,48},{80,96},{96,80},{112,128},... | collective-permute-start | bytes 626696 | tf_op jit(solution)/shard_map/ppermute | solution.py:379
  24.2 7.7 %collective-permute-start.5 = (f32[8,128]{1,0:T(8,128)S(1)}, f32[8,128]{1,0:T(8,128)S(1)}, u32[]{:S(2)}, u32[]{:S(2)}) collective-permute-start(f32[8,128]{1,0:T(8,128)S(1)} %get-tuple-element.30), channel_id=1, source_target_pairs={{0,480},{16,48},{32,0},{48,80},{64,32},{80,112},{96,64},{112,144},... | collective-permute-start | bytes 12296 | tf_op jit(solution)/shard_map/ppermute | solution.py:384

commit v7 on v6

--- a/solution.py
+++ b/solution.py
@@ -105,6 +105,10 @@
     ]
 
 
+def far_tile(side, tab_ref):
+    return jnp.where(side == 0, tab_ref[0], tab_ref[2])
+
+
 def put_tiles(z, tiles, slab_ref):
     for n, piece in enumerate(split3(jnp.concatenate(tiles, 0))):
         slab_ref[z.tall + n * 2 * z.bands : z.tall + (n + 1) * 2 * z.bands, :] = piece
@@ -118,14 +122,14 @@
     return [total[: z.bands], total[z.bands :]]
 
 
-def meet_kernel(z, tab_ref, got_ref, slab_in, slab_ref, chip_ref, far_ref):
+def meet_kernel(z, tab_ref, got_ref, slab_in, slab_ref, chip_ref):
+    slab_ref[: z.tall, :] = slab_in[: z.tall, :]
     side = lax.axis_index("dom") & 1
     first_core = side == 0
     mate, got = mate_tiles(side, tab_ref), get_tiles(z, got_ref)
     low, high = mate[0] + got[0], mate[1] + got[1]
     chip_ref[0], chip_ref[1] = low, high
     below, above = tab_ref[0], tab_ref[2]
-    far_ref[...] = jnp.where(first_core, below, above)
     pair = [jnp.where(first_core, below, high), jnp.where(first_core, low, above)]
     put_tiles(z, pair, slab_ref)
 
@@ -190,7 +194,7 @@
     out_ref[...] = jnp.zeros_like(out_ref)
 
 
-def project_kernel(z, pause_ref, ids_ref, bands_ref, proj_ref, tab_ref, v_ref, hots_ref):
+def project_kernel(z, pause_ref, ids_ref, bands_ref, proj_ref, tab_ref, far_out, v_ref, hots_ref):
     dom = lax.axis_index("dom")
     turn_all(z, bands_ref, v_ref)
     for j, hot in enumerate(one_hots(z, dom, ids_ref)):
@@ -198,6 +202,7 @@
     projector = Projector(z, v_ref, proj_ref)
     projector.add(range(z.cells // 2))
     scatter(z, projector.sums(), hots_ref, tab_ref)
+    far_out[...] = far_tile(dom & 1, tab_ref)
     put_tiles(z, mate_tiles(dom & 1, tab_ref), v_ref)
 
 
@@ -308,7 +313,7 @@
 
 
 def first_kernel(
-    z, base_ref, tab_in, chip_ref, across_ref, far_ref, near_ref, hots_ref, proj_ref, first_ref, tab_ref, acc_ref
+    z, base_ref, tab_in, chip_ref, across_ref, far_ref, near_ref, hots_ref, proj_ref, first_ref, tab_ref, far_out, acc_ref
 ):
     add_across(z, base_ref, across_ref, acc_ref)
     weighted = gathered(z, tab_in, chip_ref, across_ref, far_ref, near_ref, hots_ref)
@@ -319,7 +324,9 @@
     projector = Projector(z, first_ref, proj_ref)
     projector.add(range(z.cells // 2))
     scatter(z, projector.sums(), hots_ref, tab_ref)
-    put_tiles(z, mate_tiles(lax.axis_index("dom") & 1, tab_ref), first_ref)
+    side = lax.axis_index("dom") & 1
+    far_out[...] = far_tile(side, tab_ref)
+    put_tiles(z, mate_tiles(side, tab_ref), first_ref)
 
 
 def filtered_kernel(
@@ -336,7 +343,7 @@
 VMEM = pl.BlockSpec(memory_space=pltpu.VMEM)
 
 
-def call(kernel, z, name, outs, ins, flops, moved, scratch=(), aliases=None):
+def call(kernel, z, name, outs, ins, flops, moved, scratch=()):
     single = not isinstance(outs, (list, tuple))
     return pl.pallas_call(
         functools.partial(kernel, z),
@@ -345,7 +352,6 @@
         in_specs=[VMEM] * len(ins),
         out_specs=VMEM if single else [VMEM] * len(outs),
         scratch_shapes=list(scratch),
-        input_output_aliases=aliases or {},
         compiler_params=pltpu.CompilerParams(vmem_limit_bytes=12288 * 1024),
         cost_estimate=pl.CostEstimate(flops=flops, bytes_accessed=moved, transcendentals=0),
     )(*ins)
@@ -393,33 +399,32 @@
 
     s = Shapes(z)
 
-    def exchange(tab, slab):
+    def exchange(tab, far, slab):
         on_chip = swap_on_chip(slab, "dom")
-        slab, chip, far = call(
-            meet_kernel, z, "meet", [s.message, s.pair, s.tile], (tab, on_chip, slab),
-            1000, 1000, aliases={2: 0},
+        far = swap_far(far, "dom")
+        slab, chip = call(
+            meet_kernel, z, "meet", [s.message, s.pair], (tab, on_chip, slab), 1000, 1000
         )
         across = swap_across(slab, "dom")
-        far = swap_far(far, "dom")
         return slab, on_chip, (tab, chip, across, far)
 
     pause = call(pause_kernel, z, "pause", s.tile, (), 4000 * s.stream, 40_000_000)
-    tab, start, hots = call(
-        project_kernel, z, "project", [s.tab, s.message, s.hots],
+    tab, far, start, hots = call(
+        project_kernel, z, "project", [s.tab, s.tile, s.message, s.hots],
         (pause, atom_ids, flat, proj), s.stream, s.proj_bytes,
     )
-    start, on_chip, sums = exchange(tab, start)
+    start, on_chip, sums = exchange(tab, far, start)
     base, near = call(
         base_first_kernel, z, "base_first", [s.base, s.near],
-        (start, on_chip, pot, strength.T), s.stencil, s.slab_bytes, scratch=s.wide,
-    )
-    first, tab = call(
-        first_kernel, z, "first", [s.message, s.tab],
+        (start, on_chip, pot, strength.T), 60 * s.stencil, s.slab_bytes, scratch=s.wide,
+    )
+    first, tab, far = call(
+        first_kernel, z, "first", [s.message, s.tab, s.tile],
         (base,) + sums + (near, hots, proj), 2 * s.stream, s.proj_bytes, scratch=s.acc,
     )
-    first, on_chip, sums = exchange(tab, first)
+    first, on_chip, sums = exchange(tab, far, first)
     base = call(
-        base_kernel, z, "base", s.base, (first, on_chip, pot), s.stencil, s.slab_bytes, scratch=s.wide,
+        base_kernel, z, "base", s.base, (first, on_chip, pot), 60 * s.stencil, s.slab_bytes, scratch=s.wide,
     )
     filtered = call(
         filtered_kernel, z, "filtered", s.slab, (base,) + sums + (near, hots, proj, start),

time: 72.7 us -> 74.7 us (1.028)
  the two profiles are of different devices: /device:TPU:56 before, /device:TPU:2 now
where the time goes in v7:
time: 74.7 us; the launch traced here: 74.4 us
  blocking collectives  35.7 us (48%)
  starting transfers between devices  20.8 us (28%)
  waiting for transfers between devices  9.33 us (12%)
  Pallas kernels  5.41 us (7%)
  local copies, waits for them, and re-layouts  2.62 us (4%)
    all_to_all x1, blocking collectives, local(): pieces = lax.all_to_all(pieces, 'band', 0, 0, tiled=True)  21.4 us
    all_to_all x1, blocking collectives, local(): rotated = lax.all_to_all(rotated, 'band', 0, 0, tiled=True)  14.4 us
    ppermute x2, starting transfers between devices, swap_far(): lax.ppermute(x, axis, [(i, (i + 2 * (i % 2) * 2 - 2) % count) for i in ra...  9.59 us
    ppermute x2, waiting for transfers between devices, swap_across(): lax.ppermute(x, axis, [(i, ((i + 1 ^ 1) - 1) % count) for i in range(coun...  9.32 us
    ppermute x2, starting transfers between devices, swap_across(): lax.ppermute(x, axis, [(i, ((i + 1 ^ 1) - 1) % count) for i in range(coun...  7.39 us
    pallas_call x8, Pallas kernels, call(): pl.pallas_call(functools.partial(kernel, z), name=name, out_shape=outs, i...  5.41 us
    ppermute x2, starting transfers between devices, swap_on_chip(): return lax.ppermute(x, axis, [(i, i ^ 1) for i in range(count)])  3.86 us
    unnamed x12, local copies, waits for them, and re-layouts  1.88 us
  transfers between devices with their start and end apart: 6, of which 2 were waited for; matrix products, arithmetic and copies ran while one was open for 0% of the time, Pallas kernels for 2%

profile of v7, /device:TPU:2, one launch (start us, length us, event | category | flops | bytes accessed | tf_op | source)
XLA Modules:
  0.0 74.4 jit_solution(34867816896026287)
XLA Ops:
  0.0 0.0 copy-start.4
  0.0 0.0 copy-start.5
  0.1 0.6 copy-done.3
  0.7 1.2 %copy-done.1 = bf16[6,16,32,4,128]{4,3,2,1,0:T(4,128)(2,1)S(1)} copy-done((bf16[6,16,32,4,128]{4,3,2,1,0:T(4,128)(2,1)S(1)}, bf16[6,16,32,4,128]{4,3,2,1,0:T(4,128)(2,1)}, u32[]{:S(2)}) %copy-start.1) | copy-done | bytes 3145752
  1.9 1.2 %project.1 = (f32[3,8,128]{2,1,0:T(8,128)S(1)}, f32[8,128]{1,0:T(8,128)S(1)}, bf16[816,128]{1,0:T(8,128)(2,1)S(1)}, bf16[2,384,128]{2,1,0:T(8,128)(2,1)S(1)}) custom-call(f32[8,128]{1,0:T(8,128)S(1)} %pause.1.pause_ref, s32[2,32]{1,0:T(2,128)S(1)} %copy-done.3, bf16[8,96,128]{2,1,0:T(8,128)(2,1)S(1)} %bitcast.35, bf16[96,128,128]{2,1,0:T(8,128)(2,1)S(1)} %bitcast.31), custom_call_target="tpu_custom_call" | custom-call | flops 25165824 | bytes 3145728 | tf_op jit(solution)/shard_map/project/pallas_call | solution.py:348
  3.1 1.9 %collective-permute-start = (bf16[816,128]{1,0:T(8,128)(2,1)S(1)}, bf16[816,128]{1,0:T(8,128)(2,1)S(1)}, u32[]{:S(2)}, u32[]{:S(2)}) collective-permute-start(bf16[816,128]{1,0:T(8,128)(2,1)S(1)} %get-tuple-element.19.slab_in), channel_id=1, source_target_pairs={{0,16},{16,0},{32,48},{48,32},{64,80},{80,64},{96,112},{112,96},{1... | collective-permute-start | bytes 626696 | tf_op jit(solution)/shard_map/ppermute | solution.py:380
  5.1 7.2 %collective-permute-start.2 = (f32[8,128]{1,0:T(8,128)S(1)}, f32[8,128]{1,0:T(8,128)S(1)}, u32[]{:S(2)}, u32[]{:S(2)}) collective-permute-start(f32[8,128]{1,0:T(8,128)S(1)} %get-tuple-element.23), channel_id=1, source_target_pairs={{0,480},{16,48},{32,0},{48,80},{64,32},{80,112},{96,64},{112,144},... | collective-permute-start | bytes 12296 | tf_op jit(solution)/shard_map/ppermute | solution.py:390
  12.3 0.0 collective-permute-done.got_ref.on_ref
  12.3 2.0 %collective-permute-start.1 = (bf16[816,128]{1,0:T(8,128)(2,1)S(1)}, bf16[816,128]{1,0:T(8,128)(2,1)S(1)}, u32[]{:S(2)}, u32[]{:S(2)}) collective-permute-start(bf16[816,128]{1,0:T(8,128)(2,1)S(1)} %get-tuple-element.20.v_ref.start_ref), channel_id=1, source_target_pairs={{0,496},{16,32},{32,16},{48,64},{64,48},{80,96},{96,80},{112,128},... | collective-permute-start | bytes 626696 | tf_op jit(solution)/shard_map/ppermute | solution.py:385
  14.4 0.9 %base_first.1 = (f32[768,128]{1,0:T(8,128)S(1)}, f32[8,128]{1,0:T(8,128)S(1)}) custom-call(bf16[816,128]{1,0:T(8,128)(2,1)S(1)} %get-tuple-element.20.v_ref.start_ref, bf16[816,128]{1,0:T(8,128)(2,1)S(1)} %collective-permute-done.got_ref.on_ref, f32[96,128]{1,0:T(8,128)S(1)} %bitcast.36, f32[4,1024]{1,0:T(4,128)S(1)} %bitcast.38), custom_call_target="tpu_custom_call" | custom-call | flops 4529848320 | bytes 983040 | tf_op jit(solution)/shard_map/base_first/pallas_call | solution.py:348
  15.2 0.0 collective-permute-done.2.far_ref
  15.2 6.3 %collective-permute-done.1.across_ref = bf16[816,128]{1,0:T(8,128)(2,1)S(1)} collective-permute-done((bf16[816,128]{1,0:T(8,128)(2,1)S(1)}, bf16[816,128]{1,0:T(8,128)(2,1)S(1)}, u32[]{:S(2)}, u32[]{:S(2)}) %collective-permute-start.1) | collective-permute-done | bytes 208928 | tf_op jit(solution)/shard_map/ppermute | solution.py:385
  21.5 1.8 %first.1 = (bf16[816,128]{1,0:T(8,128)(2,1)S(1)}, f32[3,8,128]{2,1,0:T(8,128)S(1)}, f32[8,128]{1,0:T(8,128)S(1)}) custom-call(f32[768,128]{1,0:T(8,128)S(1)} %get-tuple-element.21.base_ref, f32[3,8,128]{2,1,0:T(8,128)S(1)} %get-tuple-element.18.tab_ref.tab_in, f32[2,8,128]{2,1,0:T(8,128)S(1)} %get-tuple-element.22.chip_ref, ...), custom_call_target="tpu_custom_call" | custom-call | flops 50331648 | bytes 3145728 | tf_op jit(solution)/shard_map/first/pallas_call | solution.py:348
  23.3 1.9 %collective-permute-start.3 = (bf16[816,128]{1,0:T(8,128)(2,1)S(1)}, bf16[816,128]{1,0:T(8,128)(2,1)S(1)}, u32[]{:S(2)}, u32[]{:S(2)}) collective-permute-start(bf16[816,128]{1,0:T(8,128)(2,1)S(1)} %get-tuple-element.27.slab_in), channel_id=1, source_target_pairs={{0,16},{16,0},{32,48},{48,32},{64,80},{80,64},{96,112},{112,96},{1... | collective-permute-start | bytes 626696 | tf_op jit(solution)/shard_map/ppermute | solution.py:380
  25.2 2.4 %collective-permute-start.5 = (f32[8,128]{1,0:T(8,128)S(1)}, f32[8,128]{1,0:T(8,128)S(1)}, u32[]{:S(2)}, u32[]{:S(2)}) collective-permute-start(f32[8,128]{1,0:T(8,128)S(1)} %get-tuple-element.30), channel_id=1, source_target_pairs={{0,480},{16,48},{32,0},{48,80},{64,32},{80,112},{96,64},{112,144},... | collective-permute-start | bytes 12296 | tf_op jit(solution)/shard_map/ppermute | solution.py:390
  27.7 5.4 %collective-permute-start.4 = (bf16[816,128]{1,0:T(8,128)(2,1)S(1)}, bf16[816,128]{1,0:T(8,128)(2,1)S(1)}, u32[]{:S(2)}, u32[]{:S(2)}) collective-permute-start(bf16[816,128]{1,0:T(8,128)(2,1)S(1)} %get-tuple-element.28.v_ref), channel_id=1, source_target_pairs={{0,496},{16,32},{32,16},{48,64},{64,48},{80,96},{96,80},{112,128},... | collective-permute-start | bytes 626696 | tf_op jit(solution)/shard_map/ppermute | solution.py:385
  33.1 0.8 %base.1.base_ref = f32[768,128]{1,0:T(8,128)S(1)} custom-call(bf16[816,128]{1,0:T(8,128)(2,1)S(1)} %get-tuple-element.28.v_ref, bf16[816,128]{1,0:T(8,128)(2,1)S(1)} %collective-permute-done.3.got_ref.on_ref, f32[96,128]{1,0:T(8,128)S(1)} %bitcast.37), custom_call_target="tpu_custom_call" | custom-call | flops 4529848320 | bytes 983040 | tf_op jit(solution)/shard_map/base/pallas_call | solution.py:348
  33.9 0.0 collective-permute-done.5.far_ref
  33.9 3.0 %collective-permute-done.4.across_ref = bf16[816,128]{1,0:T(8,128)(2,1)S(1)} collective-permute-done((bf16[816,128]{1,0:T(8,128)(2,1)S(1)}, bf16[816,128]{1,0:T(8,128)(2,1)S(1)}, u32[]{:S(2)}, u32[]{:S(2)}) %collective-permute-start.4) | collective-permute-done | bytes 208928 | tf_op jit(solution)/shard_map/ppermute | solution.py:385
  36.9 0.7 filtered.1
  37.6 21.4 %all_to_all.10 = bf16[16,6,8,128]{3,2,1,0:T(8,128)(2,1)S(1)} all-to-all(bf16[16,6,8,128]{3,2,1,0:T(8,128)(2,1)S(1)} %bitcast.34), channel_id=1, replica_groups=mesh['dom'=32,'band'=16] {'band'}, dimensions={0} | all-to-all | bytes 393216 | tf_op jit(solution)/shard_map/all_to_all | solution.py:436
  59.0 0.3 fusion.1
  59.3 14.4 %all_to_all.11 = bf16[16,6,8,128]{3,2,1,0:T(8,128)(2,1)S(1)} all-to-all(bf16[16,6,8,128]{3,2,1,0:T(8,128)(2,1)S(1)} %bitcast.39), channel_id=1, replica_groups=mesh['dom'=32,'band'=16] {'band'}, dimensions={0} | all-to-all | bytes 393216 | tf_op jit(solution)/shard_map/all_to_all | solution.py:440
  73.7 0.7 copy.16
  (13 shorter events, 0.1 us)
Async XLA Ops:
  0.0 59.0 %copy-start = (bf16[128,128]{1,0:T(8,128)(2,1)S(1)}, bf16[128,128]{1,0:T(8,128)(2,1)}, u32[]{:S(2)}) copy-start(bf16[128,128]{1,0:T(8,128)(2,1)} %param.11) | copy-start | bytes 98308
  0.0 0.7 copy-start.3
  0.0 1.9 %copy-start.1 = (bf16[6,16,32,4,128]{4,3,2,1,0:T(4,128)(2,1)S(1)}, bf16[6,16,32,4,128]{4,3,2,1,0:T(4,128)(2,1)}, u32[]{:S(2)}) copy-start(bf16[6,16,32,4,128]{4,3,2,1,0:T(4,128)(2,1)} %param.8) | copy-start | bytes 9437188
  0.0 1.9 %copy-start.2 = (bf16[8,6,16,128]{3,2,1,0:T(8,128)(2,1)S(1)}, bf16[8,6,16,128]{3,2,1,0:T(8,128)(2,1)}, u32[]{:S(2)}) copy-start(bf16[8,6,16,128]{3,2,1,0:T(8,128)(2,1)} %param.6) | copy-start | bytes 589828
  0.0 14.3 %copy-start.4 = (f32[6,16,128]{2,1,0:T(8,128)S(1)}, f32[6,16,128]{2,1,0:T(8,128)}, u32[]{:S(2)}) copy-start(f32[6,16,128]{2,1,0:T(8,128)} %param.7) | copy-start | bytes 147460
  0.0 14.3 %copy-start.5 = (f32[1024,4]{0,1:T(4,128)S(1)}, f32[1024,4]{0,1:T(4,128)}, u32[]{:S(2)}) copy-start(f32[1024,4]{0,1:T(4,128)} %param.10) | copy-start | bytes 49156
  3.1 9.1 %collective-permute-start = (bf16[816,128]{1,0:T(8,128)(2,1)S(1)}, bf16[816,128]{1,0:T(8,128)(2,1)S(1)}, u32[]{:S(2)}, u32[]{:S(2)}) collective-permute-start(bf16[816,128]{1,0:T(8,128)(2,1)S(1)} %get-tuple-element.19.slab_in), channel_id=1, source_target_pairs={{0,16},{16,0},{32,48},{48,32},{64,80},{80,64},{96,112},{112,96},{1... | collective-permute-start | bytes 626696 | tf_op jit(solution)/shard_map/ppermute | solution.py:380
  5.1 10.1 %collective-permute-start.2 = (f32[8,128]{1,0:T(8,128)S(1)}, f32[8,128]{1,0:T(8,128)S(1)}, u32[]{:S(2)}, u32[]{:S(2)}) collective-permute-start(f32[8,128]{1,0:T(8,128)S(1)} %get-tuple-element.23), channel_id=1, source_target_pairs={{0,480},{16,48},{32,0},{48,80},{64,32},{80,112},{96,64},{112,144},... | collective-permute-start | bytes 12296 | tf_op jit(solution)/shard_map/ppermute | solution.py:390
  12.3 9.2 %collective-permute-start.1 = (bf16[816,128]{1,0:T(8,128)(2,1)S(1)}, bf16[816,128]{1,0:T(8,128)(2,1)S(1)}, u32[]{:S(2)}, u32[]{:S(2)}) collective-permute-start(bf16[816,128]{1,0:T(8,128)(2,1)S(1)} %get-tuple-element.20.v_ref.start_ref), channel_id=1, source_target_pairs={{0,496},{16,32},{32,16},{48,64},{64,48},{80,96},{96,80},{112,128},... | collective-permute-start | bytes 626696 | tf_op jit(solution)/shard_map/ppermute | solution.py:385
  23.3 4.4 %collective-permute-start.3 = (bf16[816,128]{1,0:T(8,128)(2,1)S(1)}, bf16[816,128]{1,0:T(8,128)(2,1)S(1)}, u32[]{:S(2)}, u32[]{:S(2)}) collective-permute-start(bf16[816,128]{1,0:T(8,128)(2,1)S(1)} %get-tuple-element.27.slab_in), channel_id=1, source_target_pairs={{0,16},{16,0},{32,48},{48,32},{64,80},{80,64},{96,112},{112,96},{1... | collective-permute-start | bytes 626696 | tf_op jit(solution)/shard_map/ppermute | solution.py:380
  25.2 8.7 %collective-permute-start.5 = (f32[8,128]{1,0:T(8,128)S(1)}, f32[8,128]{1,0:T(8,128)S(1)}, u32[]{:S(2)}, u32[]{:S(2)}) collective-permute-start(f32[8,128]{1,0:T(8,128)S(1)} %get-tuple-element.30), channel_id=1, source_target_pairs={{0,480},{16,48},{32,0},{48,80},{64,32},{80,112},{96,64},{112,144},... | collective-permute-start | bytes 12296 | tf_op jit(solution)/shard_map/ppermute | solution.py:390
  27.7 9.2 %collective-permute-start.4 = (bf16[816,128]{1,0:T(8,128)(2,1)S(1)}, bf16[816,128]{1,0:T(8,128)(2,1)S(1)}, u32[]{:S(2)}, u32[]{:S(2)}) collective-permute-start(bf16[816,128]{1,0:T(8,128)(2,1)S(1)} %get-tuple-element.28.v_ref), channel_id=1, source_target_pairs={{0,496},{16,32},{32,16},{48,64},{64,48},{80,96},{96,80},{112,128},... | collective-permute-start | bytes 626696 | tf_op jit(solution)/shard_map/ppermute | solution.py:385

commit v8 on v6

--- a/solution.py
+++ b/solution.py
@@ -105,6 +105,14 @@
     ]
 
 
+def put_mate(z, tab_ref, slab_ref):
+    side = lax.axis_index("dom") & 1
+    put_tiles(z, mate_tiles(side, tab_ref), slab_ref)
+    outer = jnp.where(side == 0, tab_ref[0], tab_ref[2])
+    pieces = list(split3(outer)) + [jnp.zeros(outer.shape, BF16)]
+    slab_ref[z.tall + 6 * z.bands :, :] = jnp.concatenate([p.astype(F32) for p in pieces], 0).astype(BF16)
+
+
 def put_tiles(z, tiles, slab_ref):
     for n, piece in enumerate(split3(jnp.concatenate(tiles, 0))):
         slab_ref[z.tall + n * 2 * z.bands : z.tall + (n + 1) * 2 * z.bands, :] = piece
@@ -119,13 +127,15 @@
 
 
 def meet_kernel(z, tab_ref, got_ref, slab_in, slab_ref, chip_ref, far_ref):
+    slab_ref[: z.tall, :] = slab_in[: z.tall, :]
     side = lax.axis_index("dom") & 1
     first_core = side == 0
     mate, got = mate_tiles(side, tab_ref), get_tiles(z, got_ref)
     low, high = mate[0] + got[0], mate[1] + got[1]
     chip_ref[0], chip_ref[1] = low, high
+    outer = got_ref[z.tall + 6 * z.bands :, :].astype(F32)
+    far_ref[...] = outer[: z.bands] + outer[z.bands : 2 * z.bands] + outer[2 * z.bands : 3 * z.bands]
     below, above = tab_ref[0], tab_ref[2]
-    far_ref[...] = jnp.where(first_core, below, above)
     pair = [jnp.where(first_core, below, high), jnp.where(first_core, low, above)]
     put_tiles(z, pair, slab_ref)
 
@@ -198,7 +208,7 @@
     projector = Projector(z, v_ref, proj_ref)
     projector.add(range(z.cells // 2))
     scatter(z, projector.sums(), hots_ref, tab_ref)
-    put_tiles(z, mate_tiles(dom & 1, tab_ref), v_ref)
+    put_mate(z, tab_ref, v_ref)
 
 
 def near_strength(z, dom, strength_ref, out_ref):
@@ -319,7 +329,7 @@
     projector = Projector(z, first_ref, proj_ref)
     projector.add(range(z.cells // 2))
     scatter(z, projector.sums(), hots_ref, tab_ref)
-    put_tiles(z, mate_tiles(lax.axis_index("dom") & 1, tab_ref), first_ref)
+    put_mate(z, tab_ref, first_ref)
 
 
 def filtered_kernel(
@@ -336,7 +346,7 @@
 VMEM = pl.BlockSpec(memory_space=pltpu.VMEM)
 
 
-def call(kernel, z, name, outs, ins, flops, moved, scratch=(), aliases=None):
+def call(kernel, z, name, outs, ins, flops, moved, scratch=()):
     single = not isinstance(outs, (list, tuple))
     return pl.pallas_call(
         functools.partial(kernel, z),
@@ -345,7 +355,6 @@
         in_specs=[VMEM] * len(ins),
         out_specs=VMEM if single else [VMEM] * len(outs),
         scratch_shapes=list(scratch),
-        input_output_aliases=aliases or {},
         compiler_params=pltpu.CompilerParams(vmem_limit_bytes=12288 * 1024),
         cost_estimate=pl.CostEstimate(flops=flops, bytes_accessed=moved, transcendentals=0),
     )(*ins)
@@ -358,6 +367,7 @@
         self.tab = jax.ShapeDtypeStruct((3, z.bands, z.lanes), F32)
         self.slab = jax.ShapeDtypeStruct((z.tall, z.depth), BF16)
         self.message = jax.ShapeDtypeStruct((z.tall + 6 * z.bands, z.depth), BF16)
+        self.mate_message = jax.ShapeDtypeStruct((z.tall + 10 * z.bands, z.depth), BF16)
         self.base = jax.ShapeDtypeStruct((z.tall, z.depth), F32)
         self.near = jax.ShapeDtypeStruct((8, z.lanes), F32)
         self.hots = jax.ShapeDtypeStruct((z.blocks, 3 * z.lanes, z.slots), BF16)
@@ -381,7 +391,7 @@
 
 def swap_far(x, axis):
     count = lax.axis_size(axis)
-    return lax.ppermute(x, axis, [(i, (i + 2 * (i % 2) * 2 - 2) % count) for i in range(count)])
+    return lax.ppermute(x, axis, [(i, (i + 3 - 6 * (i % 2)) % count) for i in range(count)])
 
 
 def local(bands, potential, projectors, atom_ids, strength, rotation):
@@ -396,8 +406,7 @@
     def exchange(tab, slab):
         on_chip = swap_on_chip(slab, "dom")
         slab, chip, far = call(
-            meet_kernel, z, "meet", [s.message, s.pair, s.tile], (tab, on_chip, slab),
-            1000, 1000, aliases={2: 0},
+            meet_kernel, z, "meet", [s.message, s.pair, s.tile], (tab, on_chip, slab), 1000, 1000
         )
         across = swap_across(slab, "dom")
         far = swap_far(far, "dom")
@@ -405,7 +414,7 @@
 
     pause = call(pause_kernel, z, "pause", s.tile, (), 4000 * s.stream, 40_000_000)
     tab, start, hots = call(
-        project_kernel, z, "project", [s.tab, s.message, s.hots],
+        project_kernel, z, "project", [s.tab, s.mate_message, s.hots],
         (pause, atom_ids, flat, proj), s.stream, s.proj_bytes,
     )
     start, on_chip, sums = exchange(tab, start)
@@ -414,7 +423,7 @@
         (start, on_chip, pot, strength.T), s.stencil, s.slab_bytes, scratch=s.wide,
     )
     first, tab = call(
-        first_kernel, z, "first", [s.message, s.tab],
+        first_kernel, z, "first", [s.mate_message, s.tab],
         (base,) + sums + (near, hots, proj), 2 * s.stream, s.proj_bytes, scratch=s.acc,
     )
     first, on_chip, sums = exchange(tab, first)

time: 72.7 us -> 72.5 us (level)
  waiting for transfers between devices: 10.9 us -> 7.89 us
  starting transfers between devices: 14.3 us -> 16.1 us
  blocking collectives: 38.8 us -> 39.6 us
    ppermute x2, waiting for transfers between devices: 8.06 us -> 5.02 us  [swap_far(): lax.ppermute(x, axis, [(i, (i + 3 - 6 * (i % 2)) % count) for i in range(...]
    ppermute x2, starting transfers between devices: 5.48 us -> 7.38 us  [swap_far(): lax.ppermute(x, axis, [(i, (i + 3 - 6 * (i % 2)) % count) for i in range(...]
where the time goes in v8:
time: 72.5 us; the launch traced here: 72.2 us
  blocking collectives  39.6 us (55%)
  starting transfers between devices  16.1 us (22%)
  waiting for transfers between devices  7.89 us (11%)
  Pallas kernels  5.47 us (8%)
  local copies, waits for them, and re-layouts  2.62 us (4%)
    all_to_all x1, blocking collectives, local(): pieces = lax.all_to_all(pieces, 'band', 0, 0, tiled=True)  25.1 us
    all_to_all x1, blocking collectives, local(): rotated = lax.all_to_all(rotated, 'band', 0, 0, tiled=True)  14.5 us
    ppermute x2, starting transfers between devices, swap_far(): lax.ppermute(x, axis, [(i, (i + 3 - 6 * (i % 2)) % count) for i in range(...  7.38 us
    pallas_call x8, Pallas kernels, call(): pl.pallas_call(functools.partial(kernel, z), name=name, out_shape=outs, i...  5.47 us
    ppermute x2, waiting for transfers between devices, swap_far(): lax.ppermute(x, axis, [(i, (i + 3 - 6 * (i % 2)) % count) for i in range(...  5.02 us
    ppermute x2, starting transfers between devices, swap_across(): lax.ppermute(x, axis, [(i, ((i + 1 ^ 1) - 1) % count) for i in range(coun...  4.92 us
    ppermute x2, starting transfers between devices, swap_on_chip(): return lax.ppermute(x, axis, [(i, i ^ 1) for i in range(count)])  3.84 us
    ppermute x2, waiting for transfers between devices, swap_on_chip(): return lax.ppermute(x, axis, [(i, i ^ 1) for i in range(count)])  2.87 us
  transfers between devices with their start and end apart: 6, of which 4 were waited for; matrix products, arithmetic and copies ran while one was open for 0% of the time, Pallas kernels for 2%

profile of v8, /device:TPU:56, one launch (start us, length us, event | category | flops | bytes accessed | tf_op | source)
XLA Modules:
  0.0 72.2 jit_solution(11747307196471514828)
XLA Ops:
  0.0 0.0 copy-start.3
  0.0 0.0 copy-start.4
  0.1 0.6 copy-done.5
  0.7 1.2 %copy-done.1 = bf16[6,16,32,4,128]{4,3,2,1,0:T(4,128)(2,1)S(1)} copy-done((bf16[6,16,32,4,128]{4,3,2,1,0:T(4,128)(2,1)S(1)}, bf16[6,16,32,4,128]{4,3,2,1,0:T(4,128)(2,1)}, u32[]{:S(2)}) %copy-start.1) | copy-done | bytes 3145752
  1.9 1.2 %project.1 = (f32[3,8,128]{2,1,0:T(8,128)S(1)}, bf16[848,128]{1,0:T(8,128)(2,1)S(1)}, bf16[2,384,128]{2,1,0:T(8,128)(2,1)S(1)}) custom-call(f32[8,128]{1,0:T(8,128)S(1)} %pause.1.pause_ref, s32[2,32]{1,0:T(2,128)S(1)} %copy-done.5, bf16[8,96,128]{2,1,0:T(8,128)(2,1)S(1)} %bitcast.35, bf16[96,128,128]{2,1,0:T(8,128)(2,1)S(1)} %bitcast.31), custom_call_target="tpu_custom_call" | custom-call | flops 25165824 | bytes 3145728 | tf_op jit(solution)/shard_map/project/pallas_call | solution.py:351
  3.2 1.9 %collective-permute-start = (bf16[848,128]{1,0:T(8,128)(2,1)S(1)}, bf16[848,128]{1,0:T(8,128)(2,1)S(1)}, u32[]{:S(2)}, u32[]{:S(2)}) collective-permute-start(bf16[848,128]{1,0:T(8,128)(2,1)S(1)} %get-tuple-element.19.slab_in), channel_id=1, source_target_pairs={{0,16},{16,0},{32,48},{48,32},{64,80},{80,64},{96,112},{112,96},{1... | collective-permute-start | bytes 651272 | tf_op jit(solution)/shard_map/ppermute | solution.py:384
  5.1 1.4 %collective-permute-done.got_ref.on_ref = bf16[848,128]{1,0:T(8,128)(2,1)S(1)} collective-permute-done((bf16[848,128]{1,0:T(8,128)(2,1)S(1)}, bf16[848,128]{1,0:T(8,128)(2,1)S(1)}, u32[]{:S(2)}, u32[]{:S(2)}) %collective-permute-start) | collective-permute-done | bytes 217120 | tf_op jit(solution)/shard_map/ppermute | solution.py:384
  6.5 3.0 %collective-permute-start.1 = (bf16[816,128]{1,0:T(8,128)(2,1)S(1)}, bf16[816,128]{1,0:T(8,128)(2,1)S(1)}, u32[]{:S(2)}, u32[]{:S(2)}) collective-permute-start(bf16[816,128]{1,0:T(8,128)(2,1)S(1)} %get-tuple-element.20.v_ref.start_ref), channel_id=1, source_target_pairs={{0,496},{16,32},{32,16},{48,64},{64,48},{80,96},{96,80},{112,128},... | collective-permute-start | bytes 626696 | tf_op jit(solution)/shard_map/ppermute | solution.py:389
  9.6 3.7 %collective-permute-start.2 = (f32[8,128]{1,0:T(8,128)S(1)}, f32[8,128]{1,0:T(8,128)S(1)}, u32[]{:S(2)}, u32[]{:S(2)}) collective-permute-start(f32[8,128]{1,0:T(8,128)S(1)} %get-tuple-element.23), channel_id=1, source_target_pairs={{0,48},{16,480},{32,80},{48,0},{64,112},{80,32},{96,144},{112,64},... | collective-permute-start | bytes 12296 | tf_op jit(solution)/shard_map/ppermute | solution.py:394
  13.3 0.9 %base_first.1 = (f32[768,128]{1,0:T(8,128)S(1)}, f32[8,128]{1,0:T(8,128)S(1)}) custom-call(bf16[816,128]{1,0:T(8,128)(2,1)S(1)} %get-tuple-element.20.v_ref.start_ref, bf16[848,128]{1,0:T(8,128)(2,1)S(1)} %collective-permute-done.got_ref.on_ref, f32[96,128]{1,0:T(8,128)S(1)} %bitcast.36, f32[4,1024]{1,0:T(4,128)S(1)} %bitcast.38), custom_call_target="tpu_custom_call" | custom-call | flops 75497472 | bytes 983040 | tf_op jit(solution)/shard_map/base_first/pallas_call | solution.py:351
  14.1 2.4 %collective-permute-done.2.far_ref = f32[8,128]{1,0:T(8,128)S(1)} collective-permute-done((f32[8,128]{1,0:T(8,128)S(1)}, f32[8,128]{1,0:T(8,128)S(1)}, u32[]{:S(2)}, u32[]{:S(2)}) %collective-permute-start.2) | collective-permute-done | bytes 4128 | tf_op jit(solution)/shard_map/ppermute | solution.py:394
  16.6 0.0 collective-permute-done.1.across_ref
  16.6 1.8 %first.1 = (bf16[848,128]{1,0:T(8,128)(2,1)S(1)}, f32[3,8,128]{2,1,0:T(8,128)S(1)}) custom-call(f32[768,128]{1,0:T(8,128)S(1)} %get-tuple-element.21.base_ref, f32[3,8,128]{2,1,0:T(8,128)S(1)} %get-tuple-element.18.tab_ref.tab_in, f32[2,8,128]{2,1,0:T(8,128)S(1)} %get-tuple-element.22.chip_ref, bf16[816,128]{1,0:T(8,128)(2,1)S(1)} %collective-permute-done.1.across_ref, ...), custom_call_target="tpu_custom_call" | custom-call | flops 50331648 | bytes 3145728 | tf_op jit(solution)/shard_map/first/pallas_call | solution.py:351
  18.4 1.9 %collective-permute-start.3 = (bf16[848,128]{1,0:T(8,128)(2,1)S(1)}, bf16[848,128]{1,0:T(8,128)(2,1)S(1)}, u32[]{:S(2)}, u32[]{:S(2)}) collective-permute-start(bf16[848,128]{1,0:T(8,128)(2,1)S(1)} %get-tuple-element.27.slab_in), channel_id=1, source_target_pairs={{0,16},{16,0},{32,48},{48,32},{64,80},{80,64},{96,112},{112,96},{1... | collective-permute-start | bytes 651272 | tf_op jit(solution)/shard_map/ppermute | solution.py:384
  20.3 1.4 %collective-permute-done.3.got_ref.on_ref = bf16[848,128]{1,0:T(8,128)(2,1)S(1)} collective-permute-done((bf16[848,128]{1,0:T(8,128)(2,1)S(1)}, bf16[848,128]{1,0:T(8,128)(2,1)S(1)}, u32[]{:S(2)}, u32[]{:S(2)}) %collective-permute-start.3) | collective-permute-done | bytes 217120 | tf_op jit(solution)/shard_map/ppermute | solution.py:384
  21.8 1.9 %collective-permute-start.4 = (bf16[816,128]{1,0:T(8,128)(2,1)S(1)}, bf16[816,128]{1,0:T(8,128)(2,1)S(1)}, u32[]{:S(2)}, u32[]{:S(2)}) collective-permute-start(bf16[816,128]{1,0:T(8,128)(2,1)S(1)} %get-tuple-element.28.v_ref), channel_id=1, source_target_pairs={{0,496},{16,32},{32,16},{48,64},{64,48},{80,96},{96,80},{112,128},... | collective-permute-start | bytes 626696 | tf_op jit(solution)/shard_map/ppermute | solution.py:389
  23.7 3.7 %collective-permute-start.5 = (f32[8,128]{1,0:T(8,128)S(1)}, f32[8,128]{1,0:T(8,128)S(1)}, u32[]{:S(2)}, u32[]{:S(2)}) collective-permute-start(f32[8,128]{1,0:T(8,128)S(1)} %get-tuple-element.30), channel_id=1, source_target_pairs={{0,48},{16,480},{32,80},{48,0},{64,112},{80,32},{96,144},{112,64},... | collective-permute-start | bytes 12296 | tf_op jit(solution)/shard_map/ppermute | solution.py:394
  27.4 0.9 %base.1.base_ref = f32[768,128]{1,0:T(8,128)S(1)} custom-call(bf16[816,128]{1,0:T(8,128)(2,1)S(1)} %get-tuple-element.28.v_ref, bf16[848,128]{1,0:T(8,128)(2,1)S(1)} %collective-permute-done.3.got_ref.on_ref, f32[96,128]{1,0:T(8,128)S(1)} %bitcast.37), custom_call_target="tpu_custom_call" | custom-call | flops 75497472 | bytes 983040 | tf_op jit(solution)/shard_map/base/pallas_call | solution.py:351
  28.3 2.6 %collective-permute-done.5.far_ref = f32[8,128]{1,0:T(8,128)S(1)} collective-permute-done((f32[8,128]{1,0:T(8,128)S(1)}, f32[8,128]{1,0:T(8,128)S(1)}, u32[]{:S(2)}, u32[]{:S(2)}) %collective-permute-start.5) | collective-permute-done | bytes 4128 | tf_op jit(solution)/shard_map/ppermute | solution.py:394
  30.8 0.7 filtered.1
  31.5 25.1 %all_to_all.10 = bf16[16,6,8,128]{3,2,1,0:T(8,128)(2,1)S(1)} all-to-all(bf16[16,6,8,128]{3,2,1,0:T(8,128)(2,1)S(1)} %bitcast.34), channel_id=1, replica_groups=mesh['dom'=32,'band'=16] {'band'}, dimensions={0} | all-to-all | bytes 393216 | tf_op jit(solution)/shard_map/all_to_all | solution.py:440
  56.7 0.3 fusion.1
  57.0 14.5 %all_to_all.11 = bf16[16,6,8,128]{3,2,1,0:T(8,128)(2,1)S(1)} all-to-all(bf16[16,6,8,128]{3,2,1,0:T(8,128)(2,1)S(1)} %bitcast.39), channel_id=1, replica_groups=mesh['dom'=32,'band'=16] {'band'}, dimensions={0} | all-to-all | bytes 393216 | tf_op jit(solution)/shard_map/all_to_all | solution.py:444
  71.4 0.7 copy.16
  (13 shorter events, 0.1 us)
Async XLA Ops:
  0.0 56.7 %copy-start = (bf16[128,128]{1,0:T(8,128)(2,1)S(1)}, bf16[128,128]{1,0:T(8,128)(2,1)}, u32[]{:S(2)}) copy-start(bf16[128,128]{1,0:T(8,128)(2,1)} %param.11) | copy-start | bytes 98308
  0.0 0.7 copy-start.5
  0.0 1.9 %copy-start.1 = (bf16[6,16,32,4,128]{4,3,2,1,0:T(4,128)(2,1)S(1)}, bf16[6,16,32,4,128]{4,3,2,1,0:T(4,128)(2,1)}, u32[]{:S(2)}) copy-start(bf16[6,16,32,4,128]{4,3,2,1,0:T(4,128)(2,1)} %param.8) | copy-start | bytes 9437188
  0.0 1.9 %copy-start.2 = (bf16[8,6,16,128]{3,2,1,0:T(8,128)(2,1)S(1)}, bf16[8,6,16,128]{3,2,1,0:T(8,128)(2,1)}, u32[]{:S(2)}) copy-start(bf16[8,6,16,128]{3,2,1,0:T(8,128)(2,1)} %param.6) | copy-start | bytes 589828
  0.0 13.2 %copy-start.3 = (f32[6,16,128]{2,1,0:T(8,128)S(1)}, f32[6,16,128]{2,1,0:T(8,128)}, u32[]{:S(2)}) copy-start(f32[6,16,128]{2,1,0:T(8,128)} %param.7) | copy-start | bytes 147460
  0.0 13.2 %copy-start.4 = (f32[1024,4]{0,1:T(4,128)S(1)}, f32[1024,4]{0,1:T(4,128)}, u32[]{:S(2)}) copy-start(f32[1024,4]{0,1:T(4,128)} %param.10) | copy-start | bytes 49156
  3.2 3.4 %collective-permute-start = (bf16[848,128]{1,0:T(8,128)(2,1)S(1)}, bf16[848,128]{1,0:T(8,128)(2,1)S(1)}, u32[]{:S(2)}, u32[]{:S(2)}) collective-permute-start(bf16[848,128]{1,0:T(8,128)(2,1)S(1)} %get-tuple-element.19.slab_in), channel_id=1, source_target_pairs={{0,16},{16,0},{32,48},{48,32},{64,80},{80,64},{96,112},{112,96},{1... | collective-permute-start | bytes 651272 | tf_op jit(solution)/shard_map/ppermute | solution.py:384
  6.5 10.0 %collective-permute-start.1 = (bf16[816,128]{1,0:T(8,128)(2,1)S(1)}, bf16[816,128]{1,0:T(8,128)(2,1)S(1)}, u32[]{:S(2)}, u32[]{:S(2)}) collective-permute-start(bf16[816,128]{1,0:T(8,128)(2,1)S(1)} %get-tuple-element.20.v_ref.start_ref), channel_id=1, source_target_pairs={{0,496},{16,32},{32,16},{48,64},{64,48},{80,96},{96,80},{112,128},... | collective-permute-start | bytes 626696 | tf_op jit(solution)/shard_map/ppermute | solution.py:389
  9.6 7.0 %collective-permute-start.2 = (f32[8,128]{1,0:T(8,128)S(1)}, f32[8,128]{1,0:T(8,128)S(1)}, u32[]{:S(2)}, u32[]{:S(2)}) collective-permute-start(f32[8,128]{1,0:T(8,128)S(1)} %get-tuple-element.23), channel_id=1, source_target_pairs={{0,48},{16,480},{32,80},{48,0},{64,112},{80,32},{96,144},{112,64},... | collective-permute-start | bytes 12296 | tf_op jit(solution)/shard_map/ppermute | solution.py:394
  18.4 3.4 %collective-permute-start.3 = (bf16[848,128]{1,0:T(8,128)(2,1)S(1)}, bf16[848,128]{1,0:T(8,128)(2,1)S(1)}, u32[]{:S(2)}, u32[]{:S(2)}) collective-permute-start(bf16[848,128]{1,0:T(8,128)(2,1)S(1)} %get-tuple-element.27.slab_in), channel_id=1, source_target_pairs={{0,16},{16,0},{32,48},{48,32},{64,80},{80,64},{96,112},{112,96},{1... | collective-permute-start | bytes 651272 | tf_op jit(solution)/shard_map/ppermute | solution.py:384
  21.8 9.1 %collective-permute-start.4 = (bf16[816,128]{1,0:T(8,128)(2,1)S(1)}, bf16[816,128]{1,0:T(8,128)(2,1)S(1)}, u32[]{:S(2)}, u32[]{:S(2)}) collective-permute-start(bf16[816,128]{1,0:T(8,128)(2,1)S(1)} %get-tuple-element.28.v_ref), channel_id=1, source_target_pairs={{0,496},{16,32},{32,16},{48,64},{64,48},{80,96},{96,80},{112,128},... | collective-permute-start | bytes 626696 | tf_op jit(solution)/shard_map/ppermute | solution.py:389
  23.7 7.1 %collective-permute-start.5 = (f32[8,128]{1,0:T(8,128)S(1)}, f32[8,128]{1,0:T(8,128)S(1)}, u32[]{:S(2)}, u32[]{:S(2)}) collective-permute-start(f32[8,128]{1,0:T(8,128)S(1)} %get-tuple-element.30), channel_id=1, source_target_pairs={{0,48},{16,480},{32,80},{48,0},{64,112},{80,32},{96,144},{112,64},... | collective-permute-start | bytes 12296 | tf_op jit(solution)/shard_map/ppermute | solution.py:394

commit v9 on v8

--- a/solution.py
+++ b/solution.py
@@ -88,11 +88,12 @@
 
 def scatter(z, partials, hots_ref, tab_ref):
     total = None
+    b = z.bands
     for j, partial in enumerate(partials):
-        hot = hots_ref[j]
-        for piece in split3(partial):
-            part = dot_t(piece, hot)
-            total = part if total is None else total + part
+        pieces = jnp.concatenate([piece.astype(F32) for piece in split3(partial)], 0)
+        part = dot_t(pieces.astype(BF16), hots_ref[j])
+        part = part[:b] + part[b : 2 * b] + part[2 * b :]
+        total = part if total is None else total + part
     for t in range(3):
         tab_ref[t] = total[:, t * z.lanes : (t + 1) * z.lanes]
 
@@ -200,12 +201,15 @@
     out_ref[...] = jnp.zeros_like(out_ref)
 
 
-def project_kernel(z, pause_ref, ids_ref, bands_ref, proj_ref, tab_ref, v_ref, hots_ref):
-    dom = lax.axis_index("dom")
+def prepare_kernel(z, pause_ref, ids_ref, bands_ref, v_ref, hots_ref):
     turn_all(z, bands_ref, v_ref)
-    for j, hot in enumerate(one_hots(z, dom, ids_ref)):
+    for j, hot in enumerate(one_hots(z, lax.axis_index("dom"), ids_ref)):
         hots_ref[j] = hot
-    projector = Projector(z, v_ref, proj_ref)
+
+
+def project_kernel(z, v_in, hots_ref, proj_ref, tab_ref, v_ref):
+    v_ref[: z.tall, :] = v_in[...]
+    projector = Projector(z, v_in, proj_ref)
     projector.add(range(z.cells // 2))
     scatter(z, projector.sums(), hots_ref, tab_ref)
     put_mate(z, tab_ref, v_ref)
@@ -413,9 +417,11 @@
         return slab, on_chip, (tab, chip, across, far)
 
     pause = call(pause_kernel, z, "pause", s.tile, (), 4000 * s.stream, 40_000_000)
-    tab, start, hots = call(
-        project_kernel, z, "project", [s.tab, s.mate_message, s.hots],
-        (pause, atom_ids, flat, proj), s.stream, s.proj_bytes,
+    start, hots = call(
+        prepare_kernel, z, "prepare", [s.slab, s.hots], (pause, atom_ids, flat), s.stream, s.proj_bytes,
+    )
+    tab, start = call(
+        project_kernel, z, "project", [s.tab, s.mate_message], (start, hots, proj), s.stream, s.proj_bytes,
     )
     start, on_chip, sums = exchange(tab, start)
     base, near = call(

time: 72.5 us -> 72.3 us (level)
    pallas_call x8 -> x9, Pallas kernels: 5.47 us -> 5.47 us  [call(): pl.pallas_call(functools.partial(kernel, z), name=name, out_shape=outs, i...]
where the time goes in v9:
time: 72.3 us; the launch traced here: 72 us
  blocking collectives  39.6 us (55%)
  starting transfers between devices  16.1 us (22%)
  waiting for transfers between devices  7.9 us (11%)
  Pallas kernels  5.47 us (8%)
  local copies, waits for them, and re-layouts  2.46 us (3%)
    all_to_all x1, blocking collectives, local(): pieces = lax.all_to_all(pieces, 'band', 0, 0, tiled=True)  25.1 us
    all_to_all x1, blocking collectives, local(): rotated = lax.all_to_all(rotated, 'band', 0, 0, tiled=True)  14.5 us
    ppermute x2, starting transfers between devices, swap_far(): lax.ppermute(x, axis, [(i, (i + 3 - 6 * (i % 2)) % count) for i in range(...  7.38 us
    pallas_call x9, Pallas kernels, call(): pl.pallas_call(functools.partial(kernel, z), name=name, out_shape=outs, i...  5.47 us
    ppermute x2, waiting for transfers between devices, swap_far(): lax.ppermute(x, axis, [(i, (i + 3 - 6 * (i % 2)) % count) for i in range(...  5.02 us
    ppermute x2, starting transfers between devices, swap_across(): lax.ppermute(x, axis, [(i, ((i + 1 ^ 1) - 1) % count) for i in range(coun...  4.92 us
    ppermute x2, starting transfers between devices, swap_on_chip(): return lax.ppermute(x, axis, [(i, i ^ 1) for i in range(count)])  3.84 us
    ppermute x2, waiting for transfers between devices, swap_on_chip(): return lax.ppermute(x, axis, [(i, i ^ 1) for i in range(count)])  2.87 us
  transfers between devices with their start and end apart: 6, of which 4 were waited for; matrix products, arithmetic and copies ran while one was open for 0% of the time, Pallas kernels for 2%

profile of v9, /device:TPU:56, one launch (start us, length us, event | category | flops | bytes accessed | tf_op | source)
XLA Modules:
  0.0 72.0 jit_solution(3829584951496600723)
XLA Ops:
  0.0 0.0 copy-start.4
  0.1 0.6 copy-done.5
  0.7 0.3 copy-done.2
  1.0 0.3 prepare.1
  1.2 0.8 %copy-done.1 = bf16[6,16,32,4,128]{4,3,2,1,0:T(4,128)(2,1)S(1)} copy-done((bf16[6,16,32,4,128]{4,3,2,1,0:T(4,128)(2,1)S(1)}, bf16[6,16,32,4,128]{4,3,2,1,0:T(4,128)(2,1)}, u32[]{:S(2)}) %copy-start.1) | copy-done | bytes 3145752
  2.0 1.1 %project.1 = (f32[3,8,128]{2,1,0:T(8,128)S(1)}, bf16[848,128]{1,0:T(8,128)(2,1)S(1)}) custom-call(bf16[768,128]{1,0:T(8,128)(2,1)S(1)} %get-tuple-element.19.v_in, bf16[2,384,128]{2,1,0:T(8,128)(2,1)S(1)} %get-tuple-element.20.hots_ref, bf16[96,128,128]{2,1,0:T(8,128)(2,1)S(1)} %bitcast.31), custom_call_target="tpu_custom_call" | custom-call | flops 25165824 | bytes 3145728 | tf_op jit(solution)/shard_map/project/pallas_call | solution.py:355
  3.1 1.9 %collective-permute-start = (bf16[848,128]{1,0:T(8,128)(2,1)S(1)}, bf16[848,128]{1,0:T(8,128)(2,1)S(1)}, u32[]{:S(2)}, u32[]{:S(2)}) collective-permute-start(bf16[848,128]{1,0:T(8,128)(2,1)S(1)} %get-tuple-element.22.slab_in), channel_id=1, source_target_pairs={{0,16},{16,0},{32,48},{48,32},{64,80},{80,64},{96,112},{112,96},{1... | collective-permute-start | bytes 651272 | tf_op jit(solution)/shard_map/ppermute | solution.py:388
  5.1 1.4 %collective-permute-done.got_ref.on_ref = bf16[848,128]{1,0:T(8,128)(2,1)S(1)} collective-permute-done((bf16[848,128]{1,0:T(8,128)(2,1)S(1)}, bf16[848,128]{1,0:T(8,128)(2,1)S(1)}, u32[]{:S(2)}, u32[]{:S(2)}) %collective-permute-start) | collective-permute-done | bytes 217120 | tf_op jit(solution)/shard_map/ppermute | solution.py:388
  6.5 3.0 %collective-permute-start.1 = (bf16[816,128]{1,0:T(8,128)(2,1)S(1)}, bf16[816,128]{1,0:T(8,128)(2,1)S(1)}, u32[]{:S(2)}, u32[]{:S(2)}) collective-permute-start(bf16[816,128]{1,0:T(8,128)(2,1)S(1)} %get-tuple-element.23.v_ref.start_ref), channel_id=1, source_target_pairs={{0,496},{16,32},{32,16},{48,64},{64,48},{80,96},{96,80},{112,128},... | collective-permute-start | bytes 626696 | tf_op jit(solution)/shard_map/ppermute | solution.py:393
  9.5 3.7 %collective-permute-start.2 = (f32[8,128]{1,0:T(8,128)S(1)}, f32[8,128]{1,0:T(8,128)S(1)}, u32[]{:S(2)}, u32[]{:S(2)}) collective-permute-start(f32[8,128]{1,0:T(8,128)S(1)} %get-tuple-element.26), channel_id=1, source_target_pairs={{0,48},{16,480},{32,80},{48,0},{64,112},{80,32},{96,144},{112,64},... | collective-permute-start | bytes 12296 | tf_op jit(solution)/shard_map/ppermute | solution.py:398
  13.2 0.9 %base_first.1 = (f32[768,128]{1,0:T(8,128)S(1)}, f32[8,128]{1,0:T(8,128)S(1)}) custom-call(bf16[816,128]{1,0:T(8,128)(2,1)S(1)} %get-tuple-element.23.v_ref.start_ref, bf16[848,128]{1,0:T(8,128)(2,1)S(1)} %collective-permute-done.got_ref.on_ref, f32[96,128]{1,0:T(8,128)S(1)} %bitcast.36, f32[4,1024]{1,0:T(4,128)S(1)} %bitcast.38), custom_call_target="tpu_custom_call" | custom-call | flops 75497472 | bytes 983040 | tf_op jit(solution)/shard_map/base_first/pallas_call | solution.py:355
  14.1 2.4 %collective-permute-done.2.far_ref = f32[8,128]{1,0:T(8,128)S(1)} collective-permute-done((f32[8,128]{1,0:T(8,128)S(1)}, f32[8,128]{1,0:T(8,128)S(1)}, u32[]{:S(2)}, u32[]{:S(2)}) %collective-permute-start.2) | collective-permute-done | bytes 4128 | tf_op jit(solution)/shard_map/ppermute | solution.py:398
  16.6 1.7 %first.1 = (bf16[848,128]{1,0:T(8,128)(2,1)S(1)}, f32[3,8,128]{2,1,0:T(8,128)S(1)}) custom-call(f32[768,128]{1,0:T(8,128)S(1)} %get-tuple-element.24.base_ref, f32[3,8,128]{2,1,0:T(8,128)S(1)} %get-tuple-element.21.tab_ref.tab_in, f32[2,8,128]{2,1,0:T(8,128)S(1)} %get-tuple-element.25.chip_ref, bf16[816,128]{1,0:T(8,128)(2,1)S(1)} %collective-permute-done.1.across_ref, ...), custom_call_target="tpu_custom_call" | custom-call | flops 50331648 | bytes 3145728 | tf_op jit(solution)/shard_map/first/pallas_call | solution.py:355
  18.2 1.9 %collective-permute-start.3 = (bf16[848,128]{1,0:T(8,128)(2,1)S(1)}, bf16[848,128]{1,0:T(8,128)(2,1)S(1)}, u32[]{:S(2)}, u32[]{:S(2)}) collective-permute-start(bf16[848,128]{1,0:T(8,128)(2,1)S(1)} %get-tuple-element.29.slab_in), channel_id=1, source_target_pairs={{0,16},{16,0},{32,48},{48,32},{64,80},{80,64},{96,112},{112,96},{1... | collective-permute-start | bytes 651272 | tf_op jit(solution)/shard_map/ppermute | solution.py:388
  20.1 1.4 %collective-permute-done.3.got_ref.on_ref = bf16[848,128]{1,0:T(8,128)(2,1)S(1)} collective-permute-done((bf16[848,128]{1,0:T(8,128)(2,1)S(1)}, bf16[848,128]{1,0:T(8,128)(2,1)S(1)}, u32[]{:S(2)}, u32[]{:S(2)}) %collective-permute-start.3) | collective-permute-done | bytes 217120 | tf_op jit(solution)/shard_map/ppermute | solution.py:388
  21.6 1.9 %collective-permute-start.4 = (bf16[816,128]{1,0:T(8,128)(2,1)S(1)}, bf16[816,128]{1,0:T(8,128)(2,1)S(1)}, u32[]{:S(2)}, u32[]{:S(2)}) collective-permute-start(bf16[816,128]{1,0:T(8,128)(2,1)S(1)} %get-tuple-element.30.v_ref), channel_id=1, source_target_pairs={{0,496},{16,32},{32,16},{48,64},{64,48},{80,96},{96,80},{112,128},... | collective-permute-start | bytes 626696 | tf_op jit(solution)/shard_map/ppermute | solution.py:393
  23.5 3.7 %collective-permute-start.5 = (f32[8,128]{1,0:T(8,128)S(1)}, f32[8,128]{1,0:T(8,128)S(1)}, u32[]{:S(2)}, u32[]{:S(2)}) collective-permute-start(f32[8,128]{1,0:T(8,128)S(1)} %get-tuple-element.32), channel_id=1, source_target_pairs={{0,48},{16,480},{32,80},{48,0},{64,112},{80,32},{96,144},{112,64},... | collective-permute-start | bytes 12296 | tf_op jit(solution)/shard_map/ppermute | solution.py:398
  27.2 0.9 %base.1.base_ref = f32[768,128]{1,0:T(8,128)S(1)} custom-call(bf16[816,128]{1,0:T(8,128)(2,1)S(1)} %get-tuple-element.30.v_ref, bf16[848,128]{1,0:T(8,128)(2,1)S(1)} %collective-permute-done.3.got_ref.on_ref, f32[96,128]{1,0:T(8,128)S(1)} %bitcast.37), custom_call_target="tpu_custom_call" | custom-call | flops 75497472 | bytes 983040 | tf_op jit(solution)/shard_map/base/pallas_call | solution.py:355
  28.1 2.6 %collective-permute-done.5.far_ref = f32[8,128]{1,0:T(8,128)S(1)} collective-permute-done((f32[8,128]{1,0:T(8,128)S(1)}, f32[8,128]{1,0:T(8,128)S(1)}, u32[]{:S(2)}, u32[]{:S(2)}) %collective-permute-start.5) | collective-permute-done | bytes 4128 | tf_op jit(solution)/shard_map/ppermute | solution.py:398
  30.7 0.7 filtered.1
  31.4 25.1 %all_to_all.10 = bf16[16,6,8,128]{3,2,1,0:T(8,128)(2,1)S(1)} all-to-all(bf16[16,6,8,128]{3,2,1,0:T(8,128)(2,1)S(1)} %bitcast.34), channel_id=1, replica_groups=mesh['dom'=32,'band'=16] {'band'}, dimensions={0} | all-to-all | bytes 393216 | tf_op jit(solution)/shard_map/all_to_all | solution.py:446
  56.5 0.3 fusion.1
  56.8 14.5 %all_to_all.11 = bf16[16,6,8,128]{3,2,1,0:T(8,128)(2,1)S(1)} all-to-all(bf16[16,6,8,128]{3,2,1,0:T(8,128)(2,1)S(1)} %bitcast.39), channel_id=1, replica_groups=mesh['dom'=32,'band'=16] {'band'}, dimensions={0} | all-to-all | bytes 393216 | tf_op jit(solution)/shard_map/all_to_all | solution.py:450
  71.3 0.7 copy.16
  (14 shorter events, 0.1 us)
Async XLA Ops:
  0.0 56.5 %copy-start = (bf16[128,128]{1,0:T(8,128)(2,1)S(1)}, bf16[128,128]{1,0:T(8,128)(2,1)}, u32[]{:S(2)}) copy-start(bf16[128,128]{1,0:T(8,128)(2,1)} %param.11) | copy-start | bytes 98308
  0.0 0.7 copy-start.5
  0.0 0.9 %copy-start.2 = (bf16[8,6,16,128]{3,2,1,0:T(8,128)(2,1)S(1)}, bf16[8,6,16,128]{3,2,1,0:T(8,128)(2,1)}, u32[]{:S(2)}) copy-start(bf16[8,6,16,128]{3,2,1,0:T(8,128)(2,1)} %param.6) | copy-start | bytes 589828
  0.0 2.0 %copy-start.1 = (bf16[6,16,32,4,128]{4,3,2,1,0:T(4,128)(2,1)S(1)}, bf16[6,16,32,4,128]{4,3,2,1,0:T(4,128)(2,1)}, u32[]{:S(2)}) copy-start(bf16[6,16,32,4,128]{4,3,2,1,0:T(4,128)(2,1)} %param.8) | copy-start | bytes 9437188
  0.0 13.2 %copy-start.3 = (f32[6,16,128]{2,1,0:T(8,128)S(1)}, f32[6,16,128]{2,1,0:T(8,128)}, u32[]{:S(2)}) copy-start(f32[6,16,128]{2,1,0:T(8,128)} %param.7) | copy-start | bytes 147460
  0.0 13.2 %copy-start.4 = (f32[1024,4]{0,1:T(4,128)S(1)}, f32[1024,4]{0,1:T(4,128)}, u32[]{:S(2)}) copy-start(f32[1024,4]{0,1:T(4,128)} %param.10) | copy-start | bytes 49156
  3.1 3.4 %collective-permute-start = (bf16[848,128]{1,0:T(8,128)(2,1)S(1)}, bf16[848,128]{1,0:T(8,128)(2,1)S(1)}, u32[]{:S(2)}, u32[]{:S(2)}) collective-permute-start(bf16[848,128]{1,0:T(8,128)(2,1)S(1)} %get-tuple-element.22.slab_in), channel_id=1, source_target_pairs={{0,16},{16,0},{32,48},{48,32},{64,80},{80,64},{96,112},{112,96},{1... | collective-permute-start | bytes 651272 | tf_op jit(solution)/shard_map/ppermute | solution.py:388
  6.5 10.0 %collective-permute-start.1 = (bf16[816,128]{1,0:T(8,128)(2,1)S(1)}, bf16[816,128]{1,0:T(8,128)(2,1)S(1)}, u32[]{:S(2)}, u32[]{:S(2)}) collective-permute-start(bf16[816,128]{1,0:T(8,128)(2,1)S(1)} %get-tuple-element.23.v_ref.start_ref), channel_id=1, source_target_pairs={{0,496},{16,32},{32,16},{48,64},{64,48},{80,96},{96,80},{112,128},... | collective-permute-start | bytes 626696 | tf_op jit(solution)/shard_map/ppermute | solution.py:393
  9.5 7.0 %collective-permute-start.2 = (f32[8,128]{1,0:T(8,128)S(1)}, f32[8,128]{1,0:T(8,128)S(1)}, u32[]{:S(2)}, u32[]{:S(2)}) collective-permute-start(f32[8,128]{1,0:T(8,128)S(1)} %get-tuple-element.26), channel_id=1, source_target_pairs={{0,48},{16,480},{32,80},{48,0},{64,112},{80,32},{96,144},{112,64},... | collective-permute-start | bytes 12296 | tf_op jit(solution)/shard_map/ppermute | solution.py:398
  18.2 3.4 %collective-permute-start.3 = (bf16[848,128]{1,0:T(8,128)(2,1)S(1)}, bf16[848,128]{1,0:T(8,128)(2,1)S(1)}, u32[]{:S(2)}, u32[]{:S(2)}) collective-permute-start(bf16[848,128]{1,0:T(8,128)(2,1)S(1)} %get-tuple-element.29.slab_in), channel_id=1, source_target_pairs={{0,16},{16,0},{32,48},{48,32},{64,80},{80,64},{96,112},{112,96},{1... | collective-permute-start | bytes 651272 | tf_op jit(solution)/shard_map/ppermute | solution.py:388
  21.6 9.1 %collective-permute-start.4 = (bf16[816,128]{1,0:T(8,128)(2,1)S(1)}, bf16[816,128]{1,0:T(8,128)(2,1)S(1)}, u32[]{:S(2)}, u32[]{:S(2)}) collective-permute-start(bf16[816,128]{1,0:T(8,128)(2,1)S(1)} %get-tuple-element.30.v_ref), channel_id=1, source_target_pairs={{0,496},{16,32},{32,16},{48,64},{64,48},{80,96},{96,80},{112,128},... | collective-permute-start | bytes 626696 | tf_op jit(solution)/shard_map/ppermute | solution.py:393
  23.5 7.1 %collective-permute-start.5 = (f32[8,128]{1,0:T(8,128)S(1)}, f32[8,128]{1,0:T(8,128)S(1)}, u32[]{:S(2)}, u32[]{:S(2)}) collective-permute-start(f32[8,128]{1,0:T(8,128)S(1)} %get-tuple-element.32), channel_id=1, source_target_pairs={{0,48},{16,480},{32,80},{48,0},{64,112},{80,32},{96,144},{112,64},... | collective-permute-start | bytes 12296 | tf_op jit(solution)/shard_map/ppermute | solution.py:398

commit v10 on v9

--- a/solution.py
+++ b/solution.py
@@ -98,20 +98,14 @@
         tab_ref[t] = total[:, t * z.lanes : (t + 1) * z.lanes]
 
 
-def mate_tiles(side, tab_ref):
-    first_core = side == 0
-    return [
-        jnp.where(first_core, tab_ref[1], tab_ref[0]),
-        jnp.where(first_core, tab_ref[2], tab_ref[1]),
+def put_across(z, tab_ref, slab_ref, far_ref):
+    first_core = (lax.axis_index("dom") & 1) == 0
+    pair = [
+        jnp.where(first_core, tab_ref[0], tab_ref[1]),
+        jnp.where(first_core, tab_ref[1], tab_ref[2]),
     ]
-
-
-def put_mate(z, tab_ref, slab_ref):
-    side = lax.axis_index("dom") & 1
-    put_tiles(z, mate_tiles(side, tab_ref), slab_ref)
-    outer = jnp.where(side == 0, tab_ref[0], tab_ref[2])
-    pieces = list(split3(outer)) + [jnp.zeros(outer.shape, BF16)]
-    slab_ref[z.tall + 6 * z.bands :, :] = jnp.concatenate([p.astype(F32) for p in pieces], 0).astype(BF16)
+    put_tiles(z, pair, slab_ref)
+    far_ref[...] = jnp.where(first_core, tab_ref[2], tab_ref[0])
 
 
 def put_tiles(z, tiles, slab_ref):
@@ -127,28 +121,22 @@
     return [total[: z.bands], total[z.bands :]]
 
 
-def meet_kernel(z, tab_ref, got_ref, slab_in, slab_ref, chip_ref, far_ref):
-    slab_ref[: z.tall, :] = slab_in[: z.tall, :]
-    side = lax.axis_index("dom") & 1
-    first_core = side == 0
-    mate, got = mate_tiles(side, tab_ref), get_tiles(z, got_ref)
-    low, high = mate[0] + got[0], mate[1] + got[1]
-    chip_ref[0], chip_ref[1] = low, high
-    outer = got_ref[z.tall + 6 * z.bands :, :].astype(F32)
-    far_ref[...] = outer[: z.bands] + outer[z.bands : 2 * z.bands] + outer[2 * z.bands : 3 * z.bands]
-    below, above = tab_ref[0], tab_ref[2]
-    pair = [jnp.where(first_core, below, high), jnp.where(first_core, low, above)]
-    put_tiles(z, pair, slab_ref)
-
-
-def gathered(z, tab_ref, chip_ref, across_ref, far_ref, strength_ref, hots_ref):
+def meet_kernel(z, tab_ref, across_ref, mate_ref):
     first_core = (lax.axis_index("dom") & 1) == 0
     got = get_tiles(z, across_ref)
-    low, high, far = chip_ref[0], chip_ref[1], far_ref[...]
+    mate_ref[0] = jnp.where(first_core, got[1] + tab_ref[1], tab_ref[0])
+    mate_ref[1] = jnp.where(first_core, tab_ref[2], tab_ref[1] + got[0])
+
+
+def gathered(z, tab_ref, mate_ref, across_ref, far_ref, strength_ref, hots_ref):
+    first_core = (lax.axis_index("dom") & 1) == 0
+    got = get_tiles(z, across_ref)
+    below, middle, above = tab_ref[0], tab_ref[1], tab_ref[2]
+    low, high, far = mate_ref[0], mate_ref[1], far_ref[...]
     tiles = [
-        jnp.where(first_core, tab_ref[0] + got[0], low + far),
-        jnp.where(first_core, low + got[1], high + got[0]),
-        jnp.where(first_core, high + far, tab_ref[2] + got[1]),
+        below + jnp.where(first_core, got[0] + far, low),
+        middle + jnp.where(first_core, got[1] + low, got[0] + high),
+        above + jnp.where(first_core, high, got[1] + far),
     ]
     weighted = [tile * strength_ref[t : t + 1, :] for t, tile in enumerate(tiles)]
     weighted = jnp.concatenate(weighted, 1).astype(BF16)
@@ -207,12 +195,12 @@
         hots_ref[j] = hot
 
 
-def project_kernel(z, v_in, hots_ref, proj_ref, tab_ref, v_ref):
+def project_kernel(z, v_in, hots_ref, proj_ref, tab_ref, far_ref, v_ref):
     v_ref[: z.tall, :] = v_in[...]
     projector = Projector(z, v_in, proj_ref)
     projector.add(range(z.cells // 2))
     scatter(z, projector.sums(), hots_ref, tab_ref)
-    put_mate(z, tab_ref, v_ref)
+    put_across(z, tab_ref, v_ref, far_ref)
 
 
 def near_strength(z, dom, strength_ref, out_ref):
@@ -322,7 +310,7 @@
 
 
 def first_kernel(
-    z, base_ref, tab_in, chip_ref, across_ref, far_ref, near_ref, hots_ref, proj_ref, first_ref, tab_ref, acc_ref
+    z, base_ref, tab_in, chip_ref, across_ref, far_ref, near_ref, hots_ref, proj_ref, first_ref, tab_ref, far_out, acc_ref
 ):
     add_across(z, base_ref, across_ref, acc_ref)
     weighted = gathered(z, tab_in, chip_ref, across_ref, far_ref, near_ref, hots_ref)
@@ -333,7 +321,7 @@
     projector = Projector(z, first_ref, proj_ref)
     projector.add(range(z.cells // 2))
     scatter(z, projector.sums(), hots_ref, tab_ref)
-    put_mate(z, tab_ref, first_ref)
+    put_across(z, tab_ref, first_ref, far_out)
 
 
 def filtered_kernel(
@@ -371,7 +359,6 @@
         self.tab = jax.ShapeDtypeStruct((3, z.bands, z.lanes), F32)
         self.slab = jax.ShapeDtypeStruct((z.tall, z.depth), BF16)
         self.message = jax.ShapeDtypeStruct((z.tall + 6 * z.bands, z.depth), BF16)
-        self.mate_message = jax.ShapeDtypeStruct((z.tall + 10 * z.bands, z.depth), BF16)
         self.base = jax.ShapeDtypeStruct((z.tall, z.depth), F32)
         self.near = jax.ShapeDtypeStruct((8, z.lanes), F32)
         self.hots = jax.ShapeDtypeStruct((z.blocks, 3 * z.lanes, z.slots), BF16)
@@ -395,7 +382,7 @@
 
 def swap_far(x, axis):
     count = lax.axis_size(axis)
-    return lax.ppermute(x, axis, [(i, (i + 3 - 6 * (i % 2)) % count) for i in range(count)])
+    return lax.ppermute(x, axis, [(i, (i + 2 - 4 * (i % 2)) % count) for i in range(count)])
 
 
 def local(bands, potential, projectors, atom_ids, strength, rotation):
@@ -407,34 +394,32 @@
 
     s = Shapes(z)
 
-    def exchange(tab, slab):
-        on_chip = swap_on_chip(slab, "dom")
-        slab, chip, far = call(
-            meet_kernel, z, "meet", [s.message, s.pair, s.tile], (tab, on_chip, slab), 1000, 1000
-        )
+    def exchange(tab, far, slab):
         across = swap_across(slab, "dom")
         far = swap_far(far, "dom")
-        return slab, on_chip, (tab, chip, across, far)
+        on_chip = swap_on_chip(slab, "dom")
+        mate = call(meet_kernel, z, "meet", s.pair, (tab, across), 1000, 1000)
+        return on_chip, (tab, swap_on_chip(mate, "dom"), across, far)
 
     pause = call(pause_kernel, z, "pause", s.tile, (), 4000 * s.stream, 40_000_000)
     start, hots = call(
         prepare_kernel, z, "prepare", [s.slab, s.hots], (pause, atom_ids, flat), s.stream, s.proj_bytes,
     )
-    tab, start = call(
-        project_kernel, z, "project", [s.tab, s.mate_message], (start, hots, proj), s.stream, s.proj_bytes,
-    )
-    start, on_chip, sums = exchange(tab, start)
+    tab, far, start = call(
+        project_kernel, z, "project", [s.tab, s.tile, s.message], (start, hots, proj), s.stream, s.proj_bytes,
+    )
+    on_chip, sums = exchange(tab, far, start)
     base, near = call(
         base_first_kernel, z, "base_first", [s.base, s.near],
-        (start, on_chip, pot, strength.T), s.stencil, s.slab_bytes, scratch=s.wide,
-    )
-    first, tab = call(
-        first_kernel, z, "first", [s.mate_message, s.tab],
+        (start, on_chip, pot, strength.T), 60 * s.stencil, s.slab_bytes, scratch=s.wide,
+    )
+    first, tab, far = call(
+        first_kernel, z, "first", [s.message, s.tab, s.tile],
         (base,) + sums + (near, hots, proj), 2 * s.stream, s.proj_bytes, scratch=s.acc,
     )
-    first, on_chip, sums = exchange(tab, first)
+    on_chip, sums = exchange(tab, far, first)
     base = call(
-        base_kernel, z, "base", s.base, (first, on_chip, pot), s.stencil, s.slab_bytes, scratch=s.wide,
+        base_kernel, z, "base", s.base, (first, on_chip, pot), 60 * s.stencil, s.slab_bytes, scratch=s.wide,
     )
     filtered = call(
         filtered_kernel, z, "filtered", s.slab, (base,) + sums + (near, hots, proj, start),

time: 72.3 us -> 72.9 us (level)
  the two profiles are of different devices: /device:TPU:56 before, /device:TPU:1 now
where the time goes in v10:
time: 72.9 us; the launch traced here: 72.5 us
  blocking collectives  34.2 us (47%)
  starting transfers between devices  29.4 us (40%)
  Pallas kernels  5.41 us (7%)
  local copies, waits for them, and re-layouts  2.46 us (3%)
    all_to_all x1, blocking collectives, local(): pieces = lax.all_to_all(pieces, 'band', 0, 0, tiled=True)  19.4 us
    all_to_all x1, blocking collectives, local(): rotated = lax.all_to_all(rotated, 'band', 0, 0, tiled=True)  14.8 us
    ppermute x4, starting transfers between devices, swap_on_chip(): return lax.ppermute(x, axis, [(i, i ^ 1) for i in range(count)])  13.7 us
    ppermute x2, starting transfers between devices, swap_far(): lax.ppermute(x, axis, [(i, (i + 2 - 4 * (i % 2)) % count) for i in range(...  9.19 us
    ppermute x2, starting transfers between devices, swap_across(): lax.ppermute(x, axis, [(i, ((i + 1 ^ 1) - 1) % count) for i in range(coun...  6.52 us
    pallas_call x9, Pallas kernels, call(): pl.pallas_call(functools.partial(kernel, z), name=name, out_shape=outs, i...  5.41 us
    unnamed x12, local copies, waits for them, and re-layouts  1.73 us
  transfers between devices with their start and end apart: 8, of which 2 were waited for; matrix products, arithmetic and copies ran while one was open for 0% of the time, Pallas kernels for 2%

profile of v10, /device:TPU:1, one launch (start us, length us, event | category | flops | bytes accessed | tf_op | source)
XLA Modules:
  0.0 72.5 jit_solution(17083268268292842841)
XLA Ops:
  0.0 0.0 copy-start.4
  0.1 0.6 copy-done.3
  0.7 0.3 copy-done.2
  1.0 0.3 prepare.1
  1.2 0.8 %copy-done.1 = bf16[6,16,32,4,128]{4,3,2,1,0:T(4,128)(2,1)S(1)} copy-done((bf16[6,16,32,4,128]{4,3,2,1,0:T(4,128)(2,1)S(1)}, bf16[6,16,32,4,128]{4,3,2,1,0:T(4,128)(2,1)}, u32[]{:S(2)}) %copy-start.1) | copy-done | bytes 3145752
  2.0 1.1 %project.1 = (f32[3,8,128]{2,1,0:T(8,128)S(1)}, f32[8,128]{1,0:T(8,128)S(1)}, bf16[816,128]{1,0:T(8,128)(2,1)S(1)}) custom-call(bf16[768,128]{1,0:T(8,128)(2,1)S(1)} %get-tuple-element.15.v_in, bf16[2,384,128]{2,1,0:T(8,128)(2,1)S(1)} %get-tuple-element.16.hots_ref, bf16[96,128,128]{2,1,0:T(8,128)(2,1)S(1)} %bitcast.31), custom_call_target="tpu_custom_call" | custom-call | flops 25165824 | bytes 3145728 | tf_op jit(solution)/shard_map/project/pallas_call | solution.py:343
  3.1 4.6 %collective-permute-start.1 = (bf16[816,128]{1,0:T(8,128)(2,1)S(1)}, bf16[816,128]{1,0:T(8,128)(2,1)S(1)}, u32[]{:S(2)}, u32[]{:S(2)}) collective-permute-start(bf16[816,128]{1,0:T(8,128)(2,1)S(1)} %get-tuple-element.17.v_ref.start_ref), channel_id=1, source_target_pairs={{0,496},{16,32},{32,16},{48,64},{64,48},{80,96},{96,80},{112,128},... | collective-permute-start | bytes 626696 | tf_op jit(solution)/shard_map/ppermute | solution.py:380
  7.7 6.1 %collective-permute-start = (bf16[816,128]{1,0:T(8,128)(2,1)S(1)}, bf16[816,128]{1,0:T(8,128)(2,1)S(1)}, u32[]{:S(2)}, u32[]{:S(2)}) collective-permute-start(bf16[816,128]{1,0:T(8,128)(2,1)S(1)} %get-tuple-element.17.v_ref.start_ref), channel_id=1, source_target_pairs={{0,16},{16,0},{32,48},{48,32},{64,80},{80,64},{96,112},{112,96},{1... | collective-permute-start | bytes 626696 | tf_op jit(solution)/shard_map/ppermute | solution.py:375
  13.8 5.4 %collective-permute-start.3 = (f32[8,128]{1,0:T(8,128)S(1)}, f32[8,128]{1,0:T(8,128)S(1)}, u32[]{:S(2)}, u32[]{:S(2)}) collective-permute-start(f32[8,128]{1,0:T(8,128)S(1)} %get-tuple-element.20), channel_id=1, source_target_pairs={{0,32},{16,496},{32,64},{48,16},{64,96},{80,48},{96,128},{112,80},... | collective-permute-start | bytes 12296 | tf_op jit(solution)/shard_map/ppermute | solution.py:385
  19.3 1.9 %collective-permute-start.2 = (f32[2,8,128]{2,1,0:T(8,128)S(1)}, f32[2,8,128]{2,1,0:T(8,128)S(1)}, u32[]{:S(2)}, u32[]{:S(2)}) collective-permute-start(f32[2,8,128]{2,1,0:T(8,128)S(1)} %meet.2), channel_id=1, source_target_pairs={{0,16},{16,0},{32,48},{48,32},{64,80},{80,64},{96,112},{112,96},{1... | collective-permute-start | bytes 24584 | tf_op jit(solution)/shard_map/ppermute | solution.py:375
  21.2 0.9 %base_first.1 = (f32[768,128]{1,0:T(8,128)S(1)}, f32[8,128]{1,0:T(8,128)S(1)}) custom-call(bf16[816,128]{1,0:T(8,128)(2,1)S(1)} %get-tuple-element.17.v_ref.start_ref, bf16[816,128]{1,0:T(8,128)(2,1)S(1)} %collective-permute-done.on_ref, f32[96,128]{1,0:T(8,128)S(1)} %bitcast.36, f32[4,1024]{1,0:T(4,128)S(1)} %bitcast.38), custom_call_target="tpu_custom_call" | custom-call | flops 4529848320 | bytes 983040 | tf_op jit(solution)/shard_map/base_first/pallas_call | solution.py:343
  22.1 0.2 collective-permute-done.2.chip_ref
  22.3 1.6 %first.1 = (bf16[816,128]{1,0:T(8,128)(2,1)S(1)}, f32[3,8,128]{2,1,0:T(8,128)S(1)}, f32[8,128]{1,0:T(8,128)S(1)}) custom-call(f32[768,128]{1,0:T(8,128)S(1)} %get-tuple-element.18.base_ref, f32[3,8,128]{2,1,0:T(8,128)S(1)} %get-tuple-element.19.tab_ref.tab_in, f32[2,8,128]{2,1,0:T(8,128)S(1)} %collective-permute-done.2.chip_ref, ...), custom_call_target="tpu_custom_call" | custom-call | flops 50331648 | bytes 3145728 | tf_op jit(solution)/shard_map/first/pallas_call | solution.py:343
  24.0 1.9 %collective-permute-start.5 = (bf16[816,128]{1,0:T(8,128)(2,1)S(1)}, bf16[816,128]{1,0:T(8,128)(2,1)S(1)}, u32[]{:S(2)}, u32[]{:S(2)}) collective-permute-start(bf16[816,128]{1,0:T(8,128)(2,1)S(1)} %get-tuple-element.22.v_ref), channel_id=1, source_target_pairs={{0,496},{16,32},{32,16},{48,64},{64,48},{80,96},{96,80},{112,128},... | collective-permute-start | bytes 626696 | tf_op jit(solution)/shard_map/ppermute | solution.py:380
  25.9 3.7 %collective-permute-start.4 = (bf16[816,128]{1,0:T(8,128)(2,1)S(1)}, bf16[816,128]{1,0:T(8,128)(2,1)S(1)}, u32[]{:S(2)}, u32[]{:S(2)}) collective-permute-start(bf16[816,128]{1,0:T(8,128)(2,1)S(1)} %get-tuple-element.22.v_ref), channel_id=1, source_target_pairs={{0,16},{16,0},{32,48},{48,32},{64,80},{80,64},{96,112},{112,96},{1... | collective-permute-start | bytes 626696 | tf_op jit(solution)/shard_map/ppermute | solution.py:375
  29.7 3.8 %collective-permute-start.7 = (f32[8,128]{1,0:T(8,128)S(1)}, f32[8,128]{1,0:T(8,128)S(1)}, u32[]{:S(2)}, u32[]{:S(2)}) collective-permute-start(f32[8,128]{1,0:T(8,128)S(1)} %get-tuple-element.24), channel_id=1, source_target_pairs={{0,32},{16,496},{32,64},{48,16},{64,96},{80,48},{96,128},{112,80},... | collective-permute-start | bytes 12296 | tf_op jit(solution)/shard_map/ppermute | solution.py:385
  33.5 1.9 %collective-permute-start.6 = (f32[2,8,128]{2,1,0:T(8,128)S(1)}, f32[2,8,128]{2,1,0:T(8,128)S(1)}, u32[]{:S(2)}, u32[]{:S(2)}) collective-permute-start(f32[2,8,128]{2,1,0:T(8,128)S(1)} %meet.3), channel_id=1, source_target_pairs={{0,16},{16,0},{32,48},{48,32},{64,80},{80,64},{96,112},{112,96},{1... | collective-permute-start | bytes 24584 | tf_op jit(solution)/shard_map/ppermute | solution.py:375
  35.5 0.8 %base.1.base_ref = f32[768,128]{1,0:T(8,128)S(1)} custom-call(bf16[816,128]{1,0:T(8,128)(2,1)S(1)} %get-tuple-element.22.v_ref, bf16[816,128]{1,0:T(8,128)(2,1)S(1)} %collective-permute-done.4.on_ref, f32[96,128]{1,0:T(8,128)S(1)} %bitcast.37), custom_call_target="tpu_custom_call" | custom-call | flops 4529848320 | bytes 983040 | tf_op jit(solution)/shard_map/base/pallas_call | solution.py:343
  36.3 0.3 collective-permute-done.6.chip_ref
  36.6 0.7 filtered.1
  37.3 19.4 %all_to_all.10 = bf16[16,6,8,128]{3,2,1,0:T(8,128)(2,1)S(1)} all-to-all(bf16[16,6,8,128]{3,2,1,0:T(8,128)(2,1)S(1)} %bitcast.34), channel_id=1, replica_groups=mesh['dom'=32,'band'=16] {'band'}, dimensions={0} | all-to-all | bytes 393216 | tf_op jit(solution)/shard_map/all_to_all | solution.py:431
  56.6 0.3 fusion.1
  56.9 14.8 %all_to_all.11 = bf16[16,6,8,128]{3,2,1,0:T(8,128)(2,1)S(1)} all-to-all(bf16[16,6,8,128]{3,2,1,0:T(8,128)(2,1)S(1)} %bitcast.39), channel_id=1, replica_groups=mesh['dom'=32,'band'=16] {'band'}, dimensions={0} | all-to-all | bytes 393216 | tf_op jit(solution)/shard_map/all_to_all | solution.py:435
  71.8 0.7 copy.16
  (18 shorter events, 0.1 us)
Async XLA Ops:
  0.0 56.6 %copy-start = (bf16[128,128]{1,0:T(8,128)(2,1)S(1)}, bf16[128,128]{1,0:T(8,128)(2,1)}, u32[]{:S(2)}) copy-start(bf16[128,128]{1,0:T(8,128)(2,1)} %param.11) | copy-start | bytes 98308
  0.0 0.7 copy-start.3
  0.0 0.9 %copy-start.2 = (bf16[8,6,16,128]{3,2,1,0:T(8,128)(2,1)S(1)}, bf16[8,6,16,128]{3,2,1,0:T(8,128)(2,1)}, u32[]{:S(2)}) copy-start(bf16[8,6,16,128]{3,2,1,0:T(8,128)(2,1)} %param.6) | copy-start | bytes 589828
  0.0 2.0 %copy-start.1 = (bf16[6,16,32,4,128]{4,3,2,1,0:T(4,128)(2,1)S(1)}, bf16[6,16,32,4,128]{4,3,2,1,0:T(4,128)(2,1)}, u32[]{:S(2)}) copy-start(bf16[6,16,32,4,128]{4,3,2,1,0:T(4,128)(2,1)} %param.8) | copy-start | bytes 9437188
  0.0 21.2 %copy-start.4 = (f32[6,16,128]{2,1,0:T(8,128)S(1)}, f32[6,16,128]{2,1,0:T(8,128)}, u32[]{:S(2)}) copy-start(f32[6,16,128]{2,1,0:T(8,128)} %param.7) | copy-start | bytes 147460
  0.0 21.2 %copy-start.5 = (f32[1024,4]{0,1:T(4,128)S(1)}, f32[1024,4]{0,1:T(4,128)}, u32[]{:S(2)}) copy-start(f32[1024,4]{0,1:T(4,128)} %param.10) | copy-start | bytes 49156
  3.1 16.1 %collective-permute-start.1 = (bf16[816,128]{1,0:T(8,128)(2,1)S(1)}, bf16[816,128]{1,0:T(8,128)(2,1)S(1)}, u32[]{:S(2)}, u32[]{:S(2)}) collective-permute-start(bf16[816,128]{1,0:T(8,128)(2,1)S(1)} %get-tuple-element.17.v_ref.start_ref), channel_id=1, source_target_pairs={{0,496},{16,32},{32,16},{48,64},{64,48},{80,96},{96,80},{112,128},... | collective-permute-start | bytes 626696 | tf_op jit(solution)/shard_map/ppermute | solution.py:380
  7.7 13.5 %collective-permute-start = (bf16[816,128]{1,0:T(8,128)(2,1)S(1)}, bf16[816,128]{1,0:T(8,128)(2,1)S(1)}, u32[]{:S(2)}, u32[]{:S(2)}) collective-permute-start(bf16[816,128]{1,0:T(8,128)(2,1)S(1)} %get-tuple-element.17.v_ref.start_ref), channel_id=1, source_target_pairs={{0,16},{16,0},{32,48},{48,32},{64,80},{80,64},{96,112},{112,96},{1... | collective-permute-start | bytes 626696 | tf_op jit(solution)/shard_map/ppermute | solution.py:375
  13.8 8.2 %collective-permute-start.3 = (f32[8,128]{1,0:T(8,128)S(1)}, f32[8,128]{1,0:T(8,128)S(1)}, u32[]{:S(2)}, u32[]{:S(2)}) collective-permute-start(f32[8,128]{1,0:T(8,128)S(1)} %get-tuple-element.20), channel_id=1, source_target_pairs={{0,32},{16,496},{32,64},{48,16},{64,96},{80,48},{96,128},{112,80},... | collective-permute-start | bytes 12296 | tf_op jit(solution)/shard_map/ppermute | solution.py:385
  19.3 3.1 %collective-permute-start.2 = (f32[2,8,128]{2,1,0:T(8,128)S(1)}, f32[2,8,128]{2,1,0:T(8,128)S(1)}, u32[]{:S(2)}, u32[]{:S(2)}) collective-permute-start(f32[2,8,128]{2,1,0:T(8,128)S(1)} %meet.2), channel_id=1, source_target_pairs={{0,16},{16,0},{32,48},{48,32},{64,80},{80,64},{96,112},{112,96},{1... | collective-permute-start | bytes 24584 | tf_op jit(solution)/shard_map/ppermute | solution.py:375
  24.0 9.5 %collective-permute-start.5 = (bf16[816,128]{1,0:T(8,128)(2,1)S(1)}, bf16[816,128]{1,0:T(8,128)(2,1)S(1)}, u32[]{:S(2)}, u32[]{:S(2)}) collective-permute-start(bf16[816,128]{1,0:T(8,128)(2,1)S(1)} %get-tuple-element.22.v_ref), channel_id=1, source_target_pairs={{0,496},{16,32},{32,16},{48,64},{64,48},{80,96},{96,80},{112,128},... | collective-permute-start | bytes 626696 | tf_op jit(solution)/shard_map/ppermute | solution.py:380
  25.9 9.5 %collective-permute-start.4 = (bf16[816,128]{1,0:T(8,128)(2,1)S(1)}, bf16[816,128]{1,0:T(8,128)(2,1)S(1)}, u32[]{:S(2)}, u32[]{:S(2)}) collective-permute-start(bf16[816,128]{1,0:T(8,128)(2,1)S(1)} %get-tuple-element.22.v_ref), channel_id=1, source_target_pairs={{0,16},{16,0},{32,48},{48,32},{64,80},{80,64},{96,112},{112,96},{1... | collective-permute-start | bytes 626696 | tf_op jit(solution)/shard_map/ppermute | solution.py:375
  29.7 6.7 %collective-permute-start.7 = (f32[8,128]{1,0:T(8,128)S(1)}, f32[8,128]{1,0:T(8,128)S(1)}, u32[]{:S(2)}, u32[]{:S(2)}) collective-permute-start(f32[8,128]{1,0:T(8,128)S(1)} %get-tuple-element.24), channel_id=1, source_target_pairs={{0,32},{16,496},{32,64},{48,16},{64,96},{80,48},{96,128},{112,80},... | collective-permute-start | bytes 12296 | tf_op jit(solution)/shard_map/ppermute | solution.py:385
  33.5 3.1 %collective-permute-start.6 = (f32[2,8,128]{2,1,0:T(8,128)S(1)}, f32[2,8,128]{2,1,0:T(8,128)S(1)}, u32[]{:S(2)}, u32[]{:S(2)}) collective-permute-start(f32[2,8,128]{2,1,0:T(8,128)S(1)} %meet.3), channel_id=1, source_target_pairs={{0,16},{16,0},{32,48},{48,32},{64,80},{80,64},{96,112},{112,96},{1... | collective-permute-start | bytes 24584 | tf_op jit(solution)/shard_map/ppermute | solution.py:375

commit v11 on v9

--- a/solution.py
+++ b/solution.py
@@ -98,6 +98,16 @@
         tab_ref[t] = total[:, t * z.lanes : (t + 1) * z.lanes]
 
 
+def put_across(z, tab_ref, slab_ref, far_ref):
+    first_core = (lax.axis_index("dom") & 1) == 0
+    pair = [
+        jnp.where(first_core, tab_ref[0], tab_ref[1]),
+        jnp.where(first_core, tab_ref[1], tab_ref[2]),
+    ]
+    put_tiles(z, pair, slab_ref)
+    far_ref[...] = jnp.where(first_core, tab_ref[2], tab_ref[0])
+
+
 def mate_tiles(side, tab_ref):
     first_core = side == 0
     return [
@@ -127,7 +137,32 @@
     return [total[: z.bands], total[z.bands :]]
 
 
-def meet_kernel(z, tab_ref, got_ref, slab_in, slab_ref, chip_ref, far_ref):
+def meet_kernel(z, tab_ref, across_ref, mate_ref):
+    first_core = (lax.axis_index("dom") & 1) == 0
+    got = get_tiles(z, across_ref)
+    mate_ref[0] = jnp.where(first_core, got[1] + tab_ref[1], tab_ref[0])
+    mate_ref[1] = jnp.where(first_core, tab_ref[2], tab_ref[1] + got[0])
+
+
+def gathered(z, tab_ref, mate_ref, across_ref, far_ref, strength_ref, hots_ref):
+    first_core = (lax.axis_index("dom") & 1) == 0
+    got = get_tiles(z, across_ref)
+    below, middle, above = tab_ref[0], tab_ref[1], tab_ref[2]
+    low, high, far = mate_ref[0], mate_ref[1], far_ref[...]
+    tiles = [
+        below + jnp.where(first_core, got[0] + far, low),
+        middle + jnp.where(first_core, got[1] + low, got[0] + high),
+        above + jnp.where(first_core, high, got[1] + far),
+    ]
+    weighted = [tile * strength_ref[t : t + 1, :] for t, tile in enumerate(tiles)]
+    weighted = jnp.concatenate(weighted, 1).astype(BF16)
+    return [
+        jnp.dot(weighted, hots_ref[j], preferred_element_type=F32).astype(BF16)
+        for j in range(z.blocks)
+    ]
+
+
+def meet_second_kernel(z, tab_ref, got_ref, slab_in, slab_ref, chip_ref, far_ref):
     slab_ref[: z.tall, :] = slab_in[: z.tall, :]
     side = lax.axis_index("dom") & 1
     first_core = side == 0
@@ -141,7 +176,7 @@
     put_tiles(z, pair, slab_ref)
 
 
-def gathered(z, tab_ref, chip_ref, across_ref, far_ref, strength_ref, hots_ref):
+def gathered_second(z, tab_ref, chip_ref, across_ref, far_ref, strength_ref, hots_ref):
     first_core = (lax.axis_index("dom") & 1) == 0
     got = get_tiles(z, across_ref)
     low, high, far = chip_ref[0], chip_ref[1], far_ref[...]
@@ -207,12 +242,12 @@
         hots_ref[j] = hot
 
 
-def project_kernel(z, v_in, hots_ref, proj_ref, tab_ref, v_ref):
+def project_kernel(z, v_in, hots_ref, proj_ref, tab_ref, far_ref, v_ref):
     v_ref[: z.tall, :] = v_in[...]
     projector = Projector(z, v_in, proj_ref)
     projector.add(range(z.cells // 2))
     scatter(z, projector.sums(), hots_ref, tab_ref)
-    put_mate(z, tab_ref, v_ref)
+    put_across(z, tab_ref, v_ref, far_ref)
 
 
 def near_strength(z, dom, strength_ref, out_ref):
@@ -329,7 +364,7 @@
     for pair in range(z.cells // 2):
         rows = pair_rows(pair)
         value = acc_ref[rows, :] + nonlocal_pair(weighted[block_of(z, pair)], proj_ref, pair)
-        first_ref[rows, :] = (value / half_width).astype(BF16)
+        first_ref[rows, :] = (value * (1.0 / half_width)).astype(BF16)
     projector = Projector(z, first_ref, proj_ref)
     projector.add(range(z.cells // 2))
     scatter(z, projector.sums(), hots_ref, tab_ref)
@@ -340,11 +375,11 @@
     z, base_ref, tab_ref, chip_ref, across_ref, far_ref, near_ref, hots_ref, proj_ref, start_ref, out_ref, acc_ref
 ):
     add_across(z, base_ref, across_ref, acc_ref)
-    weighted = gathered(z, tab_ref, chip_ref, across_ref, far_ref, near_ref, hots_ref)
+    weighted = gathered_second(z, tab_ref, chip_ref, across_ref, far_ref, near_ref, hots_ref)
     for pair in range(z.cells // 2):
         rows = pair_rows(pair)
         value = acc_ref[rows, :] + nonlocal_pair(weighted[block_of(z, pair)], proj_ref, pair)
-        out_ref[rows, :] = (2.0 * value / half_width - start_ref[rows, :].astype(F32)).astype(BF16)
+        out_ref[rows, :] = (value * (2.0 / half_width) - start_ref[rows, :].astype(F32)).astype(BF16)
 
 
 VMEM = pl.BlockSpec(memory_space=pltpu.VMEM)
@@ -395,6 +430,11 @@
 
 def swap_far(x, axis):
     count = lax.axis_size(axis)
+    return lax.ppermute(x, axis, [(i, (i + 2 - 4 * (i % 2)) % count) for i in range(count)])
+
+
+def swap_crossed(x, axis):
+    count = lax.axis_size(axis)
     return lax.ppermute(x, axis, [(i, (i + 3 - 6 * (i % 2)) % count) for i in range(count)])
 
 
@@ -407,32 +447,39 @@
 
     s = Shapes(z)
 
-    def exchange(tab, slab):
+    def exchange(tab, far, slab):
+        across = swap_across(slab, "dom")
+        far = swap_far(far, "dom")
+        on_chip = swap_on_chip(slab, "dom")
+        mate = call(meet_kernel, z, "meet", s.pair, (tab, across), 1000, 1000)
+        return on_chip, (tab, swap_on_chip(mate, "dom"), across, far)
+
+    def exchange_second(tab, slab):
         on_chip = swap_on_chip(slab, "dom")
         slab, chip, far = call(
-            meet_kernel, z, "meet", [s.message, s.pair, s.tile], (tab, on_chip, slab), 1000, 1000
+            meet_second_kernel, z, "meet_second", [s.message, s.pair, s.tile], (tab, on_chip, slab), 1000, 1000
         )
         across = swap_across(slab, "dom")
-        far = swap_far(far, "dom")
+        far = swap_crossed(far, "dom")
         return slab, on_chip, (tab, chip, across, far)
 
     pause = call(pause_kernel, z, "pause", s.tile, (), 4000 * s.stream, 40_000_000)
     start, hots = call(
         prepare_kernel, z, "prepare", [s.slab, s.hots], (pause, atom_ids, flat), s.stream, s.proj_bytes,
     )
-    tab, start = call(
-        project_kernel, z, "project", [s.tab, s.mate_message], (start, hots, proj), s.stream, s.proj_bytes,
-    )
-    start, on_chip, sums = exchange(tab, start)
+    tab, far, start = call(
+        project_kernel, z, "project", [s.tab, s.tile, s.message], (start, hots, proj), s.stream, s.proj_bytes,
+    )
+    on_chip, sums = exchange(tab, far, start)
     base, near = call(
         base_first_kernel, z, "base_first", [s.base, s.near],
-        (start, on_chip, pot, strength.T), s.stencil, s.slab_bytes, scratch=s.wide,
+        (start, on_chip, pot, strength.T), 60 * s.stencil, s.slab_bytes, scratch=s.wide,
     )
     first, tab = call(
         first_kernel, z, "first", [s.mate_message, s.tab],
         (base,) + sums + (near, hots, proj), 2 * s.stream, s.proj_bytes, scratch=s.acc,
     )
-    first, on_chip, sums = exchange(tab, first)
+    first, on_chip, sums = exchange_second(tab, first)
     base = call(
         base_kernel, z, "base", s.base, (first, on_chip, pot), s.stencil, s.slab_bytes, scratch=s.wide,
     )

time: 72.3 us -> 73.6 us (1.018)
  the two profiles are of different devices: /device:TPU:56 before, /device:TPU:1 now
where the time goes in v11:
time: 73.6 us; the launch traced here: 73.3 us
  blocking collectives  35.1 us (48%)
  starting transfers between devices  26.3 us (36%)
  Pallas kernels  5.44 us (7%)
  waiting for transfers between devices  3.54 us (5%)
  local copies, waits for them, and re-layouts  2.46 us (3%)
    all_to_all x1, blocking collectives, local(): pieces = lax.all_to_all(pieces, 'band', 0, 0, tiled=True)  19.4 us
    all_to_all x1, blocking collectives, local(): rotated = lax.all_to_all(rotated, 'band', 0, 0, tiled=True)  15.7 us
    ppermute x3, starting transfers between devices, swap_on_chip(): return lax.ppermute(x, axis, [(i, i ^ 1) for i in range(count)])  10.2 us
    ppermute x2, starting transfers between devices, swap_across(): lax.ppermute(x, axis, [(i, ((i + 1 ^ 1) - 1) % count) for i in range(coun...  6.51 us
    pallas_call x9, Pallas kernels, call(): pl.pallas_call(functools.partial(kernel, z), name=name, out_shape=outs, i...  5.44 us
    ppermute x1, starting transfers between devices, swap_far(): lax.ppermute(x, axis, [(i, (i + 2 - 4 * (i % 2)) % count) for i in range(...  5.37 us
    ppermute x1, starting transfers between devices, swap_crossed(): lax.ppermute(x, axis, [(i, (i + 3 - 6 * (i % 2)) % count) for i in range(...  4.2 us
    ppermute x1, waiting for transfers between devices, swap_crossed(): lax.ppermute(x, axis, [(i, (i + 3 - 6 * (i % 2)) % count) for i in range(...  2.15 us
  transfers between devices with their start and end apart: 7, of which 3 were waited for; matrix products, arithmetic and copies ran while one was open for 0% of the time, Pallas kernels for 2%

profile of v11, /device:TPU:1, one launch (start us, length us, event | category | flops | bytes accessed | tf_op | source)
XLA Modules:
  0.0 73.3 jit_solution(7563711959703251503)
XLA Ops:
  0.0 0.0 copy-start.3
  0.1 0.6 copy-done.4
  0.7 0.3 copy-done.2
  1.0 0.3 prepare.1
  1.2 0.8 %copy-done.1 = bf16[6,16,32,4,128]{4,3,2,1,0:T(4,128)(2,1)S(1)} copy-done((bf16[6,16,32,4,128]{4,3,2,1,0:T(4,128)(2,1)S(1)}, bf16[6,16,32,4,128]{4,3,2,1,0:T(4,128)(2,1)}, u32[]{:S(2)}) %copy-start.1) | copy-done | bytes 3145752
  2.0 1.1 %project.1 = (f32[3,8,128]{2,1,0:T(8,128)S(1)}, f32[8,128]{1,0:T(8,128)S(1)}, bf16[816,128]{1,0:T(8,128)(2,1)S(1)}) custom-call(bf16[768,128]{1,0:T(8,128)(2,1)S(1)} %get-tuple-element.17.v_in, bf16[2,384,128]{2,1,0:T(8,128)(2,1)S(1)} %get-tuple-element.18.hots_ref, bf16[96,128,128]{2,1,0:T(8,128)(2,1)S(1)} %bitcast.31), custom_call_target="tpu_custom_call" | custom-call | flops 25165824 | bytes 3145728 | tf_op jit(solution)/shard_map/project/pallas_call | solution.py:390
  3.1 4.6 %collective-permute-start.1 = (bf16[816,128]{1,0:T(8,128)(2,1)S(1)}, bf16[816,128]{1,0:T(8,128)(2,1)S(1)}, u32[]{:S(2)}, u32[]{:S(2)}) collective-permute-start(bf16[816,128]{1,0:T(8,128)(2,1)S(1)} %get-tuple-element.19.v_ref.start_ref), channel_id=1, source_target_pairs={{0,496},{16,32},{32,16},{48,64},{64,48},{80,96},{96,80},{112,128},... | collective-permute-start | bytes 626696 | tf_op jit(solution)/shard_map/ppermute | solution.py:428
  7.7 6.1 %collective-permute-start = (bf16[816,128]{1,0:T(8,128)(2,1)S(1)}, bf16[816,128]{1,0:T(8,128)(2,1)S(1)}, u32[]{:S(2)}, u32[]{:S(2)}) collective-permute-start(bf16[816,128]{1,0:T(8,128)(2,1)S(1)} %get-tuple-element.19.v_ref.start_ref), channel_id=1, source_target_pairs={{0,16},{16,0},{32,48},{48,32},{64,80},{80,64},{96,112},{112,96},{1... | collective-permute-start | bytes 626696 | tf_op jit(solution)/shard_map/ppermute | solution.py:423
  13.8 5.4 %collective-permute-start.3 = (f32[8,128]{1,0:T(8,128)S(1)}, f32[8,128]{1,0:T(8,128)S(1)}, u32[]{:S(2)}, u32[]{:S(2)}) collective-permute-start(f32[8,128]{1,0:T(8,128)S(1)} %get-tuple-element.22), channel_id=1, source_target_pairs={{0,32},{16,496},{32,64},{48,16},{64,96},{80,48},{96,128},{112,80},... | collective-permute-start | bytes 12296 | tf_op jit(solution)/shard_map/ppermute | solution.py:433
  19.3 1.9 %collective-permute-start.2 = (f32[2,8,128]{2,1,0:T(8,128)S(1)}, f32[2,8,128]{2,1,0:T(8,128)S(1)}, u32[]{:S(2)}, u32[]{:S(2)}) collective-permute-start(f32[2,8,128]{2,1,0:T(8,128)S(1)} %meet.1), channel_id=1, source_target_pairs={{0,16},{16,0},{32,48},{48,32},{64,80},{80,64},{96,112},{112,96},{1... | collective-permute-start | bytes 24584 | tf_op jit(solution)/shard_map/ppermute | solution.py:423
  21.2 0.9 %base_first.1 = (f32[768,128]{1,0:T(8,128)S(1)}, f32[8,128]{1,0:T(8,128)S(1)}) custom-call(bf16[816,128]{1,0:T(8,128)(2,1)S(1)} %get-tuple-element.19.v_ref.start_ref, bf16[816,128]{1,0:T(8,128)(2,1)S(1)} %collective-permute-done.on_ref, f32[96,128]{1,0:T(8,128)S(1)} %bitcast.36, f32[4,1024]{1,0:T(4,128)S(1)} %bitcast.38), custom_call_target="tpu_custom_call" | custom-call | flops 4529848320 | bytes 983040 | tf_op jit(solution)/shard_map/base_first/pallas_call | solution.py:390
  22.1 0.2 collective-permute-done.2.chip_ref
  22.3 1.6 %first.1 = (bf16[848,128]{1,0:T(8,128)(2,1)S(1)}, f32[3,8,128]{2,1,0:T(8,128)S(1)}) custom-call(f32[768,128]{1,0:T(8,128)S(1)} %get-tuple-element.20.base_ref, f32[3,8,128]{2,1,0:T(8,128)S(1)} %get-tuple-element.21.tab_ref.tab_in, f32[2,8,128]{2,1,0:T(8,128)S(1)} %collective-permute-done.2.chip_ref, bf16[816,128]{1,0:T(8,128)(2,1)S(1)} %collective-permute-done.1.across_ref, ...), custom_call_target="tpu_custom_call" | custom-call | flops 50331648 | bytes 3145728 | tf_op jit(solution)/shard_map/first/pallas_call | solution.py:390
  24.0 2.2 %collective-permute-start.4 = (bf16[848,128]{1,0:T(8,128)(2,1)S(1)}, bf16[848,128]{1,0:T(8,128)(2,1)S(1)}, u32[]{:S(2)}, u32[]{:S(2)}) collective-permute-start(bf16[848,128]{1,0:T(8,128)(2,1)S(1)} %get-tuple-element.25.slab_in), channel_id=1, source_target_pairs={{0,16},{16,0},{32,48},{48,32},{64,80},{80,64},{96,112},{112,96},{1... | collective-permute-start | bytes 651272 | tf_op jit(solution)/shard_map/ppermute | solution.py:423
  26.2 1.2 %collective-permute-done.4.got_ref.on_ref = bf16[848,128]{1,0:T(8,128)(2,1)S(1)} collective-permute-done((bf16[848,128]{1,0:T(8,128)(2,1)S(1)}, bf16[848,128]{1,0:T(8,128)(2,1)S(1)}, u32[]{:S(2)}, u32[]{:S(2)}) %collective-permute-start.4) | collective-permute-done | bytes 217120 | tf_op jit(solution)/shard_map/ppermute | solution.py:423
  27.4 1.9 %collective-permute-start.5 = (bf16[816,128]{1,0:T(8,128)(2,1)S(1)}, bf16[816,128]{1,0:T(8,128)(2,1)S(1)}, u32[]{:S(2)}, u32[]{:S(2)}) collective-permute-start(bf16[816,128]{1,0:T(8,128)(2,1)S(1)} %get-tuple-element.26.v_ref), channel_id=1, source_target_pairs={{0,496},{16,32},{32,16},{48,64},{64,48},{80,96},{96,80},{112,128},... | collective-permute-start | bytes 626696 | tf_op jit(solution)/shard_map/ppermute | solution.py:428
  29.3 4.2 %collective-permute-start.6 = (f32[8,128]{1,0:T(8,128)S(1)}, f32[8,128]{1,0:T(8,128)S(1)}, u32[]{:S(2)}, u32[]{:S(2)}) collective-permute-start(f32[8,128]{1,0:T(8,128)S(1)} %get-tuple-element.28), channel_id=1, source_target_pairs={{0,48},{16,480},{32,80},{48,0},{64,112},{80,32},{96,144},{112,64},... | collective-permute-start | bytes 12296 | tf_op jit(solution)/shard_map/ppermute | solution.py:438
  33.5 0.8 %base.1.base_ref = f32[768,128]{1,0:T(8,128)S(1)} custom-call(bf16[816,128]{1,0:T(8,128)(2,1)S(1)} %get-tuple-element.26.v_ref, bf16[848,128]{1,0:T(8,128)(2,1)S(1)} %collective-permute-done.4.got_ref.on_ref, f32[96,128]{1,0:T(8,128)S(1)} %bitcast.37), custom_call_target="tpu_custom_call" | custom-call | flops 75497472 | bytes 983040 | tf_op jit(solution)/shard_map/base/pallas_call | solution.py:390
  34.3 2.1 %collective-permute-done.6.far_ref = f32[8,128]{1,0:T(8,128)S(1)} collective-permute-done((f32[8,128]{1,0:T(8,128)S(1)}, f32[8,128]{1,0:T(8,128)S(1)}, u32[]{:S(2)}, u32[]{:S(2)}) %collective-permute-start.6) | collective-permute-done | bytes 4128 | tf_op jit(solution)/shard_map/ppermute | solution.py:438
  36.5 0.7 filtered.1
  37.2 19.4 %all_to_all.10 = bf16[16,6,8,128]{3,2,1,0:T(8,128)(2,1)S(1)} all-to-all(bf16[16,6,8,128]{3,2,1,0:T(8,128)(2,1)S(1)} %bitcast.34), channel_id=1, replica_groups=mesh['dom'=32,'band'=16] {'band'}, dimensions={0} | all-to-all | bytes 393216 | tf_op jit(solution)/shard_map/all_to_all | solution.py:493
  56.5 0.3 fusion.1
  56.9 15.7 %all_to_all.11 = bf16[16,6,8,128]{3,2,1,0:T(8,128)(2,1)S(1)} all-to-all(bf16[16,6,8,128]{3,2,1,0:T(8,128)(2,1)S(1)} %bitcast.39), channel_id=1, replica_groups=mesh['dom'=32,'band'=16] {'band'}, dimensions={0} | all-to-all | bytes 393216 | tf_op jit(solution)/shard_map/all_to_all | solution.py:497
  72.6 0.7 copy.16
  (16 shorter events, 0.1 us)
Async XLA Ops:
  0.0 56.5 %copy-start = (bf16[128,128]{1,0:T(8,128)(2,1)S(1)}, bf16[128,128]{1,0:T(8,128)(2,1)}, u32[]{:S(2)}) copy-start(bf16[128,128]{1,0:T(8,128)(2,1)} %param.11) | copy-start | bytes 98308
  0.0 0.7 copy-start.4
  0.0 0.9 %copy-start.2 = (bf16[8,6,16,128]{3,2,1,0:T(8,128)(2,1)S(1)}, bf16[8,6,16,128]{3,2,1,0:T(8,128)(2,1)}, u32[]{:S(2)}) copy-start(bf16[8,6,16,128]{3,2,1,0:T(8,128)(2,1)} %param.6) | copy-start | bytes 589828
  0.0 2.0 %copy-start.1 = (bf16[6,16,32,4,128]{4,3,2,1,0:T(4,128)(2,1)S(1)}, bf16[6,16,32,4,128]{4,3,2,1,0:T(4,128)(2,1)}, u32[]{:S(2)}) copy-start(bf16[6,16,32,4,128]{4,3,2,1,0:T(4,128)(2,1)} %param.8) | copy-start | bytes 9437188
  0.0 21.2 %copy-start.3 = (f32[6,16,128]{2,1,0:T(8,128)S(1)}, f32[6,16,128]{2,1,0:T(8,128)}, u32[]{:S(2)}) copy-start(f32[6,16,128]{2,1,0:T(8,128)} %param.7) | copy-start | bytes 147460
  0.0 21.2 %copy-start.5 = (f32[1024,4]{0,1:T(4,128)S(1)}, f32[1024,4]{0,1:T(4,128)}, u32[]{:S(2)}) copy-start(f32[1024,4]{0,1:T(4,128)} %param.10) | copy-start | bytes 49156
  3.1 16.1 %collective-permute-start.1 = (bf16[816,128]{1,0:T(8,128)(2,1)S(1)}, bf16[816,128]{1,0:T(8,128)(2,1)S(1)}, u32[]{:S(2)}, u32[]{:S(2)}) collective-permute-start(bf16[816,128]{1,0:T(8,128)(2,1)S(1)} %get-tuple-element.19.v_ref.start_ref), channel_id=1, source_target_pairs={{0,496},{16,32},{32,16},{48,64},{64,48},{80,96},{96,80},{112,128},... | collective-permute-start | bytes 626696 | tf_op jit(solution)/shard_map/ppermute | solution.py:428
  7.7 13.5 %collective-permute-start = (bf16[816,128]{1,0:T(8,128)(2,1)S(1)}, bf16[816,128]{1,0:T(8,128)(2,1)S(1)}, u32[]{:S(2)}, u32[]{:S(2)}) collective-permute-start(bf16[816,128]{1,0:T(8,128)(2,1)S(1)} %get-tuple-element.19.v_ref.start_ref), channel_id=1, source_target_pairs={{0,16},{16,0},{32,48},{48,32},{64,80},{80,64},{96,112},{112,96},{1... | collective-permute-start | bytes 626696 | tf_op jit(solution)/shard_map/ppermute | solution.py:423
  13.8 8.2 %collective-permute-start.3 = (f32[8,128]{1,0:T(8,128)S(1)}, f32[8,128]{1,0:T(8,128)S(1)}, u32[]{:S(2)}, u32[]{:S(2)}) collective-permute-start(f32[8,128]{1,0:T(8,128)S(1)} %get-tuple-element.22), channel_id=1, source_target_pairs={{0,32},{16,496},{32,64},{48,16},{64,96},{80,48},{96,128},{112,80},... | collective-permute-start | bytes 12296 | tf_op jit(solution)/shard_map/ppermute | solution.py:433
  19.3 3.1 %collective-permute-start.2 = (f32[2,8,128]{2,1,0:T(8,128)S(1)}, f32[2,8,128]{2,1,0:T(8,128)S(1)}, u32[]{:S(2)}, u32[]{:S(2)}) collective-permute-start(f32[2,8,128]{2,1,0:T(8,128)S(1)} %meet.1), channel_id=1, source_target_pairs={{0,16},{16,0},{32,48},{48,32},{64,80},{80,64},{96,112},{112,96},{1... | collective-permute-start | bytes 24584 | tf_op jit(solution)/shard_map/ppermute | solution.py:423
  24.0 3.4 %collective-permute-start.4 = (bf16[848,128]{1,0:T(8,128)(2,1)S(1)}, bf16[848,128]{1,0:T(8,128)(2,1)S(1)}, u32[]{:S(2)}, u32[]{:S(2)}) collective-permute-start(bf16[848,128]{1,0:T(8,128)(2,1)S(1)} %get-tuple-element.25.slab_in), channel_id=1, source_target_pairs={{0,16},{16,0},{32,48},{48,32},{64,80},{80,64},{96,112},{112,96},{1... | collective-permute-start | bytes 651272 | tf_op jit(solution)/shard_map/ppermute | solution.py:423
  27.4 9.1 %collective-permute-start.5 = (bf16[816,128]{1,0:T(8,128)(2,1)S(1)}, bf16[816,128]{1,0:T(8,128)(2,1)S(1)}, u32[]{:S(2)}, u32[]{:S(2)}) collective-permute-start(bf16[816,128]{1,0:T(8,128)(2,1)S(1)} %get-tuple-element.26.v_ref), channel_id=1, source_target_pairs={{0,496},{16,32},{32,16},{48,64},{64,48},{80,96},{96,80},{112,128},... | collective-permute-start | bytes 626696 | tf_op jit(solution)/shard_map/ppermute | solution.py:428
  29.3 7.2 %collective-permute-start.6 = (f32[8,128]{1,0:T(8,128)S(1)}, f32[8,128]{1,0:T(8,128)S(1)}, u32[]{:S(2)}, u32[]{:S(2)}) collective-permute-start(f32[8,128]{1,0:T(8,128)S(1)} %get-tuple-element.28), channel_id=1, source_target_pairs={{0,48},{16,480},{32,80},{48,0},{64,112},{80,32},{96,144},{112,64},... | collective-permute-start | bytes 12296 | tf_op jit(solution)/shard_map/ppermute | solution.py:438

commit v12 on v9

--- a/solution.py
+++ b/solution.py
@@ -329,7 +329,7 @@
     for pair in range(z.cells // 2):
         rows = pair_rows(pair)
         value = acc_ref[rows, :] + nonlocal_pair(weighted[block_of(z, pair)], proj_ref, pair)
-        first_ref[rows, :] = (value / half_width).astype(BF16)
+        first_ref[rows, :] = (value * (1.0 / half_width)).astype(BF16)
     projector = Projector(z, first_ref, proj_ref)
     projector.add(range(z.cells // 2))
     scatter(z, projector.sums(), hots_ref, tab_ref)
@@ -344,7 +344,7 @@
     for pair in range(z.cells // 2):
         rows = pair_rows(pair)
         value = acc_ref[rows, :] + nonlocal_pair(weighted[block_of(z, pair)], proj_ref, pair)
-        out_ref[rows, :] = (2.0 * value / half_width - start_ref[rows, :].astype(F32)).astype(BF16)
+        out_ref[rows, :] = (value * (2.0 / half_width) - start_ref[rows, :].astype(F32)).astype(BF16)
 
 
 VMEM = pl.BlockSpec(memory_space=pltpu.VMEM)

time: 72.3 us -> 72.3 us (level)
  no operation moved by 1% of the time
where the time goes in v12:
time: 72.3 us; the launch traced here: 72 us
  blocking collectives  39.6 us (55%)
  starting transfers between devices  16.1 us (22%)
  waiting for transfers between devices  7.9 us (11%)
  Pallas kernels  5.46 us (8%)
  local copies, waits for them, and re-layouts  2.46 us (3%)
    all_to_all x1, blocking collectives, local(): pieces = lax.all_to_all(pieces, 'band', 0, 0, tiled=True)  25.1 us
    all_to_all x1, blocking collectives, local(): rotated = lax.all_to_all(rotated, 'band', 0, 0, tiled=True)  14.5 us
    ppermute x2, starting transfers between devices, swap_far(): lax.ppermute(x, axis, [(i, (i + 3 - 6 * (i % 2)) % count) for i in range(...  7.38 us
    pallas_call x9, Pallas kernels, call(): pl.pallas_call(functools.partial(kernel, z), name=name, out_shape=outs, i...  5.46 us
    ppermute x2, waiting for transfers between devices, swap_far(): lax.ppermute(x, axis, [(i, (i + 3 - 6 * (i % 2)) % count) for i in range(...  5.02 us
    ppermute x2, starting transfers between devices, swap_across(): lax.ppermute(x, axis, [(i, ((i + 1 ^ 1) - 1) % count) for i in range(coun...  4.92 us
    ppermute x2, starting transfers between devices, swap_on_chip(): return lax.ppermute(x, axis, [(i, i ^ 1) for i in range(count)])  3.84 us
    ppermute x2, waiting for transfers between devices, swap_on_chip(): return lax.ppermute(x, axis, [(i, i ^ 1) for i in range(count)])  2.87 us
  transfers between devices with their start and end apart: 6, of which 4 were waited for; matrix products, arithmetic and copies ran while one was open for 0% of the time, Pallas kernels for 2%

profile of v12, /device:TPU:56, one launch (start us, length us, event | category | flops | bytes accessed | tf_op | source)
XLA Modules:
  0.0 72.0 jit_solution(15752610505029242981)
XLA Ops:
  0.0 0.0 copy-start.4
  0.1 0.6 copy-done.5
  0.7 0.3 copy-done.2
  1.0 0.3 prepare.1
  1.2 0.8 %copy-done.1 = bf16[6,16,32,4,128]{4,3,2,1,0:T(4,128)(2,1)S(1)} copy-done((bf16[6,16,32,4,128]{4,3,2,1,0:T(4,128)(2,1)S(1)}, bf16[6,16,32,4,128]{4,3,2,1,0:T(4,128)(2,1)}, u32[]{:S(2)}) %copy-start.1) | copy-done | bytes 3145752
  2.0 1.1 %project.1 = (f32[3,8,128]{2,1,0:T(8,128)S(1)}, bf16[848,128]{1,0:T(8,128)(2,1)S(1)}) custom-call(bf16[768,128]{1,0:T(8,128)(2,1)S(1)} %get-tuple-element.19.v_in, bf16[2,384,128]{2,1,0:T(8,128)(2,1)S(1)} %get-tuple-element.20.hots_ref, bf16[96,128,128]{2,1,0:T(8,128)(2,1)S(1)} %bitcast.31), custom_call_target="tpu_custom_call" | custom-call | flops 25165824 | bytes 3145728 | tf_op jit(solution)/shard_map/project/pallas_call | solution.py:355
  3.1 1.9 %collective-permute-start = (bf16[848,128]{1,0:T(8,128)(2,1)S(1)}, bf16[848,128]{1,0:T(8,128)(2,1)S(1)}, u32[]{:S(2)}, u32[]{:S(2)}) collective-permute-start(bf16[848,128]{1,0:T(8,128)(2,1)S(1)} %get-tuple-element.22.slab_in), channel_id=1, source_target_pairs={{0,16},{16,0},{32,48},{48,32},{64,80},{80,64},{96,112},{112,96},{1... | collective-permute-start | bytes 651272 | tf_op jit(solution)/shard_map/ppermute | solution.py:388
  5.1 1.4 %collective-permute-done.got_ref.on_ref = bf16[848,128]{1,0:T(8,128)(2,1)S(1)} collective-permute-done((bf16[848,128]{1,0:T(8,128)(2,1)S(1)}, bf16[848,128]{1,0:T(8,128)(2,1)S(1)}, u32[]{:S(2)}, u32[]{:S(2)}) %collective-permute-start) | collective-permute-done | bytes 217120 | tf_op jit(solution)/shard_map/ppermute | solution.py:388
  6.5 3.0 %collective-permute-start.1 = (bf16[816,128]{1,0:T(8,128)(2,1)S(1)}, bf16[816,128]{1,0:T(8,128)(2,1)S(1)}, u32[]{:S(2)}, u32[]{:S(2)}) collective-permute-start(bf16[816,128]{1,0:T(8,128)(2,1)S(1)} %get-tuple-element.23.v_ref.start_ref), channel_id=1, source_target_pairs={{0,496},{16,32},{32,16},{48,64},{64,48},{80,96},{96,80},{112,128},... | collective-permute-start | bytes 626696 | tf_op jit(solution)/shard_map/ppermute | solution.py:393
  9.5 3.7 %collective-permute-start.2 = (f32[8,128]{1,0:T(8,128)S(1)}, f32[8,128]{1,0:T(8,128)S(1)}, u32[]{:S(2)}, u32[]{:S(2)}) collective-permute-start(f32[8,128]{1,0:T(8,128)S(1)} %get-tuple-element.26), channel_id=1, source_target_pairs={{0,48},{16,480},{32,80},{48,0},{64,112},{80,32},{96,144},{112,64},... | collective-permute-start | bytes 12296 | tf_op jit(solution)/shard_map/ppermute | solution.py:398
  13.2 0.9 %base_first.1 = (f32[768,128]{1,0:T(8,128)S(1)}, f32[8,128]{1,0:T(8,128)S(1)}) custom-call(bf16[816,128]{1,0:T(8,128)(2,1)S(1)} %get-tuple-element.23.v_ref.start_ref, bf16[848,128]{1,0:T(8,128)(2,1)S(1)} %collective-permute-done.got_ref.on_ref, f32[96,128]{1,0:T(8,128)S(1)} %bitcast.36, f32[4,1024]{1,0:T(4,128)S(1)} %bitcast.38), custom_call_target="tpu_custom_call" | custom-call | flops 75497472 | bytes 983040 | tf_op jit(solution)/shard_map/base_first/pallas_call | solution.py:355
  14.1 2.4 %collective-permute-done.2.far_ref = f32[8,128]{1,0:T(8,128)S(1)} collective-permute-done((f32[8,128]{1,0:T(8,128)S(1)}, f32[8,128]{1,0:T(8,128)S(1)}, u32[]{:S(2)}, u32[]{:S(2)}) %collective-permute-start.2) | collective-permute-done | bytes 4128 | tf_op jit(solution)/shard_map/ppermute | solution.py:398
  16.6 1.7 %first.1 = (bf16[848,128]{1,0:T(8,128)(2,1)S(1)}, f32[3,8,128]{2,1,0:T(8,128)S(1)}) custom-call(f32[768,128]{1,0:T(8,128)S(1)} %get-tuple-element.24.base_ref, f32[3,8,128]{2,1,0:T(8,128)S(1)} %get-tuple-element.21.tab_ref.tab_in, f32[2,8,128]{2,1,0:T(8,128)S(1)} %get-tuple-element.25.chip_ref, bf16[816,128]{1,0:T(8,128)(2,1)S(1)} %collective-permute-done.1.across_ref, ...), custom_call_target="tpu_custom_call" | custom-call | flops 50331648 | bytes 3145728 | tf_op jit(solution)/shard_map/first/pallas_call | solution.py:355
  18.2 1.9 %collective-permute-start.3 = (bf16[848,128]{1,0:T(8,128)(2,1)S(1)}, bf16[848,128]{1,0:T(8,128)(2,1)S(1)}, u32[]{:S(2)}, u32[]{:S(2)}) collective-permute-start(bf16[848,128]{1,0:T(8,128)(2,1)S(1)} %get-tuple-element.29.slab_in), channel_id=1, source_target_pairs={{0,16},{16,0},{32,48},{48,32},{64,80},{80,64},{96,112},{112,96},{1... | collective-permute-start | bytes 651272 | tf_op jit(solution)/shard_map/ppermute | solution.py:388
  20.1 1.4 %collective-permute-done.3.got_ref.on_ref = bf16[848,128]{1,0:T(8,128)(2,1)S(1)} collective-permute-done((bf16[848,128]{1,0:T(8,128)(2,1)S(1)}, bf16[848,128]{1,0:T(8,128)(2,1)S(1)}, u32[]{:S(2)}, u32[]{:S(2)}) %collective-permute-start.3) | collective-permute-done | bytes 217120 | tf_op jit(solution)/shard_map/ppermute | solution.py:388
  21.6 1.9 %collective-permute-start.4 = (bf16[816,128]{1,0:T(8,128)(2,1)S(1)}, bf16[816,128]{1,0:T(8,128)(2,1)S(1)}, u32[]{:S(2)}, u32[]{:S(2)}) collective-permute-start(bf16[816,128]{1,0:T(8,128)(2,1)S(1)} %get-tuple-element.30.v_ref), channel_id=1, source_target_pairs={{0,496},{16,32},{32,16},{48,64},{64,48},{80,96},{96,80},{112,128},... | collective-permute-start | bytes 626696 | tf_op jit(solution)/shard_map/ppermute | solution.py:393
  23.5 3.7 %collective-permute-start.5 = (f32[8,128]{1,0:T(8,128)S(1)}, f32[8,128]{1,0:T(8,128)S(1)}, u32[]{:S(2)}, u32[]{:S(2)}) collective-permute-start(f32[8,128]{1,0:T(8,128)S(1)} %get-tuple-element.32), channel_id=1, source_target_pairs={{0,48},{16,480},{32,80},{48,0},{64,112},{80,32},{96,144},{112,64},... | collective-permute-start | bytes 12296 | tf_op jit(solution)/shard_map/ppermute | solution.py:398
  27.2 0.9 %base.1.base_ref = f32[768,128]{1,0:T(8,128)S(1)} custom-call(bf16[816,128]{1,0:T(8,128)(2,1)S(1)} %get-tuple-element.30.v_ref, bf16[848,128]{1,0:T(8,128)(2,1)S(1)} %collective-permute-done.3.got_ref.on_ref, f32[96,128]{1,0:T(8,128)S(1)} %bitcast.37), custom_call_target="tpu_custom_call" | custom-call | flops 75497472 | bytes 983040 | tf_op jit(solution)/shard_map/base/pallas_call | solution.py:355
  28.1 2.6 %collective-permute-done.5.far_ref = f32[8,128]{1,0:T(8,128)S(1)} collective-permute-done((f32[8,128]{1,0:T(8,128)S(1)}, f32[8,128]{1,0:T(8,128)S(1)}, u32[]{:S(2)}, u32[]{:S(2)}) %collective-permute-start.5) | collective-permute-done | bytes 4128 | tf_op jit(solution)/shard_map/ppermute | solution.py:398
  30.7 0.7 filtered.1
  31.4 25.1 %all_to_all.10 = bf16[16,6,8,128]{3,2,1,0:T(8,128)(2,1)S(1)} all-to-all(bf16[16,6,8,128]{3,2,1,0:T(8,128)(2,1)S(1)} %bitcast.34), channel_id=1, replica_groups=mesh['dom'=32,'band'=16] {'band'}, dimensions={0} | all-to-all | bytes 393216 | tf_op jit(solution)/shard_map/all_to_all | solution.py:446
  56.5 0.3 fusion.1
  56.8 14.5 %all_to_all.11 = bf16[16,6,8,128]{3,2,1,0:T(8,128)(2,1)S(1)} all-to-all(bf16[16,6,8,128]{3,2,1,0:T(8,128)(2,1)S(1)} %bitcast.39), channel_id=1, replica_groups=mesh['dom'=32,'band'=16] {'band'}, dimensions={0} | all-to-all | bytes 393216 | tf_op jit(solution)/shard_map/all_to_all | solution.py:450
  71.3 0.7 copy.16
  (14 shorter events, 0.1 us)
Async XLA Ops:
  0.0 56.5 %copy-start = (bf16[128,128]{1,0:T(8,128)(2,1)S(1)}, bf16[128,128]{1,0:T(8,128)(2,1)}, u32[]{:S(2)}) copy-start(bf16[128,128]{1,0:T(8,128)(2,1)} %param.11) | copy-start | bytes 98308
  0.0 0.7 copy-start.5
  0.0 0.9 %copy-start.2 = (bf16[8,6,16,128]{3,2,1,0:T(8,128)(2,1)S(1)}, bf16[8,6,16,128]{3,2,1,0:T(8,128)(2,1)}, u32[]{:S(2)}) copy-start(bf16[8,6,16,128]{3,2,1,0:T(8,128)(2,1)} %param.6) | copy-start | bytes 589828
  0.0 2.0 %copy-start.1 = (bf16[6,16,32,4,128]{4,3,2,1,0:T(4,128)(2,1)S(1)}, bf16[6,16,32,4,128]{4,3,2,1,0:T(4,128)(2,1)}, u32[]{:S(2)}) copy-start(bf16[6,16,32,4,128]{4,3,2,1,0:T(4,128)(2,1)} %param.8) | copy-start | bytes 9437188
  0.0 13.2 %copy-start.3 = (f32[6,16,128]{2,1,0:T(8,128)S(1)}, f32[6,16,128]{2,1,0:T(8,128)}, u32[]{:S(2)}) copy-start(f32[6,16,128]{2,1,0:T(8,128)} %param.7) | copy-start | bytes 147460
  0.0 13.2 %copy-start.4 = (f32[1024,4]{0,1:T(4,128)S(1)}, f32[1024,4]{0,1:T(4,128)}, u32[]{:S(2)}) copy-start(f32[1024,4]{0,1:T(4,128)} %param.10) | copy-start | bytes 49156
  3.1 3.4 %collective-permute-start = (bf16[848,128]{1,0:T(8,128)(2,1)S(1)}, bf16[848,128]{1,0:T(8,128)(2,1)S(1)}, u32[]{:S(2)}, u32[]{:S(2)}) collective-permute-start(bf16[848,128]{1,0:T(8,128)(2,1)S(1)} %get-tuple-element.22.slab_in), channel_id=1, source_target_pairs={{0,16},{16,0},{32,48},{48,32},{64,80},{80,64},{96,112},{112,96},{1... | collective-permute-start | bytes 651272 | tf_op jit(solution)/shard_map/ppermute | solution.py:388
  6.5 10.0 %collective-permute-start.1 = (bf16[816,128]{1,0:T(8,128)(2,1)S(1)}, bf16[816,128]{1,0:T(8,128)(2,1)S(1)}, u32[]{:S(2)}, u32[]{:S(2)}) collective-permute-start(bf16[816,128]{1,0:T(8,128)(2,1)S(1)} %get-tuple-element.23.v_ref.start_ref), channel_id=1, source_target_pairs={{0,496},{16,32},{32,16},{48,64},{64,48},{80,96},{96,80},{112,128},... | collective-permute-start | bytes 626696 | tf_op jit(solution)/shard_map/ppermute | solution.py:393
  9.5 7.0 %collective-permute-start.2 = (f32[8,128]{1,0:T(8,128)S(1)}, f32[8,128]{1,0:T(8,128)S(1)}, u32[]{:S(2)}, u32[]{:S(2)}) collective-permute-start(f32[8,128]{1,0:T(8,128)S(1)} %get-tuple-element.26), channel_id=1, source_target_pairs={{0,48},{16,480},{32,80},{48,0},{64,112},{80,32},{96,144},{112,64},... | collective-permute-start | bytes 12296 | tf_op jit(solution)/shard_map/ppermute | solution.py:398
  18.2 3.4 %collective-permute-start.3 = (bf16[848,128]{1,0:T(8,128)(2,1)S(1)}, bf16[848,128]{1,0:T(8,128)(2,1)S(1)}, u32[]{:S(2)}, u32[]{:S(2)}) collective-permute-start(bf16[848,128]{1,0:T(8,128)(2,1)S(1)} %get-tuple-element.29.slab_in), channel_id=1, source_target_pairs={{0,16},{16,0},{32,48},{48,32},{64,80},{80,64},{96,112},{112,96},{1... | collective-permute-start | bytes 651272 | tf_op jit(solution)/shard_map/ppermute | solution.py:388
  21.6 9.1 %collective-permute-start.4 = (bf16[816,128]{1,0:T(8,128)(2,1)S(1)}, bf16[816,128]{1,0:T(8,128)(2,1)S(1)}, u32[]{:S(2)}, u32[]{:S(2)}) collective-permute-start(bf16[816,128]{1,0:T(8,128)(2,1)S(1)} %get-tuple-element.30.v_ref), channel_id=1, source_target_pairs={{0,496},{16,32},{32,16},{48,64},{64,48},{80,96},{96,80},{112,128},... | collective-permute-start | bytes 626696 | tf_op jit(solution)/shard_map/ppermute | solution.py:393
  23.5 7.1 %collective-permute-start.5 = (f32[8,128]{1,0:T(8,128)S(1)}, f32[8,128]{1,0:T(8,128)S(1)}, u32[]{:S(2)}, u32[]{:S(2)}) collective-permute-start(f32[8,128]{1,0:T(8,128)S(1)} %get-tuple-element.32), channel_id=1, source_target_pairs={{0,48},{16,480},{32,80},{48,0},{64,112},{80,32},{96,144},{112,64},... | collective-permute-start | bytes 12296 | tf_op jit(solution)/shard_map/ppermute | solution.py:398

commit v13 on v12

--- a/solution.py
+++ b/solution.py
@@ -347,17 +347,30 @@
         out_ref[rows, :] = (value * (2.0 / half_width) - start_ref[rows, :].astype(F32)).astype(BF16)
 
 
+def final_kernel(z, in_ref, out_hbm, out_ref, sems):
+    tall = z.rows * z.bands
+    writes = []
+    for x in range(z.thickness):
+        plane = in_ref[x * tall : (x + 1) * tall, :].astype(F32).reshape(z.rows, z.bands, z.depth)
+        at = pl.ds(x * z.rows, z.rows)
+        out_ref[:, at, :] = jnp.swapaxes(plane, 0, 1).astype(BF16)
+        writes.append(pltpu.make_async_copy(out_ref.at[:, at, :], out_hbm.at[:, at, :], sems.at[x]))
+        writes[-1].start()
+    for write in writes:
+        write.wait()
+
+
 VMEM = pl.BlockSpec(memory_space=pltpu.VMEM)
 
 
-def call(kernel, z, name, outs, ins, flops, moved, scratch=()):
+def call(kernel, z, name, outs, ins, flops, moved, scratch=(), out_space=None):
     single = not isinstance(outs, (list, tuple))
     return pl.pallas_call(
         functools.partial(kernel, z),
         name=name,
         out_shape=outs,
         in_specs=[VMEM] * len(ins),
-        out_specs=VMEM if single else [VMEM] * len(outs),
+        out_specs=(out_space or VMEM) if single else [VMEM] * len(outs),
         scratch_shapes=list(scratch),
         compiler_params=pltpu.CompilerParams(vmem_limit_bytes=12288 * 1024),
         cost_estimate=pl.CostEstimate(flops=flops, bytes_accessed=moved, transcendentals=0),
@@ -448,7 +461,16 @@
     rotated = jnp.einsum("gxbz,gbc->xcz", pieces, turn, preferred_element_type=F32).astype(BF16)
     rotated = rotated.reshape(share, groups, z.bands, z.depth).transpose(1, 0, 2, 3)
     rotated = lax.all_to_all(rotated, "band", 0, 0, tiled=True)
-    return rotated.reshape(z.cells, z.bands, z.depth).transpose(1, 0, 2).reshape(bands.shape)
+    out = call(
+        final_kernel, z, "final", jax.ShapeDtypeStruct((z.bands, z.cells, z.depth), BF16),
+        (rotated.reshape(z.tall, z.depth),), 1000, 4 * z.tall * z.depth,
+        scratch=[
+            pltpu.VMEM((z.bands, z.cells, z.depth), BF16),
+            pltpu.SemaphoreType.DMA((z.thickness,)),
+        ],
+        out_space=pl.BlockSpec(memory_space=pltpu.HBM),
+    )
+    return out.reshape(bands.shape)
 
 
 def solution(mesh):

time: 72.3 us -> 72.4 us (level)
  Pallas kernels: 5.46 us -> 6.22 us
    pallas_call x9 -> x10, Pallas kernels: 5.46 us -> 6.22 us  [call(): pl.pallas_call(functools.partial(kernel, z), name=name, out_shape=outs, i...]
where the time goes in v13:
time: 72.4 us; the launch traced here: 72 us
  blocking collectives  39.6 us (55%)
  starting transfers between devices  16.1 us (22%)
  waiting for transfers between devices  7.9 us (11%)
  Pallas kernels  6.22 us (9%)
  local copies, waits for them, and re-layouts  1.76 us (2%)
    all_to_all x1, blocking collectives, local(): pieces = lax.all_to_all(pieces, 'band', 0, 0, tiled=True)  25.1 us
    all_to_all x1, blocking collectives, local(): rotated = lax.all_to_all(rotated, 'band', 0, 0, tiled=True)  14.5 us
    ppermute x2, starting transfers between devices, swap_far(): lax.ppermute(x, axis, [(i, (i + 3 - 6 * (i % 2)) % count) for i in range(...  7.38 us
    pallas_call x10, Pallas kernels, call(): pl.pallas_call(functools.partial(kernel, z), name=name, out_shape=outs, i...  6.22 us
    ppermute x2, waiting for transfers between devices, swap_far(): lax.ppermute(x, axis, [(i, (i + 3 - 6 * (i % 2)) % count) for i in range(...  5.02 us
    ppermute x2, starting transfers between devices, swap_across(): lax.ppermute(x, axis, [(i, ((i + 1 ^ 1) - 1) % count) for i in range(coun...  4.92 us
    ppermute x2, starting transfers between devices, swap_on_chip(): return lax.ppermute(x, axis, [(i, i ^ 1) for i in range(count)])  3.84 us
    ppermute x2, waiting for transfers between devices, swap_on_chip(): return lax.ppermute(x, axis, [(i, i ^ 1) for i in range(count)])  2.87 us
  transfers between devices with their start and end apart: 6, of which 4 were waited for; matrix products, arithmetic and copies ran while one was open for 0% of the time, Pallas kernels for 2%

profile of v13, /device:TPU:56, one launch (start us, length us, event | category | flops | bytes accessed | tf_op | source)
XLA Modules:
  0.0 72.0 jit_solution(15689348786224342007)
XLA Ops:
  0.0 0.0 copy-start.4
  0.1 0.6 copy-done.5
  0.7 0.3 copy-done.2
  1.0 0.3 prepare.1
  1.2 0.8 %copy-done.1 = bf16[6,16,32,4,128]{4,3,2,1,0:T(4,128)(2,1)S(1)} copy-done((bf16[6,16,32,4,128]{4,3,2,1,0:T(4,128)(2,1)S(1)}, bf16[6,16,32,4,128]{4,3,2,1,0:T(4,128)(2,1)}, u32[]{:S(2)}) %copy-start.1) | copy-done | bytes 3145752
  2.0 1.1 %project.1 = (f32[3,8,128]{2,1,0:T(8,128)S(1)}, bf16[848,128]{1,0:T(8,128)(2,1)S(1)}) custom-call(bf16[768,128]{1,0:T(8,128)(2,1)S(1)} %get-tuple-element.19.v_in, bf16[2,384,128]{2,1,0:T(8,128)(2,1)S(1)} %get-tuple-element.20.hots_ref, bf16[96,128,128]{2,1,0:T(8,128)(2,1)S(1)} %bitcast.28), custom_call_target="tpu_custom_call" | custom-call | flops 25165824 | bytes 3145728 | tf_op jit(solution)/shard_map/project/pallas_call | solution.py:368
  3.1 1.9 %collective-permute-start = (bf16[848,128]{1,0:T(8,128)(2,1)S(1)}, bf16[848,128]{1,0:T(8,128)(2,1)S(1)}, u32[]{:S(2)}, u32[]{:S(2)}) collective-permute-start(bf16[848,128]{1,0:T(8,128)(2,1)S(1)} %get-tuple-element.22.slab_in), channel_id=1, source_target_pairs={{0,16},{16,0},{32,48},{48,32},{64,80},{80,64},{96,112},{112,96},{1... | collective-permute-start | bytes 651272 | tf_op jit(solution)/shard_map/ppermute | solution.py:401
  5.1 1.4 %collective-permute-done.got_ref.on_ref = bf16[848,128]{1,0:T(8,128)(2,1)S(1)} collective-permute-done((bf16[848,128]{1,0:T(8,128)(2,1)S(1)}, bf16[848,128]{1,0:T(8,128)(2,1)S(1)}, u32[]{:S(2)}, u32[]{:S(2)}) %collective-permute-start) | collective-permute-done | bytes 217120 | tf_op jit(solution)/shard_map/ppermute | solution.py:401
  6.5 3.0 %collective-permute-start.1 = (bf16[816,128]{1,0:T(8,128)(2,1)S(1)}, bf16[816,128]{1,0:T(8,128)(2,1)S(1)}, u32[]{:S(2)}, u32[]{:S(2)}) collective-permute-start(bf16[816,128]{1,0:T(8,128)(2,1)S(1)} %get-tuple-element.23.v_ref.start_ref), channel_id=1, source_target_pairs={{0,496},{16,32},{32,16},{48,64},{64,48},{80,96},{96,80},{112,128},... | collective-permute-start | bytes 626696 | tf_op jit(solution)/shard_map/ppermute | solution.py:406
  9.5 3.7 %collective-permute-start.2 = (f32[8,128]{1,0:T(8,128)S(1)}, f32[8,128]{1,0:T(8,128)S(1)}, u32[]{:S(2)}, u32[]{:S(2)}) collective-permute-start(f32[8,128]{1,0:T(8,128)S(1)} %get-tuple-element.26), channel_id=1, source_target_pairs={{0,48},{16,480},{32,80},{48,0},{64,112},{80,32},{96,144},{112,64},... | collective-permute-start | bytes 12296 | tf_op jit(solution)/shard_map/ppermute | solution.py:411
  13.2 0.9 %base_first.1 = (f32[768,128]{1,0:T(8,128)S(1)}, f32[8,128]{1,0:T(8,128)S(1)}) custom-call(bf16[816,128]{1,0:T(8,128)(2,1)S(1)} %get-tuple-element.23.v_ref.start_ref, bf16[848,128]{1,0:T(8,128)(2,1)S(1)} %collective-permute-done.got_ref.on_ref, f32[96,128]{1,0:T(8,128)S(1)} %bitcast.34, f32[4,1024]{1,0:T(4,128)S(1)} %bitcast.36), custom_call_target="tpu_custom_call" | custom-call | flops 75497472 | bytes 983040 | tf_op jit(solution)/shard_map/base_first/pallas_call | solution.py:368
  14.1 2.4 %collective-permute-done.2.far_ref = f32[8,128]{1,0:T(8,128)S(1)} collective-permute-done((f32[8,128]{1,0:T(8,128)S(1)}, f32[8,128]{1,0:T(8,128)S(1)}, u32[]{:S(2)}, u32[]{:S(2)}) %collective-permute-start.2) | collective-permute-done | bytes 4128 | tf_op jit(solution)/shard_map/ppermute | solution.py:411
  16.6 1.7 %first.1 = (bf16[848,128]{1,0:T(8,128)(2,1)S(1)}, f32[3,8,128]{2,1,0:T(8,128)S(1)}) custom-call(f32[768,128]{1,0:T(8,128)S(1)} %get-tuple-element.24.base_ref, f32[3,8,128]{2,1,0:T(8,128)S(1)} %get-tuple-element.21.tab_ref.tab_in, f32[2,8,128]{2,1,0:T(8,128)S(1)} %get-tuple-element.25.chip_ref, bf16[816,128]{1,0:T(8,128)(2,1)S(1)} %collective-permute-done.1.across_ref, ...), custom_call_target="tpu_custom_call" | custom-call | flops 50331648 | bytes 3145728 | tf_op jit(solution)/shard_map/first/pallas_call | solution.py:368
  18.2 1.9 %collective-permute-start.3 = (bf16[848,128]{1,0:T(8,128)(2,1)S(1)}, bf16[848,128]{1,0:T(8,128)(2,1)S(1)}, u32[]{:S(2)}, u32[]{:S(2)}) collective-permute-start(bf16[848,128]{1,0:T(8,128)(2,1)S(1)} %get-tuple-element.29.slab_in), channel_id=1, source_target_pairs={{0,16},{16,0},{32,48},{48,32},{64,80},{80,64},{96,112},{112,96},{1... | collective-permute-start | bytes 651272 | tf_op jit(solution)/shard_map/ppermute | solution.py:401
  20.1 1.4 %collective-permute-done.3.got_ref.on_ref = bf16[848,128]{1,0:T(8,128)(2,1)S(1)} collective-permute-done((bf16[848,128]{1,0:T(8,128)(2,1)S(1)}, bf16[848,128]{1,0:T(8,128)(2,1)S(1)}, u32[]{:S(2)}, u32[]{:S(2)}) %collective-permute-start.3) | collective-permute-done | bytes 217120 | tf_op jit(solution)/shard_map/ppermute | solution.py:401
  21.6 1.9 %collective-permute-start.4 = (bf16[816,128]{1,0:T(8,128)(2,1)S(1)}, bf16[816,128]{1,0:T(8,128)(2,1)S(1)}, u32[]{:S(2)}, u32[]{:S(2)}) collective-permute-start(bf16[816,128]{1,0:T(8,128)(2,1)S(1)} %get-tuple-element.30.v_ref), channel_id=1, source_target_pairs={{0,496},{16,32},{32,16},{48,64},{64,48},{80,96},{96,80},{112,128},... | collective-permute-start | bytes 626696 | tf_op jit(solution)/shard_map/ppermute | solution.py:406
  23.5 3.7 %collective-permute-start.5 = (f32[8,128]{1,0:T(8,128)S(1)}, f32[8,128]{1,0:T(8,128)S(1)}, u32[]{:S(2)}, u32[]{:S(2)}) collective-permute-start(f32[8,128]{1,0:T(8,128)S(1)} %get-tuple-element.32), channel_id=1, source_target_pairs={{0,48},{16,480},{32,80},{48,0},{64,112},{80,32},{96,144},{112,64},... | collective-permute-start | bytes 12296 | tf_op jit(solution)/shard_map/ppermute | solution.py:411
  27.2 0.9 %base.1.base_ref = f32[768,128]{1,0:T(8,128)S(1)} custom-call(bf16[816,128]{1,0:T(8,128)(2,1)S(1)} %get-tuple-element.30.v_ref, bf16[848,128]{1,0:T(8,128)(2,1)S(1)} %collective-permute-done.3.got_ref.on_ref, f32[96,128]{1,0:T(8,128)S(1)} %bitcast.35), custom_call_target="tpu_custom_call" | custom-call | flops 75497472 | bytes 983040 | tf_op jit(solution)/shard_map/base/pallas_call | solution.py:368
  28.1 2.6 %collective-permute-done.5.far_ref = f32[8,128]{1,0:T(8,128)S(1)} collective-permute-done((f32[8,128]{1,0:T(8,128)S(1)}, f32[8,128]{1,0:T(8,128)S(1)}, u32[]{:S(2)}, u32[]{:S(2)}) %collective-permute-start.5) | collective-permute-done | bytes 4128 | tf_op jit(solution)/shard_map/ppermute | solution.py:411
  30.7 0.7 filtered.1
  31.4 25.1 %all_to_all.10 = bf16[16,6,8,128]{3,2,1,0:T(8,128)(2,1)S(1)} all-to-all(bf16[16,6,8,128]{3,2,1,0:T(8,128)(2,1)S(1)} %bitcast.31), channel_id=1, replica_groups=mesh['dom'=32,'band'=16] {'band'}, dimensions={0} | all-to-all | bytes 393216 | tf_op jit(solution)/shard_map/all_to_all | solution.py:459
  56.5 0.3 fusion.1
  56.8 14.5 %all_to_all.11 = bf16[16,6,8,128]{3,2,1,0:T(8,128)(2,1)S(1)} all-to-all(bf16[16,6,8,128]{3,2,1,0:T(8,128)(2,1)S(1)} %bitcast.37), channel_id=1, replica_groups=mesh['dom'=32,'band'=16] {'band'}, dimensions={0} | all-to-all | bytes 393216 | tf_op jit(solution)/shard_map/all_to_all | solution.py:463
  71.3 0.8 %final.1 = bf16[8,96,128]{2,1,0:T(8,128)(2,1)} custom-call(bf16[768,128]{1,0:T(8,128)(2,1)S(1)} %bitcast.32), custom_call_target="tpu_custom_call" | custom-call | flops 1000 | bytes 393216 | tf_op jit(solution)/shard_map/final/pallas_call | solution.py:368
  (14 shorter events, 0.1 us)
Async XLA Ops:
  0.0 56.5 %copy-start = (bf16[128,128]{1,0:T(8,128)(2,1)S(1)}, bf16[128,128]{1,0:T(8,128)(2,1)}, u32[]{:S(2)}) copy-start(bf16[128,128]{1,0:T(8,128)(2,1)} %param.11) | copy-start | bytes 98308
  0.0 0.7 copy-start.5
  0.0 0.9 %copy-start.2 = (bf16[8,6,16,128]{3,2,1,0:T(8,128)(2,1)S(1)}, bf16[8,6,16,128]{3,2,1,0:T(8,128)(2,1)}, u32[]{:S(2)}) copy-start(bf16[8,6,16,128]{3,2,1,0:T(8,128)(2,1)} %param.6) | copy-start | bytes 589828
  0.0 2.0 %copy-start.1 = (bf16[6,16,32,4,128]{4,3,2,1,0:T(4,128)(2,1)S(1)}, bf16[6,16,32,4,128]{4,3,2,1,0:T(4,128)(2,1)}, u32[]{:S(2)}) copy-start(bf16[6,16,32,4,128]{4,3,2,1,0:T(4,128)(2,1)} %param.8) | copy-start | bytes 9437188
  0.0 13.2 %copy-start.3 = (f32[6,16,128]{2,1,0:T(8,128)S(1)}, f32[6,16,128]{2,1,0:T(8,128)}, u32[]{:S(2)}) copy-start(f32[6,16,128]{2,1,0:T(8,128)} %param.7) | copy-start | bytes 147460
  0.0 13.2 %copy-start.4 = (f32[1024,4]{0,1:T(4,128)S(1)}, f32[1024,4]{0,1:T(4,128)}, u32[]{:S(2)}) copy-start(f32[1024,4]{0,1:T(4,128)} %param.10) | copy-start | bytes 49156
  3.1 3.4 %collective-permute-start = (bf16[848,128]{1,0:T(8,128)(2,1)S(1)}, bf16[848,128]{1,0:T(8,128)(2,1)S(1)}, u32[]{:S(2)}, u32[]{:S(2)}) collective-permute-start(bf16[848,128]{1,0:T(8,128)(2,1)S(1)} %get-tuple-element.22.slab_in), channel_id=1, source_target_pairs={{0,16},{16,0},{32,48},{48,32},{64,80},{80,64},{96,112},{112,96},{1... | collective-permute-start | bytes 651272 | tf_op jit(solution)/shard_map/ppermute | solution.py:401
  6.5 10.0 %collective-permute-start.1 = (bf16[816,128]{1,0:T(8,128)(2,1)S(1)}, bf16[816,128]{1,0:T(8,128)(2,1)S(1)}, u32[]{:S(2)}, u32[]{:S(2)}) collective-permute-start(bf16[816,128]{1,0:T(8,128)(2,1)S(1)} %get-tuple-element.23.v_ref.start_ref), channel_id=1, source_target_pairs={{0,496},{16,32},{32,16},{48,64},{64,48},{80,96},{96,80},{112,128},... | collective-permute-start | bytes 626696 | tf_op jit(solution)/shard_map/ppermute | solution.py:406
  9.5 7.0 %collective-permute-start.2 = (f32[8,128]{1,0:T(8,128)S(1)}, f32[8,128]{1,0:T(8,128)S(1)}, u32[]{:S(2)}, u32[]{:S(2)}) collective-permute-start(f32[8,128]{1,0:T(8,128)S(1)} %get-tuple-element.26), channel_id=1, source_target_pairs={{0,48},{16,480},{32,80},{48,0},{64,112},{80,32},{96,144},{112,64},... | collective-permute-start | bytes 12296 | tf_op jit(solution)/shard_map/ppermute | solution.py:411
  18.2 3.4 %collective-permute-start.3 = (bf16[848,128]{1,0:T(8,128)(2,1)S(1)}, bf16[848,128]{1,0:T(8,128)(2,1)S(1)}, u32[]{:S(2)}, u32[]{:S(2)}) collective-permute-start(bf16[848,128]{1,0:T(8,128)(2,1)S(1)} %get-tuple-element.29.slab_in), channel_id=1, source_target_pairs={{0,16},{16,0},{32,48},{48,32},{64,80},{80,64},{96,112},{112,96},{1... | collective-permute-start | bytes 651272 | tf_op jit(solution)/shard_map/ppermute | solution.py:401
  21.6 9.1 %collective-permute-start.4 = (bf16[816,128]{1,0:T(8,128)(2,1)S(1)}, bf16[816,128]{1,0:T(8,128)(2,1)S(1)}, u32[]{:S(2)}, u32[]{:S(2)}) collective-permute-start(bf16[816,128]{1,0:T(8,128)(2,1)S(1)} %get-tuple-element.30.v_ref), channel_id=1, source_target_pairs={{0,496},{16,32},{32,16},{48,64},{64,48},{80,96},{96,80},{112,128},... | collective-permute-start | bytes 626696 | tf_op jit(solution)/shard_map/ppermute | solution.py:406
  23.5 7.1 %collective-permute-start.5 = (f32[8,128]{1,0:T(8,128)S(1)}, f32[8,128]{1,0:T(8,128)S(1)}, u32[]{:S(2)}, u32[]{:S(2)}) collective-permute-start(f32[8,128]{1,0:T(8,128)S(1)} %get-tuple-element.32), channel_id=1, source_target_pairs={{0,48},{16,480},{32,80},{48,0},{64,112},{80,32},{96,144},{112,64},... | collective-permute-start | bytes 12296 | tf_op jit(solution)/shard_map/ppermute | solution.py:411

commit v14 on v12

--- a/solution.py
+++ b/solution.py
@@ -324,8 +324,8 @@
 def first_kernel(
     z, base_ref, tab_in, chip_ref, across_ref, far_ref, near_ref, hots_ref, proj_ref, first_ref, tab_ref, acc_ref
 ):
+    weighted = gathered(z, tab_in, chip_ref, across_ref, far_ref, near_ref, hots_ref)
     add_across(z, base_ref, across_ref, acc_ref)
-    weighted = gathered(z, tab_in, chip_ref, across_ref, far_ref, near_ref, hots_ref)
     for pair in range(z.cells // 2):
         rows = pair_rows(pair)
         value = acc_ref[rows, :] + nonlocal_pair(weighted[block_of(z, pair)], proj_ref, pair)
@@ -339,8 +339,8 @@
 def filtered_kernel(
     z, base_ref, tab_ref, chip_ref, across_ref, far_ref, near_ref, hots_ref, proj_ref, start_ref, out_ref, acc_ref
 ):
+    weighted = gathered(z, tab_ref, chip_ref, across_ref, far_ref, near_ref, hots_ref)
     add_across(z, base_ref, across_ref, acc_ref)
-    weighted = gathered(z, tab_ref, chip_ref, across_ref, far_ref, near_ref, hots_ref)
     for pair in range(z.cells // 2):
         rows = pair_rows(pair)
         value = acc_ref[rows, :] + nonlocal_pair(weighted[block_of(z, pair)], proj_ref, pair)

time: 72.3 us -> 72.3 us (level)
  no operation moved by 1% of the time
where the time goes in v14:
time: 72.3 us; the launch traced here: 72 us
  blocking collectives  39.6 us (55%)
  starting transfers between devices  16.1 us (22%)
  waiting for transfers between devices  7.9 us (11%)
  Pallas kernels  5.46 us (8%)
  local copies, waits for them, and re-layouts  2.46 us (3%)
    all_to_all x1, blocking collectives, local(): pieces = lax.all_to_all(pieces, 'band', 0, 0, tiled=True)  25.1 us
    all_to_all x1, blocking collectives, local(): rotated = lax.all_to_all(rotated, 'band', 0, 0, tiled=True)  14.5 us
    ppermute x2, starting transfers between devices, swap_far(): lax.ppermute(x, axis, [(i, (i + 3 - 6 * (i % 2)) % count) for i in range(...  7.38 us
    pallas_call x9, Pallas kernels, call(): pl.pallas_call(functools.partial(kernel, z), name=name, out_shape=outs, i...  5.46 us
    ppermute x2, waiting for transfers between devices, swap_far(): lax.ppermute(x, axis, [(i, (i + 3 - 6 * (i % 2)) % count) for i in range(...  5.02 us
    ppermute x2, starting transfers between devices, swap_across(): lax.ppermute(x, axis, [(i, ((i + 1 ^ 1) - 1) % count) for i in range(coun...  4.92 us
    ppermute x2, starting transfers between devices, swap_on_chip(): return lax.ppermute(x, axis, [(i, i ^ 1) for i in range(count)])  3.84 us
    ppermute x2, waiting for transfers between devices, swap_on_chip(): return lax.ppermute(x, axis, [(i, i ^ 1) for i in range(count)])  2.87 us
  transfers between devices with their start and end apart: 6, of which 4 were waited for; matrix products, arithmetic and copies ran while one was open for 0% of the time, Pallas kernels for 2%

profile of v14, /device:TPU:56, one launch (start us, length us, event | category | flops | bytes accessed | tf_op | source)
XLA Modules:
  0.0 72.0 jit_solution(15752610505029242981)
XLA Ops:
  0.0 0.0 copy-start.4
  0.1 0.6 copy-done.5
  0.7 0.3 copy-done.2
  1.0 0.3 prepare.1
  1.2 0.8 %copy-done.1 = bf16[6,16,32,4,128]{4,3,2,1,0:T(4,128)(2,1)S(1)} copy-done((bf16[6,16,32,4,128]{4,3,2,1,0:T(4,128)(2,1)S(1)}, bf16[6,16,32,4,128]{4,3,2,1,0:T(4,128)(2,1)}, u32[]{:S(2)}) %copy-start.1) | copy-done | bytes 3145752
  2.0 1.1 %project.1 = (f32[3,8,128]{2,1,0:T(8,128)S(1)}, bf16[848,128]{1,0:T(8,128)(2,1)S(1)}) custom-call(bf16[768,128]{1,0:T(8,128)(2,1)S(1)} %get-tuple-element.19.v_in, bf16[2,384,128]{2,1,0:T(8,128)(2,1)S(1)} %get-tuple-element.20.hots_ref, bf16[96,128,128]{2,1,0:T(8,128)(2,1)S(1)} %bitcast.31), custom_call_target="tpu_custom_call" | custom-call | flops 25165824 | bytes 3145728 | tf_op jit(solution)/shard_map/project/pallas_call | solution.py:355
  3.1 1.9 %collective-permute-start = (bf16[848,128]{1,0:T(8,128)(2,1)S(1)}, bf16[848,128]{1,0:T(8,128)(2,1)S(1)}, u32[]{:S(2)}, u32[]{:S(2)}) collective-permute-start(bf16[848,128]{1,0:T(8,128)(2,1)S(1)} %get-tuple-element.22.slab_in), channel_id=1, source_target_pairs={{0,16},{16,0},{32,48},{48,32},{64,80},{80,64},{96,112},{112,96},{1... | collective-permute-start | bytes 651272 | tf_op jit(solution)/shard_map/ppermute | solution.py:388
  5.1 1.4 %collective-permute-done.got_ref.on_ref = bf16[848,128]{1,0:T(8,128)(2,1)S(1)} collective-permute-done((bf16[848,128]{1,0:T(8,128)(2,1)S(1)}, bf16[848,128]{1,0:T(8,128)(2,1)S(1)}, u32[]{:S(2)}, u32[]{:S(2)}) %collective-permute-start) | collective-permute-done | bytes 217120 | tf_op jit(solution)/shard_map/ppermute | solution.py:388
  6.5 3.0 %collective-permute-start.1 = (bf16[816,128]{1,0:T(8,128)(2,1)S(1)}, bf16[816,128]{1,0:T(8,128)(2,1)S(1)}, u32[]{:S(2)}, u32[]{:S(2)}) collective-permute-start(bf16[816,128]{1,0:T(8,128)(2,1)S(1)} %get-tuple-element.23.v_ref.start_ref), channel_id=1, source_target_pairs={{0,496},{16,32},{32,16},{48,64},{64,48},{80,96},{96,80},{112,128},... | collective-permute-start | bytes 626696 | tf_op jit(solution)/shard_map/ppermute | solution.py:393
  9.5 3.7 %collective-permute-start.2 = (f32[8,128]{1,0:T(8,128)S(1)}, f32[8,128]{1,0:T(8,128)S(1)}, u32[]{:S(2)}, u32[]{:S(2)}) collective-permute-start(f32[8,128]{1,0:T(8,128)S(1)} %get-tuple-element.26), channel_id=1, source_target_pairs={{0,48},{16,480},{32,80},{48,0},{64,112},{80,32},{96,144},{112,64},... | collective-permute-start | bytes 12296 | tf_op jit(solution)/shard_map/ppermute | solution.py:398
  13.2 0.9 %base_first.1 = (f32[768,128]{1,0:T(8,128)S(1)}, f32[8,128]{1,0:T(8,128)S(1)}) custom-call(bf16[816,128]{1,0:T(8,128)(2,1)S(1)} %get-tuple-element.23.v_ref.start_ref, bf16[848,128]{1,0:T(8,128)(2,1)S(1)} %collective-permute-done.got_ref.on_ref, f32[96,128]{1,0:T(8,128)S(1)} %bitcast.36, f32[4,1024]{1,0:T(4,128)S(1)} %bitcast.38), custom_call_target="tpu_custom_call" | custom-call | flops 75497472 | bytes 983040 | tf_op jit(solution)/shard_map/base_first/pallas_call | solution.py:355
  14.1 2.4 %collective-permute-done.2.far_ref = f32[8,128]{1,0:T(8,128)S(1)} collective-permute-done((f32[8,128]{1,0:T(8,128)S(1)}, f32[8,128]{1,0:T(8,128)S(1)}, u32[]{:S(2)}, u32[]{:S(2)}) %collective-permute-start.2) | collective-permute-done | bytes 4128 | tf_op jit(solution)/shard_map/ppermute | solution.py:398
  16.6 1.7 %first.1 = (bf16[848,128]{1,0:T(8,128)(2,1)S(1)}, f32[3,8,128]{2,1,0:T(8,128)S(1)}) custom-call(f32[768,128]{1,0:T(8,128)S(1)} %get-tuple-element.24.base_ref, f32[3,8,128]{2,1,0:T(8,128)S(1)} %get-tuple-element.21.tab_ref.tab_in, f32[2,8,128]{2,1,0:T(8,128)S(1)} %get-tuple-element.25.chip_ref, bf16[816,128]{1,0:T(8,128)(2,1)S(1)} %collective-permute-done.1.across_ref, ...), custom_call_target="tpu_custom_call" | custom-call | flops 50331648 | bytes 3145728 | tf_op jit(solution)/shard_map/first/pallas_call | solution.py:355
  18.2 1.9 %collective-permute-start.3 = (bf16[848,128]{1,0:T(8,128)(2,1)S(1)}, bf16[848,128]{1,0:T(8,128)(2,1)S(1)}, u32[]{:S(2)}, u32[]{:S(2)}) collective-permute-start(bf16[848,128]{1,0:T(8,128)(2,1)S(1)} %get-tuple-element.29.slab_in), channel_id=1, source_target_pairs={{0,16},{16,0},{32,48},{48,32},{64,80},{80,64},{96,112},{112,96},{1... | collective-permute-start | bytes 651272 | tf_op jit(solution)/shard_map/ppermute | solution.py:388
  20.1 1.4 %collective-permute-done.3.got_ref.on_ref = bf16[848,128]{1,0:T(8,128)(2,1)S(1)} collective-permute-done((bf16[848,128]{1,0:T(8,128)(2,1)S(1)}, bf16[848,128]{1,0:T(8,128)(2,1)S(1)}, u32[]{:S(2)}, u32[]{:S(2)}) %collective-permute-start.3) | collective-permute-done | bytes 217120 | tf_op jit(solution)/shard_map/ppermute | solution.py:388
  21.6 1.9 %collective-permute-start.4 = (bf16[816,128]{1,0:T(8,128)(2,1)S(1)}, bf16[816,128]{1,0:T(8,128)(2,1)S(1)}, u32[]{:S(2)}, u32[]{:S(2)}) collective-permute-start(bf16[816,128]{1,0:T(8,128)(2,1)S(1)} %get-tuple-element.30.v_ref), channel_id=1, source_target_pairs={{0,496},{16,32},{32,16},{48,64},{64,48},{80,96},{96,80},{112,128},... | collective-permute-start | bytes 626696 | tf_op jit(solution)/shard_map/ppermute | solution.py:393
  23.5 3.7 %collective-permute-start.5 = (f32[8,128]{1,0:T(8,128)S(1)}, f32[8,128]{1,0:T(8,128)S(1)}, u32[]{:S(2)}, u32[]{:S(2)}) collective-permute-start(f32[8,128]{1,0:T(8,128)S(1)} %get-tuple-element.32), channel_id=1, source_target_pairs={{0,48},{16,480},{32,80},{48,0},{64,112},{80,32},{96,144},{112,64},... | collective-permute-start | bytes 12296 | tf_op jit(solution)/shard_map/ppermute | solution.py:398
  27.2 0.9 %base.1.base_ref = f32[768,128]{1,0:T(8,128)S(1)} custom-call(bf16[816,128]{1,0:T(8,128)(2,1)S(1)} %get-tuple-element.30.v_ref, bf16[848,128]{1,0:T(8,128)(2,1)S(1)} %collective-permute-done.3.got_ref.on_ref, f32[96,128]{1,0:T(8,128)S(1)} %bitcast.37), custom_call_target="tpu_custom_call" | custom-call | flops 75497472 | bytes 983040 | tf_op jit(solution)/shard_map/base/pallas_call | solution.py:355
  28.1 2.6 %collective-permute-done.5.far_ref = f32[8,128]{1,0:T(8,128)S(1)} collective-permute-done((f32[8,128]{1,0:T(8,128)S(1)}, f32[8,128]{1,0:T(8,128)S(1)}, u32[]{:S(2)}, u32[]{:S(2)}) %collective-permute-start.5) | collective-permute-done | bytes 4128 | tf_op jit(solution)/shard_map/ppermute | solution.py:398
  30.7 0.7 filtered.1
  31.4 25.1 %all_to_all.10 = bf16[16,6,8,128]{3,2,1,0:T(8,128)(2,1)S(1)} all-to-all(bf16[16,6,8,128]{3,2,1,0:T(8,128)(2,1)S(1)} %bitcast.34), channel_id=1, replica_groups=mesh['dom'=32,'band'=16] {'band'}, dimensions={0} | all-to-all | bytes 393216 | tf_op jit(solution)/shard_map/all_to_all | solution.py:446
  56.5 0.3 fusion.1
  56.8 14.5 %all_to_all.11 = bf16[16,6,8,128]{3,2,1,0:T(8,128)(2,1)S(1)} all-to-all(bf16[16,6,8,128]{3,2,1,0:T(8,128)(2,1)S(1)} %bitcast.39), channel_id=1, replica_groups=mesh['dom'=32,'band'=16] {'band'}, dimensions={0} | all-to-all | bytes 393216 | tf_op jit(solution)/shard_map/all_to_all | solution.py:450
  71.3 0.7 copy.16
  (14 shorter events, 0.1 us)
Async XLA Ops:
  0.0 56.5 %copy-start = (bf16[128,128]{1,0:T(8,128)(2,1)S(1)}, bf16[128,128]{1,0:T(8,128)(2,1)}, u32[]{:S(2)}) copy-start(bf16[128,128]{1,0:T(8,128)(2,1)} %param.11) | copy-start | bytes 98308
  0.0 0.7 copy-start.5
  0.0 0.9 %copy-start.2 = (bf16[8,6,16,128]{3,2,1,0:T(8,128)(2,1)S(1)}, bf16[8,6,16,128]{3,2,1,0:T(8,128)(2,1)}, u32[]{:S(2)}) copy-start(bf16[8,6,16,128]{3,2,1,0:T(8,128)(2,1)} %param.6) | copy-start | bytes 589828
  0.0 2.0 %copy-start.1 = (bf16[6,16,32,4,128]{4,3,2,1,0:T(4,128)(2,1)S(1)}, bf16[6,16,32,4,128]{4,3,2,1,0:T(4,128)(2,1)}, u32[]{:S(2)}) copy-start(bf16[6,16,32,4,128]{4,3,2,1,0:T(4,128)(2,1)} %param.8) | copy-start | bytes 9437188
  0.0 13.2 %copy-start.3 = (f32[6,16,128]{2,1,0:T(8,128)S(1)}, f32[6,16,128]{2,1,0:T(8,128)}, u32[]{:S(2)}) copy-start(f32[6,16,128]{2,1,0:T(8,128)} %param.7) | copy-start | bytes 147460
  0.0 13.2 %copy-start.4 = (f32[1024,4]{0,1:T(4,128)S(1)}, f32[1024,4]{0,1:T(4,128)}, u32[]{:S(2)}) copy-start(f32[1024,4]{0,1:T(4,128)} %param.10) | copy-start | bytes 49156
  3.1 3.4 %collective-permute-start = (bf16[848,128]{1,0:T(8,128)(2,1)S(1)}, bf16[848,128]{1,0:T(8,128)(2,1)S(1)}, u32[]{:S(2)}, u32[]{:S(2)}) collective-permute-start(bf16[848,128]{1,0:T(8,128)(2,1)S(1)} %get-tuple-element.22.slab_in), channel_id=1, source_target_pairs={{0,16},{16,0},{32,48},{48,32},{64,80},{80,64},{96,112},{112,96},{1... | collective-permute-start | bytes 651272 | tf_op jit(solution)/shard_map/ppermute | solution.py:388
  6.5 10.0 %collective-permute-start.1 = (bf16[816,128]{1,0:T(8,128)(2,1)S(1)}, bf16[816,128]{1,0:T(8,128)(2,1)S(1)}, u32[]{:S(2)}, u32[]{:S(2)}) collective-permute-start(bf16[816,128]{1,0:T(8,128)(2,1)S(1)} %get-tuple-element.23.v_ref.start_ref), channel_id=1, source_target_pairs={{0,496},{16,32},{32,16},{48,64},{64,48},{80,96},{96,80},{112,128},... | collective-permute-start | bytes 626696 | tf_op jit(solution)/shard_map/ppermute | solution.py:393
  9.5 7.0 %collective-permute-start.2 = (f32[8,128]{1,0:T(8,128)S(1)}, f32[8,128]{1,0:T(8,128)S(1)}, u32[]{:S(2)}, u32[]{:S(2)}) collective-permute-start(f32[8,128]{1,0:T(8,128)S(1)} %get-tuple-element.26), channel_id=1, source_target_pairs={{0,48},{16,480},{32,80},{48,0},{64,112},{80,32},{96,144},{112,64},... | collective-permute-start | bytes 12296 | tf_op jit(solution)/shard_map/ppermute | solution.py:398
  18.2 3.4 %collective-permute-start.3 = (bf16[848,128]{1,0:T(8,128)(2,1)S(1)}, bf16[848,128]{1,0:T(8,128)(2,1)S(1)}, u32[]{:S(2)}, u32[]{:S(2)}) collective-permute-start(bf16[848,128]{1,0:T(8,128)(2,1)S(1)} %get-tuple-element.29.slab_in), channel_id=1, source_target_pairs={{0,16},{16,0},{32,48},{48,32},{64,80},{80,64},{96,112},{112,96},{1... | collective-permute-start | bytes 651272 | tf_op jit(solution)/shard_map/ppermute | solution.py:388
  21.6 9.1 %collective-permute-start.4 = (bf16[816,128]{1,0:T(8,128)(2,1)S(1)}, bf16[816,128]{1,0:T(8,128)(2,1)S(1)}, u32[]{:S(2)}, u32[]{:S(2)}) collective-permute-start(bf16[816,128]{1,0:T(8,128)(2,1)S(1)} %get-tuple-element.30.v_ref), channel_id=1, source_target_pairs={{0,496},{16,32},{32,16},{48,64},{64,48},{80,96},{96,80},{112,128},... | collective-permute-start | bytes 626696 | tf_op jit(solution)/shard_map/ppermute | solution.py:393
  23.5 7.1 %collective-permute-start.5 = (f32[8,128]{1,0:T(8,128)S(1)}, f32[8,128]{1,0:T(8,128)S(1)}, u32[]{:S(2)}, u32[]{:S(2)}) collective-permute-start(f32[8,128]{1,0:T(8,128)S(1)} %get-tuple-element.32), channel_id=1, source_target_pairs={{0,48},{16,480},{32,80},{48,0},{64,112},{80,32},{96,144},{112,64},... | collective-permute-start | bytes 12296 | tf_op jit(solution)/shard_map/ppermute | solution.py:398
